TPU v7x, 32 devices: a whole 2x2x4 slice. The times are simulated.
32 devices in a mesh: seq: 8 (over z, x), head: 4 (over y, core).
Axes of the slice: x: 2, y: 2, z: 4, core: 2. Of those that a mesh axis runs over, the one named last changes fastest.
Arguments:
- history: bfloat16 [6144, 1024], P('seq'), may hold values from -6 to 6
- ln_gain: bfloat16 [1024], replicated, may hold values from 0.5 to 1.5
- w_in: bfloat16 [4, 1024, 1024], P(None, None, 'head'), may hold values from -0.1875 to 0.1875
- out_gain: bfloat16 [1024], P('head'), may hold values from 0.5 to 1.5
- w_out: bfloat16 [1024, 1024], P('head'), may hold values from -0.25 to 0.25
- block_lists: int32 [48, 16], P('seq'), may hold values from 0 to 47, as said below
- counts: int32 [48], P('seq'), may hold values from 1 to 16, as said below
Outputs:
- mixed: bfloat16 [6144, 1024], P('seq', 'head')
Inputs may be any that keep to these rules, and one draw needn't show every extreme that they name: For query block b, entries 0 to counts[b] - 1 of block_lists[b] are distinct blocks from max(0, b - 31) to b, and entry 0 is b itself; later entries equal b and are not live. counts[b] is at most min(16, b + 1); the last block has min(16, 32, 48) live entries.
All inputs are finite; a program needn't handle non-finite values.
Results may differ from a plain program's by a relative error of at most 0.008.
Values may be sent and summed in bfloat16 or wider, within the bound.
No kernel may reach another device: no remote copies, remote signals or barrier semaphores. Data moves between devices by JAX's collectives and lax.ppermute only.
A program may use at most 64 MiB of HBM per device.

v0:
```python
import jax
import jax.numpy as jnp
from jax import lax
from jax.experimental import pallas as pl
from jax.experimental.pallas import tpu as pltpu
from jax.sharding import PartitionSpec as P

DH = 128
BLK = 128
WIN = 32
MAXK = 16
EPS = 1e-05
PLANES = 2
FAR = 2 * PLANES + 1
SCALE = 0.5 * DH ** (-0.5)

NT = (((1,), (1,)), ((), ()))


def params(mib=12):
    return pltpu.CompilerParams(vmem_limit_bytes=mib << 20)


def cost(us):
    return pl.CostEstimate(flops=int(us * 1e9 * 0.3), bytes_accessed=int(us * 3e6 * 0.3), transcendentals=0)


def silu(v):
    half = 0.5 * v
    return half * jnp.tanh(half) + half


def project(rows, w):
    return silu(jnp.dot(rows, w, preferred_element_type=jnp.float32))


def normed(rows, gain):
    floats = rows.astype(jnp.float32)
    centre = jnp.mean(floats, axis=-1, keepdims=True)
    off = floats - centre
    spread_sq = jnp.mean(jnp.square(off), axis=-1, keepdims=True)
    return (off * lax.rsqrt(spread_sq + EPS) * gain.astype(jnp.float32)).astype(jnp.bfloat16)


def norm_kernel(history_ref, gain_ref, out_ref, rows_ref, gain_rows_ref, sems):
    share = out_ref.shape[0]
    steps = sems.shape[0] - 1
    step = share // steps
    first = lax.axis_index("head") * share
    gain_copy = pltpu.make_async_copy(gain_ref, gain_rows_ref, sems.at[steps])
    gain_copy.start()
    copies = []
    for i in range(steps):
        at = pl.ds(pl.multiple_of(first + i * step, step), step)
        copies.append(
            pltpu.make_async_copy(history_ref.at[at], rows_ref.at[pl.ds(i * step, step)], sems.at[i])
        )
        copies[i].start()
    gain_copy.wait()
    gain = gain_rows_ref[...].reshape(1, -1)
    for i in range(steps):
        copies[i].wait()
        at = pl.ds(i * step, step)
        out_ref[at, :] = normed(rows_ref[at, :], gain)


def mark(live_ref, told_ref, base, key_blocks, first):
    for b in range(told_ref.shape[0]):
        for g in range(key_blocks):
            live_ref[(first + b) * 8 + g] = 0.0

        def entry(t, unused):
            g = told_ref[b, t] - base
            live_ref[(first + b) * 8 + jnp.where((g >= 0) & (g < key_blocks), g, 7)] = SCALE
            return unused

        lax.fori_loop(0, told_ref[b, MAXK], entry, 0)


def tile(scores, factor):
    half = scores * factor
    return half * jnp.tanh(half) + half


def attend_dense(query_ref, rows, sums_ref, keys_t_ref, values_ref, factors):
    n, blocks = len(factors), len(factors[0])
    for h in range(query_ref.shape[1] // DH):
        cols = pl.ds(h * DH, DH)
        scores = jnp.dot(
            query_ref[rows, cols], keys_t_ref[cols, :], preferred_element_type=jnp.float32
        )
        weights = [
            jnp.concatenate(
                [
                    tile(scores[i * BLK : (i + 1) * BLK, g * BLK : (g + 1) * BLK], factors[i][g])
                    for i in range(n)
                ],
                axis=0,
            ).astype(jnp.bfloat16)
            for g in range(blocks)
        ]
        sums_ref[rows, cols] += jnp.dot(
            jnp.concatenate(weights, axis=1), values_ref[:, cols], preferred_element_type=jnp.float32
        )


def attend_all(query_ref, sums_ref, keys_t_ref, values_ref, live_ref, live_first, key_blocks):
    n = 2

    def some(p, unused):
        factors = [
            [live_ref[(live_first + n * p + i) * 8 + g] for g in range(key_blocks)] for i in range(n)
        ]

        @pl.when(sum(sum(f) for f in factors) > 0.0)
        def _():
            rows = pl.ds(pl.multiple_of(p * n * BLK, n * BLK), n * BLK)
            attend_dense(query_ref, rows, sums_ref, keys_t_ref, values_ref, factors)

        return unused

    lax.fori_loop(0, query_ref.shape[0] // (n * BLK), some, 0)


def fetch(pairs, sems):
    copies = [pltpu.make_async_copy(a, b, sems.at[i]) for i, (a, b) in enumerate(pairs)]
    for copy in copies:
        copy.start()
    return copies


def wait(copies):
    for copy in copies:
        copy.wait()


def own_kernel(
    told_ref, history_hbm, gain_hbm, w_ref,
    gate_hbm, values_hbm, query_hbm, keys_t_hbm, tail_hbm, sums_hbm,
    history_ref, gain_ref, gate_ref, values_ref, query_ref, keys_t_ref, tail_ref, sums_ref, live_ref, sems, out_sems,
):
    rows, cols = query_ref.shape
    blocks = rows // BLK
    part = 2 * BLK
    parts = [pl.ds(p * part, part) for p in range(rows // part)]
    gain_copy, *copies = fetch(
        [(gain_hbm, gain_ref)] + [(history_hbm.at[at], history_ref.at[at]) for at in parts], sems
    )
    mark(live_ref, told_ref, lax.axis_index("seq") * blocks, blocks, 0)
    gain_copy.wait()
    gain = gain_ref[...].reshape(1, -1)
    for at, copy in zip(parts, copies):
        copy.wait()
        here = normed(history_ref[at, :], gain)
        query_ref[at, :] = project(here, w_ref[2]).astype(jnp.bfloat16)
        keys = project(here, w_ref[3])
        keys_t_ref[:, at] = keys.T.astype(jnp.bfloat16)
        values = project(here, w_ref[1]).astype(jnp.bfloat16)
        values_ref[at, :] = values
        gate_ref[at, :] = project(here, w_ref[0]).astype(jnp.bfloat16)
    tail_ref[0] = keys[-BLK:].astype(jnp.bfloat16)
    tail_ref[1] = values[-BLK:]
    done = [
        (query_ref, query_hbm), (values_ref, values_hbm), (keys_t_ref, keys_t_hbm),
        (gate_ref, gate_hbm), (tail_ref, tail_hbm), (sums_ref, sums_hbm),
    ]
    out = fetch(done[:-1], out_sems)
    behind = lax.broadcasted_iota(jnp.int32, (BLK, BLK), 1) <= lax.broadcasted_iota(
        jnp.int32, (BLK, BLK), 0
    )
    for p in range(blocks // 2):
        q_rows = pl.ds(p * 2 * BLK, 2 * BLK)
        seen = pl.ds(0, (2 * p + 2) * BLK)
        for h in range(cols // DH):
            at = pl.ds(h * DH, DH)
            scores = jnp.dot(
                query_ref[q_rows, at], keys_t_ref[at, seen], preferred_element_type=jnp.float32
            )
            weights = []
            for g in range(2 * p + 2):
                column = []
                for i in range(2):
                    b = 2 * p + i
                    if g > b:
                        column.append(jnp.zeros((BLK, BLK), jnp.float32))
                        continue
                    some = tile(
                        scores[i * BLK : (i + 1) * BLK, g * BLK : (g + 1) * BLK], live_ref[b * 8 + g]
                    )
                    column.append(jnp.where(behind, some, 0.0) if g == b else some)
                weights.append(jnp.concatenate(column, axis=0).astype(jnp.bfloat16))
            sums_ref[q_rows, at] = jnp.dot(
                jnp.concatenate(weights, axis=1),
                values_ref[seen, at],
                preferred_element_type=jnp.float32,
            )
    last = pltpu.make_async_copy(sums_ref, sums_hbm, out_sems.at[len(done) - 1])
    last.start()
    wait(out + [last])


def centred(part):
    return part - jnp.mean(part, axis=-1, keepdims=True)


def send_off(sums_ref, send_ref):
    for h in range(send_ref.shape[1] // DH):
        at = pl.ds(h * DH, DH)
        send_ref[:, at] = centred(sums_ref[:, at]).astype(jnp.bfloat16)


def far_kernel(
    told_ref, query_ref, keys_t_hbm, values_hbm, send_ref, keys_t_ref, values_ref, sums_ref, live_ref, sems
):
    blocks = query_ref.shape[0] // BLK
    here = lax.axis_index("seq")

    @pl.when((here % 2 == 1) & (here + FAR < lax.axis_size("seq")))
    def _():
        copies = fetch([(keys_t_hbm, keys_t_ref), (values_hbm, values_ref)], sems)
        mark(live_ref, told_ref, here * blocks, blocks, 0)
        sums_ref[...] = jnp.zeros_like(sums_ref)
        wait(copies)
        attend_all(query_ref, sums_ref, keys_t_ref, values_ref, live_ref, 0, blocks)
        send_off(sums_ref, send_ref)


def chunk_keys(pieces, w_ref, keys_ref, keys_t_ref, values_ref):
    share = pieces[0].shape[0]
    for m, piece in enumerate(pieces):
        at = pl.ds(pl.multiple_of((lax.axis_index("head") ^ m) * share, share), share)
        keys_ref[at, :] = project(piece[...], w_ref[3])
        values_ref[at, :] = project(piece[...], w_ref[1]).astype(jnp.bfloat16)
    keys_t_ref[...] = keys_ref[...].T.astype(jnp.bfloat16)


def make_chunk_kernel(back, n_head):
    def kernel(told_ref, told_x_ref, *refs):
        pieces, refs = refs[:n_head], refs[n_head:]
        w_ref, query_hbm, query_x_hbm, own_t_hbm, own_values_hbm, before_hbm, sums_hbm, sums_x_hbm = refs[:8]
        query_ref, query_x_ref, own_t_ref, own_values_ref, sums_ref, sums_x_ref = refs[8:14]
        keys_ref, keys_t_ref, values_ref, live_ref, sems, out_sems = refs[14:]
        blocks = query_ref.shape[0] // BLK
        here = lax.axis_index("seq")
        source = here - 2 * back
        copies = fetch(
            [
                (query_x_hbm, query_x_ref), (own_t_hbm, own_t_ref), (own_values_hbm, own_values_ref),
                (before_hbm, sums_ref), (query_hbm, query_ref),
            ],
            sems,
        )
        sums_x_ref[...] = jnp.zeros_like(sums_x_ref)
        mark(live_ref, told_x_ref, here * blocks, blocks, 0)

        @pl.when(source >= 0)
        def _():
            chunk_keys(pieces, w_ref, keys_ref, keys_t_ref, values_ref)

        wait(copies)
        attend_all(query_x_ref, sums_x_ref, own_t_ref, own_values_ref, live_ref, 0, blocks)

        @pl.when(source >= 0)
        def _():
            mark(live_ref, told_ref, source * blocks, blocks, 0)
            mark(live_ref, told_x_ref, source * blocks, blocks, blocks)
            attend_all(query_ref, sums_ref, keys_t_ref, values_ref, live_ref, 0, blocks)
            attend_all(query_x_ref, sums_x_ref, keys_t_ref, values_ref, live_ref, blocks, blocks)

        wait(fetch([(sums_ref, sums_hbm), (sums_x_ref, sums_x_hbm)], out_sems))

    return kernel


def make_last_kernel(back, n_head):
    def kernel(told_x_ref, *refs):
        pieces, refs = refs[:n_head], refs[n_head:]
        w_ref, query_x_hbm, before_hbm, send_ref, keys_t_ref, values_ref = refs[:6]
        query_x_ref, sums_ref, keys_ref, live_ref, sems = refs[6:]
        blocks = query_x_ref.shape[0] // BLK
        source = lax.axis_index("seq") - 2 * back
        copies = fetch([(query_x_hbm, query_x_ref), (before_hbm, sums_ref)], sems)

        @pl.when(source >= 0)
        def _():
            chunk_keys(pieces, w_ref, keys_ref, keys_t_ref, values_ref)
            mark(live_ref, told_x_ref, source * blocks, blocks, 0)

        wait(copies)

        @pl.when(source >= 0)
        def _():
            attend_all(query_x_ref, sums_ref, keys_t_ref, values_ref, live_ref, 0, blocks)

        send_off(sums_ref, send_ref)

    return kernel


def make_own_last_kernel(back):
    def kernel(
        told_ref, query_hbm, keys_t_ref, values_ref, tail_ref, before_hbm, sums_ref, query_ref, live_ref, sems
    ):
        rows, cols = query_ref.shape
        blocks = rows // BLK
        here = lax.axis_index("seq")
        source = here - 2 * back
        copies = fetch([(query_hbm, query_ref), (before_hbm, sums_ref)], sems)
        mark(live_ref, told_ref, source * blocks, blocks, 0)
        wait(copies)

        @pl.when(source >= 0)
        def _():
            attend_all(query_ref, sums_ref, keys_t_ref, values_ref, live_ref, 0, blocks)

        farthest = here - FAR - 1

        @pl.when(farthest >= 0)
        def _():
            mark(live_ref, told_ref, farthest * blocks + blocks - 1, 1, 0)
            for h in range(cols // DH):
                at = pl.ds(h * DH, DH)
                scores = lax.dot_general(
                    query_ref[0:BLK, at], tail_ref[0, :, at], NT, preferred_element_type=jnp.float32
                )
                weights = tile(scores, live_ref[0]).astype(jnp.bfloat16)
                sums_ref[0:BLK, at] += jnp.dot(
                    weights, tail_ref[1, :, at], preferred_element_type=jnp.float32
                )

    return kernel


def finish_kernel(sums_ref, near_ref, far_ref, gate_ref, gain_ref, out_ref):
    for h in range(sums_ref.shape[1] // DH):
        at = pl.ds(h * DH, DH)
        part = centred(sums_ref[:, at])
        part = part + near_ref[:, at].astype(jnp.float32) + far_ref[:, at].astype(jnp.float32)
        off = centred(part)
        spread_sq = jnp.mean(jnp.square(off), axis=-1, keepdims=True)
        out_ref[:, at] = (
            off
            * lax.rsqrt(spread_sq + EPS)
            * gain_ref[at].reshape(1, -1).astype(jnp.float32)
            * gate_ref[:, at].astype(jnp.float32)
        ).astype(jnp.bfloat16)


def mix(total, pieces, first, w_ref):
    cols = pieces[0].shape[1]
    for m, piece in enumerate(pieces, start=first):
        at = pl.ds(pl.multiple_of((lax.axis_index("head") ^ m) * cols, cols), cols)
        total = total + jnp.dot(piece[...], w_ref[at, :], preferred_element_type=jnp.float32)
    return total


def near_out_kernel(*refs):
    *pieces, w_ref, history_hbm, out_ref, history_ref, sem = refs
    cols = out_ref.shape[1]
    at = pl.ds(pl.multiple_of(lax.axis_index("head") * cols, cols), cols)
    copy = pltpu.make_async_copy(history_hbm.at[:, at], history_ref, sem)
    copy.start()
    total = mix(jnp.zeros(out_ref.shape, jnp.float32), pieces, 0, w_ref)
    copy.wait()
    out_ref[...] = total + history_ref[...].astype(jnp.float32)


def far_out_kernel(*refs):
    *pieces, w_ref, near_ref, out_ref = refs
    out_ref[...] = mix(near_ref[...], pieces, len(pieces), w_ref).astype(jnp.bfloat16)


def crossed(array, axis, bit):
    return lax.ppermute(array, axis, [(i, i ^ bit) for i in range(lax.axis_size(axis))])


def spread(piece, bit):
    pieces = {0: piece}
    while bit:
        pieces.update({m + bit: crossed(p, "head", bit) for m, p in list(pieces.items())})
        bit //= 2
    return [pieces[m] for m in sorted(pieces)]


def body(history, ln_gain, w_in, out_gain, w_out, block_lists, counts):
    tok_rows, width = history.shape
    blocks = counts.shape[0]
    cols = w_in.shape[2]
    n_seq, n_head = lax.axis_size("seq"), lax.axis_size("head")
    assert 2 * (PLANES + 1) * blocks - (WIN - 1) == blocks - 1
    barrier = lax.optimization_barrier

    shape = lambda like, *dims: jax.ShapeDtypeStruct(dims, like)
    bf16, f32 = jnp.bfloat16, jnp.float32
    wide = pl.BlockSpec(memory_space=pltpu.VMEM)
    flat = pl.BlockSpec(memory_space=pltpu.SMEM)
    far_off = pl.BlockSpec(memory_space=pltpu.HBM)
    n_live = 2 * blocks * 8
    upright, lying = (tok_rows, cols), (cols, tok_rows)
    sems = lambda n: pltpu.SemaphoreType.DMA((n,))
    live = pltpu.SMEM((n_live,), f32)

    told = jnp.concatenate([block_lists, counts[:, None]], axis=1)
    share_rows = tok_rows // n_head
    steps = share_rows // 48
    share = pl.pallas_call(
        norm_kernel,
        in_specs=[far_off] * 2,
        out_specs=wide,
        out_shape=shape(bf16, share_rows, width),
        scratch_shapes=[
            pltpu.VMEM((share_rows, width), bf16),
            pltpu.VMEM((width,), bf16),
            sems(steps + 1),
        ],
        cost_estimate=cost(2),
        compiler_params=params(60),
    )(history, ln_gain)
    gain, told, share = barrier((ln_gain, told, share))
    upward = [(i, i + 2) for i in range(n_seq - 2)]
    downward = [(i, i - FAR) for i in range(FAR + 1, n_seq, 2)]
    share_1 = lax.ppermute(share, "seq", upward)
    told_x = crossed(told, "seq", 1)
    told_far = lax.ppermute(told, "seq", downward)

    gate, values, query, keys_t, tail, own_sums = pl.pallas_call(
        own_kernel,
        in_specs=[flat, far_off, far_off, wide],
        out_specs=[far_off] * 6,
        out_shape=[shape(bf16, *upright)] * 3
        + [shape(bf16, *lying), shape(bf16, 2, BLK, cols), shape(f32, *upright)],
        scratch_shapes=[pltpu.VMEM((tok_rows, width), bf16), pltpu.VMEM((width,), bf16)]
        + [pltpu.VMEM(upright, bf16)] * 3
        + [pltpu.VMEM(lying, bf16), pltpu.VMEM((2, BLK, cols), bf16), pltpu.VMEM(upright, f32), live]
        + [sems(1 + tok_rows // (2 * BLK)), sems(6)],
        compiler_params=params(),
        cost_estimate=cost(6),
    )(told, history, gain, w_in)
    query_x = crossed(query, "seq", 1)

    share_1, query, told_x, told_far = barrier((share_1, query, told_x, told_far))
    share_2 = lax.ppermute(share_1, "seq", upward)
    chunk_1 = spread(share_1, n_head // 2)
    query_far = lax.ppermute(query, "seq", downward)
    tail = lax.ppermute(tail, "seq", [(i, i + FAR + 1) for i in range(n_seq - FAR - 1)])
    cross_2 = crossed(share_2, "head", n_head // 2)
    near_2 = spread(share_2, n_head // 4)

    far = pl.pallas_call(
        far_kernel,
        in_specs=[flat, wide, far_off, far_off],
        out_specs=wide,
        out_shape=shape(bf16, *upright),
        scratch_shapes=[
            pltpu.VMEM(lying, bf16), pltpu.VMEM(upright, bf16), pltpu.VMEM(upright, f32), live, sems(2)
        ],
        compiler_params=params(),
        cost_estimate=cost(2),
    )(told_far, query_far, keys_t, values)

    sums, sums_x = pl.pallas_call(
        make_chunk_kernel(1, n_head),
        in_specs=[flat] * 2 + [wide] * (n_head + 1) + [far_off] * 5,
        out_specs=[far_off] * 2,
        out_shape=[shape(f32, *upright)] * 2,
        scratch_shapes=[
            pltpu.VMEM(dims, kind)
            for dims, kind in (
                (upright, bf16), (upright, bf16), (lying, bf16), (upright, bf16), (upright, f32),
                (upright, f32), (upright, f32), (lying, bf16), (upright, bf16),
            )
        ]
        + [live, sems(5), sems(2)],
        compiler_params=params(16),
        cost_estimate=cost(6),
    )(told, told_x, *chunk_1, w_in, query, query_x, keys_t, values, own_sums)

    cross_2, sums_x, far, tail = barrier((cross_2, sums_x, far, tail))
    far = lax.ppermute(far, "seq", [(i, i + FAR) for i in range(1, n_seq - FAR, 2)])
    send, keys_t, values = pl.pallas_call(
        make_last_kernel(PLANES, n_head),
        in_specs=[flat] + [wide] * (n_head + 1) + [far_off] * 2,
        out_specs=[wide] * 3,
        out_shape=[shape(bf16, *upright), shape(bf16, *lying), shape(bf16, *upright)],
        scratch_shapes=[
            pltpu.VMEM(upright, bf16), pltpu.VMEM(upright, f32), pltpu.VMEM(upright, f32), live, sems(2)
        ],
        compiler_params=params(),
        cost_estimate=cost(4),
    )(told_x, *near_2, *spread(cross_2, n_head // 4), w_in, query_x, sums_x)
    near = crossed(send, "seq", 1)
    w_out, send = barrier((w_out, send))
    w_mine = lax.all_to_all(w_out, "head", split_axis=1, concat_axis=0, tiled=True)
    mine = pl.pallas_call(
        make_own_last_kernel(PLANES),
        in_specs=[flat, far_off, wide, wide, wide, far_off],
        out_specs=wide,
        out_shape=shape(f32, *upright),
        scratch_shapes=[pltpu.VMEM(upright, bf16), live, sems(2)],
        compiler_params=params(),
        cost_estimate=cost(3),
    )(told, query, keys_t, values, tail, sums)
    near, mine, w_mine = barrier((near, mine, w_mine))
    gated = pl.pallas_call(
        finish_kernel,
        in_specs=[wide] * 5,
        out_specs=wide,
        out_shape=shape(bf16, *upright),
        compiler_params=params(),
        cost_estimate=cost(1),
    )(mine, near, far, gate, out_gain)

    out_cols = width // n_head
    cross_gated = crossed(gated, "head", n_head // 2)
    near_gated = spread(gated, n_head // 4)
    mixed = pl.pallas_call(
        near_out_kernel,
        in_specs=[wide] * (n_head // 2 + 1) + [far_off],
        out_specs=wide,
        out_shape=shape(f32, tok_rows, out_cols),
        scratch_shapes=[pltpu.VMEM((tok_rows, out_cols), bf16), pltpu.SemaphoreType.DMA],
        compiler_params=params(),
        cost_estimate=cost(2),
    )(*near_gated, w_mine, history)
    cross_gated, mixed = barrier((cross_gated, mixed))
    return pl.pallas_call(
        far_out_kernel,
        in_specs=[wide] * (n_head // 2 + 2),
        out_specs=wide,
        out_shape=shape(bf16, tok_rows, out_cols),
        compiler_params=params(),
        cost_estimate=cost(2),
    )(*spread(cross_gated, n_head // 4), w_mine, mixed)


def solution(mesh):
    placed = (
        P("seq", None),
        P(),
        P(None, None, "head"),
        P("head"),
        P("head", None),
        P("seq", None),
        P("seq"),
    )
    return jax.shard_map(
        body, mesh=mesh, in_specs=placed, out_specs=P("seq", "head"), check_vma=False
    )
```

profile of v0, /device:TPU:25, one launch (start us, length us, event | category | flops | bytes accessed | tf_op | source)
XLA Modules:
  0.0 94.7 jit_solution(1350790743921829072)
XLA Ops:
  0.0 0.9 copy.8
  0.9 2.5 %shard_map.73 = bf16[192,1024]{1,0:T(8,128)(2,1)} custom-call(bf16[768,1024]{1,0:T(8,128)(2,1)} %refs_3_.1, bf16[1024]{0:T(1024)(128)(2,1)} %gain_hbm), custom_call_target="tpu_custom_call" | custom-call | flops 600000000 | bytes 1800000 | tf_op jit(solution)/shard_map/pallas_call | solution.py:406
  3.4 0.1 pad_add_fusion.told_ref
  3.5 1.3 %collective-permute-start = (bf16[192,1024]{1,0:T(8,128)(2,1)}, bf16[192,1024]{1,0:T(8,128)(2,1)S(1)}, u32[]{:S(2)}, u32[]{:S(2)}) collective-permute-start(bf16[192,1024]{1,0:T(8,128)(2,1)} %shard_map.73), channel_id=1, source_target_pairs={{0,8},{4,12},{8,16},{12,20},{16,24},{20,28},{1,9},{5,13},{9,17},{1... | collective-permute-start | bytes 1179656 | tf_op jit(solution)/shard_map/ppermute | solution.py:422
  4.8 1.3 %collective-permute-start.1 = (s32[6,17]{1,0:T(8,128)S(1)}, s32[6,17]{1,0:T(8,128)S(1)}, u32[]{:S(2)}, u32[]{:S(2)}) collective-permute-start(s32[6,17]{1,0:T(8,128)S(1)} %pad_add_fusion.told_ref), channel_id=1, source_target_pairs={{0,4},{4,0},{8,12},{12,8},{16,20},{20,16},{24,28},{28,24},{1,5},{5... | collective-permute-start | bytes 1232 | tf_op jit(solution)/shard_map/ppermute | solution.py:374
  6.1 3.7 %collective-permute-start.2 = (s32[6,17]{1,0:T(8,128)S(1)}, s32[6,17]{1,0:T(8,128)S(1)}, u32[]{:S(2)}, u32[]{:S(2)}) collective-permute-start(s32[6,17]{1,0:T(8,128)S(1)} %pad_add_fusion.told_ref), channel_id=1, source_target_pairs={{24,4},{25,5},{26,6},{27,7}} | collective-permute-start | bytes 1232 | tf_op jit(solution)/shard_map/ppermute | solution.py:424
  9.9 0.0 copy-start.1
  9.9 1.4 %copy-done.1 = bf16[768,1024]{1,0:T(8,128)(2,1)S(1)} copy-done((bf16[768,1024]{1,0:T(8,128)(2,1)S(1)}, bf16[768,1024]{1,0:T(8,128)(2,1)}, u32[]{:S(2)}) %copy-start.1) | copy-done | bytes 1572888
  11.3 6.5 %shard_map.74 = (bf16[768,256]{1,0:T(8,128)(2,1)S(1)}, bf16[768,256]{1,0:T(8,128)(2,1)S(1)}, bf16[768,256]{1,0:T(8,128)(2,1)S(1)}, bf16[256,768]{1,0:T(8,128)(2,...) custom-call(s32[6,17]{1,0:T(8,128)S(1)} %pad_add_fusion.told_ref, bf16[768,1024]{1,0:T(8,128)(2,1)S(1)} %copy-done.1, ...), custom_call_target="tpu_custom_call" | custom-call | flops 1800000000 | bytes 5400000 | tf_op jit(solution)/shard_map/pallas_call | solution.py:426
  17.8 0.0 copy-start.4
  17.8 1.3 %collective-permute-start.7 = (bf16[192,1024]{1,0:T(8,128)(2,1)S(1)}, bf16[192,1024]{1,0:T(8,128)(2,1)S(1)}, u32[]{:S(2)}, u32[]{:S(2)}) collective-permute-start(bf16[192,1024]{1,0:T(8,128)(2,1)S(1)} %collective-permute-done.refs_0_), channel_id=1, source_target_pairs={{0,2},{1,3},{2,0},{3,1},{4,6},{5,7},{6,4},{7,5},{8,10},{9,11},{10,... | collective-permute-start | bytes 1179656 | tf_op jit(solution)/shard_map/ppermute | solution.py:374
  19.1 1.3 %collective-permute-start.3 = (bf16[192,1024]{1,0:T(8,128)(2,1)S(1)}, bf16[192,1024]{1,0:T(8,128)(2,1)S(1)}, u32[]{:S(2)}, u32[]{:S(2)}) collective-permute-start(bf16[192,1024]{1,0:T(8,128)(2,1)S(1)} %collective-permute-done.refs_0_), channel_id=1, source_target_pairs={{0,8},{4,12},{8,16},{12,20},{16,24},{20,28},{1,9},{5,13},{9,17},{1... | collective-permute-start | bytes 1179656 | tf_op jit(solution)/shard_map/ppermute | solution.py:442
  20.4 2.8 %collective-permute-start.10 = (bf16[768,256]{1,0:T(8,128)(2,1)S(1)}, bf16[768,256]{1,0:T(8,128)(2,1)S(1)}, u32[]{:S(2)}, u32[]{:S(2)}) collective-permute-start(bf16[768,256]{1,0:T(8,128)(2,1)S(1)} %get-tuple-element.39.refs_5_.query_hbm), channel_id=1, source_target_pairs={{24,4},{25,5},{26,6},{27,7}} | collective-permute-start | bytes 1179656 | tf_op jit(solution)/shard_map/ppermute | solution.py:444
  23.2 0.1 collective-permute-start.9
  23.3 2.1 %collective-permute-start.6 = (bf16[192,1024]{1,0:T(8,128)(2,1)S(1)}, bf16[192,1024]{1,0:T(8,128)(2,1)S(1)}, u32[]{:S(2)}, u32[]{:S(2)}) collective-permute-start(bf16[192,1024]{1,0:T(8,128)(2,1)S(1)} %collective-permute-done.refs_0_), channel_id=1, source_target_pairs={{0,1},{1,0},{2,3},{3,2},{4,5},{5,4},{6,7},{7,6},{8,9},{9,8},{10,11... | collective-permute-start | bytes 1179656 | tf_op jit(solution)/shard_map/ppermute | solution.py:374
  25.4 1.6 %collective-permute-done.7.refs_2_ = bf16[192,1024]{1,0:T(8,128)(2,1)S(1)} collective-permute-done((bf16[192,1024]{1,0:T(8,128)(2,1)S(1)}, bf16[192,1024]{1,0:T(8,128)(2,1)S(1)}, u32[]{:S(2)}, u32[]{:S(2)}) %collective-permute-start.7) | collective-permute-done | bytes 393248 | tf_op jit(solution)/shard_map/ppermute | solution.py:374
  27.0 2.4 %collective-permute-start.8 = (bf16[192,1024]{1,0:T(8,128)(2,1)S(1)}, bf16[192,1024]{1,0:T(8,128)(2,1)S(1)}, u32[]{:S(2)}, u32[]{:S(2)}) collective-permute-start(bf16[192,1024]{1,0:T(8,128)(2,1)S(1)} %collective-permute-done.7.refs_2_), channel_id=1, source_target_pairs={{0,1},{1,0},{2,3},{3,2},{4,5},{5,4},{6,7},{7,6},{8,9},{9,8},{10,11... | collective-permute-start | bytes 1179656 | tf_op jit(solution)/shard_map/ppermute | solution.py:374
  29.4 0.4 collective-permute-done.3.refs_0_
  29.8 0.8 collective-permute-start.5
  30.7 1.3 %collective-permute-start.11 = (bf16[2,128,256]{2,1,0:T(8,128)(2,1)S(1)}, bf16[2,128,256]{2,1,0:T(8,128)(2,1)S(1)}, u32[]{:S(2)}, u32[]{:S(2)}) collective-permute-start(bf16[2,128,256]{2,1,0:T(8,128)(2,1)S(1)} %get-tuple-element.45), channel_id=1, source_target_pairs={{0,24},{4,28},{1,25},{5,29},{2,26},{6,30},{3,27},{7,31}} | collective-permute-start | bytes 393224 | tf_op jit(solution)/shard_map/ppermute | solution.py:445
  31.9 1.4 %shard_map.76 = bf16[768,256]{1,0:T(8,128)(2,1)} custom-call(s32[6,17]{1,0:T(8,128)S(1)} %collective-permute-done.2.told_ref, bf16[768,256]{1,0:T(8,128)(2,1)S(1)} %collective-permute-done.10.query_ref, bf16[256,768]{1,0:T(8,128)(2,1)S(1)} %get-tuple-element.40.refs_7_.keys_t_hbm, bf16[768,256]{1,0:T(8,128)(2,1)S(1)} %get-tuple-element.41.refs_8_.values_hbm), custom_call_target="tpu_custom_call" | custom-call | flops 600000000 | bytes 1800000 | tf_op jit(solution)/shard_map/pallas_call | solution.py:449
  33.4 2.5 %collective-permute-start.4 = (bf16[192,1024]{1,0:T(8,128)(2,1)S(1)}, bf16[192,1024]{1,0:T(8,128)(2,1)S(1)}, u32[]{:S(2)}, u32[]{:S(2)}) collective-permute-start(bf16[192,1024]{1,0:T(8,128)(2,1)S(1)} %collective-permute-done.3.refs_0_), channel_id=1, source_target_pairs={{0,1},{1,0},{2,3},{3,2},{4,5},{5,4},{6,7},{7,6},{8,9},{9,8},{10,11... | collective-permute-start | bytes 1179656 | tf_op jit(solution)/shard_map/ppermute | solution.py:374
  35.8 10.4 %shard_map.75 = (f32[768,256]{1,0:T(8,128)S(1)}, f32[768,256]{1,0:T(8,128)S(1)}) custom-call(s32[6,17]{1,0:T(8,128)S(1)} %pad_add_fusion.told_ref, s32[6,17]{1,0:T(8,128)S(1)} %collective-permute-done.1.told_x_ref, bf16[192,1024]{1,0:T(8,128)(2,1)S(1)} %collective-permute-done.refs_0_, bf16[192,1024]{1,0:T(8,128)(2,1)S(1)} %collective-permute-done.6.refs_1_, ...), custom_call_target="tpu_custom_call" | custom-call | flops 1800000000 | bytes 5400000 | tf_op jit(solution)/shard_map/pallas_call | solution.py:461
  46.3 0.0 copy-start.14
  46.3 0.1 collective-permute-start.12
  46.4 1.7 %collective-permute-done.12.refs_3_ = bf16[192,1024]{1,0:T(8,128)(2,1)S(1)} collective-permute-done((bf16[192,1024]{1,0:T(8,128)(2,1)S(1)}, bf16[192,1024]{1,0:T(8,128)(2,1)S(1)}, u32[]{:S(2)}, u32[]{:S(2)}) %collective-permute-start.12) | collective-permute-done | bytes 393248 | tf_op jit(solution)/shard_map/ppermute | solution.py:374
  48.1 4.9 %shard_map.77 = (bf16[768,256]{1,0:T(8,128)(2,1)S(1)}, bf16[256,768]{1,0:T(8,128)(2,1)S(1)}, bf16[768,256]{1,0:T(8,128)(2,1)S(1)}) custom-call(s32[6,17]{1,0:T(8,128)S(1)} %collective-permute-done.1.told_x_ref, bf16[192,1024]{1,0:T(8,128)(2,1)S(1)} %collective-permute-done.3.refs_0_, bf16[192,1024]{1,0:T(8,128)(2,1)S(1)} %collective-permute-done.4.refs_1_, ...), custom_call_target="tpu_custom_call" | custom-call | flops 1200000000 | bytes 3600000 | tf_op jit(solution)/shard_map/pallas_call | solution.py:480
  53.0 0.7 copy-done.9
  53.8 0.9 copy.12
  54.7 0.0 copy-done.6
  54.7 0.1 copy-done.7
  54.8 3.7 %all-to-all-start = ((bf16[256,4,256]{2,0,1:T(8,128)(2,1)}), bf16[256,4,256]{2,0,1:T(8,128)(2,1)S(1)}, u32[]{:S(2)}, u32[]{:S(2)}) async-start(bf16[256,4,256]{2,0,1:T(8,128)(2,1)} %bitcast.7), calls=%async_computation | async-start | bytes 1048576 | tf_op jit(solution)/shard_map/all_to_all | solution.py:493
  58.5 1.5 %collective-permute-start.14 = (bf16[768,256]{1,0:T(8,128)(2,1)}, bf16[768,256]{1,0:T(8,128)(2,1)}, u32[]{:S(2)}, u32[]{:S(2)}) collective-permute-start(bf16[768,256]{1,0:T(8,128)(2,1)} %shard_map.76), channel_id=1, source_target_pairs={{4,24},{5,25},{6,26},{7,27}} | collective-permute-start | bytes 1179656 | tf_op jit(solution)/shard_map/ppermute | solution.py:479
  60.0 0.0 copy-start.5
  60.0 1.0 %copy-done.5 = bf16[768,256]{1,0:T(8,128)(2,1)S(1)} copy-done((bf16[768,256]{1,0:T(8,128)(2,1)S(1)}, bf16[768,256]{1,0:T(8,128)(2,1)}, u32[]{:S(2)}) %copy-start.5) | copy-done | bytes 393240
  61.0 1.0 %copy-done.8 = bf16[256,768]{1,0:T(8,128)(2,1)S(1)} copy-done((bf16[256,768]{1,0:T(8,128)(2,1)S(1)}, bf16[256,768]{1,0:T(8,128)(2,1)}, u32[]{:S(2)}) %copy-start.8) | copy-done | bytes 393240
  62.0 1.0 %copy-done.10 = bf16[768,256]{1,0:T(8,128)(2,1)S(1)} copy-done((bf16[768,256]{1,0:T(8,128)(2,1)S(1)}, bf16[768,256]{1,0:T(8,128)(2,1)}, u32[]{:S(2)}) %copy-start.10) | copy-done | bytes 393240
  63.0 1.1 %copy-done.13 = f32[768,256]{1,0:T(8,128)S(1)} copy-done((f32[768,256]{1,0:T(8,128)S(1)}, f32[768,256]{1,0:T(8,128)}, u32[]{:S(2)}) %copy-start.13) | copy-done | bytes 786456
  64.1 4.3 %shard_map.78.sums_ref = f32[768,256]{1,0:T(8,128)S(1)} custom-call(s32[6,17]{1,0:T(8,128)S(1)} %pad_add_fusion.told_ref, bf16[768,256]{1,0:T(8,128)(2,1)S(1)} %copy-done.5, bf16[256,768]{1,0:T(8,128)(2,1)S(1)} %copy-done.8, bf16[768,256]{1,0:T(8,128)(2,1)S(1)} %copy-done.10, bf16[2,128,256]{2,1,0:T(8,128)(2,1)S(1)} %collective-permute-done.11.tail_ref, ...), custom_call_target="tpu_custom_call" | custom-call | flops 900000000 | bytes 2700000 | tf_op jit(solution)/shard_map/pallas_call | solution.py:494
  68.4 9.5 %collective-permute-done.13.near_ref = bf16[768,256]{1,0:T(8,128)(2,1)} collective-permute-done((bf16[768,256]{1,0:T(8,128)(2,1)}, bf16[768,256]{1,0:T(8,128)(2,1)}, u32[]{:S(2)}, u32[]{:S(2)}) %collective-permute-start.13) | collective-permute-done | bytes 393248 | tf_op jit(solution)/shard_map/ppermute | solution.py:374
  78.0 1.8 %shard_map.79.refs_0_ = bf16[768,256]{1,0:T(8,128)(2,1)S(1)} custom-call(f32[768,256]{1,0:T(8,128)S(1)} %shard_map.78.sums_ref, bf16[768,256]{1,0:T(8,128)(2,1)} %collective-permute-done.13.near_ref, bf16[768,256]{1,0:T(8,128)(2,1)} %collective-permute-done.14.far_ref, bf16[768,256]{1,0:T(8,128)(2,1)S(1)} %get-tuple-element.57.gate_ref, ...), custom_call_target="tpu_custom_call" | custom-call | flops 300000000 | bytes 900000 | tf_op jit(solution)/shard_map/pallas_call | solution.py:504
  79.8 0.9 collective-permute-start.16
  80.7 1.4 %collective-permute-start.15 = (bf16[768,256]{1,0:T(8,128)(2,1)S(1)}, bf16[768,256]{1,0:T(8,128)(2,1)S(1)}, u32[]{:S(2)}, u32[]{:S(2)}) collective-permute-start(bf16[768,256]{1,0:T(8,128)(2,1)S(1)} %shard_map.79.refs_0_), channel_id=1, source_target_pairs={{0,2},{1,3},{2,0},{3,1},{4,6},{5,7},{6,4},{7,5},{8,10},{9,11},{10,... | collective-permute-start | bytes 1179656 | tf_op jit(solution)/shard_map/ppermute | solution.py:374
  82.1 0.5 shard_map.80.refs_3_
  82.6 8.8 %collective-permute-done.15.refs_0_ = bf16[768,256]{1,0:T(8,128)(2,1)S(1)} collective-permute-done((bf16[768,256]{1,0:T(8,128)(2,1)S(1)}, bf16[768,256]{1,0:T(8,128)(2,1)S(1)}, u32[]{:S(2)}, u32[]{:S(2)}) %collective-permute-start.15) | collective-permute-done | bytes 393248 | tf_op jit(solution)/shard_map/ppermute | solution.py:374
  91.4 0.8 collective-permute-start.17
  92.3 1.3 %collective-permute-done.17.refs_1_ = bf16[768,256]{1,0:T(8,128)(2,1)S(1)} collective-permute-done((bf16[768,256]{1,0:T(8,128)(2,1)S(1)}, bf16[768,256]{1,0:T(8,128)(2,1)S(1)}, u32[]{:S(2)}, u32[]{:S(2)}) %collective-permute-start.17) | collective-permute-done | bytes 393248 | tf_op jit(solution)/shard_map/ppermute | solution.py:374
  93.6 1.1 %shard_map.81 = bf16[768,256]{1,0:T(8,128)(2,1)} custom-call(bf16[768,256]{1,0:T(8,128)(2,1)S(1)} %collective-permute-done.15.refs_0_, bf16[768,256]{1,0:T(8,128)(2,1)S(1)} %collective-permute-done.17.refs_1_, bf16[1024,256]{1,0:T(8,128)(2,1)S(1)} %bitcast.9, f32[768,256]{1,0:T(8,128)S(1)} %shard_map.80.refs_3_), custom_call_target="tpu_custom_call" | custom-call | flops 600000000 | bytes 1800000 | tf_op jit(solution)/shard_map/pallas_call | solution.py:526
  (34 shorter events, 0.1 us)
Async XLA Ops:
  0.0 9.8 %copy-start.11 = (bf16[1024]{0:T(1024)(128)(2,1)S(1)}, bf16[1024]{0:T(1024)(128)(2,1)}, u32[]{:S(2)}) copy-start(bf16[1024]{0:T(1024)(128)(2,1)} %gain_hbm) | copy-start | bytes 6148
  0.0 3.4 %copy-start.15 = (s32[6,16]{1,0:T(8,128)S(1)}, s32[6,16]{1,0:T(8,128)}, u32[]{:S(2)}) copy-start(s32[6,16]{1,0:T(8,128)} %param.12) | copy-start | bytes 1156
  0.0 9.8 %copy-start = (bf16[4,1024,256]{2,1,0:T(8,128)(2,1)S(1)}, bf16[4,1024,256]{2,1,0:T(8,128)(2,1)}, u32[]{:S(2)}) copy-start(bf16[4,1024,256]{2,1,0:T(8,128)(2,1)} %refs_4_.3) | copy-start | bytes 6291460
  3.5 14.3 %collective-permute-start = (bf16[192,1024]{1,0:T(8,128)(2,1)}, bf16[192,1024]{1,0:T(8,128)(2,1)S(1)}, u32[]{:S(2)}, u32[]{:S(2)}) collective-permute-start(bf16[192,1024]{1,0:T(8,128)(2,1)} %shard_map.73), channel_id=1, source_target_pairs={{0,8},{4,12},{8,16},{12,20},{16,24},{20,28},{1,9},{5,13},{9,17},{1... | collective-permute-start | bytes 1179656 | tf_op jit(solution)/shard_map/ppermute | solution.py:422
  4.8 13.0 %collective-permute-start.1 = (s32[6,17]{1,0:T(8,128)S(1)}, s32[6,17]{1,0:T(8,128)S(1)}, u32[]{:S(2)}, u32[]{:S(2)}) collective-permute-start(s32[6,17]{1,0:T(8,128)S(1)} %pad_add_fusion.told_ref), channel_id=1, source_target_pairs={{0,4},{4,0},{8,12},{12,8},{16,20},{20,16},{24,28},{28,24},{1,5},{5... | collective-permute-start | bytes 1232 | tf_op jit(solution)/shard_map/ppermute | solution.py:374
  6.1 11.7 %collective-permute-start.2 = (s32[6,17]{1,0:T(8,128)S(1)}, s32[6,17]{1,0:T(8,128)S(1)}, u32[]{:S(2)}, u32[]{:S(2)}) collective-permute-start(s32[6,17]{1,0:T(8,128)S(1)} %pad_add_fusion.told_ref), channel_id=1, source_target_pairs={{24,4},{25,5},{26,6},{27,7}} | collective-permute-start | bytes 1232 | tf_op jit(solution)/shard_map/ppermute | solution.py:424
  9.9 1.4 %copy-start.1 = (bf16[768,1024]{1,0:T(8,128)(2,1)S(1)}, bf16[768,1024]{1,0:T(8,128)(2,1)}, u32[]{:S(2)}) copy-start(bf16[768,1024]{1,0:T(8,128)(2,1)} %refs_3_.1) | copy-start | bytes 4718596
  17.8 28.5 %copy-start.4 = (bf16[768,256]{1,0:T(8,128)(2,1)}, bf16[768,256]{1,0:T(8,128)(2,1)S(1)}, u32[]{:S(2)}) copy-start(bf16[768,256]{1,0:T(8,128)(2,1)S(1)} %get-tuple-element.39.refs_5_.query_hbm) | copy-start | bytes 1179652
  17.8 9.2 %collective-permute-start.7 = (bf16[192,1024]{1,0:T(8,128)(2,1)S(1)}, bf16[192,1024]{1,0:T(8,128)(2,1)S(1)}, u32[]{:S(2)}, u32[]{:S(2)}) collective-permute-start(bf16[192,1024]{1,0:T(8,128)(2,1)S(1)} %collective-permute-done.refs_0_), channel_id=1, source_target_pairs={{0,2},{1,3},{2,0},{3,1},{4,6},{5,7},{6,4},{7,5},{8,10},{9,11},{10,... | collective-permute-start | bytes 1179656 | tf_op jit(solution)/shard_map/ppermute | solution.py:374
  19.1 10.7 %collective-permute-start.3 = (bf16[192,1024]{1,0:T(8,128)(2,1)S(1)}, bf16[192,1024]{1,0:T(8,128)(2,1)S(1)}, u32[]{:S(2)}, u32[]{:S(2)}) collective-permute-start(bf16[192,1024]{1,0:T(8,128)(2,1)S(1)} %collective-permute-done.refs_0_), channel_id=1, source_target_pairs={{0,8},{4,12},{8,16},{12,20},{16,24},{20,28},{1,9},{5,13},{9,17},{1... | collective-permute-start | bytes 1179656 | tf_op jit(solution)/shard_map/ppermute | solution.py:442
  20.4 10.2 %collective-permute-start.10 = (bf16[768,256]{1,0:T(8,128)(2,1)S(1)}, bf16[768,256]{1,0:T(8,128)(2,1)S(1)}, u32[]{:S(2)}, u32[]{:S(2)}) collective-permute-start(bf16[768,256]{1,0:T(8,128)(2,1)S(1)} %get-tuple-element.39.refs_5_.query_hbm), channel_id=1, source_target_pairs={{24,4},{25,5},{26,6},{27,7}} | collective-permute-start | bytes 1179656 | tf_op jit(solution)/shard_map/ppermute | solution.py:444
  23.2 10.2 %collective-permute-start.9 = (bf16[768,256]{1,0:T(8,128)(2,1)S(1)}, bf16[768,256]{1,0:T(8,128)(2,1)S(1)}, u32[]{:S(2)}, u32[]{:S(2)}) collective-permute-start(bf16[768,256]{1,0:T(8,128)(2,1)S(1)} %get-tuple-element.39.refs_5_.query_hbm), channel_id=1, source_target_pairs={{0,4},{4,0},{8,12},{12,8},{16,20},{20,16},{24,28},{28,24},{1,5},{5... | collective-permute-start | bytes 1179656 | tf_op jit(solution)/shard_map/ppermute | solution.py:374
  23.3 12.5 %collective-permute-start.6 = (bf16[192,1024]{1,0:T(8,128)(2,1)S(1)}, bf16[192,1024]{1,0:T(8,128)(2,1)S(1)}, u32[]{:S(2)}, u32[]{:S(2)}) collective-permute-start(bf16[192,1024]{1,0:T(8,128)(2,1)S(1)} %collective-permute-done.refs_0_), channel_id=1, source_target_pairs={{0,1},{1,0},{2,3},{3,2},{4,5},{5,4},{6,7},{7,6},{8,9},{9,8},{10,11... | collective-permute-start | bytes 1179656 | tf_op jit(solution)/shard_map/ppermute | solution.py:374
  27.0 8.8 %collective-permute-start.8 = (bf16[192,1024]{1,0:T(8,128)(2,1)S(1)}, bf16[192,1024]{1,0:T(8,128)(2,1)S(1)}, u32[]{:S(2)}, u32[]{:S(2)}) collective-permute-start(bf16[192,1024]{1,0:T(8,128)(2,1)S(1)} %collective-permute-done.7.refs_2_), channel_id=1, source_target_pairs={{0,1},{1,0},{2,3},{3,2},{4,5},{5,4},{6,7},{7,6},{8,9},{9,8},{10,11... | collective-permute-start | bytes 1179656 | tf_op jit(solution)/shard_map/ppermute | solution.py:374
  29.8 16.5 %collective-permute-start.5 = (bf16[192,1024]{1,0:T(8,128)(2,1)S(1)}, bf16[192,1024]{1,0:T(8,128)(2,1)S(1)}, u32[]{:S(2)}, u32[]{:S(2)}) collective-permute-start(bf16[192,1024]{1,0:T(8,128)(2,1)S(1)} %collective-permute-done.3.refs_0_), channel_id=1, source_target_pairs={{0,2},{1,3},{2,0},{3,1},{4,6},{5,7},{6,4},{7,5},{8,10},{9,11},{10,... | collective-permute-start | bytes 1179656 | tf_op jit(solution)/shard_map/ppermute | solution.py:374
  30.7 15.6 %collective-permute-start.11 = (bf16[2,128,256]{2,1,0:T(8,128)(2,1)S(1)}, bf16[2,128,256]{2,1,0:T(8,128)(2,1)S(1)}, u32[]{:S(2)}, u32[]{:S(2)}) collective-permute-start(bf16[2,128,256]{2,1,0:T(8,128)(2,1)S(1)} %get-tuple-element.45), channel_id=1, source_target_pairs={{0,24},{4,28},{1,25},{5,29},{2,26},{6,30},{3,27},{7,31}} | collective-permute-start | bytes 393224 | tf_op jit(solution)/shard_map/ppermute | solution.py:445
  33.4 13.0 %collective-permute-start.4 = (bf16[192,1024]{1,0:T(8,128)(2,1)S(1)}, bf16[192,1024]{1,0:T(8,128)(2,1)S(1)}, u32[]{:S(2)}, u32[]{:S(2)}) collective-permute-start(bf16[192,1024]{1,0:T(8,128)(2,1)S(1)} %collective-permute-done.3.refs_0_), channel_id=1, source_target_pairs={{0,1},{1,0},{2,3},{3,2},{4,5},{5,4},{6,7},{7,6},{8,9},{9,8},{10,11... | collective-permute-start | bytes 1179656 | tf_op jit(solution)/shard_map/ppermute | solution.py:374
  46.2 6.7 %copy-start.12 = (f32[768,256]{1,0:T(8,128)}, f32[768,256]{1,0:T(8,128)S(1)}, u32[]{:S(2)}) copy-start(f32[768,256]{1,0:T(8,128)S(1)} %get-tuple-element.52.before_hbm) | copy-start | bytes 2359300
  46.3 7.5 %copy-start.14 = (bf16[256,1024]{1,0:T(8,128)(2,1)S(1)}, bf16[256,1024]{1,0:T(8,128)(2,1)}, u32[]{:S(2)}) copy-start(bf16[256,1024]{1,0:T(8,128)(2,1)} %param.11) | copy-start | bytes 1572868
  46.3 1.8 %collective-permute-start.12 = (bf16[192,1024]{1,0:T(8,128)(2,1)S(1)}, bf16[192,1024]{1,0:T(8,128)(2,1)S(1)}, u32[]{:S(2)}, u32[]{:S(2)}) collective-permute-start(bf16[192,1024]{1,0:T(8,128)(2,1)S(1)} %collective-permute-done.5.refs_2_), channel_id=1, source_target_pairs={{0,1},{1,0},{2,3},{3,2},{4,5},{5,4},{6,7},{7,6},{8,9},{9,8},{10,11... | collective-permute-start | bytes 1179656 | tf_op jit(solution)/shard_map/ppermute | solution.py:374
  53.0 0.8 copy-start.9
  53.8 0.9 copy-start.6
  53.8 1.1 %copy-start.7 = (bf16[256,768]{1,0:T(8,128)(2,1)}, bf16[256,768]{1,0:T(8,128)(2,1)S(1)}, u32[]{:S(2)}) copy-start(bf16[256,768]{1,0:T(8,128)(2,1)S(1)} %get-tuple-element.49.keys_t_ref) | copy-start | bytes 1179652
  54.8 23.1 %copy-start.3 = (bf16[256]{0:T(256)(128)(2,1)S(1)}, bf16[256]{0:T(256)(128)(2,1)}, u32[]{:S(2)}) copy-start(bf16[256]{0:T(256)(128)(2,1)} %gain_ref.3) | copy-start | bytes 1540
  54.8 13.6 %all-to-all-start = ((bf16[256,4,256]{2,0,1:T(8,128)(2,1)}), bf16[256,4,256]{2,0,1:T(8,128)(2,1)S(1)}, u32[]{:S(2)}, u32[]{:S(2)}) async-start(bf16[256,4,256]{2,0,1:T(8,128)(2,1)} %bitcast.7), calls=%async_computation | async-start | bytes 1048576 | tf_op jit(solution)/shard_map/all_to_all | solution.py:493
  58.5 19.4 %collective-permute-start.13 = (bf16[768,256]{1,0:T(8,128)(2,1)}, bf16[768,256]{1,0:T(8,128)(2,1)}, u32[]{:S(2)}, u32[]{:S(2)}) collective-permute-start(bf16[768,256]{1,0:T(8,128)(2,1)} %copy-done.6), channel_id=1, source_target_pairs={{0,4},{4,0},{8,12},{12,8},{16,20},{20,16},{24,28},{28,24},{1,5},{5... | collective-permute-start | bytes 1179656 | tf_op jit(solution)/shard_map/ppermute | solution.py:374
  58.5 19.4 %collective-permute-start.14 = (bf16[768,256]{1,0:T(8,128)(2,1)}, bf16[768,256]{1,0:T(8,128)(2,1)}, u32[]{:S(2)}, u32[]{:S(2)}) collective-permute-start(bf16[768,256]{1,0:T(8,128)(2,1)} %shard_map.76), channel_id=1, source_target_pairs={{4,24},{5,25},{6,26},{7,27}} | collective-permute-start | bytes 1179656 | tf_op jit(solution)/shard_map/ppermute | solution.py:479
  60.0 1.0 %copy-start.5 = (bf16[768,256]{1,0:T(8,128)(2,1)S(1)}, bf16[768,256]{1,0:T(8,128)(2,1)}, u32[]{:S(2)}) copy-start(bf16[768,256]{1,0:T(8,128)(2,1)} %copy-done.4) | copy-start | bytes 1179652
  61.0 1.0 %copy-start.8 = (bf16[256,768]{1,0:T(8,128)(2,1)S(1)}, bf16[256,768]{1,0:T(8,128)(2,1)}, u32[]{:S(2)}) copy-start(bf16[256,768]{1,0:T(8,128)(2,1)} %copy-done.7) | copy-start | bytes 1179652
  62.0 1.0 %copy-start.10 = (bf16[768,256]{1,0:T(8,128)(2,1)S(1)}, bf16[768,256]{1,0:T(8,128)(2,1)}, u32[]{:S(2)}) copy-start(bf16[768,256]{1,0:T(8,128)(2,1)} %copy-done.9) | copy-start | bytes 1179652
  63.0 1.1 %copy-start.13 = (f32[768,256]{1,0:T(8,128)S(1)}, f32[768,256]{1,0:T(8,128)}, u32[]{:S(2)}) copy-start(f32[768,256]{1,0:T(8,128)} %copy-done.12) | copy-start | bytes 2359300
  64.1 18.0 %copy-start.2 = (bf16[768,1024]{1,0:T(8,128)(2,1)S(1)}, bf16[768,1024]{1,0:T(8,128)(2,1)}, u32[]{:S(2)}) copy-start(bf16[768,1024]{1,0:T(8,128)(2,1)} %refs_3_.1) | copy-start | bytes 4718596
  79.8 2.3 %collective-permute-start.16 = (bf16[768,256]{1,0:T(8,128)(2,1)S(1)}, bf16[768,256]{1,0:T(8,128)(2,1)S(1)}, u32[]{:S(2)}, u32[]{:S(2)}) collective-permute-start(bf16[768,256]{1,0:T(8,128)(2,1)S(1)} %shard_map.79.refs_0_), channel_id=1, source_target_pairs={{0,1},{1,0},{2,3},{3,2},{4,5},{5,4},{6,7},{7,6},{8,9},{9,8},{10,11... | collective-permute-start | bytes 1179656 | tf_op jit(solution)/shard_map/ppermute | solution.py:374
  80.7 10.7 %collective-permute-start.15 = (bf16[768,256]{1,0:T(8,128)(2,1)S(1)}, bf16[768,256]{1,0:T(8,128)(2,1)S(1)}, u32[]{:S(2)}, u32[]{:S(2)}) collective-permute-start(bf16[768,256]{1,0:T(8,128)(2,1)S(1)} %shard_map.79.refs_0_), channel_id=1, source_target_pairs={{0,2},{1,3},{2,0},{3,1},{4,6},{5,7},{6,4},{7,5},{8,10},{9,11},{10,... | collective-permute-start | bytes 1179656 | tf_op jit(solution)/shard_map/ppermute | solution.py:374
  91.4 2.2 %collective-permute-start.17 = (bf16[768,256]{1,0:T(8,128)(2,1)S(1)}, bf16[768,256]{1,0:T(8,128)(2,1)S(1)}, u32[]{:S(2)}, u32[]{:S(2)}) collective-permute-start(bf16[768,256]{1,0:T(8,128)(2,1)S(1)} %collective-permute-done.15.refs_0_), channel_id=1, source_target_pairs={{0,1},{1,0},{2,3},{3,2},{4,5},{5,4},{6,7},{7,6},{8,9},{9,8},{10,11... | collective-permute-start | bytes 1179656 | tf_op jit(solution)/shard_map/ppermute | solution.py:374
where the time goes:
time: 95.1 us; the launch traced here: 94.7 us
  Pallas kernels  33.4 us (35%)
  starting transfers between devices  29.3 us (31%)
  waiting for transfers between devices  23.4 us (25%)
  local copies, waits for them, and re-layouts  8.28 us (9%)
    ppermute x12, waiting for transfers between devices, crossed(): lax.ppermute(array, axis, [(i, i ^ bit) for i in range(lax.axis_size(axis...  23 us
    ppermute x12, starting transfers between devices, crossed(): lax.ppermute(array, axis, [(i, i ^ bit) for i in range(lax.axis_size(axis...  13.8 us
    pallas_call x1, Pallas kernels, body(): pl.pallas_call(make_chunk_kernel(1, n_head), in_specs=[flat] * 2 + [wide]...  10.4 us
    pallas_call x1, Pallas kernels, body(): pl.pallas_call(own_kernel, in_specs=[flat, far_off, far_off, wide], out_s...  6.5 us
    unnamed x32, local copies, waits for them, and re-layouts  6.48 us
    pallas_call x1, Pallas kernels, body(): pl.pallas_call(make_last_kernel(PLANES, n_head), in_specs=[flat] + [wide]...  4.91 us
    pallas_call x1, Pallas kernels, body(): pl.pallas_call(make_own_last_kernel(PLANES), in_specs=[flat, far_off, wid...  4.27 us
    ppermute x1, starting transfers between devices, body(): told_far = lax.ppermute(told, 'seq', downward)  3.74 us
  transfers between devices with their start and end apart: 19, of which 6 were waited for; matrix products, arithmetic and copies ran while one was open for 0% of the time, Pallas kernels for 24%

commit v1 on v0

--- a/solution.py
+++ b/solution.py
@@ -135,18 +135,15 @@
 
 
 def own_kernel(
-    told_ref, history_hbm, gain_hbm, w_ref,
-    gate_hbm, values_hbm, query_hbm, keys_t_hbm, tail_hbm, sums_hbm,
-    history_ref, gain_ref, gate_ref, values_ref, query_ref, keys_t_ref, tail_ref, sums_ref, live_ref, sems, out_sems,
+    history_hbm, gain_hbm, w_ref, gate_hbm, values_hbm, query_hbm, keys_t_hbm, tail_hbm,
+    history_ref, gain_ref, gate_ref, values_ref, query_ref, keys_t_ref, tail_ref, sems, out_sems,
 ):
-    rows, cols = query_ref.shape
-    blocks = rows // BLK
+    rows = query_ref.shape[0]
     part = 2 * BLK
     parts = [pl.ds(p * part, part) for p in range(rows // part)]
     gain_copy, *copies = fetch(
         [(gain_hbm, gain_ref)] + [(history_hbm.at[at], history_ref.at[at]) for at in parts], sems
     )
-    mark(live_ref, told_ref, lax.axis_index("seq") * blocks, blocks, 0)
     gain_copy.wait()
     gain = gain_ref[...].reshape(1, -1)
     for at, copy in zip(parts, copies):
@@ -160,11 +157,27 @@
         gate_ref[at, :] = project(here, w_ref[0]).astype(jnp.bfloat16)
     tail_ref[0] = keys[-BLK:].astype(jnp.bfloat16)
     tail_ref[1] = values[-BLK:]
-    done = [
-        (query_ref, query_hbm), (values_ref, values_hbm), (keys_t_ref, keys_t_hbm),
-        (gate_ref, gate_hbm), (tail_ref, tail_hbm), (sums_ref, sums_hbm),
-    ]
-    out = fetch(done[:-1], out_sems)
+    wait(
+        fetch(
+            [
+                (query_ref, query_hbm), (values_ref, values_hbm), (keys_t_ref, keys_t_hbm),
+                (gate_ref, gate_hbm), (tail_ref, tail_hbm),
+            ],
+            out_sems,
+        )
+    )
+
+
+def own_attend_kernel(
+    told_ref, query_hbm, keys_t_hbm, values_hbm, sums_hbm, query_ref, keys_t_ref, values_ref, sums_ref, live_ref, sems
+):
+    rows, cols = query_ref.shape
+    blocks = rows // BLK
+    copies = fetch(
+        [(query_hbm, query_ref), (keys_t_hbm, keys_t_ref), (values_hbm, values_ref)], sems
+    )
+    mark(live_ref, told_ref, lax.axis_index("seq") * blocks, blocks, 0)
+    wait(copies)
     behind = lax.broadcasted_iota(jnp.int32, (BLK, BLK), 1) <= lax.broadcasted_iota(
         jnp.int32, (BLK, BLK), 0
     )
@@ -194,9 +207,7 @@
                 values_ref[seen, at],
                 preferred_element_type=jnp.float32,
             )
-    last = pltpu.make_async_copy(sums_ref, sums_hbm, out_sems.at[len(done) - 1])
-    last.start()
-    wait(out + [last])
+    wait(fetch([(sums_ref, sums_hbm)], sems))
 
 
 def centred(part):
@@ -299,13 +310,14 @@
 
 def make_own_last_kernel(back):
     def kernel(
-        told_ref, query_hbm, keys_t_ref, values_ref, tail_ref, before_hbm, sums_ref, query_ref, live_ref, sems
+        told_ref, query_hbm, keys_t_ref, values_ref, tail_ref, before_hbm, gate_hbm, gain_ref,
+        sums_ref, scale_ref, query_ref, gate_ref, live_ref, sems,
     ):
         rows, cols = query_ref.shape
         blocks = rows // BLK
         here = lax.axis_index("seq")
         source = here - 2 * back
-        copies = fetch([(query_hbm, query_ref), (before_hbm, sums_ref)], sems)
+        copies = fetch([(query_hbm, query_ref), (before_hbm, sums_ref), (gate_hbm, gate_ref)], sems)
         mark(live_ref, told_ref, source * blocks, blocks, 0)
         wait(copies)
 
@@ -328,46 +340,56 @@
                     weights, tail_ref[1, :, at], preferred_element_type=jnp.float32
                 )
 
+        scale_ref[...] = gain_ref[...].reshape(1, -1).astype(jnp.float32) * gate_ref[...].astype(
+            jnp.float32
+        )
+        for h in range(cols // DH):
+            at = pl.ds(h * DH, DH)
+            sums_ref[:, at] = centred(sums_ref[:, at])
+
     return kernel
 
 
-def finish_kernel(sums_ref, near_ref, far_ref, gate_ref, gain_ref, out_ref):
+def finish_kernel(sums_ref, near_ref, far_ref, scale_ref, out_ref):
     for h in range(sums_ref.shape[1] // DH):
         at = pl.ds(h * DH, DH)
-        part = centred(sums_ref[:, at])
-        part = part + near_ref[:, at].astype(jnp.float32) + far_ref[:, at].astype(jnp.float32)
+        part = sums_ref[:, at] + near_ref[:, at].astype(jnp.float32) + far_ref[:, at].astype(jnp.float32)
         off = centred(part)
         spread_sq = jnp.mean(jnp.square(off), axis=-1, keepdims=True)
-        out_ref[:, at] = (
-            off
-            * lax.rsqrt(spread_sq + EPS)
-            * gain_ref[at].reshape(1, -1).astype(jnp.float32)
-            * gate_ref[:, at].astype(jnp.float32)
-        ).astype(jnp.bfloat16)
-
-
-def mix(total, pieces, first, w_ref):
+        out_ref[:, at] = (off * lax.rsqrt(spread_sq + EPS) * scale_ref[:, at]).astype(jnp.bfloat16)
+
+
+def mix(total, pieces, w_ref):
     cols = pieces[0].shape[1]
-    for m, piece in enumerate(pieces, start=first):
-        at = pl.ds(pl.multiple_of((lax.axis_index("head") ^ m) * cols, cols), cols)
-        total = total + jnp.dot(piece[...], w_ref[at, :], preferred_element_type=jnp.float32)
+    for m, piece in enumerate(pieces):
+        w = w_ref[m * cols : (m + 1) * cols, :]
+        total = total + jnp.dot(piece[...], w, preferred_element_type=jnp.float32)
     return total
 
 
 def near_out_kernel(*refs):
-    *pieces, w_ref, history_hbm, out_ref, history_ref, sem = refs
+    n = (len(refs) - 7) // 3
+    pieces, w_hbm, refs = refs[:n], refs[n : 3 * n], refs[3 * n :]
+    history_hbm, out_ref, w_far_ref, w_near_ref, history_ref, sems, w_sems = refs
     cols = out_ref.shape[1]
+    rows = w_hbm[0].shape[0]
     at = pl.ds(pl.multiple_of(lax.axis_index("head") * cols, cols), cols)
-    copy = pltpu.make_async_copy(history_hbm.at[:, at], history_ref, sem)
-    copy.start()
-    total = mix(jnp.zeros(out_ref.shape, jnp.float32), pieces, 0, w_ref)
-    copy.wait()
-    out_ref[...] = total + history_ref[...].astype(jnp.float32)
+    copies = fetch([(history_hbm.at[:, at], history_ref)], sems)
+    w_copies = fetch(
+        [
+            (w.at[:, at], (w_near_ref if m < n else w_far_ref).at[pl.ds(m % n * rows, rows)])
+            for m, w in enumerate(w_hbm)
+        ],
+        w_sems,
+    )
+    wait(copies)
+    wait(w_copies)
+    out_ref[...] = mix(history_ref[...].astype(jnp.float32), pieces, w_near_ref)
 
 
 def far_out_kernel(*refs):
     *pieces, w_ref, near_ref, out_ref = refs
-    out_ref[...] = mix(near_ref[...], pieces, len(pieces), w_ref).astype(jnp.bfloat16)
+    out_ref[...] = mix(near_ref[...], pieces, w_ref).astype(jnp.bfloat16)
 
 
 def crossed(array, axis, bit):
@@ -400,7 +422,6 @@
     sems = lambda n: pltpu.SemaphoreType.DMA((n,))
     live = pltpu.SMEM((n_live,), f32)
 
-    told = jnp.concatenate([block_lists, counts[:, None]], axis=1)
     share_rows = tok_rows // n_head
     steps = share_rows // 48
     share = pl.pallas_call(
@@ -416,33 +437,45 @@
         cost_estimate=cost(2),
         compiler_params=params(60),
     )(history, ln_gain)
-    gain, told, share = barrier((ln_gain, told, share))
+    gain, block_lists, counts, w_out, share = barrier((ln_gain, block_lists, counts, w_out, share))
+    told = jnp.concatenate([block_lists, counts[:, None]], axis=1)
     upward = [(i, i + 2) for i in range(n_seq - 2)]
     downward = [(i, i - FAR) for i in range(FAR + 1, n_seq, 2)]
     share_1 = lax.ppermute(share, "seq", upward)
-    told_x = crossed(told, "seq", 1)
-    told_far = lax.ppermute(told, "seq", downward)
-
-    gate, values, query, keys_t, tail, own_sums = pl.pallas_call(
+
+    gate, values, query, keys_t, tail = pl.pallas_call(
         own_kernel,
-        in_specs=[flat, far_off, far_off, wide],
-        out_specs=[far_off] * 6,
-        out_shape=[shape(bf16, *upright)] * 3
-        + [shape(bf16, *lying), shape(bf16, 2, BLK, cols), shape(f32, *upright)],
+        in_specs=[far_off, far_off, wide],
+        out_specs=[far_off] * 5,
+        out_shape=[shape(bf16, *upright)] * 3 + [shape(bf16, *lying), shape(bf16, 2, BLK, cols)],
         scratch_shapes=[pltpu.VMEM((tok_rows, width), bf16), pltpu.VMEM((width,), bf16)]
         + [pltpu.VMEM(upright, bf16)] * 3
-        + [pltpu.VMEM(lying, bf16), pltpu.VMEM((2, BLK, cols), bf16), pltpu.VMEM(upright, f32), live]
-        + [sems(1 + tok_rows // (2 * BLK)), sems(6)],
-        compiler_params=params(),
-        cost_estimate=cost(6),
-    )(told, history, gain, w_in)
-    query_x = crossed(query, "seq", 1)
-
-    share_1, query, told_x, told_far = barrier((share_1, query, told_x, told_far))
+        + [pltpu.VMEM(lying, bf16), pltpu.VMEM((2, BLK, cols), bf16)]
+        + [sems(1 + tok_rows // (2 * BLK)), sems(5)],
+        compiler_params=params(),
+        cost_estimate=cost(4),
+    )(history, gain, w_in)
+
+    w_cross = crossed(w_out, "head", n_head // 2)
+    share_1, query, w_cross = barrier((share_1, query, w_cross))
     share_2 = lax.ppermute(share_1, "seq", upward)
-    chunk_1 = spread(share_1, n_head // 2)
-    query_far = lax.ppermute(query, "seq", downward)
+    cross_1 = crossed(share_1, "head", n_head // 2)
+    query_x, told_x = crossed(query, "seq", 1), crossed(told, "seq", 1)
+    query_far, told_far = (lax.ppermute(a, "seq", downward) for a in (query, told))
     tail = lax.ppermute(tail, "seq", [(i, i + FAR + 1) for i in range(n_seq - FAR - 1)])
+    told, told_x, told_far = barrier((told, told_x, told_far))
+    own_sums = pl.pallas_call(
+        own_attend_kernel,
+        in_specs=[flat] + [far_off] * 3,
+        out_specs=far_off,
+        out_shape=shape(f32, *upright),
+        scratch_shapes=[pltpu.VMEM(upright, bf16), pltpu.VMEM(lying, bf16), pltpu.VMEM(upright, bf16)]
+        + [pltpu.VMEM(upright, f32), live, sems(3)],
+        compiler_params=params(),
+        cost_estimate=cost(4),
+    )(told, query, keys_t, values)
+    share_2, cross_1, own_sums = barrier((share_2, cross_1, own_sums))
+    chunk_1 = spread(share_1, n_head // 4) + spread(cross_1, n_head // 4)
     cross_2 = crossed(share_2, "head", n_head // 2)
     near_2 = spread(share_2, n_head // 4)
 
@@ -489,48 +522,52 @@
         cost_estimate=cost(4),
     )(told_x, *near_2, *spread(cross_2, n_head // 4), w_in, query_x, sums_x)
     near = crossed(send, "seq", 1)
-    w_out, send = barrier((w_out, send))
-    w_mine = lax.all_to_all(w_out, "head", split_axis=1, concat_axis=0, tiled=True)
-    mine = pl.pallas_call(
+    send, w_out, w_cross = barrier((send, w_out, w_cross))
+    w_all = spread(w_out, n_head // 4) + spread(w_cross, n_head // 4)
+    mine, scale = pl.pallas_call(
         make_own_last_kernel(PLANES),
-        in_specs=[flat, far_off, wide, wide, wide, far_off],
-        out_specs=wide,
-        out_shape=shape(f32, *upright),
-        scratch_shapes=[pltpu.VMEM(upright, bf16), live, sems(2)],
+        in_specs=[flat, far_off, wide, wide, wide, far_off, far_off, wide],
+        out_specs=[wide] * 2,
+        out_shape=[shape(f32, *upright)] * 2,
+        scratch_shapes=[pltpu.VMEM(upright, bf16)] * 2 + [live, sems(3)],
         compiler_params=params(),
         cost_estimate=cost(3),
-    )(told, query, keys_t, values, tail, sums)
-    near, mine, w_mine = barrier((near, mine, w_mine))
+    )(told, query, keys_t, values, tail, sums, gate, out_gain)
+    near, mine, w_all = barrier((near, mine, tuple(w_all)))
     gated = pl.pallas_call(
         finish_kernel,
-        in_specs=[wide] * 5,
+        in_specs=[wide] * 4,
         out_specs=wide,
         out_shape=shape(bf16, *upright),
         compiler_params=params(),
         cost_estimate=cost(1),
-    )(mine, near, far, gate, out_gain)
+    )(mine, near, far, scale)
 
     out_cols = width // n_head
     cross_gated = crossed(gated, "head", n_head // 2)
     near_gated = spread(gated, n_head // 4)
-    mixed = pl.pallas_call(
+    half = n_head // 2
+    mixed, w_far = pl.pallas_call(
         near_out_kernel,
-        in_specs=[wide] * (n_head // 2 + 1) + [far_off],
-        out_specs=wide,
-        out_shape=shape(f32, tok_rows, out_cols),
-        scratch_shapes=[pltpu.VMEM((tok_rows, out_cols), bf16), pltpu.SemaphoreType.DMA],
+        in_specs=[wide] * half + [far_off] * (n_head + 1),
+        out_specs=[wide] * 2,
+        out_shape=[shape(f32, tok_rows, out_cols), shape(bf16, half * cols, out_cols)],
+        scratch_shapes=[
+            pltpu.VMEM((half * cols, out_cols), bf16), pltpu.VMEM((tok_rows, out_cols), bf16),
+            sems(1), sems(n_head),
+        ],
         compiler_params=params(),
         cost_estimate=cost(2),
-    )(*near_gated, w_mine, history)
+    )(*near_gated, *w_all, history)
     cross_gated, mixed = barrier((cross_gated, mixed))
     return pl.pallas_call(
         far_out_kernel,
-        in_specs=[wide] * (n_head // 2 + 2),
+        in_specs=[wide] * (half + 2),
         out_specs=wide,
         out_shape=shape(bf16, tok_rows, out_cols),
         compiler_params=params(),
         cost_estimate=cost(2),
-    )(*spread(cross_gated, n_head // 4), w_mine, mixed)
+    )(*spread(cross_gated, n_head // 4), w_far, mixed)
 
 
 def solution(mesh):

time: 95.1 us -> 98.5 us (1.036)
  waiting for transfers between devices: 23.4 us -> 31.5 us
  local copies, waits for them, and re-layouts: 8.28 us -> 5.77 us
  starting transfers between devices: 29.3 us -> 27.5 us
    ppermute x2, starting transfers between devices: 6.52 us -> 10.3 us  [body(): lax.ppermute(a, 'seq', downward)]
    all_to_all x1 -> x0, starting transfers between devices: 3.69 us -> none  [body(): lax.all_to_all(w_out, 'head', split_axis=1, concat_axis=0, tiled=True)]
    ppermute x2, waiting for transfers between devices: 0.01 us -> 3.21 us  [body(): lax.ppermute(a, 'seq', downward)]
    ppermute x1, waiting for transfers between devices: 0.01 us -> 2.81 us  [body(): share_1 = lax.ppermute(share, 'seq', upward)]
    ppermute x12 -> x15, waiting for transfers between devices: 23 us -> 25.5 us  [crossed(): lax.ppermute(array, axis, [(i, i ^ bit) for i in range(lax.axis_size(axis...]
    ppermute x12 -> x15, starting transfers between devices: 13.8 us -> 12 us  [crossed(): lax.ppermute(array, axis, [(i, i ^ bit) for i in range(lax.axis_size(axis...]
    pallas_call x4 -> x5, Pallas kernels: 9.91 us -> 9.27 us  [the longest x1 4.07 us: body(): pl.pallas_call(own_kernel, in_specs=[far_off, far_off, wide], out_specs=[...]
  transfers between devices with their start and end apart: 19 -> 21, of which waited for: 6 -> 8; matrix products, arithmetic and copies ran while one was open for 0% -> 0% of each run, Pallas kernels for 24% -> 24%
where the time goes in v1:
time: 98.5 us; the launch traced here: 97.9 us
  Pallas kernels  32.8 us (33%)
  waiting for transfers between devices  31.5 us (32%)
  starting transfers between devices  27.5 us (28%)
  local copies, waits for them, and re-layouts  5.77 us (6%)
    ppermute x15, waiting for transfers between devices, crossed(): lax.ppermute(array, axis, [(i, i ^ bit) for i in range(lax.axis_size(axis...  25.5 us
    ppermute x15, starting transfers between devices, crossed(): lax.ppermute(array, axis, [(i, i ^ bit) for i in range(lax.axis_size(axis...  12 us
    pallas_call x1, Pallas kernels, body(): pl.pallas_call(make_chunk_kernel(1, n_head), in_specs=[flat] * 2 + [wide]...  11 us
    ppermute x2, starting transfers between devices, body(): lax.ppermute(a, 'seq', downward)  10.3 us
    unnamed x32, local copies, waits for them, and re-layouts  5.68 us
    pallas_call x1, Pallas kernels, body(): pl.pallas_call(make_own_last_kernel(PLANES), in_specs=[flat, far_off, wid...  4.75 us
    pallas_call x1, Pallas kernels, body(): pl.pallas_call(make_last_kernel(PLANES, n_head), in_specs=[flat] + [wide]...  4.52 us
    pallas_call x1, Pallas kernels, body(): pl.pallas_call(own_kernel, in_specs=[far_off, far_off, wide], out_specs=[...  4.07 us
  transfers between devices with their start and end apart: 21, of which 8 were waited for; matrix products, arithmetic and copies ran while one was open for 0% of the time, Pallas kernels for 24%

profile of v1, /device:TPU:25, one launch (start us, length us, event | category | flops | bytes accessed | tf_op | source)
XLA Modules:
  0.0 97.9 jit_solution(766891459813446001)
XLA Ops:
  0.0 2.7 %shard_map.73 = bf16[192,1024]{1,0:T(8,128)(2,1)} custom-call(bf16[768,1024]{1,0:T(8,128)(2,1)} %refs_6_.1, bf16[1024]{0:T(1024)(128)(2,1)} %gain_hbm), custom_call_target="tpu_custom_call" | custom-call | flops 600000000 | bytes 1800000 | tf_op jit(solution)/shard_map/pallas_call | solution.py:427
  2.7 1.3 %collective-permute-start.3 = (bf16[256,1024]{1,0:T(8,128)(2,1)}, bf16[256,1024]{1,0:T(8,128)(2,1)S(1)}, u32[]{:S(2)}, u32[]{:S(2)}) collective-permute-start(bf16[256,1024]{1,0:T(8,128)(2,1)} %refs_2_), channel_id=1, source_target_pairs={{0,2},{1,3},{2,0},{3,1},{4,6},{5,7},{6,4},{7,5},{8,10},{9,11},{10,... | collective-permute-start | bytes 1572872 | tf_op jit(solution)/shard_map/ppermute | solution.py:396
  4.0 1.3 %collective-permute-start.2 = (bf16[192,1024]{1,0:T(8,128)(2,1)}, bf16[192,1024]{1,0:T(8,128)(2,1)}, u32[]{:S(2)}, u32[]{:S(2)}) collective-permute-start(bf16[192,1024]{1,0:T(8,128)(2,1)} %shard_map.73), channel_id=1, source_target_pairs={{0,8},{4,12},{8,16},{12,20},{16,24},{20,28},{1,9},{5,13},{9,17},{1... | collective-permute-start | bytes 1179656 | tf_op jit(solution)/shard_map/ppermute | solution.py:444
  5.3 0.0 copy-start.1
  5.3 1.4 %copy-done.1 = bf16[768,1024]{1,0:T(8,128)(2,1)S(1)} copy-done((bf16[768,1024]{1,0:T(8,128)(2,1)S(1)}, bf16[768,1024]{1,0:T(8,128)(2,1)}, u32[]{:S(2)}) %copy-start.1) | copy-done | bytes 1572888
  6.7 4.1 %shard_map.74 = (bf16[768,256]{1,0:T(8,128)(2,1)S(1)}, bf16[768,256]{1,0:T(8,128)(2,1)S(1)}, bf16[768,256]{1,0:T(8,128)(2,1)S(1)}, bf16[256,768]{1,0:T(8,128)(2,1)S(1)}, bf16[2,128,256]{2,1,0:T(8,128)(2,1)S(1)}) custom-call(bf16[768,1024]{1,0:T(8,128)(2,1)S(1)} %copy-done.1, bf16[1024]{0:T(1024)(128)(2,1)S(1)} %copy-done.4, bf16[4,1024,256]{2,1,0:T(8,128)(2,1)S(1)} %copy-done), custom_call_target="tpu_custom_call" | custom-call | flops 1200000000 | bytes 3600000 | tf_op jit(solution)/shard_map/pallas_call | solution.py:446
  10.8 0.7 copy-done.6
  11.6 0.7 copy-done.9
  12.3 0.8 copy-done.12
  13.1 2.8 %collective-permute-done.2.refs_0_ = bf16[192,1024]{1,0:T(8,128)(2,1)} collective-permute-done((bf16[192,1024]{1,0:T(8,128)(2,1)}, bf16[192,1024]{1,0:T(8,128)(2,1)}, u32[]{:S(2)}, u32[]{:S(2)}) %collective-permute-start.2) | collective-permute-done | bytes 393248 | tf_op jit(solution)/shard_map/ppermute | solution.py:444
  15.9 1.3 %collective-permute-start.4 = (bf16[192,1024]{1,0:T(8,128)(2,1)}, bf16[192,1024]{1,0:T(8,128)(2,1)S(1)}, u32[]{:S(2)}, u32[]{:S(2)}) collective-permute-start(bf16[192,1024]{1,0:T(8,128)(2,1)} %collective-permute-done.2.refs_0_), channel_id=1, source_target_pairs={{0,8},{4,12},{8,16},{12,20},{16,24},{20,28},{1,9},{5,13},{9,17},{1... | collective-permute-start | bytes 1179656 | tf_op jit(solution)/shard_map/ppermute | solution.py:461
  17.2 1.3 %collective-permute-start.5 = (bf16[192,1024]{1,0:T(8,128)(2,1)}, bf16[192,1024]{1,0:T(8,128)(2,1)}, u32[]{:S(2)}, u32[]{:S(2)}) collective-permute-start(bf16[192,1024]{1,0:T(8,128)(2,1)} %collective-permute-done.2.refs_0_), channel_id=1, source_target_pairs={{0,2},{1,3},{2,0},{3,1},{4,6},{5,7},{6,4},{7,5},{8,10},{9,11},{10,... | collective-permute-start | bytes 1179656 | tf_op jit(solution)/shard_map/ppermute | solution.py:396
  18.5 0.1 copy.8
  18.6 0.1 pad_add_fusion.told_ref
  18.6 1.2 %collective-permute-start = (s32[6,17]{1,0:T(8,128)S(1)}, s32[6,17]{1,0:T(8,128)S(1)}, u32[]{:S(2)}, u32[]{:S(2)}) collective-permute-start(s32[6,17]{1,0:T(8,128)S(1)} %pad_add_fusion.told_ref), channel_id=1, source_target_pairs={{0,4},{4,0},{8,12},{12,8},{16,20},{20,16},{24,28},{28,24},{1,5},{5... | collective-permute-start | bytes 1232 | tf_op jit(solution)/shard_map/ppermute | solution.py:396
  19.8 3.7 %collective-permute-start.1 = (s32[6,17]{1,0:T(8,128)S(1)}, s32[6,17]{1,0:T(8,128)S(1)}, u32[]{:S(2)}, u32[]{:S(2)}) collective-permute-start(s32[6,17]{1,0:T(8,128)S(1)} %pad_add_fusion.told_ref), channel_id=1, source_target_pairs={{24,4},{25,5},{26,6},{27,7}} | collective-permute-start | bytes 1232 | tf_op jit(solution)/shard_map/ppermute | solution.py:464
  23.6 0.7 collective-permute-done.1.told_ref
  24.3 3.1 %collective-permute-start.8 = (bf16[192,1024]{1,0:T(8,128)(2,1)}, bf16[192,1024]{1,0:T(8,128)(2,1)S(1)}, u32[]{:S(2)}, u32[]{:S(2)}) collective-permute-start(bf16[192,1024]{1,0:T(8,128)(2,1)} %collective-permute-done.2.refs_0_), channel_id=1, source_target_pairs={{0,1},{1,0},{2,3},{3,2},{4,5},{5,4},{6,7},{7,6},{8,9},{9,8},{10,11... | collective-permute-start | bytes 1179656 | tf_op jit(solution)/shard_map/ppermute | solution.py:396
  27.5 6.6 %collective-permute-start.11 = (bf16[768,256]{1,0:T(8,128)(2,1)S(1)}, bf16[768,256]{1,0:T(8,128)(2,1)S(1)}, u32[]{:S(2)}, u32[]{:S(2)}) collective-permute-start(bf16[768,256]{1,0:T(8,128)(2,1)S(1)} %get-tuple-element.56.query_hbm.refs_5_), channel_id=1, source_target_pairs={{24,4},{25,5},{26,6},{27,7}} | collective-permute-start | bytes 1179656 | tf_op jit(solution)/shard_map/ppermute | solution.py:464
  34.1 1.0 %copy-done.7 = bf16[768,256]{1,0:T(8,128)(2,1)S(1)} copy-done((bf16[768,256]{1,0:T(8,128)(2,1)S(1)}, bf16[768,256]{1,0:T(8,128)(2,1)}, u32[]{:S(2)}) %copy-start.7) | copy-done | bytes 393240
  35.1 1.0 %copy-done.10 = bf16[256,768]{1,0:T(8,128)(2,1)S(1)} copy-done((bf16[256,768]{1,0:T(8,128)(2,1)S(1)}, bf16[256,768]{1,0:T(8,128)(2,1)}, u32[]{:S(2)}) %copy-start.10) | copy-done | bytes 393240
  36.1 3.0 %shard_map.75.refs_9_ = f32[768,256]{1,0:T(8,128)S(1)} custom-call(s32[6,17]{1,0:T(8,128)S(1)} %pad_add_fusion.told_ref, bf16[768,256]{1,0:T(8,128)(2,1)S(1)} %get-tuple-element.56.query_hbm.refs_5_, bf16[256,768]{1,0:T(8,128)(2,1)S(1)} %copy-done.10, bf16[768,256]{1,0:T(8,128)(2,1)S(1)} %copy-done.7), custom_call_target="tpu_custom_call" | custom-call | flops 1200000000 | bytes 3600000 | tf_op jit(solution)/shard_map/pallas_call | solution.py:467
  39.1 0.3 collective-permute-start.9
  39.5 0.6 collective-permute-start.7
  40.1 2.5 %collective-permute-done.11.query_ref = bf16[768,256]{1,0:T(8,128)(2,1)S(1)} collective-permute-done((bf16[768,256]{1,0:T(8,128)(2,1)S(1)}, bf16[768,256]{1,0:T(8,128)(2,1)S(1)}, u32[]{:S(2)}, u32[]{:S(2)}) %collective-permute-start.11) | collective-permute-done | bytes 393248 | tf_op jit(solution)/shard_map/ppermute | solution.py:464
  42.6 1.3 %collective-permute-start.12 = (bf16[2,128,256]{2,1,0:T(8,128)(2,1)S(1)}, bf16[2,128,256]{2,1,0:T(8,128)(2,1)S(1)}, u32[]{:S(2)}, u32[]{:S(2)}) collective-permute-start(bf16[2,128,256]{2,1,0:T(8,128)(2,1)S(1)} %get-tuple-element.64), channel_id=1, source_target_pairs={{0,24},{4,28},{1,25},{5,29},{2,26},{6,30},{3,27},{7,31}} | collective-permute-start | bytes 393224 | tf_op jit(solution)/shard_map/ppermute | solution.py:465
  43.9 0.6 shard_map.77
  44.6 0.8 collective-permute-start.6
  45.4 11.0 %shard_map.76 = (f32[768,256]{1,0:T(8,128)S(1)}, f32[768,256]{1,0:T(8,128)S(1)}) custom-call(s32[6,17]{1,0:T(8,128)S(1)} %pad_add_fusion.told_ref, s32[6,17]{1,0:T(8,128)S(1)} %collective-permute-done.told_x_ref, bf16[192,1024]{1,0:T(8,128)(2,1)} %collective-permute-done.2.refs_0_, bf16[192,1024]{1,0:T(8,128)(2,1)S(1)} %collective-permute-done.8.refs_1_, ...), custom_call_target="tpu_custom_call" | custom-call | flops 1800000000 | bytes 5400000 | tf_op jit(solution)/shard_map/pallas_call | solution.py:494
  56.4 0.0 copy-start.3
  56.5 0.1 collective-permute-start.13
  56.6 1.7 %collective-permute-done.13.refs_3_ = bf16[192,1024]{1,0:T(8,128)(2,1)S(1)} collective-permute-done((bf16[192,1024]{1,0:T(8,128)(2,1)S(1)}, bf16[192,1024]{1,0:T(8,128)(2,1)S(1)}, u32[]{:S(2)}, u32[]{:S(2)}) %collective-permute-start.13) | collective-permute-done | bytes 393248 | tf_op jit(solution)/shard_map/ppermute | solution.py:396
  58.2 4.5 %shard_map.78 = (bf16[768,256]{1,0:T(8,128)(2,1)S(1)}, bf16[256,768]{1,0:T(8,128)(2,1)S(1)}, bf16[768,256]{1,0:T(8,128)(2,1)S(1)}) custom-call(s32[6,17]{1,0:T(8,128)S(1)} %collective-permute-done.told_x_ref, bf16[192,1024]{1,0:T(8,128)(2,1)S(1)} %collective-permute-done.4.refs_0_, bf16[192,1024]{1,0:T(8,128)(2,1)S(1)} %collective-permute-done.6.refs_1_, ...), custom_call_target="tpu_custom_call" | custom-call | flops 1200000000 | bytes 3600000 | tf_op jit(solution)/shard_map/pallas_call | solution.py:513
  62.8 0.2 collective-permute-start.15
  63.0 0.4 collective-permute-start.16
  63.4 1.3 %collective-permute-start.17 = (bf16[768,256]{1,0:T(8,128)(2,1)S(1)}, bf16[768,256]{1,0:T(8,128)(2,1)S(1)}, u32[]{:S(2)}, u32[]{:S(2)}) collective-permute-start(bf16[768,256]{1,0:T(8,128)(2,1)S(1)} %shard_map.77), channel_id=1, source_target_pairs={{4,24},{5,25},{6,26},{7,27}} | collective-permute-start | bytes 1179656 | tf_op jit(solution)/shard_map/ppermute | solution.py:512
  64.7 4.8 %shard_map.79 = (f32[768,256]{1,0:T(8,128)S(1)}, f32[768,256]{1,0:T(8,128)S(1)}) custom-call(s32[6,17]{1,0:T(8,128)S(1)} %pad_add_fusion.told_ref, bf16[768,256]{1,0:T(8,128)(2,1)S(1)} %get-tuple-element.56.query_hbm.refs_5_, bf16[256,768]{1,0:T(8,128)(2,1)S(1)} %get-tuple-element.68.keys_t_ref, bf16[768,256]{1,0:T(8,128)(2,1)S(1)} %get-tuple-element.69.values_ref, ...), custom_call_target="tpu_custom_call" | custom-call | flops 900000000 | bytes 2700000 | tf_op jit(solution)/shard_map/pallas_call | solution.py:527
  69.4 0.0 copy-start.2
  69.4 12.9 %collective-permute-done.14.near_ref = bf16[768,256]{1,0:T(8,128)(2,1)S(1)} collective-permute-done((bf16[768,256]{1,0:T(8,128)(2,1)S(1)}, bf16[768,256]{1,0:T(8,128)(2,1)S(1)}, u32[]{:S(2)}, u32[]{:S(2)}) %collective-permute-start.14) | collective-permute-done | bytes 393248 | tf_op jit(solution)/shard_map/ppermute | solution.py:396
  82.4 0.5 shard_map.80.refs_0_
  82.9 1.0 %collective-permute-start.19 = (bf16[768,256]{1,0:T(8,128)(2,1)S(1)}, bf16[768,256]{1,0:T(8,128)(2,1)S(1)}, u32[]{:S(2)}, u32[]{:S(2)}) collective-permute-start(bf16[768,256]{1,0:T(8,128)(2,1)S(1)} %shard_map.80.refs_0_), channel_id=1, source_target_pairs={{0,1},{1,0},{2,3},{3,2},{4,5},{5,4},{6,7},{7,6},{8,9},{9,8},{10,11... | collective-permute-start | bytes 1179656 | tf_op jit(solution)/shard_map/ppermute | solution.py:396
  83.9 0.7 collective-permute-start.18
  84.6 0.7 collective-permute-done.19.refs_1_
  85.3 0.5 shard_map.81
  85.8 8.8 %collective-permute-done.18.refs_0_ = bf16[768,256]{1,0:T(8,128)(2,1)S(1)} collective-permute-done((bf16[768,256]{1,0:T(8,128)(2,1)S(1)}, bf16[768,256]{1,0:T(8,128)(2,1)S(1)}, u32[]{:S(2)}, u32[]{:S(2)}) %collective-permute-start.18) | collective-permute-done | bytes 393248 | tf_op jit(solution)/shard_map/ppermute | solution.py:396
  94.6 0.8 collective-permute-start.20
  95.5 1.3 %collective-permute-done.20.refs_1_ = bf16[768,256]{1,0:T(8,128)(2,1)S(1)} collective-permute-done((bf16[768,256]{1,0:T(8,128)(2,1)S(1)}, bf16[768,256]{1,0:T(8,128)(2,1)S(1)}, u32[]{:S(2)}, u32[]{:S(2)}) %collective-permute-start.20) | collective-permute-done | bytes 393248 | tf_op jit(solution)/shard_map/ppermute | solution.py:396
  96.8 1.1 %shard_map.82 = bf16[768,256]{1,0:T(8,128)(2,1)} custom-call(bf16[768,256]{1,0:T(8,128)(2,1)S(1)} %collective-permute-done.18.refs_0_, bf16[768,256]{1,0:T(8,128)(2,1)S(1)} %collective-permute-done.20.refs_1_, bf16[512,256]{1,0:T(8,128)(2,1)S(1)} %get-tuple-element.87.refs_2_, f32[768,256]{1,0:T(8,128)S(1)} %get-tuple-element.88.refs_3_), custom_call_target="tpu_custom_call" | custom-call | flops 600000000 | bytes 1800000 | tf_op jit(solution)/shard_map/pallas_call | solution.py:563
  (38 shorter events, 0.1 us)
Async XLA Ops:
  0.0 5.3 %copy-start.4 = (bf16[1024]{0:T(1024)(128)(2,1)S(1)}, bf16[1024]{0:T(1024)(128)(2,1)}, u32[]{:S(2)}) copy-start(bf16[1024]{0:T(1024)(128)(2,1)} %gain_hbm) | copy-start | bytes 6148
  0.0 5.3 %copy-start = (bf16[4,1024,256]{2,1,0:T(8,128)(2,1)S(1)}, bf16[4,1024,256]{2,1,0:T(8,128)(2,1)}, u32[]{:S(2)}) copy-start(bf16[4,1024,256]{2,1,0:T(8,128)(2,1)} %refs_4_.3) | copy-start | bytes 6291460
  0.0 18.5 %copy-start.15 = (s32[6]{0:T(128)S(1)}, s32[6]{0:T(128)}, u32[]{:S(2)}) copy-start(s32[6]{0:T(128)} %param.13) | copy-start | bytes 76
  0.0 18.5 %copy-start.14 = (s32[6,16]{1,0:T(8,128)S(1)}, s32[6,16]{1,0:T(8,128)}, u32[]{:S(2)}) copy-start(s32[6,16]{1,0:T(8,128)} %param.12) | copy-start | bytes 1156
  2.7 13.2 %collective-permute-start.3 = (bf16[256,1024]{1,0:T(8,128)(2,1)}, bf16[256,1024]{1,0:T(8,128)(2,1)S(1)}, u32[]{:S(2)}, u32[]{:S(2)}) collective-permute-start(bf16[256,1024]{1,0:T(8,128)(2,1)} %refs_2_), channel_id=1, source_target_pairs={{0,2},{1,3},{2,0},{3,1},{4,6},{5,7},{6,4},{7,5},{8,10},{9,11},{10,... | collective-permute-start | bytes 1572872 | tf_op jit(solution)/shard_map/ppermute | solution.py:396
  4.0 11.9 %collective-permute-start.2 = (bf16[192,1024]{1,0:T(8,128)(2,1)}, bf16[192,1024]{1,0:T(8,128)(2,1)}, u32[]{:S(2)}, u32[]{:S(2)}) collective-permute-start(bf16[192,1024]{1,0:T(8,128)(2,1)} %shard_map.73), channel_id=1, source_target_pairs={{0,8},{4,12},{8,16},{12,20},{16,24},{20,28},{1,9},{5,13},{9,17},{1... | collective-permute-start | bytes 1179656 | tf_op jit(solution)/shard_map/ppermute | solution.py:444
  5.3 1.4 %copy-start.1 = (bf16[768,1024]{1,0:T(8,128)(2,1)S(1)}, bf16[768,1024]{1,0:T(8,128)(2,1)}, u32[]{:S(2)}) copy-start(bf16[768,1024]{1,0:T(8,128)(2,1)} %refs_6_.1) | copy-start | bytes 4718596
  10.8 0.8 copy-start.6
  11.6 0.7 copy-start.9
  12.3 0.8 copy-start.12
  15.9 23.2 %collective-permute-start.4 = (bf16[192,1024]{1,0:T(8,128)(2,1)}, bf16[192,1024]{1,0:T(8,128)(2,1)S(1)}, u32[]{:S(2)}, u32[]{:S(2)}) collective-permute-start(bf16[192,1024]{1,0:T(8,128)(2,1)} %collective-permute-done.2.refs_0_), channel_id=1, source_target_pairs={{0,8},{4,12},{8,16},{12,20},{16,24},{20,28},{1,9},{5,13},{9,17},{1... | collective-permute-start | bytes 1179656 | tf_op jit(solution)/shard_map/ppermute | solution.py:461
  17.2 21.9 %collective-permute-start.5 = (bf16[192,1024]{1,0:T(8,128)(2,1)}, bf16[192,1024]{1,0:T(8,128)(2,1)}, u32[]{:S(2)}, u32[]{:S(2)}) collective-permute-start(bf16[192,1024]{1,0:T(8,128)(2,1)} %collective-permute-done.2.refs_0_), channel_id=1, source_target_pairs={{0,2},{1,3},{2,0},{3,1},{4,6},{5,7},{6,4},{7,5},{8,10},{9,11},{10,... | collective-permute-start | bytes 1179656 | tf_op jit(solution)/shard_map/ppermute | solution.py:396
  18.6 5.0 %collective-permute-start = (s32[6,17]{1,0:T(8,128)S(1)}, s32[6,17]{1,0:T(8,128)S(1)}, u32[]{:S(2)}, u32[]{:S(2)}) collective-permute-start(s32[6,17]{1,0:T(8,128)S(1)} %pad_add_fusion.told_ref), channel_id=1, source_target_pairs={{0,4},{4,0},{8,12},{12,8},{16,20},{20,16},{24,28},{28,24},{1,5},{5... | collective-permute-start | bytes 1232 | tf_op jit(solution)/shard_map/ppermute | solution.py:396
  19.8 4.5 %collective-permute-start.1 = (s32[6,17]{1,0:T(8,128)S(1)}, s32[6,17]{1,0:T(8,128)S(1)}, u32[]{:S(2)}, u32[]{:S(2)}) collective-permute-start(s32[6,17]{1,0:T(8,128)S(1)} %pad_add_fusion.told_ref), channel_id=1, source_target_pairs={{24,4},{25,5},{26,6},{27,7}} | collective-permute-start | bytes 1232 | tf_op jit(solution)/shard_map/ppermute | solution.py:464
  24.3 21.1 %collective-permute-start.8 = (bf16[192,1024]{1,0:T(8,128)(2,1)}, bf16[192,1024]{1,0:T(8,128)(2,1)S(1)}, u32[]{:S(2)}, u32[]{:S(2)}) collective-permute-start(bf16[192,1024]{1,0:T(8,128)(2,1)} %collective-permute-done.2.refs_0_), channel_id=1, source_target_pairs={{0,1},{1,0},{2,3},{3,2},{4,5},{5,4},{6,7},{7,6},{8,9},{9,8},{10,11... | collective-permute-start | bytes 1179656 | tf_op jit(solution)/shard_map/ppermute | solution.py:396
  27.5 17.1 %collective-permute-start.10 = (bf16[768,256]{1,0:T(8,128)(2,1)S(1)}, bf16[768,256]{1,0:T(8,128)(2,1)S(1)}, u32[]{:S(2)}, u32[]{:S(2)}) collective-permute-start(bf16[768,256]{1,0:T(8,128)(2,1)S(1)} %get-tuple-element.56.query_hbm.refs_5_), channel_id=1, source_target_pairs={{0,4},{4,0},{8,12},{12,8},{16,20},{20,16},{24,28},{28,24},{1,5},{5... | collective-permute-start | bytes 1179656 | tf_op jit(solution)/shard_map/ppermute | solution.py:396
  27.5 15.1 %collective-permute-start.11 = (bf16[768,256]{1,0:T(8,128)(2,1)S(1)}, bf16[768,256]{1,0:T(8,128)(2,1)S(1)}, u32[]{:S(2)}, u32[]{:S(2)}) collective-permute-start(bf16[768,256]{1,0:T(8,128)(2,1)S(1)} %get-tuple-element.56.query_hbm.refs_5_), channel_id=1, source_target_pairs={{24,4},{25,5},{26,6},{27,7}} | collective-permute-start | bytes 1179656 | tf_op jit(solution)/shard_map/ppermute | solution.py:464
  34.1 1.0 %copy-start.7 = (bf16[768,256]{1,0:T(8,128)(2,1)S(1)}, bf16[768,256]{1,0:T(8,128)(2,1)}, u32[]{:S(2)}) copy-start(bf16[768,256]{1,0:T(8,128)(2,1)} %copy-done.6) | copy-start | bytes 1179652
  35.1 1.0 %copy-start.10 = (bf16[256,768]{1,0:T(8,128)(2,1)S(1)}, bf16[256,768]{1,0:T(8,128)(2,1)}, u32[]{:S(2)}) copy-start(bf16[256,768]{1,0:T(8,128)(2,1)} %copy-done.9) | copy-start | bytes 1179652
  36.1 7.8 %copy-start.8 = (bf16[768,256]{1,0:T(8,128)(2,1)S(1)}, bf16[768,256]{1,0:T(8,128)(2,1)}, u32[]{:S(2)}) copy-start(bf16[768,256]{1,0:T(8,128)(2,1)} %copy-done.6) | copy-start | bytes 1179652
  36.1 7.8 %copy-start.11 = (bf16[256,768]{1,0:T(8,128)(2,1)S(1)}, bf16[256,768]{1,0:T(8,128)(2,1)}, u32[]{:S(2)}) copy-start(bf16[256,768]{1,0:T(8,128)(2,1)} %copy-done.9) | copy-start | bytes 1179652
  39.1 6.3 %collective-permute-start.9 = (bf16[192,1024]{1,0:T(8,128)(2,1)}, bf16[192,1024]{1,0:T(8,128)(2,1)S(1)}, u32[]{:S(2)}, u32[]{:S(2)}) collective-permute-start(bf16[192,1024]{1,0:T(8,128)(2,1)} %collective-permute-done.5.refs_2_), channel_id=1, source_target_pairs={{0,1},{1,0},{2,3},{3,2},{4,5},{5,4},{6,7},{7,6},{8,9},{9,8},{10,11... | collective-permute-start | bytes 1179656 | tf_op jit(solution)/shard_map/ppermute | solution.py:396
  39.5 17.0 %collective-permute-start.7 = (bf16[192,1024]{1,0:T(8,128)(2,1)S(1)}, bf16[192,1024]{1,0:T(8,128)(2,1)S(1)}, u32[]{:S(2)}, u32[]{:S(2)}) collective-permute-start(bf16[192,1024]{1,0:T(8,128)(2,1)S(1)} %collective-permute-done.4.refs_0_), channel_id=1, source_target_pairs={{0,2},{1,3},{2,0},{3,1},{4,6},{5,7},{6,4},{7,5},{8,10},{9,11},{10,... | collective-permute-start | bytes 1179656 | tf_op jit(solution)/shard_map/ppermute | solution.py:396
  42.6 13.8 %collective-permute-start.12 = (bf16[2,128,256]{2,1,0:T(8,128)(2,1)S(1)}, bf16[2,128,256]{2,1,0:T(8,128)(2,1)S(1)}, u32[]{:S(2)}, u32[]{:S(2)}) collective-permute-start(bf16[2,128,256]{2,1,0:T(8,128)(2,1)S(1)} %get-tuple-element.64), channel_id=1, source_target_pairs={{0,24},{4,28},{1,25},{5,29},{2,26},{6,30},{3,27},{7,31}} | collective-permute-start | bytes 393224 | tf_op jit(solution)/shard_map/ppermute | solution.py:465
  44.6 12.0 %collective-permute-start.6 = (bf16[192,1024]{1,0:T(8,128)(2,1)S(1)}, bf16[192,1024]{1,0:T(8,128)(2,1)S(1)}, u32[]{:S(2)}, u32[]{:S(2)}) collective-permute-start(bf16[192,1024]{1,0:T(8,128)(2,1)S(1)} %collective-permute-done.4.refs_0_), channel_id=1, source_target_pairs={{0,1},{1,0},{2,3},{3,2},{4,5},{5,4},{6,7},{7,6},{8,9},{9,8},{10,11... | collective-permute-start | bytes 1179656 | tf_op jit(solution)/shard_map/ppermute | solution.py:396
  56.4 6.3 %copy-start.3 = (bf16[256,1024]{1,0:T(8,128)(2,1)S(1)}, bf16[256,1024]{1,0:T(8,128)(2,1)}, u32[]{:S(2)}) copy-start(bf16[256,1024]{1,0:T(8,128)(2,1)} %refs_2_) | copy-start | bytes 1572868
  56.4 8.2 %copy-start.5 = (bf16[256]{0:T(256)(128)(2,1)S(1)}, bf16[256]{0:T(256)(128)(2,1)}, u32[]{:S(2)}) copy-start(bf16[256]{0:T(256)(128)(2,1)} %gain_ref.3) | copy-start | bytes 1540
  56.4 8.2 %copy-start.13 = (bf16[768,256]{1,0:T(8,128)(2,1)S(1)}, bf16[768,256]{1,0:T(8,128)(2,1)}, u32[]{:S(2)}) copy-start(bf16[768,256]{1,0:T(8,128)(2,1)} %copy-done.12) | copy-start | bytes 1179652
  56.5 1.8 %collective-permute-start.13 = (bf16[192,1024]{1,0:T(8,128)(2,1)S(1)}, bf16[192,1024]{1,0:T(8,128)(2,1)S(1)}, u32[]{:S(2)}, u32[]{:S(2)}) collective-permute-start(bf16[192,1024]{1,0:T(8,128)(2,1)S(1)} %collective-permute-done.7.refs_2_), channel_id=1, source_target_pairs={{0,1},{1,0},{2,3},{3,2},{4,5},{5,4},{6,7},{7,6},{8,9},{9,8},{10,11... | collective-permute-start | bytes 1179656 | tf_op jit(solution)/shard_map/ppermute | solution.py:396
  62.8 19.6 %collective-permute-start.15 = (bf16[256,1024]{1,0:T(8,128)(2,1)S(1)}, bf16[256,1024]{1,0:T(8,128)(2,1)S(1)}, u32[]{:S(2)}, u32[]{:S(2)}) collective-permute-start(bf16[256,1024]{1,0:T(8,128)(2,1)S(1)} %copy-done.3), channel_id=1, source_target_pairs={{0,1},{1,0},{2,3},{3,2},{4,5},{5,4},{6,7},{7,6},{8,9},{9,8},{10,11... | collective-permute-start | bytes 1572872 | tf_op jit(solution)/shard_map/ppermute | solution.py:396
  63.0 19.4 %collective-permute-start.16 = (bf16[256,1024]{1,0:T(8,128)(2,1)S(1)}, bf16[256,1024]{1,0:T(8,128)(2,1)S(1)}, u32[]{:S(2)}, u32[]{:S(2)}) collective-permute-start(bf16[256,1024]{1,0:T(8,128)(2,1)S(1)} %collective-permute-done.3.refs_4_), channel_id=1, source_target_pairs={{0,1},{1,0},{2,3},{3,2},{4,5},{5,4},{6,7},{7,6},{8,9},{9,8},{10,11... | collective-permute-start | bytes 1572872 | tf_op jit(solution)/shard_map/ppermute | solution.py:396
  63.4 19.0 %collective-permute-start.14 = (bf16[768,256]{1,0:T(8,128)(2,1)S(1)}, bf16[768,256]{1,0:T(8,128)(2,1)S(1)}, u32[]{:S(2)}, u32[]{:S(2)}) collective-permute-start(bf16[768,256]{1,0:T(8,128)(2,1)S(1)} %get-tuple-element.67), channel_id=1, source_target_pairs={{0,4},{4,0},{8,12},{12,8},{16,20},{20,16},{24,28},{28,24},{1,5},{5... | collective-permute-start | bytes 1179656 | tf_op jit(solution)/shard_map/ppermute | solution.py:396
  63.4 19.0 %collective-permute-start.17 = (bf16[768,256]{1,0:T(8,128)(2,1)S(1)}, bf16[768,256]{1,0:T(8,128)(2,1)S(1)}, u32[]{:S(2)}, u32[]{:S(2)}) collective-permute-start(bf16[768,256]{1,0:T(8,128)(2,1)S(1)} %shard_map.77), channel_id=1, source_target_pairs={{4,24},{5,25},{6,26},{7,27}} | collective-permute-start | bytes 1179656 | tf_op jit(solution)/shard_map/ppermute | solution.py:512
  69.4 15.9 %copy-start.2 = (bf16[768,1024]{1,0:T(8,128)(2,1)S(1)}, bf16[768,1024]{1,0:T(8,128)(2,1)}, u32[]{:S(2)}) copy-start(bf16[768,1024]{1,0:T(8,128)(2,1)} %refs_6_.1) | copy-start | bytes 4718596
  82.9 2.4 %collective-permute-start.19 = (bf16[768,256]{1,0:T(8,128)(2,1)S(1)}, bf16[768,256]{1,0:T(8,128)(2,1)S(1)}, u32[]{:S(2)}, u32[]{:S(2)}) collective-permute-start(bf16[768,256]{1,0:T(8,128)(2,1)S(1)} %shard_map.80.refs_0_), channel_id=1, source_target_pairs={{0,1},{1,0},{2,3},{3,2},{4,5},{5,4},{6,7},{7,6},{8,9},{9,8},{10,11... | collective-permute-start | bytes 1179656 | tf_op jit(solution)/shard_map/ppermute | solution.py:396
  83.9 10.7 %collective-permute-start.18 = (bf16[768,256]{1,0:T(8,128)(2,1)S(1)}, bf16[768,256]{1,0:T(8,128)(2,1)S(1)}, u32[]{:S(2)}, u32[]{:S(2)}) collective-permute-start(bf16[768,256]{1,0:T(8,128)(2,1)S(1)} %shard_map.80.refs_0_), channel_id=1, source_target_pairs={{0,2},{1,3},{2,0},{3,1},{4,6},{5,7},{6,4},{7,5},{8,10},{9,11},{10,... | collective-permute-start | bytes 1179656 | tf_op jit(solution)/shard_map/ppermute | solution.py:396
  94.6 2.2 %collective-permute-start.20 = (bf16[768,256]{1,0:T(8,128)(2,1)S(1)}, bf16[768,256]{1,0:T(8,128)(2,1)S(1)}, u32[]{:S(2)}, u32[]{:S(2)}) collective-permute-start(bf16[768,256]{1,0:T(8,128)(2,1)S(1)} %collective-permute-done.18.refs_0_), channel_id=1, source_target_pairs={{0,1},{1,0},{2,3},{3,2},{4,5},{5,4},{6,7},{7,6},{8,9},{9,8},{10,11... | collective-permute-start | bytes 1179656 | tf_op jit(solution)/shard_map/ppermute | solution.py:396

commit v2 on v1

--- a/solution.py
+++ b/solution.py
@@ -135,8 +135,8 @@
 
 
 def own_kernel(
-    history_hbm, gain_hbm, w_ref, gate_hbm, values_hbm, query_hbm, keys_t_hbm, tail_hbm,
-    history_ref, gain_ref, gate_ref, values_ref, query_ref, keys_t_ref, tail_ref, sems, out_sems,
+    history_hbm, gain_hbm, w_ref, gate_hbm, both_hbm, query_hbm, keys_t_hbm, tail_hbm,
+    history_ref, gain_ref, gate_ref, both_ref, query_ref, keys_t_ref, sems, out_sems,
 ):
     rows = query_ref.shape[0]
     part = 2 * BLK
@@ -146,22 +146,21 @@
     )
     gain_copy.wait()
     gain = gain_ref[...].reshape(1, -1)
-    for at, copy in zip(parts, copies):
+    for p, (at, copy) in enumerate(zip(parts, copies)):
         copy.wait()
         here = normed(history_ref[at, :], gain)
         query_ref[at, :] = project(here, w_ref[2]).astype(jnp.bfloat16)
         keys = project(here, w_ref[3])
         keys_t_ref[:, at] = keys.T.astype(jnp.bfloat16)
-        values = project(here, w_ref[1]).astype(jnp.bfloat16)
-        values_ref[at, :] = values
+        both_ref[at, :] = keys.astype(jnp.bfloat16)
+        both_ref[pl.ds(rows + p * part, part), :] = project(here, w_ref[1]).astype(jnp.bfloat16)
         gate_ref[at, :] = project(here, w_ref[0]).astype(jnp.bfloat16)
-    tail_ref[0] = keys[-BLK:].astype(jnp.bfloat16)
-    tail_ref[1] = values[-BLK:]
     wait(
         fetch(
             [
-                (query_ref, query_hbm), (values_ref, values_hbm), (keys_t_ref, keys_t_hbm),
-                (gate_ref, gate_hbm), (tail_ref, tail_hbm),
+                (query_ref, query_hbm), (both_ref, both_hbm), (keys_t_ref, keys_t_hbm), (gate_ref, gate_hbm),
+                (both_ref.at[pl.ds(rows - BLK, BLK)], tail_hbm.at[0]),
+                (both_ref.at[pl.ds(2 * rows - BLK, BLK)], tail_hbm.at[1]),
             ],
             out_sems,
         )
@@ -169,12 +168,16 @@
 
 
 def own_attend_kernel(
-    told_ref, query_hbm, keys_t_hbm, values_hbm, sums_hbm, query_ref, keys_t_ref, values_ref, sums_ref, live_ref, sems
+    told_ref, query_hbm, keys_t_hbm, both_hbm, sums_hbm, query_ref, keys_t_ref, values_ref, sums_ref, live_ref, sems
 ):
     rows, cols = query_ref.shape
     blocks = rows // BLK
     copies = fetch(
-        [(query_hbm, query_ref), (keys_t_hbm, keys_t_ref), (values_hbm, values_ref)], sems
+        [
+            (query_hbm, query_ref), (keys_t_hbm, keys_t_ref),
+            (both_hbm.at[pl.ds(rows, rows)], values_ref),
+        ],
+        sems,
     )
     mark(live_ref, told_ref, lax.axis_index("seq") * blocks, blocks, 0)
     wait(copies)
@@ -220,22 +223,6 @@
         send_ref[:, at] = centred(sums_ref[:, at]).astype(jnp.bfloat16)
 
 
-def far_kernel(
-    told_ref, query_ref, keys_t_hbm, values_hbm, send_ref, keys_t_ref, values_ref, sums_ref, live_ref, sems
-):
-    blocks = query_ref.shape[0] // BLK
-    here = lax.axis_index("seq")
-
-    @pl.when((here % 2 == 1) & (here + FAR < lax.axis_size("seq")))
-    def _():
-        copies = fetch([(keys_t_hbm, keys_t_ref), (values_hbm, values_ref)], sems)
-        mark(live_ref, told_ref, here * blocks, blocks, 0)
-        sums_ref[...] = jnp.zeros_like(sums_ref)
-        wait(copies)
-        attend_all(query_ref, sums_ref, keys_t_ref, values_ref, live_ref, 0, blocks)
-        send_off(sums_ref, send_ref)
-
-
 def chunk_keys(pieces, w_ref, keys_ref, keys_t_ref, values_ref):
     share = pieces[0].shape[0]
     for m, piece in enumerate(pieces):
@@ -248,7 +235,7 @@
 def make_chunk_kernel(back, n_head):
     def kernel(told_ref, told_x_ref, *refs):
         pieces, refs = refs[:n_head], refs[n_head:]
-        w_ref, query_hbm, query_x_hbm, own_t_hbm, own_values_hbm, before_hbm, sums_hbm, sums_x_hbm = refs[:8]
+        w_ref, query_hbm, query_x_hbm, own_t_hbm, own_both_hbm, before_hbm, sums_hbm, sums_x_hbm = refs[:8]
         query_ref, query_x_ref, own_t_ref, own_values_ref, sums_ref, sums_x_ref = refs[8:14]
         keys_ref, keys_t_ref, values_ref, live_ref, sems, out_sems = refs[14:]
         blocks = query_ref.shape[0] // BLK
@@ -256,7 +243,8 @@
         source = here - 2 * back
         copies = fetch(
             [
-                (query_x_hbm, query_x_ref), (own_t_hbm, own_t_ref), (own_values_hbm, own_values_ref),
+                (query_x_hbm, query_x_ref), (own_t_hbm, own_t_ref),
+                (own_both_hbm.at[pl.ds(blocks * BLK, blocks * BLK)], own_values_ref),
                 (before_hbm, sums_ref), (query_hbm, query_ref),
             ],
             sems,
@@ -310,20 +298,30 @@
 
 def make_own_last_kernel(back):
     def kernel(
-        told_ref, query_hbm, keys_t_ref, values_ref, tail_ref, before_hbm, gate_hbm, gain_ref,
-        sums_ref, scale_ref, query_ref, gate_ref, live_ref, sems,
+        told_ref, query_hbm, keys_t_ref, values_ref, tail_ref, far_hbm, before_hbm, gate_hbm, gain_ref,
+        sums_ref, scale_ref, query_ref, gate_ref, far_ref, far_t_ref, live_ref, sems, far_sems,
     ):
         rows, cols = query_ref.shape
         blocks = rows // BLK
         here = lax.axis_index("seq")
         source = here - 2 * back
         copies = fetch([(query_hbm, query_ref), (before_hbm, sums_ref), (gate_hbm, gate_ref)], sems)
+        far_copies = fetch([(far_hbm, far_ref)], far_sems)
         mark(live_ref, told_ref, source * blocks, blocks, 0)
         wait(copies)
 
         @pl.when(source >= 0)
         def _():
             attend_all(query_ref, sums_ref, keys_t_ref, values_ref, live_ref, 0, blocks)
+
+        wait(far_copies)
+        far = here - FAR
+
+        @pl.when((far >= 0) & (here % 2 == 0))
+        def _():
+            far_t_ref[...] = far_ref[0:rows, :].astype(jnp.float32).T.astype(jnp.bfloat16)
+            mark(live_ref, told_ref, far * blocks, blocks, 0)
+            attend_all(query_ref, sums_ref, far_t_ref, far_ref.at[pl.ds(rows, rows)], live_ref, 0, blocks)
 
         farthest = here - FAR - 1
 
@@ -350,10 +348,10 @@
     return kernel
 
 
-def finish_kernel(sums_ref, near_ref, far_ref, scale_ref, out_ref):
+def finish_kernel(sums_ref, near_ref, scale_ref, out_ref):
     for h in range(sums_ref.shape[1] // DH):
         at = pl.ds(h * DH, DH)
-        part = sums_ref[:, at] + near_ref[:, at].astype(jnp.float32) + far_ref[:, at].astype(jnp.float32)
+        part = sums_ref[:, at] + near_ref[:, at].astype(jnp.float32)
         off = centred(part)
         spread_sq = jnp.mean(jnp.square(off), axis=-1, keepdims=True)
         out_ref[:, at] = (off * lax.rsqrt(spread_sq + EPS) * scale_ref[:, at]).astype(jnp.bfloat16)
@@ -440,19 +438,22 @@
     gain, block_lists, counts, w_out, share = barrier((ln_gain, block_lists, counts, w_out, share))
     told = jnp.concatenate([block_lists, counts[:, None]], axis=1)
     upward = [(i, i + 2) for i in range(n_seq - 2)]
-    downward = [(i, i - FAR) for i in range(FAR + 1, n_seq, 2)]
     share_1 = lax.ppermute(share, "seq", upward)
 
-    gate, values, query, keys_t, tail = pl.pallas_call(
+    gate, both, query, keys_t, tail = pl.pallas_call(
         own_kernel,
         in_specs=[far_off, far_off, wide],
         out_specs=[far_off] * 5,
-        out_shape=[shape(bf16, *upright)] * 3 + [shape(bf16, *lying), shape(bf16, 2, BLK, cols)],
-        scratch_shapes=[pltpu.VMEM((tok_rows, width), bf16), pltpu.VMEM((width,), bf16)]
-        + [pltpu.VMEM(upright, bf16)] * 3
-        + [pltpu.VMEM(lying, bf16), pltpu.VMEM((2, BLK, cols), bf16)]
-        + [sems(1 + tok_rows // (2 * BLK)), sems(5)],
-        compiler_params=params(),
+        out_shape=[
+            shape(bf16, *upright), shape(bf16, 2 * tok_rows, cols), shape(bf16, *upright),
+            shape(bf16, *lying), shape(bf16, 2, BLK, cols),
+        ],
+        scratch_shapes=[
+            pltpu.VMEM((tok_rows, width), bf16), pltpu.VMEM((width,), bf16), pltpu.VMEM(upright, bf16),
+            pltpu.VMEM((2 * tok_rows, cols), bf16), pltpu.VMEM(upright, bf16), pltpu.VMEM(lying, bf16),
+            sems(1 + tok_rows // (2 * BLK)), sems(6),
+        ],
+        compiler_params=params(60),
         cost_estimate=cost(4),
     )(history, gain, w_in)
 
@@ -461,9 +462,8 @@
     share_2 = lax.ppermute(share_1, "seq", upward)
     cross_1 = crossed(share_1, "head", n_head // 2)
     query_x, told_x = crossed(query, "seq", 1), crossed(told, "seq", 1)
-    query_far, told_far = (lax.ppermute(a, "seq", downward) for a in (query, told))
     tail = lax.ppermute(tail, "seq", [(i, i + FAR + 1) for i in range(n_seq - FAR - 1)])
-    told, told_x, told_far = barrier((told, told_x, told_far))
+    told, told_x = barrier((told, told_x))
     own_sums = pl.pallas_call(
         own_attend_kernel,
         in_specs=[flat] + [far_off] * 3,
@@ -473,23 +473,14 @@
         + [pltpu.VMEM(upright, f32), live, sems(3)],
         compiler_params=params(),
         cost_estimate=cost(4),
-    )(told, query, keys_t, values)
+    )(told, query, keys_t, both)
     share_2, cross_1, own_sums = barrier((share_2, cross_1, own_sums))
     chunk_1 = spread(share_1, n_head // 4) + spread(cross_1, n_head // 4)
     cross_2 = crossed(share_2, "head", n_head // 2)
     near_2 = spread(share_2, n_head // 4)
 
-    far = pl.pallas_call(
-        far_kernel,
-        in_specs=[flat, wide, far_off, far_off],
-        out_specs=wide,
-        out_shape=shape(bf16, *upright),
-        scratch_shapes=[
-            pltpu.VMEM(lying, bf16), pltpu.VMEM(upright, bf16), pltpu.VMEM(upright, f32), live, sems(2)
-        ],
-        compiler_params=params(),
-        cost_estimate=cost(2),
-    )(told_far, query_far, keys_t, values)
+    both, share_2 = barrier((both, share_2))
+    far = lax.ppermute(both, "seq", [(i, i + FAR) for i in range(1, n_seq - FAR, 2)])
 
     sums, sums_x = pl.pallas_call(
         make_chunk_kernel(1, n_head),
@@ -506,10 +497,9 @@
         + [live, sems(5), sems(2)],
         compiler_params=params(16),
         cost_estimate=cost(6),
-    )(told, told_x, *chunk_1, w_in, query, query_x, keys_t, values, own_sums)
+    )(told, told_x, *chunk_1, w_in, query, query_x, keys_t, both, own_sums)
 
     cross_2, sums_x, far, tail = barrier((cross_2, sums_x, far, tail))
-    far = lax.ppermute(far, "seq", [(i, i + FAR) for i in range(1, n_seq - FAR, 2)])
     send, keys_t, values = pl.pallas_call(
         make_last_kernel(PLANES, n_head),
         in_specs=[flat] + [wide] * (n_head + 1) + [far_off] * 2,
@@ -526,22 +516,23 @@
     w_all = spread(w_out, n_head // 4) + spread(w_cross, n_head // 4)
     mine, scale = pl.pallas_call(
         make_own_last_kernel(PLANES),
-        in_specs=[flat, far_off, wide, wide, wide, far_off, far_off, wide],
+        in_specs=[flat, far_off, wide, wide, wide, far_off, far_off, far_off, wide],
         out_specs=[wide] * 2,
         out_shape=[shape(f32, *upright)] * 2,
-        scratch_shapes=[pltpu.VMEM(upright, bf16)] * 2 + [live, sems(3)],
+        scratch_shapes=[pltpu.VMEM(upright, bf16)] * 2
+        + [pltpu.VMEM((2 * tok_rows, cols), bf16), pltpu.VMEM(lying, bf16), live, sems(3), sems(1)],
         compiler_params=params(),
         cost_estimate=cost(3),
-    )(told, query, keys_t, values, tail, sums, gate, out_gain)
+    )(told, query, keys_t, values, tail, far, sums, gate, out_gain)
     near, mine, w_all = barrier((near, mine, tuple(w_all)))
     gated = pl.pallas_call(
         finish_kernel,
-        in_specs=[wide] * 4,
+        in_specs=[wide] * 3,
         out_specs=wide,
         out_shape=shape(bf16, *upright),
         compiler_params=params(),
         cost_estimate=cost(1),
-    )(mine, near, far, scale)
+    )(mine, near, scale)
 
     out_cols = width // n_head
     cross_gated = crossed(gated, "head", n_head // 2)

time: 98.5 us -> 103 us (1.046)
  waiting for transfers between devices: 31.5 us -> 46.8 us
  starting transfers between devices: 27.5 us -> 16.7 us
  Pallas kernels: 32.8 us -> 36.8 us
  local copies, waits for them, and re-layouts: 5.77 us -> 2.13 us
    ppermute x15, waiting for transfers between devices: 25.5 us -> 42.1 us  [crossed(): lax.ppermute(array, axis, [(i, i ^ bit) for i in range(lax.axis_size(axis...]
    ppermute x3 -> x1, starting transfers between devices: 11.6 us -> 1.28 us  [body(): lax.ppermute(both, 'seq', [(i, i + FAR) for i in range(1, n_seq - FAR, 2)])]
    unnamed x32 -> x24, local copies, waits for them, and re-layouts: 5.68 us -> 2.04 us
    ppermute x3 -> x1, waiting for transfers between devices: 3.21 us -> 0.01 us  [body(): lax.ppermute(both, 'seq', [(i, i + FAR) for i in range(1, n_seq - FAR, 2)])]
    pallas_call x1, Pallas kernels: 4.75 us -> 7.57 us  [body(): pl.pallas_call(make_own_last_kernel(PLANES), in_specs=[flat, far_off, wid...]
    pallas_call x1, Pallas kernels: 4.07 us -> 6.85 us  [body(): pl.pallas_call(own_kernel, in_specs=[far_off, far_off, wide], out_specs=[...]
    pallas_call x1, Pallas kernels: 11 us -> 9.51 us  [body(): pl.pallas_call(make_chunk_kernel(1, n_head), in_specs=[flat] * 2 + [wide]...]
    ppermute x1, waiting for transfers between devices: 0.01 us -> 1.1 us  [body(): share_2 = lax.ppermute(share_1, 'seq', upward)]
  transfers between devices with their start and end apart: 21 -> 19, of which waited for: 8 -> 9; matrix products, arithmetic and copies ran while one was open for 0% -> 0% of each run, Pallas kernels for 24% -> 27%
where the time goes in v2:
time: 103 us
  waiting for transfers between devices  46.8 us (45%)
  Pallas kernels  36.8 us (36%)
  starting transfers between devices  16.7 us (16%)
  local copies, waits for them, and re-layouts  2.13 us (2%)
    ppermute x15, waiting for transfers between devices, crossed(): lax.ppermute(array, axis, [(i, i ^ bit) for i in range(lax.axis_size(axis...  42.1 us
    ppermute x15, starting transfers between devices, crossed(): lax.ppermute(array, axis, [(i, i ^ bit) for i in range(lax.axis_size(axis...  11.6 us
    pallas_call x1, Pallas kernels, body(): pl.pallas_call(make_chunk_kernel(1, n_head), in_specs=[flat] * 2 + [wide]...  9.51 us
    pallas_call x1, Pallas kernels, body(): pl.pallas_call(make_own_last_kernel(PLANES), in_specs=[flat, far_off, wid...  7.57 us
    pallas_call x1, Pallas kernels, body(): pl.pallas_call(own_kernel, in_specs=[far_off, far_off, wide], out_specs=[...  6.85 us
    pallas_call x1, Pallas kernels, body(): pl.pallas_call(make_last_kernel(PLANES, n_head), in_specs=[flat] + [wide]...  4.8 us
    ppermute x1, waiting for transfers between devices, body(): share_1 = lax.ppermute(share, 'seq', upward)  3.61 us
    pallas_call x1, Pallas kernels, body(): pl.pallas_call(own_attend_kernel, in_specs=[flat] + [far_off] * 3, out_sp...  3.32 us
  transfers between devices with their start and end apart: 19, of which 9 were waited for; matrix products, arithmetic and copies ran while one was open for 0% of the time, Pallas kernels for 27%

profile of v2, /device:TPU:25, one launch (start us, length us, event | category | flops | bytes accessed | tf_op | source)
XLA Modules:
  0.0 102.8 jit_solution(99347061079694131)
XLA Ops:
  0.0 2.6 %shard_map.73 = bf16[192,1024]{1,0:T(8,128)(2,1)} custom-call(bf16[768,1024]{1,0:T(8,128)(2,1)} %refs_6_.1, bf16[1024]{0:T(1024)(128)(2,1)} %gain_hbm), custom_call_target="tpu_custom_call" | custom-call | flops 600000000 | bytes 1800000 | tf_op jit(solution)/shard_map/pallas_call | solution.py:425
  2.6 0.0 copy-start.10
  2.6 0.0 copy-start.9
  2.6 1.3 %collective-permute-start.2 = (bf16[256,1024]{1,0:T(8,128)(2,1)S(1)}, bf16[256,1024]{1,0:T(8,128)(2,1)S(1)}, u32[]{:S(2)}, u32[]{:S(2)}) collective-permute-start(bf16[256,1024]{1,0:T(8,128)(2,1)S(1)} %copy-done.2), channel_id=1, source_target_pairs={{0,2},{1,3},{2,0},{3,1},{4,6},{5,7},{6,4},{7,5},{8,10},{9,11},{10,... | collective-permute-start | bytes 1572872 | tf_op jit(solution)/shard_map/ppermute | solution.py:394
  3.9 1.3 %collective-permute-start.1 = (bf16[192,1024]{1,0:T(8,128)(2,1)}, bf16[192,1024]{1,0:T(8,128)(2,1)S(1)}, u32[]{:S(2)}, u32[]{:S(2)}) collective-permute-start(bf16[192,1024]{1,0:T(8,128)(2,1)} %shard_map.73), channel_id=1, source_target_pairs={{0,8},{4,12},{8,16},{12,20},{16,24},{20,28},{1,9},{5,13},{9,17},{1... | collective-permute-start | bytes 1179656 | tf_op jit(solution)/shard_map/ppermute | solution.py:441
  5.2 6.8 %shard_map.74 = (bf16[768,256]{1,0:T(8,128)(2,1)}, bf16[1536,256]{1,0:T(8,128)(2,1)}, bf16[768,256]{1,0:T(8,128)(2,1)}, bf16[256,768]{1,0:T(8,128)(2,1)}, bf16[2,128,256]{2,1,0:T(8,128)(2,1)}) custom-call(bf16[768,1024]{1,0:T(8,128)(2,1)} %refs_6_.1, bf16[1024]{0:T(1024)(128)(2,1)} %gain_hbm, bf16[4,1024,256]{2,1,0:T(8,128)(2,1)} %refs_4_.3), custom_call_target="tpu_custom_call" | custom-call | flops 1200000000 | bytes 3600000 | tf_op jit(solution)/shard_map/pallas_call | solution.py:443
  12.1 3.6 %collective-permute-done.1.refs_0_ = bf16[192,1024]{1,0:T(8,128)(2,1)S(1)} collective-permute-done((bf16[192,1024]{1,0:T(8,128)(2,1)}, bf16[192,1024]{1,0:T(8,128)(2,1)S(1)}, u32[]{:S(2)}, u32[]{:S(2)}) %collective-permute-start.1) | collective-permute-done | bytes 393248 | tf_op jit(solution)/shard_map/ppermute | solution.py:441
  15.7 0.0 collective-permute-done.2.refs_4_
  15.7 1.0 %collective-permute-start.4 = (bf16[192,1024]{1,0:T(8,128)(2,1)S(1)}, bf16[192,1024]{1,0:T(8,128)(2,1)S(1)}, u32[]{:S(2)}, u32[]{:S(2)}) collective-permute-start(bf16[192,1024]{1,0:T(8,128)(2,1)S(1)} %collective-permute-done.1.refs_0_), channel_id=1, source_target_pairs={{0,2},{1,3},{2,0},{3,1},{4,6},{5,7},{6,4},{7,5},{8,10},{9,11},{10,... | collective-permute-start | bytes 1179656 | tf_op jit(solution)/shard_map/ppermute | solution.py:394
  16.7 1.3 %collective-permute-start.3 = (bf16[192,1024]{1,0:T(8,128)(2,1)S(1)}, bf16[192,1024]{1,0:T(8,128)(2,1)S(1)}, u32[]{:S(2)}, u32[]{:S(2)}) collective-permute-start(bf16[192,1024]{1,0:T(8,128)(2,1)S(1)} %collective-permute-done.1.refs_0_), channel_id=1, source_target_pairs={{0,8},{4,12},{8,16},{12,20},{16,24},{20,28},{1,9},{5,13},{9,17},{1... | collective-permute-start | bytes 1179656 | tf_op jit(solution)/shard_map/ppermute | solution.py:462
  18.0 0.1 copy.8
  18.1 0.1 pad_add_fusion.told_ref
  18.2 1.2 %collective-permute-start = (s32[6,17]{1,0:T(8,128)S(1)}, s32[6,17]{1,0:T(8,128)S(1)}, u32[]{:S(2)}, u32[]{:S(2)}) collective-permute-start(s32[6,17]{1,0:T(8,128)S(1)} %pad_add_fusion.told_ref), channel_id=1, source_target_pairs={{0,4},{4,0},{8,12},{12,8},{16,20},{20,16},{24,28},{28,24},{1,5},{5... | collective-permute-start | bytes 1232 | tf_op jit(solution)/shard_map/ppermute | solution.py:394
  19.4 1.5 %collective-permute-done.told_x_ref = s32[6,17]{1,0:T(8,128)S(1)} collective-permute-done((s32[6,17]{1,0:T(8,128)S(1)}, s32[6,17]{1,0:T(8,128)S(1)}, u32[]{:S(2)}, u32[]{:S(2)}) %collective-permute-start) | collective-permute-done | bytes 440 | tf_op jit(solution)/shard_map/ppermute | solution.py:394
  20.9 1.0 copy-done.3
  21.9 1.0 copy-done.7
  22.9 3.3 %shard_map.75.refs_9_ = f32[768,256]{1,0:T(8,128)S(1)} custom-call(s32[6,17]{1,0:T(8,128)S(1)} %pad_add_fusion.told_ref, bf16[768,256]{1,0:T(8,128)(2,1)S(1)} %copy-done.3, bf16[256,768]{1,0:T(8,128)(2,1)S(1)} %copy-done.7, bf16[1536,256]{1,0:T(8,128)(2,1)} %get-tuple-element.61.both_hbm.refs_8_), custom_call_target="tpu_custom_call" | custom-call | flops 1200000000 | bytes 3600000 | tf_op jit(solution)/shard_map/pallas_call | solution.py:467
  26.3 0.0 collective-permute-done.4.refs_2_
  26.3 1.1 %collective-permute-done.3.refs_0_ = bf16[192,1024]{1,0:T(8,128)(2,1)S(1)} collective-permute-done((bf16[192,1024]{1,0:T(8,128)(2,1)S(1)}, bf16[192,1024]{1,0:T(8,128)(2,1)S(1)}, u32[]{:S(2)}, u32[]{:S(2)}) %collective-permute-start.3) | collective-permute-done | bytes 393248 | tf_op jit(solution)/shard_map/ppermute | solution.py:462
  27.4 1.3 %collective-permute-start.10 = (bf16[1536,256]{1,0:T(8,128)(2,1)}, bf16[1536,256]{1,0:T(8,128)(2,1)S(1)}, u32[]{:S(2)}, u32[]{:S(2)}) collective-permute-start(bf16[1536,256]{1,0:T(8,128)(2,1)} %get-tuple-element.61.both_hbm.refs_8_), channel_id=1, source_target_pairs={{4,24},{5,25},{6,26},{7,27}} | collective-permute-start | bytes 2359304 | tf_op jit(solution)/shard_map/ppermute | solution.py:483
  28.7 2.8 %collective-permute-start.7 = (bf16[192,1024]{1,0:T(8,128)(2,1)S(1)}, bf16[192,1024]{1,0:T(8,128)(2,1)S(1)}, u32[]{:S(2)}, u32[]{:S(2)}) collective-permute-start(bf16[192,1024]{1,0:T(8,128)(2,1)S(1)} %collective-permute-done.1.refs_0_), channel_id=1, source_target_pairs={{0,1},{1,0},{2,3},{3,2},{4,5},{5,4},{6,7},{7,6},{8,9},{9,8},{10,11... | collective-permute-start | bytes 1179656 | tf_op jit(solution)/shard_map/ppermute | solution.py:394
  31.5 0.6 collective-permute-start.9
  32.1 0.3 collective-permute-start.8
  32.5 0.4 collective-permute-start.6
  32.9 0.0 collective-permute-done.7.refs_1_
  32.9 1.3 %collective-permute-start.11 = (bf16[2,128,256]{2,1,0:T(8,128)(2,1)S(1)}, bf16[2,128,256]{2,1,0:T(8,128)(2,1)S(1)}, u32[]{:S(2)}, u32[]{:S(2)}) collective-permute-start(bf16[2,128,256]{2,1,0:T(8,128)(2,1)S(1)} %copy-done.11), channel_id=1, source_target_pairs={{0,24},{4,28},{1,25},{5,29},{2,26},{6,30},{3,27},{7,31}} | collective-permute-start | bytes 393224 | tf_op jit(solution)/shard_map/ppermute | solution.py:465
  34.2 24.8 %collective-permute-done.9.refs_6_.refs_5_ = bf16[768,256]{1,0:T(8,128)(2,1)S(1)} collective-permute-done((bf16[768,256]{1,0:T(8,128)(2,1)S(1)}, bf16[768,256]{1,0:T(8,128)(2,1)S(1)}, u32[]{:S(2)}, u32[]{:S(2)}) %collective-permute-start.9) | collective-permute-done | bytes 393248 | tf_op jit(solution)/shard_map/ppermute | solution.py:394
  59.0 0.8 collective-permute-start.5
  59.9 9.5 %shard_map.76 = (f32[768,256]{1,0:T(8,128)S(1)}, f32[768,256]{1,0:T(8,128)S(1)}) custom-call(s32[6,17]{1,0:T(8,128)S(1)} %pad_add_fusion.told_ref, s32[6,17]{1,0:T(8,128)S(1)} %collective-permute-done.told_x_ref, bf16[192,1024]{1,0:T(8,128)(2,1)S(1)} %collective-permute-done.1.refs_0_, bf16[192,1024]{1,0:T(8,128)(2,1)S(1)} %collective-permute-done.7.refs_1_, ...), custom_call_target="tpu_custom_call" | custom-call | flops 1800000000 | bytes 5400000 | tf_op jit(solution)/shard_map/pallas_call | solution.py:485
  69.4 0.0 copy-start.5
  69.5 0.0 copy-start.6
  69.5 0.1 collective-permute-start.12
  69.6 1.7 %collective-permute-done.12.refs_3_ = bf16[192,1024]{1,0:T(8,128)(2,1)S(1)} collective-permute-done((bf16[192,1024]{1,0:T(8,128)(2,1)S(1)}, bf16[192,1024]{1,0:T(8,128)(2,1)S(1)}, u32[]{:S(2)}, u32[]{:S(2)}) %collective-permute-start.12) | collective-permute-done | bytes 393248 | tf_op jit(solution)/shard_map/ppermute | solution.py:394
  71.3 4.8 %shard_map.77 = (bf16[768,256]{1,0:T(8,128)(2,1)S(1)}, bf16[256,768]{1,0:T(8,128)(2,1)S(1)}, bf16[768,256]{1,0:T(8,128)(2,1)S(1)}) custom-call(s32[6,17]{1,0:T(8,128)S(1)} %collective-permute-done.told_x_ref, bf16[192,1024]{1,0:T(8,128)(2,1)S(1)} %collective-permute-done.3.refs_0_, bf16[192,1024]{1,0:T(8,128)(2,1)S(1)} %collective-permute-done.5.refs_1_, ...), custom_call_target="tpu_custom_call" | custom-call | flops 1200000000 | bytes 3600000 | tf_op jit(solution)/shard_map/pallas_call | solution.py:503
  76.1 0.2 collective-permute-start.14
  76.3 0.4 collective-permute-start.15
  76.7 0.0 copy-start.1
  76.7 7.6 %shard_map.78 = (f32[768,256]{1,0:T(8,128)S(1)}, f32[768,256]{1,0:T(8,128)S(1)}) custom-call(s32[6,17]{1,0:T(8,128)S(1)} %pad_add_fusion.told_ref, bf16[768,256]{1,0:T(8,128)(2,1)S(1)} %copy-done.4, bf16[256,768]{1,0:T(8,128)(2,1)S(1)} %get-tuple-element.68.keys_t_ref, bf16[768,256]{1,0:T(8,128)(2,1)S(1)} %get-tuple-element.69.values_ref, ...), custom_call_target="tpu_custom_call" | custom-call | flops 900000000 | bytes 2700000 | tf_op jit(solution)/shard_map/pallas_call | solution.py:517
  84.2 3.0 %collective-permute-done.13.near_ref = bf16[768,256]{1,0:T(8,128)(2,1)S(1)} collective-permute-done((bf16[768,256]{1,0:T(8,128)(2,1)S(1)}, bf16[768,256]{1,0:T(8,128)(2,1)S(1)}, u32[]{:S(2)}, u32[]{:S(2)}) %collective-permute-start.13) | collective-permute-done | bytes 393248 | tf_op jit(solution)/shard_map/ppermute | solution.py:394
  87.2 0.5 shard_map.79.refs_0_
  87.7 1.0 collective-permute-start.17
  88.8 0.4 collective-permute-start.16
  89.2 0.9 collective-permute-done.17.refs_1_
  90.1 0.5 shard_map.80
  90.7 8.8 %collective-permute-done.16.refs_0_ = bf16[768,256]{1,0:T(8,128)(2,1)S(1)} collective-permute-done((bf16[768,256]{1,0:T(8,128)(2,1)S(1)}, bf16[768,256]{1,0:T(8,128)(2,1)S(1)}, u32[]{:S(2)}, u32[]{:S(2)}) %collective-permute-start.16) | collective-permute-done | bytes 393248 | tf_op jit(solution)/shard_map/ppermute | solution.py:394
  99.5 0.8 collective-permute-start.18
  100.3 1.3 %collective-permute-done.18.refs_1_ = bf16[768,256]{1,0:T(8,128)(2,1)S(1)} collective-permute-done((bf16[768,256]{1,0:T(8,128)(2,1)S(1)}, bf16[768,256]{1,0:T(8,128)(2,1)S(1)}, u32[]{:S(2)}, u32[]{:S(2)}) %collective-permute-start.18) | collective-permute-done | bytes 393248 | tf_op jit(solution)/shard_map/ppermute | solution.py:394
  101.7 1.1 %shard_map.81 = bf16[768,256]{1,0:T(8,128)(2,1)} custom-call(bf16[768,256]{1,0:T(8,128)(2,1)S(1)} %collective-permute-done.16.refs_0_, bf16[768,256]{1,0:T(8,128)(2,1)S(1)} %collective-permute-done.18.refs_1_, bf16[512,256]{1,0:T(8,128)(2,1)S(1)} %get-tuple-element.87.refs_2_, f32[768,256]{1,0:T(8,128)S(1)} %get-tuple-element.88.refs_3_), custom_call_target="tpu_custom_call" | custom-call | flops 600000000 | bytes 1800000 | tf_op jit(solution)/shard_map/pallas_call | solution.py:554
  (25 shorter events, 0.1 us)
Async XLA Ops:
  0.0 2.6 %copy-start.2 = (bf16[256,1024]{1,0:T(8,128)(2,1)S(1)}, bf16[256,1024]{1,0:T(8,128)(2,1)}, u32[]{:S(2)}) copy-start(bf16[256,1024]{1,0:T(8,128)(2,1)} %refs_2_) | copy-start | bytes 1572868
  2.6 15.4 %copy-start.10 = (s32[6]{0:T(128)S(1)}, s32[6]{0:T(128)}, u32[]{:S(2)}) copy-start(s32[6]{0:T(128)} %param.13) | copy-start | bytes 76
  2.6 15.5 %copy-start.9 = (s32[6,16]{1,0:T(8,128)S(1)}, s32[6,16]{1,0:T(8,128)}, u32[]{:S(2)}) copy-start(s32[6,16]{1,0:T(8,128)} %param.12) | copy-start | bytes 1156
  2.6 13.1 %collective-permute-start.2 = (bf16[256,1024]{1,0:T(8,128)(2,1)S(1)}, bf16[256,1024]{1,0:T(8,128)(2,1)S(1)}, u32[]{:S(2)}, u32[]{:S(2)}) collective-permute-start(bf16[256,1024]{1,0:T(8,128)(2,1)S(1)} %copy-done.2), channel_id=1, source_target_pairs={{0,2},{1,3},{2,0},{3,1},{4,6},{5,7},{6,4},{7,5},{8,10},{9,11},{10,... | collective-permute-start | bytes 1572872 | tf_op jit(solution)/shard_map/ppermute | solution.py:394
  3.9 11.8 %collective-permute-start.1 = (bf16[192,1024]{1,0:T(8,128)(2,1)}, bf16[192,1024]{1,0:T(8,128)(2,1)S(1)}, u32[]{:S(2)}, u32[]{:S(2)}) collective-permute-start(bf16[192,1024]{1,0:T(8,128)(2,1)} %shard_map.73), channel_id=1, source_target_pairs={{0,8},{4,12},{8,16},{12,20},{16,24},{20,28},{1,9},{5,13},{9,17},{1... | collective-permute-start | bytes 1179656 | tf_op jit(solution)/shard_map/ppermute | solution.py:441
  15.7 10.6 %collective-permute-start.4 = (bf16[192,1024]{1,0:T(8,128)(2,1)S(1)}, bf16[192,1024]{1,0:T(8,128)(2,1)S(1)}, u32[]{:S(2)}, u32[]{:S(2)}) collective-permute-start(bf16[192,1024]{1,0:T(8,128)(2,1)S(1)} %collective-permute-done.1.refs_0_), channel_id=1, source_target_pairs={{0,2},{1,3},{2,0},{3,1},{4,6},{5,7},{6,4},{7,5},{8,10},{9,11},{10,... | collective-permute-start | bytes 1179656 | tf_op jit(solution)/shard_map/ppermute | solution.py:394
  16.7 10.7 %collective-permute-start.3 = (bf16[192,1024]{1,0:T(8,128)(2,1)S(1)}, bf16[192,1024]{1,0:T(8,128)(2,1)S(1)}, u32[]{:S(2)}, u32[]{:S(2)}) collective-permute-start(bf16[192,1024]{1,0:T(8,128)(2,1)S(1)} %collective-permute-done.1.refs_0_), channel_id=1, source_target_pairs={{0,8},{4,12},{8,16},{12,20},{16,24},{20,28},{1,9},{5,13},{9,17},{1... | collective-permute-start | bytes 1179656 | tf_op jit(solution)/shard_map/ppermute | solution.py:462
  18.2 2.8 %collective-permute-start = (s32[6,17]{1,0:T(8,128)S(1)}, s32[6,17]{1,0:T(8,128)S(1)}, u32[]{:S(2)}, u32[]{:S(2)}) collective-permute-start(s32[6,17]{1,0:T(8,128)S(1)} %pad_add_fusion.told_ref), channel_id=1, source_target_pairs={{0,4},{4,0},{8,12},{12,8},{16,20},{20,16},{24,28},{28,24},{1,5},{5... | collective-permute-start | bytes 1232 | tf_op jit(solution)/shard_map/ppermute | solution.py:394
  20.9 1.0 copy-start.3
  21.9 1.0 copy-start.7
  22.9 10.0 %copy-start.11 = (bf16[2,128,256]{2,1,0:T(8,128)(2,1)S(1)}, bf16[2,128,256]{2,1,0:T(8,128)(2,1)}, u32[]{:S(2)}) copy-start(bf16[2,128,256]{2,1,0:T(8,128)(2,1)} %get-tuple-element.64) | copy-start | bytes 393220
  22.9 37.0 %copy-start = (bf16[4,1024,256]{2,1,0:T(8,128)(2,1)S(1)}, bf16[4,1024,256]{2,1,0:T(8,128)(2,1)}, u32[]{:S(2)}) copy-start(bf16[4,1024,256]{2,1,0:T(8,128)(2,1)} %refs_4_.3) | copy-start | bytes 6291460
  22.9 37.0 %copy-start.4 = (bf16[768,256]{1,0:T(8,128)(2,1)S(1)}, bf16[768,256]{1,0:T(8,128)(2,1)}, u32[]{:S(2)}) copy-start(bf16[768,256]{1,0:T(8,128)(2,1)} %get-tuple-element.56.query_hbm.refs_5_) | copy-start | bytes 1179652
  22.9 37.0 %copy-start.8 = (bf16[256,768]{1,0:T(8,128)(2,1)S(1)}, bf16[256,768]{1,0:T(8,128)(2,1)}, u32[]{:S(2)}) copy-start(bf16[256,768]{1,0:T(8,128)(2,1)} %get-tuple-element.57.keys_t_hbm.refs_7_) | copy-start | bytes 1179652
  27.4 42.1 %collective-permute-start.10 = (bf16[1536,256]{1,0:T(8,128)(2,1)}, bf16[1536,256]{1,0:T(8,128)(2,1)S(1)}, u32[]{:S(2)}, u32[]{:S(2)}) collective-permute-start(bf16[1536,256]{1,0:T(8,128)(2,1)} %get-tuple-element.61.both_hbm.refs_8_), channel_id=1, source_target_pairs={{4,24},{5,25},{6,26},{7,27}} | collective-permute-start | bytes 2359304 | tf_op jit(solution)/shard_map/ppermute | solution.py:483
  28.7 4.2 %collective-permute-start.7 = (bf16[192,1024]{1,0:T(8,128)(2,1)S(1)}, bf16[192,1024]{1,0:T(8,128)(2,1)S(1)}, u32[]{:S(2)}, u32[]{:S(2)}) collective-permute-start(bf16[192,1024]{1,0:T(8,128)(2,1)S(1)} %collective-permute-done.1.refs_0_), channel_id=1, source_target_pairs={{0,1},{1,0},{2,3},{3,2},{4,5},{5,4},{6,7},{7,6},{8,9},{9,8},{10,11... | collective-permute-start | bytes 1179656 | tf_op jit(solution)/shard_map/ppermute | solution.py:394
  31.5 27.5 %collective-permute-start.9 = (bf16[768,256]{1,0:T(8,128)(2,1)S(1)}, bf16[768,256]{1,0:T(8,128)(2,1)S(1)}, u32[]{:S(2)}, u32[]{:S(2)}) collective-permute-start(bf16[768,256]{1,0:T(8,128)(2,1)S(1)} %copy-done.3), channel_id=1, source_target_pairs={{0,4},{4,0},{8,12},{12,8},{16,20},{20,16},{24,28},{28,24},{1,5},{5... | collective-permute-start | bytes 1179656 | tf_op jit(solution)/shard_map/ppermute | solution.py:394
  32.1 27.8 %collective-permute-start.8 = (bf16[192,1024]{1,0:T(8,128)(2,1)S(1)}, bf16[192,1024]{1,0:T(8,128)(2,1)S(1)}, u32[]{:S(2)}, u32[]{:S(2)}) collective-permute-start(bf16[192,1024]{1,0:T(8,128)(2,1)S(1)} %collective-permute-done.4.refs_2_), channel_id=1, source_target_pairs={{0,1},{1,0},{2,3},{3,2},{4,5},{5,4},{6,7},{7,6},{8,9},{9,8},{10,11... | collective-permute-start | bytes 1179656 | tf_op jit(solution)/shard_map/ppermute | solution.py:394
  32.5 37.0 %collective-permute-start.6 = (bf16[192,1024]{1,0:T(8,128)(2,1)S(1)}, bf16[192,1024]{1,0:T(8,128)(2,1)S(1)}, u32[]{:S(2)}, u32[]{:S(2)}) collective-permute-start(bf16[192,1024]{1,0:T(8,128)(2,1)S(1)} %collective-permute-done.3.refs_0_), channel_id=1, source_target_pairs={{0,2},{1,3},{2,0},{3,1},{4,6},{5,7},{6,4},{7,5},{8,10},{9,11},{10,... | collective-permute-start | bytes 1179656 | tf_op jit(solution)/shard_map/ppermute | solution.py:394
  32.9 36.5 %collective-permute-start.11 = (bf16[2,128,256]{2,1,0:T(8,128)(2,1)S(1)}, bf16[2,128,256]{2,1,0:T(8,128)(2,1)S(1)}, u32[]{:S(2)}, u32[]{:S(2)}) collective-permute-start(bf16[2,128,256]{2,1,0:T(8,128)(2,1)S(1)} %copy-done.11), channel_id=1, source_target_pairs={{0,24},{4,28},{1,25},{5,29},{2,26},{6,30},{3,27},{7,31}} | collective-permute-start | bytes 393224 | tf_op jit(solution)/shard_map/ppermute | solution.py:465
  59.0 10.5 %collective-permute-start.5 = (bf16[192,1024]{1,0:T(8,128)(2,1)S(1)}, bf16[192,1024]{1,0:T(8,128)(2,1)S(1)}, u32[]{:S(2)}, u32[]{:S(2)}) collective-permute-start(bf16[192,1024]{1,0:T(8,128)(2,1)S(1)} %collective-permute-done.3.refs_0_), channel_id=1, source_target_pairs={{0,1},{1,0},{2,3},{3,2},{4,5},{5,4},{6,7},{7,6},{8,9},{9,8},{10,11... | collective-permute-start | bytes 1179656 | tf_op jit(solution)/shard_map/ppermute | solution.py:394
  69.4 7.2 %copy-start.5 = (bf16[256]{0:T(256)(128)(2,1)S(1)}, bf16[256]{0:T(256)(128)(2,1)}, u32[]{:S(2)}) copy-start(bf16[256]{0:T(256)(128)(2,1)} %gain_ref.3) | copy-start | bytes 1540
  69.5 7.2 %copy-start.6 = (bf16[768,256]{1,0:T(8,128)(2,1)S(1)}, bf16[768,256]{1,0:T(8,128)(2,1)}, u32[]{:S(2)}) copy-start(bf16[768,256]{1,0:T(8,128)(2,1)} %get-tuple-element.73.gate_hbm) | copy-start | bytes 1179652
  69.5 1.8 %collective-permute-start.12 = (bf16[192,1024]{1,0:T(8,128)(2,1)S(1)}, bf16[192,1024]{1,0:T(8,128)(2,1)S(1)}, u32[]{:S(2)}, u32[]{:S(2)}) collective-permute-start(bf16[192,1024]{1,0:T(8,128)(2,1)S(1)} %collective-permute-done.6.refs_2_), channel_id=1, source_target_pairs={{0,1},{1,0},{2,3},{3,2},{4,5},{5,4},{6,7},{7,6},{8,9},{9,8},{10,11... | collective-permute-start | bytes 1179656 | tf_op jit(solution)/shard_map/ppermute | solution.py:394
  76.1 11.2 %collective-permute-start.14 = (bf16[256,1024]{1,0:T(8,128)(2,1)S(1)}, bf16[256,1024]{1,0:T(8,128)(2,1)S(1)}, u32[]{:S(2)}, u32[]{:S(2)}) collective-permute-start(bf16[256,1024]{1,0:T(8,128)(2,1)S(1)} %copy-done.2), channel_id=1, source_target_pairs={{0,1},{1,0},{2,3},{3,2},{4,5},{5,4},{6,7},{7,6},{8,9},{9,8},{10,11... | collective-permute-start | bytes 1572872 | tf_op jit(solution)/shard_map/ppermute | solution.py:394
  76.3 11.0 %collective-permute-start.15 = (bf16[256,1024]{1,0:T(8,128)(2,1)S(1)}, bf16[256,1024]{1,0:T(8,128)(2,1)S(1)}, u32[]{:S(2)}, u32[]{:S(2)}) collective-permute-start(bf16[256,1024]{1,0:T(8,128)(2,1)S(1)} %collective-permute-done.2.refs_4_), channel_id=1, source_target_pairs={{0,1},{1,0},{2,3},{3,2},{4,5},{5,4},{6,7},{7,6},{8,9},{9,8},{10,11... | collective-permute-start | bytes 1572872 | tf_op jit(solution)/shard_map/ppermute | solution.py:394
  76.6 10.6 %collective-permute-start.13 = (bf16[768,256]{1,0:T(8,128)(2,1)S(1)}, bf16[768,256]{1,0:T(8,128)(2,1)S(1)}, u32[]{:S(2)}, u32[]{:S(2)}) collective-permute-start(bf16[768,256]{1,0:T(8,128)(2,1)S(1)} %get-tuple-element.67), channel_id=1, source_target_pairs={{0,4},{4,0},{8,12},{12,8},{16,20},{20,16},{24,28},{28,24},{1,5},{5... | collective-permute-start | bytes 1179656 | tf_op jit(solution)/shard_map/ppermute | solution.py:394
  76.7 13.5 %copy-start.1 = (bf16[768,1024]{1,0:T(8,128)(2,1)S(1)}, bf16[768,1024]{1,0:T(8,128)(2,1)}, u32[]{:S(2)}) copy-start(bf16[768,1024]{1,0:T(8,128)(2,1)} %refs_6_.1) | copy-start | bytes 4718596
  87.7 2.4 %collective-permute-start.17 = (bf16[768,256]{1,0:T(8,128)(2,1)S(1)}, bf16[768,256]{1,0:T(8,128)(2,1)S(1)}, u32[]{:S(2)}, u32[]{:S(2)}) collective-permute-start(bf16[768,256]{1,0:T(8,128)(2,1)S(1)} %shard_map.79.refs_0_), channel_id=1, source_target_pairs={{0,1},{1,0},{2,3},{3,2},{4,5},{5,4},{6,7},{7,6},{8,9},{9,8},{10,11... | collective-permute-start | bytes 1179656 | tf_op jit(solution)/shard_map/ppermute | solution.py:394
  88.8 10.7 %collective-permute-start.16 = (bf16[768,256]{1,0:T(8,128)(2,1)S(1)}, bf16[768,256]{1,0:T(8,128)(2,1)S(1)}, u32[]{:S(2)}, u32[]{:S(2)}) collective-permute-start(bf16[768,256]{1,0:T(8,128)(2,1)S(1)} %shard_map.79.refs_0_), channel_id=1, source_target_pairs={{0,2},{1,3},{2,0},{3,1},{4,6},{5,7},{6,4},{7,5},{8,10},{9,11},{10,... | collective-permute-start | bytes 1179656 | tf_op jit(solution)/shard_map/ppermute | solution.py:394
  99.5 2.2 %collective-permute-start.18 = (bf16[768,256]{1,0:T(8,128)(2,1)S(1)}, bf16[768,256]{1,0:T(8,128)(2,1)S(1)}, u32[]{:S(2)}, u32[]{:S(2)}) collective-permute-start(bf16[768,256]{1,0:T(8,128)(2,1)S(1)} %collective-permute-done.16.refs_0_), channel_id=1, source_target_pairs={{0,1},{1,0},{2,3},{3,2},{4,5},{5,4},{6,7},{7,6},{8,9},{9,8},{10,11... | collective-permute-start | bytes 1179656 | tf_op jit(solution)/shard_map/ppermute | solution.py:394

commit v3 on v2

--- a/solution.py
+++ b/solution.py
@@ -458,10 +458,11 @@
     )(history, gain, w_in)
 
     w_cross = crossed(w_out, "head", n_head // 2)
+    query_x = crossed(query, "seq", 1)
     share_1, query, w_cross = barrier((share_1, query, w_cross))
     share_2 = lax.ppermute(share_1, "seq", upward)
     cross_1 = crossed(share_1, "head", n_head // 2)
-    query_x, told_x = crossed(query, "seq", 1), crossed(told, "seq", 1)
+    told_x = crossed(told, "seq", 1)
     tail = lax.ppermute(tail, "seq", [(i, i + FAR + 1) for i in range(n_seq - FAR - 1)])
     told, told_x = barrier((told, told_x))
     own_sums = pl.pallas_call(
@@ -474,12 +475,12 @@
         compiler_params=params(),
         cost_estimate=cost(4),
     )(told, query, keys_t, both)
-    share_2, cross_1, own_sums = barrier((share_2, cross_1, own_sums))
+    share_2, cross_1, own_sums, query_x = barrier((share_2, cross_1, own_sums, query_x))
     chunk_1 = spread(share_1, n_head // 4) + spread(cross_1, n_head // 4)
     cross_2 = crossed(share_2, "head", n_head // 2)
     near_2 = spread(share_2, n_head // 4)
 
-    both, share_2 = barrier((both, share_2))
+    both, query_x, share_2 = barrier((both, query_x, share_2))
     far = lax.ppermute(both, "seq", [(i, i + FAR) for i in range(1, n_seq - FAR, 2)])
 
     sums, sums_x = pl.pallas_call(
@@ -499,7 +500,7 @@
         cost_estimate=cost(6),
     )(told, told_x, *chunk_1, w_in, query, query_x, keys_t, both, own_sums)
 
-    cross_2, sums_x, far, tail = barrier((cross_2, sums_x, far, tail))
+    cross_2, sums_x, tail = barrier((cross_2, sums_x, tail))
     send, keys_t, values = pl.pallas_call(
         make_last_kernel(PLANES, n_head),
         in_specs=[flat] + [wide] * (n_head + 1) + [far_off] * 2,
@@ -511,6 +512,7 @@
         compiler_params=params(),
         cost_estimate=cost(4),
     )(told_x, *near_2, *spread(cross_2, n_head // 4), w_in, query_x, sums_x)
+    send, far = barrier((send, far))
     near = crossed(send, "seq", 1)
     send, w_out, w_cross = barrier((send, w_out, w_cross))
     w_all = spread(w_out, n_head // 4) + spread(w_cross, n_head // 4)

time: 103 us -> 90.6 us (0.88)
  waiting for transfers between devices: 46.8 us -> 22.7 us
  starting transfers between devices: 16.7 us -> 27.6 us
    ppermute x15, waiting for transfers between devices: 42.1 us -> 16.4 us  [crossed(): lax.ppermute(array, axis, [(i, i ^ bit) for i in range(lax.axis_size(axis...]
    ppermute x15, starting transfers between devices: 11.6 us -> 22.4 us  [crossed(): lax.ppermute(array, axis, [(i, i ^ bit) for i in range(lax.axis_size(axis...]
    ppermute x1, waiting for transfers between devices: 0.01 us -> 3.98 us  [body(): lax.ppermute(both, 'seq', [(i, i + FAR) for i in range(1, n_seq - FAR, 2)])]
    ppermute x1, waiting for transfers between devices: 3.61 us -> 2.34 us  [body(): share_1 = lax.ppermute(share, 'seq', upward)]
    ppermute x1, waiting for transfers between devices: 1.1 us -> 0.01 us  [body(): share_2 = lax.ppermute(share_1, 'seq', upward)]
  transfers between devices with their start and end apart: 19 -> 19, of which waited for: 9 -> 8; matrix products, arithmetic and copies ran while one was open for 0% -> 0% of each run, Pallas kernels for 27% -> 37%
where the time goes in v3:
time: 90.6 us; the launch traced here: 89.8 us
  Pallas kernels  37.1 us (41%)
  starting transfers between devices  27.6 us (30%)
  waiting for transfers between devices  22.7 us (25%)
  local copies, waits for them, and re-layouts  2.13 us (2%)
    ppermute x15, starting transfers between devices, crossed(): lax.ppermute(array, axis, [(i, i ^ bit) for i in range(lax.axis_size(axis...  22.4 us
    ppermute x15, waiting for transfers between devices, crossed(): lax.ppermute(array, axis, [(i, i ^ bit) for i in range(lax.axis_size(axis...  16.4 us
    pallas_call x1, Pallas kernels, body(): pl.pallas_call(make_chunk_kernel(1, n_head), in_specs=[flat] * 2 + [wide]...  10.1 us
    pallas_call x1, Pallas kernels, body(): pl.pallas_call(make_own_last_kernel(PLANES), in_specs=[flat, far_off, wid...  7.39 us
    pallas_call x1, Pallas kernels, body(): pl.pallas_call(own_kernel, in_specs=[far_off, far_off, wide], out_specs=[...  6.84 us
    pallas_call x1, Pallas kernels, body(): pl.pallas_call(make_last_kernel(PLANES, n_head), in_specs=[flat] + [wide]...  4.79 us
    ppermute x1, waiting for transfers between devices, body(): lax.ppermute(both, 'seq', [(i, i + FAR) for i in range(1, n_seq - FAR, 2)])  3.98 us
    pallas_call x1, Pallas kernels, body(): pl.pallas_call(own_attend_kernel, in_specs=[flat] + [far_off] * 3, out_sp...  3.31 us
  transfers between devices with their start and end apart: 19, of which 8 were waited for; matrix products, arithmetic and copies ran while one was open for 0% of the time, Pallas kernels for 37%

profile of v3, /device:TPU:25, one launch (start us, length us, event | category | flops | bytes accessed | tf_op | source)
XLA Modules:
  0.0 89.8 jit_solution(382981684766871289)
XLA Ops:
  0.0 2.6 %shard_map.73 = bf16[192,1024]{1,0:T(8,128)(2,1)} custom-call(bf16[768,1024]{1,0:T(8,128)(2,1)} %refs_6_.1, bf16[1024]{0:T(1024)(128)(2,1)} %gain_hbm), custom_call_target="tpu_custom_call" | custom-call | flops 600000000 | bytes 1800000 | tf_op jit(solution)/shard_map/pallas_call | solution.py:425
  2.6 0.0 copy-start.9
  2.6 0.0 copy-start.8
  2.6 1.3 %collective-permute-start.2 = (bf16[256,1024]{1,0:T(8,128)(2,1)S(1)}, bf16[256,1024]{1,0:T(8,128)(2,1)S(1)}, u32[]{:S(2)}, u32[]{:S(2)}) collective-permute-start(bf16[256,1024]{1,0:T(8,128)(2,1)S(1)} %copy-done.2), channel_id=1, source_target_pairs={{0,2},{1,3},{2,0},{3,1},{4,6},{5,7},{6,4},{7,5},{8,10},{9,11},{10,... | collective-permute-start | bytes 1572872 | tf_op jit(solution)/shard_map/ppermute | solution.py:394
  3.9 1.3 %collective-permute-start.1 = (bf16[192,1024]{1,0:T(8,128)(2,1)}, bf16[192,1024]{1,0:T(8,128)(2,1)S(1)}, u32[]{:S(2)}, u32[]{:S(2)}) collective-permute-start(bf16[192,1024]{1,0:T(8,128)(2,1)} %shard_map.73), channel_id=1, source_target_pairs={{0,8},{4,12},{8,16},{12,20},{16,24},{20,28},{1,9},{5,13},{9,17},{1... | collective-permute-start | bytes 1179656 | tf_op jit(solution)/shard_map/ppermute | solution.py:441
  5.2 6.8 %shard_map.74 = (bf16[768,256]{1,0:T(8,128)(2,1)}, bf16[1536,256]{1,0:T(8,128)(2,1)}, bf16[768,256]{1,0:T(8,128)(2,1)}, bf16[256,768]{1,0:T(8,128)(2,1)}, bf16[2,128,256]{2,1,0:T(8,128)(2,1)}) custom-call(bf16[768,1024]{1,0:T(8,128)(2,1)} %refs_6_.1, bf16[1024]{0:T(1024)(128)(2,1)} %gain_hbm, bf16[4,1024,256]{2,1,0:T(8,128)(2,1)} %refs_4_.3), custom_call_target="tpu_custom_call" | custom-call | flops 1200000000 | bytes 3600000 | tf_op jit(solution)/shard_map/pallas_call | solution.py:443
  12.1 1.3 %collective-permute-start.5 = (bf16[768,256]{1,0:T(8,128)(2,1)}, bf16[768,256]{1,0:T(8,128)(2,1)S(1)}, u32[]{:S(2)}, u32[]{:S(2)}) collective-permute-start(bf16[768,256]{1,0:T(8,128)(2,1)} %get-tuple-element.59.query_hbm.refs_5_), channel_id=1, source_target_pairs={{0,4},{4,0},{8,12},{12,8},{16,20},{20,16},{24,28},{28,24},{1,5},{5... | collective-permute-start | bytes 1179656 | tf_op jit(solution)/shard_map/ppermute | solution.py:394
  13.3 2.3 %collective-permute-done.1.refs_0_ = bf16[192,1024]{1,0:T(8,128)(2,1)S(1)} collective-permute-done((bf16[192,1024]{1,0:T(8,128)(2,1)}, bf16[192,1024]{1,0:T(8,128)(2,1)S(1)}, u32[]{:S(2)}, u32[]{:S(2)}) %collective-permute-start.1) | collective-permute-done | bytes 393248 | tf_op jit(solution)/shard_map/ppermute | solution.py:441
  15.7 0.0 collective-permute-done.2.refs_4_
  15.7 1.0 %collective-permute-start.4 = (bf16[192,1024]{1,0:T(8,128)(2,1)S(1)}, bf16[192,1024]{1,0:T(8,128)(2,1)S(1)}, u32[]{:S(2)}, u32[]{:S(2)}) collective-permute-start(bf16[192,1024]{1,0:T(8,128)(2,1)S(1)} %collective-permute-done.1.refs_0_), channel_id=1, source_target_pairs={{0,2},{1,3},{2,0},{3,1},{4,6},{5,7},{6,4},{7,5},{8,10},{9,11},{10,... | collective-permute-start | bytes 1179656 | tf_op jit(solution)/shard_map/ppermute | solution.py:394
  16.7 1.3 %collective-permute-start.3 = (bf16[192,1024]{1,0:T(8,128)(2,1)S(1)}, bf16[192,1024]{1,0:T(8,128)(2,1)S(1)}, u32[]{:S(2)}, u32[]{:S(2)}) collective-permute-start(bf16[192,1024]{1,0:T(8,128)(2,1)S(1)} %collective-permute-done.1.refs_0_), channel_id=1, source_target_pairs={{0,8},{4,12},{8,16},{12,20},{16,24},{20,28},{1,9},{5,13},{9,17},{1... | collective-permute-start | bytes 1179656 | tf_op jit(solution)/shard_map/ppermute | solution.py:463
  18.0 0.1 copy.8
  18.1 0.1 pad_add_fusion.told_ref
  18.2 1.2 %collective-permute-start = (s32[6,17]{1,0:T(8,128)S(1)}, s32[6,17]{1,0:T(8,128)S(1)}, u32[]{:S(2)}, u32[]{:S(2)}) collective-permute-start(s32[6,17]{1,0:T(8,128)S(1)} %pad_add_fusion.told_ref), channel_id=1, source_target_pairs={{0,4},{4,0},{8,12},{12,8},{16,20},{20,16},{24,28},{28,24},{1,5},{5... | collective-permute-start | bytes 1232 | tf_op jit(solution)/shard_map/ppermute | solution.py:394
  19.4 2.7 %collective-permute-done.told_x_ref = s32[6,17]{1,0:T(8,128)S(1)} collective-permute-done((s32[6,17]{1,0:T(8,128)S(1)}, s32[6,17]{1,0:T(8,128)S(1)}, u32[]{:S(2)}, u32[]{:S(2)}) %collective-permute-start) | collective-permute-done | bytes 440 | tf_op jit(solution)/shard_map/ppermute | solution.py:394
  22.1 1.9 %collective-permute-start.8 = (bf16[192,1024]{1,0:T(8,128)(2,1)S(1)}, bf16[192,1024]{1,0:T(8,128)(2,1)S(1)}, u32[]{:S(2)}, u32[]{:S(2)}) collective-permute-start(bf16[192,1024]{1,0:T(8,128)(2,1)S(1)} %collective-permute-done.1.refs_0_), channel_id=1, source_target_pairs={{0,1},{1,0},{2,3},{3,2},{4,5},{5,4},{6,7},{7,6},{8,9},{9,8},{10,11... | collective-permute-start | bytes 1179656 | tf_op jit(solution)/shard_map/ppermute | solution.py:394
  24.0 1.0 %copy-done.3 = bf16[768,256]{1,0:T(8,128)(2,1)S(1)} copy-done((bf16[768,256]{1,0:T(8,128)(2,1)S(1)}, bf16[768,256]{1,0:T(8,128)(2,1)}, u32[]{:S(2)}) %copy-start.3) | copy-done | bytes 393240
  25.0 1.0 %copy-done.7 = bf16[256,768]{1,0:T(8,128)(2,1)S(1)} copy-done((bf16[256,768]{1,0:T(8,128)(2,1)S(1)}, bf16[256,768]{1,0:T(8,128)(2,1)}, u32[]{:S(2)}) %copy-start.7) | copy-done | bytes 393240
  26.0 3.3 %shard_map.75.refs_9_ = f32[768,256]{1,0:T(8,128)S(1)} custom-call(s32[6,17]{1,0:T(8,128)S(1)} %pad_add_fusion.told_ref, bf16[768,256]{1,0:T(8,128)(2,1)S(1)} %copy-done.3, bf16[256,768]{1,0:T(8,128)(2,1)S(1)} %copy-done.7, bf16[1536,256]{1,0:T(8,128)(2,1)} %get-tuple-element.66.both_hbm.refs_8_), custom_call_target="tpu_custom_call" | custom-call | flops 1200000000 | bytes 3600000 | tf_op jit(solution)/shard_map/pallas_call | solution.py:468
  29.3 0.0 collective-permute-done.5.refs_6_.refs_5_
  29.3 0.8 collective-permute-start.9
  30.1 0.4 collective-permute-start.7
  30.6 1.3 %collective-permute-start.12 = (bf16[1536,256]{1,0:T(8,128)(2,1)}, bf16[1536,256]{1,0:T(8,128)(2,1)S(1)}, u32[]{:S(2)}, u32[]{:S(2)}) collective-permute-start(bf16[1536,256]{1,0:T(8,128)(2,1)} %get-tuple-element.66.both_hbm.refs_8_), channel_id=1, source_target_pairs={{4,24},{5,25},{6,26},{7,27}} | collective-permute-start | bytes 2359304 | tf_op jit(solution)/shard_map/ppermute | solution.py:484
  31.9 1.3 %collective-permute-start.10 = (bf16[2,128,256]{2,1,0:T(8,128)(2,1)S(1)}, bf16[2,128,256]{2,1,0:T(8,128)(2,1)S(1)}, u32[]{:S(2)}, u32[]{:S(2)}) collective-permute-start(bf16[2,128,256]{2,1,0:T(8,128)(2,1)S(1)} %copy-done.10), channel_id=1, source_target_pairs={{0,24},{4,28},{1,25},{5,29},{2,26},{6,30},{3,27},{7,31}} | collective-permute-start | bytes 393224 | tf_op jit(solution)/shard_map/ppermute | solution.py:466
  33.2 0.0 collective-permute-done.8.refs_1_
  33.2 0.3 collective-permute-start.6
  33.5 10.1 %shard_map.76 = (f32[768,256]{1,0:T(8,128)S(1)}, f32[768,256]{1,0:T(8,128)S(1)}) custom-call(s32[6,17]{1,0:T(8,128)S(1)} %pad_add_fusion.told_ref, s32[6,17]{1,0:T(8,128)S(1)} %collective-permute-done.told_x_ref, bf16[192,1024]{1,0:T(8,128)(2,1)S(1)} %collective-permute-done.1.refs_0_, bf16[192,1024]{1,0:T(8,128)(2,1)S(1)} %collective-permute-done.8.refs_1_, ...), custom_call_target="tpu_custom_call" | custom-call | flops 1800000000 | bytes 5400000 | tf_op jit(solution)/shard_map/pallas_call | solution.py:486
  43.6 0.0 collective-permute-done.10.tail_ref
  43.6 0.0 copy-start.5
  43.6 0.0 copy-start.6
  43.6 0.3 collective-permute-start.11
  43.9 1.5 %collective-permute-done.11.refs_3_ = bf16[192,1024]{1,0:T(8,128)(2,1)S(1)} collective-permute-done((bf16[192,1024]{1,0:T(8,128)(2,1)S(1)}, bf16[192,1024]{1,0:T(8,128)(2,1)S(1)}, u32[]{:S(2)}, u32[]{:S(2)}) %collective-permute-start.11) | collective-permute-done | bytes 393248 | tf_op jit(solution)/shard_map/ppermute | solution.py:394
  45.4 4.8 %shard_map.77 = (bf16[768,256]{1,0:T(8,128)(2,1)S(1)}, bf16[256,768]{1,0:T(8,128)(2,1)S(1)}, bf16[768,256]{1,0:T(8,128)(2,1)S(1)}) custom-call(s32[6,17]{1,0:T(8,128)S(1)} %collective-permute-done.told_x_ref, bf16[192,1024]{1,0:T(8,128)(2,1)S(1)} %collective-permute-done.3.refs_0_, bf16[192,1024]{1,0:T(8,128)(2,1)S(1)} %collective-permute-done.6.refs_1_, ...), custom_call_target="tpu_custom_call" | custom-call | flops 1200000000 | bytes 3600000 | tf_op jit(solution)/shard_map/pallas_call | solution.py:504
  50.2 4.0 %collective-permute-done.12.far_hbm = bf16[1536,256]{1,0:T(8,128)(2,1)S(1)} collective-permute-done((bf16[1536,256]{1,0:T(8,128)(2,1)}, bf16[1536,256]{1,0:T(8,128)(2,1)S(1)}, u32[]{:S(2)}, u32[]{:S(2)}) %collective-permute-start.12) | collective-permute-done | bytes 786464 | tf_op jit(solution)/shard_map/ppermute | solution.py:484
  54.2 1.8 %collective-permute-start.14 = (bf16[256,1024]{1,0:T(8,128)(2,1)S(1)}, bf16[256,1024]{1,0:T(8,128)(2,1)S(1)}, u32[]{:S(2)}, u32[]{:S(2)}) collective-permute-start(bf16[256,1024]{1,0:T(8,128)(2,1)S(1)} %copy-done.2), channel_id=1, source_target_pairs={{0,1},{1,0},{2,3},{3,2},{4,5},{5,4},{6,7},{7,6},{8,9},{9,8},{10,11... | collective-permute-start | bytes 1572872 | tf_op jit(solution)/shard_map/ppermute | solution.py:394
  56.0 0.0 collective-permute-start.15
  56.0 9.1 %collective-permute-start.13 = (bf16[768,256]{1,0:T(8,128)(2,1)S(1)}, bf16[768,256]{1,0:T(8,128)(2,1)S(1)}, u32[]{:S(2)}, u32[]{:S(2)}) collective-permute-start(bf16[768,256]{1,0:T(8,128)(2,1)S(1)} %get-tuple-element.73), channel_id=1, source_target_pairs={{0,4},{4,0},{8,12},{12,8},{16,20},{20,16},{24,28},{28,24},{1,5},{5... | collective-permute-start | bytes 1179656 | tf_op jit(solution)/shard_map/ppermute | solution.py:394
  65.2 7.4 %shard_map.78 = (f32[768,256]{1,0:T(8,128)S(1)}, f32[768,256]{1,0:T(8,128)S(1)}) custom-call(s32[6,17]{1,0:T(8,128)S(1)} %pad_add_fusion.told_ref, bf16[768,256]{1,0:T(8,128)(2,1)S(1)} %copy-done.4, bf16[256,768]{1,0:T(8,128)(2,1)S(1)} %get-tuple-element.74.keys_t_ref, bf16[768,256]{1,0:T(8,128)(2,1)S(1)} %get-tuple-element.75.values_ref, ...), custom_call_target="tpu_custom_call" | custom-call | flops 900000000 | bytes 2700000 | tf_op jit(solution)/shard_map/pallas_call | solution.py:519
  72.6 1.8 %collective-permute-done.13.near_ref = bf16[768,256]{1,0:T(8,128)(2,1)S(1)} collective-permute-done((bf16[768,256]{1,0:T(8,128)(2,1)S(1)}, bf16[768,256]{1,0:T(8,128)(2,1)S(1)}, u32[]{:S(2)}, u32[]{:S(2)}) %collective-permute-start.13) | collective-permute-done | bytes 393248 | tf_op jit(solution)/shard_map/ppermute | solution.py:394
  74.3 0.5 shard_map.79.refs_0_
  74.8 1.0 %collective-permute-start.17 = (bf16[768,256]{1,0:T(8,128)(2,1)S(1)}, bf16[768,256]{1,0:T(8,128)(2,1)S(1)}, u32[]{:S(2)}, u32[]{:S(2)}) collective-permute-start(bf16[768,256]{1,0:T(8,128)(2,1)S(1)} %shard_map.79.refs_0_), channel_id=1, source_target_pairs={{0,1},{1,0},{2,3},{3,2},{4,5},{5,4},{6,7},{7,6},{8,9},{9,8},{10,11... | collective-permute-start | bytes 1179656 | tf_op jit(solution)/shard_map/ppermute | solution.py:394
  75.8 1.1 %collective-permute-start.16 = (bf16[768,256]{1,0:T(8,128)(2,1)S(1)}, bf16[768,256]{1,0:T(8,128)(2,1)S(1)}, u32[]{:S(2)}, u32[]{:S(2)}) collective-permute-start(bf16[768,256]{1,0:T(8,128)(2,1)S(1)} %shard_map.79.refs_0_), channel_id=1, source_target_pairs={{0,2},{1,3},{2,0},{3,1},{4,6},{5,7},{6,4},{7,5},{8,10},{9,11},{10,... | collective-permute-start | bytes 1179656 | tf_op jit(solution)/shard_map/ppermute | solution.py:394
  76.9 0.3 collective-permute-done.17.refs_1_
  77.2 0.5 shard_map.80
  77.7 8.8 %collective-permute-done.16.refs_0_ = bf16[768,256]{1,0:T(8,128)(2,1)S(1)} collective-permute-done((bf16[768,256]{1,0:T(8,128)(2,1)S(1)}, bf16[768,256]{1,0:T(8,128)(2,1)S(1)}, u32[]{:S(2)}, u32[]{:S(2)}) %collective-permute-start.16) | collective-permute-done | bytes 393248 | tf_op jit(solution)/shard_map/ppermute | solution.py:394
  86.5 0.8 collective-permute-start.18
  87.4 1.3 %collective-permute-done.18.refs_1_ = bf16[768,256]{1,0:T(8,128)(2,1)S(1)} collective-permute-done((bf16[768,256]{1,0:T(8,128)(2,1)S(1)}, bf16[768,256]{1,0:T(8,128)(2,1)S(1)}, u32[]{:S(2)}, u32[]{:S(2)}) %collective-permute-start.18) | collective-permute-done | bytes 393248 | tf_op jit(solution)/shard_map/ppermute | solution.py:394
  88.7 1.1 %shard_map.81 = bf16[768,256]{1,0:T(8,128)(2,1)} custom-call(bf16[768,256]{1,0:T(8,128)(2,1)S(1)} %collective-permute-done.16.refs_0_, bf16[768,256]{1,0:T(8,128)(2,1)S(1)} %collective-permute-done.18.refs_1_, bf16[512,256]{1,0:T(8,128)(2,1)S(1)} %get-tuple-element.93.refs_2_, f32[768,256]{1,0:T(8,128)S(1)} %get-tuple-element.94.refs_3_), custom_call_target="tpu_custom_call" | custom-call | flops 600000000 | bytes 1800000 | tf_op jit(solution)/shard_map/pallas_call | solution.py:556
  (23 shorter events, 0.0 us)
Async XLA Ops:
  0.0 2.6 %copy-start.2 = (bf16[256,1024]{1,0:T(8,128)(2,1)S(1)}, bf16[256,1024]{1,0:T(8,128)(2,1)}, u32[]{:S(2)}) copy-start(bf16[256,1024]{1,0:T(8,128)(2,1)} %refs_2_) | copy-start | bytes 1572868
  2.6 15.4 %copy-start.9 = (s32[6]{0:T(128)S(1)}, s32[6]{0:T(128)}, u32[]{:S(2)}) copy-start(s32[6]{0:T(128)} %param.13) | copy-start | bytes 76
  2.6 15.5 %copy-start.8 = (s32[6,16]{1,0:T(8,128)S(1)}, s32[6,16]{1,0:T(8,128)}, u32[]{:S(2)}) copy-start(s32[6,16]{1,0:T(8,128)} %param.12) | copy-start | bytes 1156
  2.6 13.1 %collective-permute-start.2 = (bf16[256,1024]{1,0:T(8,128)(2,1)S(1)}, bf16[256,1024]{1,0:T(8,128)(2,1)S(1)}, u32[]{:S(2)}, u32[]{:S(2)}) collective-permute-start(bf16[256,1024]{1,0:T(8,128)(2,1)S(1)} %copy-done.2), channel_id=1, source_target_pairs={{0,2},{1,3},{2,0},{3,1},{4,6},{5,7},{6,4},{7,5},{8,10},{9,11},{10,... | collective-permute-start | bytes 1572872 | tf_op jit(solution)/shard_map/ppermute | solution.py:394
  3.9 11.8 %collective-permute-start.1 = (bf16[192,1024]{1,0:T(8,128)(2,1)}, bf16[192,1024]{1,0:T(8,128)(2,1)S(1)}, u32[]{:S(2)}, u32[]{:S(2)}) collective-permute-start(bf16[192,1024]{1,0:T(8,128)(2,1)} %shard_map.73), channel_id=1, source_target_pairs={{0,8},{4,12},{8,16},{12,20},{16,24},{20,28},{1,9},{5,13},{9,17},{1... | collective-permute-start | bytes 1179656 | tf_op jit(solution)/shard_map/ppermute | solution.py:441
  12.1 17.2 %collective-permute-start.5 = (bf16[768,256]{1,0:T(8,128)(2,1)}, bf16[768,256]{1,0:T(8,128)(2,1)S(1)}, u32[]{:S(2)}, u32[]{:S(2)}) collective-permute-start(bf16[768,256]{1,0:T(8,128)(2,1)} %get-tuple-element.59.query_hbm.refs_5_), channel_id=1, source_target_pairs={{0,4},{4,0},{8,12},{12,8},{16,20},{20,16},{24,28},{28,24},{1,5},{5... | collective-permute-start | bytes 1179656 | tf_op jit(solution)/shard_map/ppermute | solution.py:394
  15.7 13.6 %collective-permute-start.4 = (bf16[192,1024]{1,0:T(8,128)(2,1)S(1)}, bf16[192,1024]{1,0:T(8,128)(2,1)S(1)}, u32[]{:S(2)}, u32[]{:S(2)}) collective-permute-start(bf16[192,1024]{1,0:T(8,128)(2,1)S(1)} %collective-permute-done.1.refs_0_), channel_id=1, source_target_pairs={{0,2},{1,3},{2,0},{3,1},{4,6},{5,7},{6,4},{7,5},{8,10},{9,11},{10,... | collective-permute-start | bytes 1179656 | tf_op jit(solution)/shard_map/ppermute | solution.py:394
  16.7 12.6 %collective-permute-start.3 = (bf16[192,1024]{1,0:T(8,128)(2,1)S(1)}, bf16[192,1024]{1,0:T(8,128)(2,1)S(1)}, u32[]{:S(2)}, u32[]{:S(2)}) collective-permute-start(bf16[192,1024]{1,0:T(8,128)(2,1)S(1)} %collective-permute-done.1.refs_0_), channel_id=1, source_target_pairs={{0,8},{4,12},{8,16},{12,20},{16,24},{20,28},{1,9},{5,13},{9,17},{1... | collective-permute-start | bytes 1179656 | tf_op jit(solution)/shard_map/ppermute | solution.py:463
  18.2 3.9 %collective-permute-start = (s32[6,17]{1,0:T(8,128)S(1)}, s32[6,17]{1,0:T(8,128)S(1)}, u32[]{:S(2)}, u32[]{:S(2)}) collective-permute-start(s32[6,17]{1,0:T(8,128)S(1)} %pad_add_fusion.told_ref), channel_id=1, source_target_pairs={{0,4},{4,0},{8,12},{12,8},{16,20},{20,16},{24,28},{28,24},{1,5},{5... | collective-permute-start | bytes 1232 | tf_op jit(solution)/shard_map/ppermute | solution.py:394
  22.1 11.1 %collective-permute-start.8 = (bf16[192,1024]{1,0:T(8,128)(2,1)S(1)}, bf16[192,1024]{1,0:T(8,128)(2,1)S(1)}, u32[]{:S(2)}, u32[]{:S(2)}) collective-permute-start(bf16[192,1024]{1,0:T(8,128)(2,1)S(1)} %collective-permute-done.1.refs_0_), channel_id=1, source_target_pairs={{0,1},{1,0},{2,3},{3,2},{4,5},{5,4},{6,7},{7,6},{8,9},{9,8},{10,11... | collective-permute-start | bytes 1179656 | tf_op jit(solution)/shard_map/ppermute | solution.py:394
  24.0 1.0 %copy-start.3 = (bf16[768,256]{1,0:T(8,128)(2,1)S(1)}, bf16[768,256]{1,0:T(8,128)(2,1)}, u32[]{:S(2)}) copy-start(bf16[768,256]{1,0:T(8,128)(2,1)} %get-tuple-element.59.query_hbm.refs_5_) | copy-start | bytes 1179652
  25.0 1.0 %copy-start.7 = (bf16[256,768]{1,0:T(8,128)(2,1)S(1)}, bf16[256,768]{1,0:T(8,128)(2,1)}, u32[]{:S(2)}) copy-start(bf16[256,768]{1,0:T(8,128)(2,1)} %get-tuple-element.60.keys_t_hbm.refs_7_) | copy-start | bytes 1179652
  25.9 5.9 %copy-start.10 = (bf16[2,128,256]{2,1,0:T(8,128)(2,1)S(1)}, bf16[2,128,256]{2,1,0:T(8,128)(2,1)}, u32[]{:S(2)}) copy-start(bf16[2,128,256]{2,1,0:T(8,128)(2,1)} %get-tuple-element.69) | copy-start | bytes 393220
  26.0 7.6 %copy-start = (bf16[4,1024,256]{2,1,0:T(8,128)(2,1)S(1)}, bf16[4,1024,256]{2,1,0:T(8,128)(2,1)}, u32[]{:S(2)}) copy-start(bf16[4,1024,256]{2,1,0:T(8,128)(2,1)} %refs_4_.3) | copy-start | bytes 6291460
  26.0 7.6 %copy-start.4 = (bf16[768,256]{1,0:T(8,128)(2,1)S(1)}, bf16[768,256]{1,0:T(8,128)(2,1)}, u32[]{:S(2)}) copy-start(bf16[768,256]{1,0:T(8,128)(2,1)} %get-tuple-element.59.query_hbm.refs_5_) | copy-start | bytes 1179652
  29.3 4.2 %collective-permute-start.9 = (bf16[192,1024]{1,0:T(8,128)(2,1)S(1)}, bf16[192,1024]{1,0:T(8,128)(2,1)S(1)}, u32[]{:S(2)}, u32[]{:S(2)}) collective-permute-start(bf16[192,1024]{1,0:T(8,128)(2,1)S(1)} %collective-permute-done.4.refs_2_), channel_id=1, source_target_pairs={{0,1},{1,0},{2,3},{3,2},{4,5},{5,4},{6,7},{7,6},{8,9},{9,8},{10,11... | collective-permute-start | bytes 1179656 | tf_op jit(solution)/shard_map/ppermute | solution.py:394
  30.1 13.5 %collective-permute-start.7 = (bf16[192,1024]{1,0:T(8,128)(2,1)S(1)}, bf16[192,1024]{1,0:T(8,128)(2,1)S(1)}, u32[]{:S(2)}, u32[]{:S(2)}) collective-permute-start(bf16[192,1024]{1,0:T(8,128)(2,1)S(1)} %collective-permute-done.3.refs_0_), channel_id=1, source_target_pairs={{0,2},{1,3},{2,0},{3,1},{4,6},{5,7},{6,4},{7,5},{8,10},{9,11},{10,... | collective-permute-start | bytes 1179656 | tf_op jit(solution)/shard_map/ppermute | solution.py:394
  30.6 23.6 %collective-permute-start.12 = (bf16[1536,256]{1,0:T(8,128)(2,1)}, bf16[1536,256]{1,0:T(8,128)(2,1)S(1)}, u32[]{:S(2)}, u32[]{:S(2)}) collective-permute-start(bf16[1536,256]{1,0:T(8,128)(2,1)} %get-tuple-element.66.both_hbm.refs_8_), channel_id=1, source_target_pairs={{4,24},{5,25},{6,26},{7,27}} | collective-permute-start | bytes 2359304 | tf_op jit(solution)/shard_map/ppermute | solution.py:484
  31.9 11.7 %collective-permute-start.10 = (bf16[2,128,256]{2,1,0:T(8,128)(2,1)S(1)}, bf16[2,128,256]{2,1,0:T(8,128)(2,1)S(1)}, u32[]{:S(2)}, u32[]{:S(2)}) collective-permute-start(bf16[2,128,256]{2,1,0:T(8,128)(2,1)S(1)} %copy-done.10), channel_id=1, source_target_pairs={{0,24},{4,28},{1,25},{5,29},{2,26},{6,30},{3,27},{7,31}} | collective-permute-start | bytes 393224 | tf_op jit(solution)/shard_map/ppermute | solution.py:466
  33.2 10.8 %collective-permute-start.6 = (bf16[192,1024]{1,0:T(8,128)(2,1)S(1)}, bf16[192,1024]{1,0:T(8,128)(2,1)S(1)}, u32[]{:S(2)}, u32[]{:S(2)}) collective-permute-start(bf16[192,1024]{1,0:T(8,128)(2,1)S(1)} %collective-permute-done.3.refs_0_), channel_id=1, source_target_pairs={{0,1},{1,0},{2,3},{3,2},{4,5},{5,4},{6,7},{7,6},{8,9},{9,8},{10,11... | collective-permute-start | bytes 1179656 | tf_op jit(solution)/shard_map/ppermute | solution.py:394
  43.6 21.6 %copy-start.5 = (bf16[256]{0:T(256)(128)(2,1)S(1)}, bf16[256]{0:T(256)(128)(2,1)}, u32[]{:S(2)}) copy-start(bf16[256]{0:T(256)(128)(2,1)} %gain_ref.3) | copy-start | bytes 1540
  43.6 21.5 %copy-start.6 = (bf16[768,256]{1,0:T(8,128)(2,1)S(1)}, bf16[768,256]{1,0:T(8,128)(2,1)}, u32[]{:S(2)}) copy-start(bf16[768,256]{1,0:T(8,128)(2,1)} %get-tuple-element.79.gate_hbm) | copy-start | bytes 1179652
  43.6 1.8 %collective-permute-start.11 = (bf16[192,1024]{1,0:T(8,128)(2,1)S(1)}, bf16[192,1024]{1,0:T(8,128)(2,1)S(1)}, u32[]{:S(2)}, u32[]{:S(2)}) collective-permute-start(bf16[192,1024]{1,0:T(8,128)(2,1)S(1)} %collective-permute-done.7.refs_2_), channel_id=1, source_target_pairs={{0,1},{1,0},{2,3},{3,2},{4,5},{5,4},{6,7},{7,6},{8,9},{9,8},{10,11... | collective-permute-start | bytes 1179656 | tf_op jit(solution)/shard_map/ppermute | solution.py:394
  54.2 20.1 %collective-permute-start.14 = (bf16[256,1024]{1,0:T(8,128)(2,1)S(1)}, bf16[256,1024]{1,0:T(8,128)(2,1)S(1)}, u32[]{:S(2)}, u32[]{:S(2)}) collective-permute-start(bf16[256,1024]{1,0:T(8,128)(2,1)S(1)} %copy-done.2), channel_id=1, source_target_pairs={{0,1},{1,0},{2,3},{3,2},{4,5},{5,4},{6,7},{7,6},{8,9},{9,8},{10,11... | collective-permute-start | bytes 1572872 | tf_op jit(solution)/shard_map/ppermute | solution.py:394
  56.0 18.3 %collective-permute-start.15 = (bf16[256,1024]{1,0:T(8,128)(2,1)S(1)}, bf16[256,1024]{1,0:T(8,128)(2,1)S(1)}, u32[]{:S(2)}, u32[]{:S(2)}) collective-permute-start(bf16[256,1024]{1,0:T(8,128)(2,1)S(1)} %collective-permute-done.2.refs_4_), channel_id=1, source_target_pairs={{0,1},{1,0},{2,3},{3,2},{4,5},{5,4},{6,7},{7,6},{8,9},{9,8},{10,11... | collective-permute-start | bytes 1572872 | tf_op jit(solution)/shard_map/ppermute | solution.py:394
  56.0 18.3 %collective-permute-start.13 = (bf16[768,256]{1,0:T(8,128)(2,1)S(1)}, bf16[768,256]{1,0:T(8,128)(2,1)S(1)}, u32[]{:S(2)}, u32[]{:S(2)}) collective-permute-start(bf16[768,256]{1,0:T(8,128)(2,1)S(1)} %get-tuple-element.73), channel_id=1, source_target_pairs={{0,4},{4,0},{8,12},{12,8},{16,20},{20,16},{24,28},{28,24},{1,5},{5... | collective-permute-start | bytes 1179656 | tf_op jit(solution)/shard_map/ppermute | solution.py:394
  65.2 12.0 %copy-start.1 = (bf16[768,1024]{1,0:T(8,128)(2,1)S(1)}, bf16[768,1024]{1,0:T(8,128)(2,1)}, u32[]{:S(2)}) copy-start(bf16[768,1024]{1,0:T(8,128)(2,1)} %refs_6_.1) | copy-start | bytes 4718596
  74.8 2.3 %collective-permute-start.17 = (bf16[768,256]{1,0:T(8,128)(2,1)S(1)}, bf16[768,256]{1,0:T(8,128)(2,1)S(1)}, u32[]{:S(2)}, u32[]{:S(2)}) collective-permute-start(bf16[768,256]{1,0:T(8,128)(2,1)S(1)} %shard_map.79.refs_0_), channel_id=1, source_target_pairs={{0,1},{1,0},{2,3},{3,2},{4,5},{5,4},{6,7},{7,6},{8,9},{9,8},{10,11... | collective-permute-start | bytes 1179656 | tf_op jit(solution)/shard_map/ppermute | solution.py:394
  75.8 10.7 %collective-permute-start.16 = (bf16[768,256]{1,0:T(8,128)(2,1)S(1)}, bf16[768,256]{1,0:T(8,128)(2,1)S(1)}, u32[]{:S(2)}, u32[]{:S(2)}) collective-permute-start(bf16[768,256]{1,0:T(8,128)(2,1)S(1)} %shard_map.79.refs_0_), channel_id=1, source_target_pairs={{0,2},{1,3},{2,0},{3,1},{4,6},{5,7},{6,4},{7,5},{8,10},{9,11},{10,... | collective-permute-start | bytes 1179656 | tf_op jit(solution)/shard_map/ppermute | solution.py:394
  86.5 2.2 %collective-permute-start.18 = (bf16[768,256]{1,0:T(8,128)(2,1)S(1)}, bf16[768,256]{1,0:T(8,128)(2,1)S(1)}, u32[]{:S(2)}, u32[]{:S(2)}) collective-permute-start(bf16[768,256]{1,0:T(8,128)(2,1)S(1)} %collective-permute-done.16.refs_0_), channel_id=1, source_target_pairs={{0,1},{1,0},{2,3},{3,2},{4,5},{5,4},{6,7},{7,6},{8,9},{9,8},{10,11... | collective-permute-start | bytes 1179656 | tf_op jit(solution)/shard_map/ppermute | solution.py:394

commit v4 on v3

--- a/solution.py
+++ b/solution.py
@@ -460,11 +460,11 @@
     w_cross = crossed(w_out, "head", n_head // 2)
     query_x = crossed(query, "seq", 1)
     share_1, query, w_cross = barrier((share_1, query, w_cross))
-    share_2 = lax.ppermute(share_1, "seq", upward)
+    share_2 = lax.ppermute(share_1, "seq", upward[2:])
     cross_1 = crossed(share_1, "head", n_head // 2)
     told_x = crossed(told, "seq", 1)
+    told, told_x, tail = barrier((told, told_x, tail))
     tail = lax.ppermute(tail, "seq", [(i, i + FAR + 1) for i in range(n_seq - FAR - 1)])
-    told, told_x = barrier((told, told_x))
     own_sums = pl.pallas_call(
         own_attend_kernel,
         in_specs=[flat] + [far_off] * 3,
@@ -475,12 +475,12 @@
         compiler_params=params(),
         cost_estimate=cost(4),
     )(told, query, keys_t, both)
-    share_2, cross_1, own_sums, query_x = barrier((share_2, cross_1, own_sums, query_x))
+    share_2, cross_1, own_sums, query_x, tail = barrier((share_2, cross_1, own_sums, query_x, tail))
     chunk_1 = spread(share_1, n_head // 4) + spread(cross_1, n_head // 4)
     cross_2 = crossed(share_2, "head", n_head // 2)
     near_2 = spread(share_2, n_head // 4)
 
-    both, query_x, share_2 = barrier((both, query_x, share_2))
+    both, query_x, share_2, tail = barrier((both, query_x, share_2, tail))
     far = lax.ppermute(both, "seq", [(i, i + FAR) for i in range(1, n_seq - FAR, 2)])
 
     sums, sums_x = pl.pallas_call(
@@ -500,7 +500,7 @@
         cost_estimate=cost(6),
     )(told, told_x, *chunk_1, w_in, query, query_x, keys_t, both, own_sums)
 
-    cross_2, sums_x, tail = barrier((cross_2, sums_x, tail))
+    cross_2, sums_x = barrier((cross_2, sums_x))
     send, keys_t, values = pl.pallas_call(
         make_last_kernel(PLANES, n_head),
         in_specs=[flat] + [wide] * (n_head + 1) + [far_off] * 2,
@@ -512,9 +512,8 @@
         compiler_params=params(),
         cost_estimate=cost(4),
     )(told_x, *near_2, *spread(cross_2, n_head // 4), w_in, query_x, sums_x)
-    send, far = barrier((send, far))
     near = crossed(send, "seq", 1)
-    send, w_out, w_cross = barrier((send, w_out, w_cross))
+    far, send, w_out, w_cross = barrier((far, send, w_out, w_cross))
     w_all = spread(w_out, n_head // 4) + spread(w_cross, n_head // 4)
     mine, scale = pl.pallas_call(
         make_own_last_kernel(PLANES),

time: 90.6 us -> 84.7 us (0.935)
  starting transfers between devices: 27.6 us -> 19.8 us
  waiting for transfers between devices: 22.7 us -> 26.2 us
  Pallas kernels: 37.1 us -> 35.8 us
    ppermute x15, starting transfers between devices: 22.4 us -> 14.7 us  [crossed(): lax.ppermute(array, axis, [(i, i ^ bit) for i in range(lax.axis_size(axis...]
    ppermute x1, waiting for transfers between devices: 3.98 us -> 5.87 us  [body(): lax.ppermute(both, 'seq', [(i, i + FAR) for i in range(1, n_seq - FAR, 2)])]
    ppermute x15, waiting for transfers between devices: 16.4 us -> 18 us  [crossed(): lax.ppermute(array, axis, [(i, i ^ bit) for i in range(lax.axis_size(axis...]
    unnamed x22 -> x20, local copies, waits for them, and re-layouts: 2.03 us -> 2.03 us
  transfers between devices with their start and end apart: 19 -> 19, of which waited for: 8 -> 8; matrix products, arithmetic and copies ran while one was open for 0% -> 0% of each run, Pallas kernels for 37% -> 38%
where the time goes in v4:
time: 84.7 us; the launch traced here: 84.3 us
  Pallas kernels  35.8 us (42%)
  waiting for transfers between devices  26.2 us (31%)
  starting transfers between devices  19.8 us (23%)
  local copies, waits for them, and re-layouts  2.13 us (3%)
    ppermute x15, waiting for transfers between devices, crossed(): lax.ppermute(array, axis, [(i, i ^ bit) for i in range(lax.axis_size(axis...  18 us
    ppermute x15, starting transfers between devices, crossed(): lax.ppermute(array, axis, [(i, i ^ bit) for i in range(lax.axis_size(axis...  14.7 us
    pallas_call x1, Pallas kernels, body(): pl.pallas_call(make_chunk_kernel(1, n_head), in_specs=[flat] * 2 + [wide]...  9.37 us
    pallas_call x1, Pallas kernels, body(): pl.pallas_call(own_kernel, in_specs=[far_off, far_off, wide], out_specs=[...  6.85 us
    pallas_call x1, Pallas kernels, body(): pl.pallas_call(make_own_last_kernel(PLANES), in_specs=[flat, far_off, wid...  6.79 us
    ppermute x1, waiting for transfers between devices, body(): lax.ppermute(both, 'seq', [(i, i + FAR) for i in range(1, n_seq - FAR, 2)])  5.87 us
    pallas_call x1, Pallas kernels, body(): pl.pallas_call(make_last_kernel(PLANES, n_head), in_specs=[flat] + [wide]...  4.76 us
    pallas_call x1, Pallas kernels, body(): pl.pallas_call(own_attend_kernel, in_specs=[flat] + [far_off] * 3, out_sp...  3.31 us
  transfers between devices with their start and end apart: 19, of which 8 were waited for; matrix products, arithmetic and copies ran while one was open for 0% of the time, Pallas kernels for 38%

profile of v4, /device:TPU:25, one launch (start us, length us, event | category | flops | bytes accessed | tf_op | source)
XLA Modules:
  0.0 84.3 jit_solution(9416681808742538011)
XLA Ops:
  0.0 2.6 %shard_map.73 = bf16[192,1024]{1,0:T(8,128)(2,1)} custom-call(bf16[768,1024]{1,0:T(8,128)(2,1)} %refs_6_.1, bf16[1024]{0:T(1024)(128)(2,1)} %gain_hbm), custom_call_target="tpu_custom_call" | custom-call | flops 600000000 | bytes 1800000 | tf_op jit(solution)/shard_map/pallas_call | solution.py:425
  2.6 0.0 copy-start.9
  2.6 0.0 copy-start.8
  2.6 1.3 %collective-permute-start.2 = (bf16[256,1024]{1,0:T(8,128)(2,1)S(1)}, bf16[256,1024]{1,0:T(8,128)(2,1)S(1)}, u32[]{:S(2)}, u32[]{:S(2)}) collective-permute-start(bf16[256,1024]{1,0:T(8,128)(2,1)S(1)} %copy-done.2), channel_id=1, source_target_pairs={{0,2},{1,3},{2,0},{3,1},{4,6},{5,7},{6,4},{7,5},{8,10},{9,11},{10,... | collective-permute-start | bytes 1572872 | tf_op jit(solution)/shard_map/ppermute | solution.py:394
  3.9 1.3 %collective-permute-start.1 = (bf16[192,1024]{1,0:T(8,128)(2,1)}, bf16[192,1024]{1,0:T(8,128)(2,1)S(1)}, u32[]{:S(2)}, u32[]{:S(2)}) collective-permute-start(bf16[192,1024]{1,0:T(8,128)(2,1)} %shard_map.73), channel_id=1, source_target_pairs={{0,8},{4,12},{8,16},{12,20},{16,24},{20,28},{1,9},{5,13},{9,17},{1... | collective-permute-start | bytes 1179656 | tf_op jit(solution)/shard_map/ppermute | solution.py:441
  5.2 6.9 %shard_map.74 = (bf16[768,256]{1,0:T(8,128)(2,1)}, bf16[1536,256]{1,0:T(8,128)(2,1)}, bf16[768,256]{1,0:T(8,128)(2,1)}, bf16[256,768]{1,0:T(8,128)(2,1)}, bf16[2,128,256]{2,1,0:T(8,128)(2,1)}) custom-call(bf16[768,1024]{1,0:T(8,128)(2,1)} %refs_6_.1, bf16[1024]{0:T(1024)(128)(2,1)} %gain_hbm, bf16[4,1024,256]{2,1,0:T(8,128)(2,1)} %refs_4_.3), custom_call_target="tpu_custom_call" | custom-call | flops 1200000000 | bytes 3600000 | tf_op jit(solution)/shard_map/pallas_call | solution.py:443
  12.1 1.3 %collective-permute-start.5 = (bf16[768,256]{1,0:T(8,128)(2,1)}, bf16[768,256]{1,0:T(8,128)(2,1)S(1)}, u32[]{:S(2)}, u32[]{:S(2)}) collective-permute-start(bf16[768,256]{1,0:T(8,128)(2,1)} %get-tuple-element.61.query_hbm.refs_5_), channel_id=1, source_target_pairs={{0,4},{4,0},{8,12},{12,8},{16,20},{20,16},{24,28},{28,24},{1,5},{5... | collective-permute-start | bytes 1179656 | tf_op jit(solution)/shard_map/ppermute | solution.py:394
  13.3 2.3 %collective-permute-done.1.refs_0_ = bf16[192,1024]{1,0:T(8,128)(2,1)S(1)} collective-permute-done((bf16[192,1024]{1,0:T(8,128)(2,1)}, bf16[192,1024]{1,0:T(8,128)(2,1)S(1)}, u32[]{:S(2)}, u32[]{:S(2)}) %collective-permute-start.1) | collective-permute-done | bytes 393248 | tf_op jit(solution)/shard_map/ppermute | solution.py:441
  15.7 1.0 %collective-permute-start.4 = (bf16[192,1024]{1,0:T(8,128)(2,1)S(1)}, bf16[192,1024]{1,0:T(8,128)(2,1)S(1)}, u32[]{:S(2)}, u32[]{:S(2)}) collective-permute-start(bf16[192,1024]{1,0:T(8,128)(2,1)S(1)} %collective-permute-done.1.refs_0_), channel_id=1, source_target_pairs={{0,2},{1,3},{2,0},{3,1},{4,6},{5,7},{6,4},{7,5},{8,10},{9,11},{10,... | collective-permute-start | bytes 1179656 | tf_op jit(solution)/shard_map/ppermute | solution.py:394
  16.7 1.3 %collective-permute-start.3 = (bf16[192,1024]{1,0:T(8,128)(2,1)S(1)}, bf16[192,1024]{1,0:T(8,128)(2,1)S(1)}, u32[]{:S(2)}, u32[]{:S(2)}) collective-permute-start(bf16[192,1024]{1,0:T(8,128)(2,1)S(1)} %collective-permute-done.1.refs_0_), channel_id=1, source_target_pairs={{8,16},{12,20},{16,24},{20,28},{9,17},{13,21},{17,25},{21,29},{10,... | collective-permute-start | bytes 1179656 | tf_op jit(solution)/shard_map/ppermute | solution.py:463
  18.0 0.1 copy.8
  18.1 0.1 pad_add_fusion.told_ref
  18.2 1.2 %collective-permute-start = (s32[6,17]{1,0:T(8,128)S(1)}, s32[6,17]{1,0:T(8,128)S(1)}, u32[]{:S(2)}, u32[]{:S(2)}) collective-permute-start(s32[6,17]{1,0:T(8,128)S(1)} %pad_add_fusion.told_ref), channel_id=1, source_target_pairs={{0,4},{4,0},{8,12},{12,8},{16,20},{20,16},{24,28},{28,24},{1,5},{5... | collective-permute-start | bytes 1232 | tf_op jit(solution)/shard_map/ppermute | solution.py:394
  19.4 2.7 %collective-permute-done.told_x_ref = s32[6,17]{1,0:T(8,128)S(1)} collective-permute-done((s32[6,17]{1,0:T(8,128)S(1)}, s32[6,17]{1,0:T(8,128)S(1)}, u32[]{:S(2)}, u32[]{:S(2)}) %collective-permute-start) | collective-permute-done | bytes 440 | tf_op jit(solution)/shard_map/ppermute | solution.py:394
  22.1 1.3 %collective-permute-start.6 = (bf16[2,128,256]{2,1,0:T(8,128)(2,1)}, bf16[2,128,256]{2,1,0:T(8,128)(2,1)S(1)}, u32[]{:S(2)}, u32[]{:S(2)}) collective-permute-start(bf16[2,128,256]{2,1,0:T(8,128)(2,1)} %get-tuple-element.64), channel_id=1, source_target_pairs={{0,24},{4,28},{1,25},{5,29},{2,26},{6,30},{3,27},{7,31}} | collective-permute-start | bytes 393224 | tf_op jit(solution)/shard_map/ppermute | solution.py:467
  23.4 1.9 %collective-permute-start.9 = (bf16[192,1024]{1,0:T(8,128)(2,1)S(1)}, bf16[192,1024]{1,0:T(8,128)(2,1)S(1)}, u32[]{:S(2)}, u32[]{:S(2)}) collective-permute-start(bf16[192,1024]{1,0:T(8,128)(2,1)S(1)} %collective-permute-done.1.refs_0_), channel_id=1, source_target_pairs={{0,1},{1,0},{2,3},{3,2},{4,5},{5,4},{6,7},{7,6},{8,9},{9,8},{10,11... | collective-permute-start | bytes 1179656 | tf_op jit(solution)/shard_map/ppermute | solution.py:394
  25.3 1.0 %copy-done.3 = bf16[768,256]{1,0:T(8,128)(2,1)S(1)} copy-done((bf16[768,256]{1,0:T(8,128)(2,1)S(1)}, bf16[768,256]{1,0:T(8,128)(2,1)}, u32[]{:S(2)}) %copy-start.3) | copy-done | bytes 393240
  26.3 1.0 %copy-done.7 = bf16[256,768]{1,0:T(8,128)(2,1)S(1)} copy-done((bf16[256,768]{1,0:T(8,128)(2,1)S(1)}, bf16[256,768]{1,0:T(8,128)(2,1)}, u32[]{:S(2)}) %copy-start.7) | copy-done | bytes 393240
  27.3 3.3 %shard_map.75.refs_9_ = f32[768,256]{1,0:T(8,128)S(1)} custom-call(s32[6,17]{1,0:T(8,128)S(1)} %pad_add_fusion.told_ref, bf16[768,256]{1,0:T(8,128)(2,1)S(1)} %copy-done.3, bf16[256,768]{1,0:T(8,128)(2,1)S(1)} %copy-done.7, bf16[1536,256]{1,0:T(8,128)(2,1)} %get-tuple-element.70.both_hbm.refs_8_), custom_call_target="tpu_custom_call" | custom-call | flops 1200000000 | bytes 3600000 | tf_op jit(solution)/shard_map/pallas_call | solution.py:468
  30.6 0.0 collective-permute-done.6.tail_ref
  30.7 0.0 collective-permute-done.4.refs_2_
  30.7 0.0 collective-permute-done.3.refs_0_
  30.7 2.3 %collective-permute-start.10 = (bf16[192,1024]{1,0:T(8,128)(2,1)S(1)}, bf16[192,1024]{1,0:T(8,128)(2,1)S(1)}, u32[]{:S(2)}, u32[]{:S(2)}) collective-permute-start(bf16[192,1024]{1,0:T(8,128)(2,1)S(1)} %collective-permute-done.4.refs_2_), channel_id=1, source_target_pairs={{0,1},{1,0},{2,3},{3,2},{4,5},{5,4},{6,7},{7,6},{8,9},{9,8},{10,11... | collective-permute-start | bytes 1179656 | tf_op jit(solution)/shard_map/ppermute | solution.py:394
  33.0 0.4 collective-permute-start.8
  33.4 1.3 %collective-permute-start.13 = (bf16[1536,256]{1,0:T(8,128)(2,1)}, bf16[1536,256]{1,0:T(8,128)(2,1)S(1)}, u32[]{:S(2)}, u32[]{:S(2)}) collective-permute-start(bf16[1536,256]{1,0:T(8,128)(2,1)} %get-tuple-element.70.both_hbm.refs_8_), channel_id=1, source_target_pairs={{4,24},{5,25},{6,26},{7,27}} | collective-permute-start | bytes 2359304 | tf_op jit(solution)/shard_map/ppermute | solution.py:484
  34.7 0.4 collective-permute-start.7
  35.2 9.4 %shard_map.76 = (f32[768,256]{1,0:T(8,128)S(1)}, f32[768,256]{1,0:T(8,128)S(1)}) custom-call(s32[6,17]{1,0:T(8,128)S(1)} %pad_add_fusion.told_ref, s32[6,17]{1,0:T(8,128)S(1)} %collective-permute-done.told_x_ref, bf16[192,1024]{1,0:T(8,128)(2,1)S(1)} %collective-permute-done.1.refs_0_, bf16[192,1024]{1,0:T(8,128)(2,1)S(1)} %collective-permute-done.9.refs_1_, ...), custom_call_target="tpu_custom_call" | custom-call | flops 1800000000 | bytes 5400000 | tf_op jit(solution)/shard_map/pallas_call | solution.py:486
  44.5 0.0 collective-permute-done.8.refs_2_
  44.6 0.0 copy-start.5
  44.6 0.0 copy-start.6
  44.6 0.2 collective-permute-start.11
  44.8 1.5 %collective-permute-done.11.refs_3_ = bf16[192,1024]{1,0:T(8,128)(2,1)S(1)} collective-permute-done((bf16[192,1024]{1,0:T(8,128)(2,1)S(1)}, bf16[192,1024]{1,0:T(8,128)(2,1)S(1)}, u32[]{:S(2)}, u32[]{:S(2)}) %collective-permute-start.11) | collective-permute-done | bytes 393248 | tf_op jit(solution)/shard_map/ppermute | solution.py:394
  46.4 4.8 %shard_map.77 = (bf16[768,256]{1,0:T(8,128)(2,1)S(1)}, bf16[256,768]{1,0:T(8,128)(2,1)S(1)}, bf16[768,256]{1,0:T(8,128)(2,1)S(1)}) custom-call(s32[6,17]{1,0:T(8,128)S(1)} %collective-permute-done.told_x_ref, bf16[192,1024]{1,0:T(8,128)(2,1)S(1)} %collective-permute-done.3.refs_0_, bf16[192,1024]{1,0:T(8,128)(2,1)S(1)} %collective-permute-done.7.refs_1_, ...), custom_call_target="tpu_custom_call" | custom-call | flops 1200000000 | bytes 3600000 | tf_op jit(solution)/shard_map/pallas_call | solution.py:504
  51.1 5.9 %collective-permute-done.13.far_hbm = bf16[1536,256]{1,0:T(8,128)(2,1)S(1)} collective-permute-done((bf16[1536,256]{1,0:T(8,128)(2,1)}, bf16[1536,256]{1,0:T(8,128)(2,1)S(1)}, u32[]{:S(2)}, u32[]{:S(2)}) %collective-permute-start.13) | collective-permute-done | bytes 786464 | tf_op jit(solution)/shard_map/ppermute | solution.py:484
  57.0 1.2 %collective-permute-start.14 = (bf16[256,1024]{1,0:T(8,128)(2,1)S(1)}, bf16[256,1024]{1,0:T(8,128)(2,1)S(1)}, u32[]{:S(2)}, u32[]{:S(2)}) collective-permute-start(bf16[256,1024]{1,0:T(8,128)(2,1)S(1)} %copy-done.2), channel_id=1, source_target_pairs={{0,1},{1,0},{2,3},{3,2},{4,5},{5,4},{6,7},{7,6},{8,9},{9,8},{10,11... | collective-permute-start | bytes 1572872 | tf_op jit(solution)/shard_map/ppermute | solution.py:394
  58.2 0.0 collective-permute-start.15
  58.2 0.0 copy-start.1
  58.2 6.8 %shard_map.78 = (f32[768,256]{1,0:T(8,128)S(1)}, f32[768,256]{1,0:T(8,128)S(1)}) custom-call(s32[6,17]{1,0:T(8,128)S(1)} %pad_add_fusion.told_ref, bf16[768,256]{1,0:T(8,128)(2,1)S(1)} %copy-done.4, bf16[256,768]{1,0:T(8,128)(2,1)S(1)} %get-tuple-element.76.keys_t_ref, bf16[768,256]{1,0:T(8,128)(2,1)S(1)} %get-tuple-element.77.values_ref, ...), custom_call_target="tpu_custom_call" | custom-call | flops 900000000 | bytes 2700000 | tf_op jit(solution)/shard_map/pallas_call | solution.py:518
  65.0 3.3 %collective-permute-done.12.near_ref = bf16[768,256]{1,0:T(8,128)(2,1)S(1)} collective-permute-done((bf16[768,256]{1,0:T(8,128)(2,1)S(1)}, bf16[768,256]{1,0:T(8,128)(2,1)S(1)}, u32[]{:S(2)}, u32[]{:S(2)}) %collective-permute-start.12) | collective-permute-done | bytes 393248 | tf_op jit(solution)/shard_map/ppermute | solution.py:394
  68.4 0.5 shard_map.79.refs_0_
  68.9 1.4 %collective-permute-start.17 = (bf16[768,256]{1,0:T(8,128)(2,1)S(1)}, bf16[768,256]{1,0:T(8,128)(2,1)S(1)}, u32[]{:S(2)}, u32[]{:S(2)}) collective-permute-start(bf16[768,256]{1,0:T(8,128)(2,1)S(1)} %shard_map.79.refs_0_), channel_id=1, source_target_pairs={{0,1},{1,0},{2,3},{3,2},{4,5},{5,4},{6,7},{7,6},{8,9},{9,8},{10,11... | collective-permute-start | bytes 1179656 | tf_op jit(solution)/shard_map/ppermute | solution.py:394
  70.3 1.1 %collective-permute-start.16 = (bf16[768,256]{1,0:T(8,128)(2,1)S(1)}, bf16[768,256]{1,0:T(8,128)(2,1)S(1)}, u32[]{:S(2)}, u32[]{:S(2)}) collective-permute-start(bf16[768,256]{1,0:T(8,128)(2,1)S(1)} %shard_map.79.refs_0_), channel_id=1, source_target_pairs={{0,2},{1,3},{2,0},{3,1},{4,6},{5,7},{6,4},{7,5},{8,10},{9,11},{10,... | collective-permute-start | bytes 1179656 | tf_op jit(solution)/shard_map/ppermute | solution.py:394
  71.4 0.3 collective-permute-done.17.refs_1_
  71.7 0.5 shard_map.80
  72.2 8.8 %collective-permute-done.16.refs_0_ = bf16[768,256]{1,0:T(8,128)(2,1)S(1)} collective-permute-done((bf16[768,256]{1,0:T(8,128)(2,1)S(1)}, bf16[768,256]{1,0:T(8,128)(2,1)S(1)}, u32[]{:S(2)}, u32[]{:S(2)}) %collective-permute-start.16) | collective-permute-done | bytes 393248 | tf_op jit(solution)/shard_map/ppermute | solution.py:394
  81.0 0.8 %collective-permute-start.18 = (bf16[768,256]{1,0:T(8,128)(2,1)S(1)}, bf16[768,256]{1,0:T(8,128)(2,1)S(1)}, u32[]{:S(2)}, u32[]{:S(2)}) collective-permute-start(bf16[768,256]{1,0:T(8,128)(2,1)S(1)} %collective-permute-done.16.refs_0_), channel_id=1, source_target_pairs={{0,1},{1,0},{2,3},{3,2},{4,5},{5,4},{6,7},{7,6},{8,9},{9,8},{10,11... | collective-permute-start | bytes 1179656 | tf_op jit(solution)/shard_map/ppermute | solution.py:394
  81.9 1.3 %collective-permute-done.18.refs_1_ = bf16[768,256]{1,0:T(8,128)(2,1)S(1)} collective-permute-done((bf16[768,256]{1,0:T(8,128)(2,1)S(1)}, bf16[768,256]{1,0:T(8,128)(2,1)S(1)}, u32[]{:S(2)}, u32[]{:S(2)}) %collective-permute-start.18) | collective-permute-done | bytes 393248 | tf_op jit(solution)/shard_map/ppermute | solution.py:394
  83.2 1.1 %shard_map.81 = bf16[768,256]{1,0:T(8,128)(2,1)} custom-call(bf16[768,256]{1,0:T(8,128)(2,1)S(1)} %collective-permute-done.16.refs_0_, bf16[768,256]{1,0:T(8,128)(2,1)S(1)} %collective-permute-done.18.refs_1_, bf16[512,256]{1,0:T(8,128)(2,1)S(1)} %get-tuple-element.95.refs_2_, f32[768,256]{1,0:T(8,128)S(1)} %get-tuple-element.96.refs_3_), custom_call_target="tpu_custom_call" | custom-call | flops 600000000 | bytes 1800000 | tf_op jit(solution)/shard_map/pallas_call | solution.py:555
  (21 shorter events, 0.0 us)
Async XLA Ops:
  0.0 2.6 %copy-start.2 = (bf16[256,1024]{1,0:T(8,128)(2,1)S(1)}, bf16[256,1024]{1,0:T(8,128)(2,1)}, u32[]{:S(2)}) copy-start(bf16[256,1024]{1,0:T(8,128)(2,1)} %refs_2_) | copy-start | bytes 1572868
  2.6 15.4 %copy-start.9 = (s32[6]{0:T(128)S(1)}, s32[6]{0:T(128)}, u32[]{:S(2)}) copy-start(s32[6]{0:T(128)} %param.13) | copy-start | bytes 76
  2.6 15.5 %copy-start.8 = (s32[6,16]{1,0:T(8,128)S(1)}, s32[6,16]{1,0:T(8,128)}, u32[]{:S(2)}) copy-start(s32[6,16]{1,0:T(8,128)} %param.12) | copy-start | bytes 1156
  2.6 13.1 %collective-permute-start.2 = (bf16[256,1024]{1,0:T(8,128)(2,1)S(1)}, bf16[256,1024]{1,0:T(8,128)(2,1)S(1)}, u32[]{:S(2)}, u32[]{:S(2)}) collective-permute-start(bf16[256,1024]{1,0:T(8,128)(2,1)S(1)} %copy-done.2), channel_id=1, source_target_pairs={{0,2},{1,3},{2,0},{3,1},{4,6},{5,7},{6,4},{7,5},{8,10},{9,11},{10,... | collective-permute-start | bytes 1572872 | tf_op jit(solution)/shard_map/ppermute | solution.py:394
  3.9 11.8 %collective-permute-start.1 = (bf16[192,1024]{1,0:T(8,128)(2,1)}, bf16[192,1024]{1,0:T(8,128)(2,1)S(1)}, u32[]{:S(2)}, u32[]{:S(2)}) collective-permute-start(bf16[192,1024]{1,0:T(8,128)(2,1)} %shard_map.73), channel_id=1, source_target_pairs={{0,8},{4,12},{8,16},{12,20},{16,24},{20,28},{1,9},{5,13},{9,17},{1... | collective-permute-start | bytes 1179656 | tf_op jit(solution)/shard_map/ppermute | solution.py:441
  12.1 18.6 %collective-permute-start.5 = (bf16[768,256]{1,0:T(8,128)(2,1)}, bf16[768,256]{1,0:T(8,128)(2,1)S(1)}, u32[]{:S(2)}, u32[]{:S(2)}) collective-permute-start(bf16[768,256]{1,0:T(8,128)(2,1)} %get-tuple-element.61.query_hbm.refs_5_), channel_id=1, source_target_pairs={{0,4},{4,0},{8,12},{12,8},{16,20},{20,16},{24,28},{28,24},{1,5},{5... | collective-permute-start | bytes 1179656 | tf_op jit(solution)/shard_map/ppermute | solution.py:394
  15.7 15.0 %collective-permute-start.4 = (bf16[192,1024]{1,0:T(8,128)(2,1)S(1)}, bf16[192,1024]{1,0:T(8,128)(2,1)S(1)}, u32[]{:S(2)}, u32[]{:S(2)}) collective-permute-start(bf16[192,1024]{1,0:T(8,128)(2,1)S(1)} %collective-permute-done.1.refs_0_), channel_id=1, source_target_pairs={{0,2},{1,3},{2,0},{3,1},{4,6},{5,7},{6,4},{7,5},{8,10},{9,11},{10,... | collective-permute-start | bytes 1179656 | tf_op jit(solution)/shard_map/ppermute | solution.py:394
  16.7 14.0 %collective-permute-start.3 = (bf16[192,1024]{1,0:T(8,128)(2,1)S(1)}, bf16[192,1024]{1,0:T(8,128)(2,1)S(1)}, u32[]{:S(2)}, u32[]{:S(2)}) collective-permute-start(bf16[192,1024]{1,0:T(8,128)(2,1)S(1)} %collective-permute-done.1.refs_0_), channel_id=1, source_target_pairs={{8,16},{12,20},{16,24},{20,28},{9,17},{13,21},{17,25},{21,29},{10,... | collective-permute-start | bytes 1179656 | tf_op jit(solution)/shard_map/ppermute | solution.py:463
  18.2 3.9 %collective-permute-start = (s32[6,17]{1,0:T(8,128)S(1)}, s32[6,17]{1,0:T(8,128)S(1)}, u32[]{:S(2)}, u32[]{:S(2)}) collective-permute-start(s32[6,17]{1,0:T(8,128)S(1)} %pad_add_fusion.told_ref), channel_id=1, source_target_pairs={{0,4},{4,0},{8,12},{12,8},{16,20},{20,16},{24,28},{28,24},{1,5},{5... | collective-permute-start | bytes 1232 | tf_op jit(solution)/shard_map/ppermute | solution.py:394
  22.1 8.5 %collective-permute-start.6 = (bf16[2,128,256]{2,1,0:T(8,128)(2,1)}, bf16[2,128,256]{2,1,0:T(8,128)(2,1)S(1)}, u32[]{:S(2)}, u32[]{:S(2)}) collective-permute-start(bf16[2,128,256]{2,1,0:T(8,128)(2,1)} %get-tuple-element.64), channel_id=1, source_target_pairs={{0,24},{4,28},{1,25},{5,29},{2,26},{6,30},{3,27},{7,31}} | collective-permute-start | bytes 393224 | tf_op jit(solution)/shard_map/ppermute | solution.py:467
  23.4 11.8 %collective-permute-start.9 = (bf16[192,1024]{1,0:T(8,128)(2,1)S(1)}, bf16[192,1024]{1,0:T(8,128)(2,1)S(1)}, u32[]{:S(2)}, u32[]{:S(2)}) collective-permute-start(bf16[192,1024]{1,0:T(8,128)(2,1)S(1)} %collective-permute-done.1.refs_0_), channel_id=1, source_target_pairs={{0,1},{1,0},{2,3},{3,2},{4,5},{5,4},{6,7},{7,6},{8,9},{9,8},{10,11... | collective-permute-start | bytes 1179656 | tf_op jit(solution)/shard_map/ppermute | solution.py:394
  25.3 1.0 %copy-start.3 = (bf16[768,256]{1,0:T(8,128)(2,1)S(1)}, bf16[768,256]{1,0:T(8,128)(2,1)}, u32[]{:S(2)}) copy-start(bf16[768,256]{1,0:T(8,128)(2,1)} %get-tuple-element.61.query_hbm.refs_5_) | copy-start | bytes 1179652
  26.3 1.0 %copy-start.7 = (bf16[256,768]{1,0:T(8,128)(2,1)S(1)}, bf16[256,768]{1,0:T(8,128)(2,1)}, u32[]{:S(2)}) copy-start(bf16[256,768]{1,0:T(8,128)(2,1)} %get-tuple-element.62.keys_t_hbm.refs_7_) | copy-start | bytes 1179652
  27.3 7.8 %copy-start = (bf16[4,1024,256]{2,1,0:T(8,128)(2,1)S(1)}, bf16[4,1024,256]{2,1,0:T(8,128)(2,1)}, u32[]{:S(2)}) copy-start(bf16[4,1024,256]{2,1,0:T(8,128)(2,1)} %refs_4_.3) | copy-start | bytes 6291460
  27.3 7.8 %copy-start.4 = (bf16[768,256]{1,0:T(8,128)(2,1)S(1)}, bf16[768,256]{1,0:T(8,128)(2,1)}, u32[]{:S(2)}) copy-start(bf16[768,256]{1,0:T(8,128)(2,1)} %get-tuple-element.61.query_hbm.refs_5_) | copy-start | bytes 1179652
  30.7 4.5 %collective-permute-start.10 = (bf16[192,1024]{1,0:T(8,128)(2,1)S(1)}, bf16[192,1024]{1,0:T(8,128)(2,1)S(1)}, u32[]{:S(2)}, u32[]{:S(2)}) collective-permute-start(bf16[192,1024]{1,0:T(8,128)(2,1)S(1)} %collective-permute-done.4.refs_2_), channel_id=1, source_target_pairs={{0,1},{1,0},{2,3},{3,2},{4,5},{5,4},{6,7},{7,6},{8,9},{9,8},{10,11... | collective-permute-start | bytes 1179656 | tf_op jit(solution)/shard_map/ppermute | solution.py:394
  33.0 11.5 %collective-permute-start.8 = (bf16[192,1024]{1,0:T(8,128)(2,1)S(1)}, bf16[192,1024]{1,0:T(8,128)(2,1)S(1)}, u32[]{:S(2)}, u32[]{:S(2)}) collective-permute-start(bf16[192,1024]{1,0:T(8,128)(2,1)S(1)} %collective-permute-done.3.refs_0_), channel_id=1, source_target_pairs={{0,2},{1,3},{2,0},{3,1},{4,6},{5,7},{6,4},{7,5},{8,10},{9,11},{10,... | collective-permute-start | bytes 1179656 | tf_op jit(solution)/shard_map/ppermute | solution.py:394
  33.4 23.6 %collective-permute-start.13 = (bf16[1536,256]{1,0:T(8,128)(2,1)}, bf16[1536,256]{1,0:T(8,128)(2,1)S(1)}, u32[]{:S(2)}, u32[]{:S(2)}) collective-permute-start(bf16[1536,256]{1,0:T(8,128)(2,1)} %get-tuple-element.70.both_hbm.refs_8_), channel_id=1, source_target_pairs={{4,24},{5,25},{6,26},{7,27}} | collective-permute-start | bytes 2359304 | tf_op jit(solution)/shard_map/ppermute | solution.py:484
  34.7 10.1 %collective-permute-start.7 = (bf16[192,1024]{1,0:T(8,128)(2,1)S(1)}, bf16[192,1024]{1,0:T(8,128)(2,1)S(1)}, u32[]{:S(2)}, u32[]{:S(2)}) collective-permute-start(bf16[192,1024]{1,0:T(8,128)(2,1)S(1)} %collective-permute-done.3.refs_0_), channel_id=1, source_target_pairs={{0,1},{1,0},{2,3},{3,2},{4,5},{5,4},{6,7},{7,6},{8,9},{9,8},{10,11... | collective-permute-start | bytes 1179656 | tf_op jit(solution)/shard_map/ppermute | solution.py:394
  44.6 13.6 %copy-start.5 = (bf16[256]{0:T(256)(128)(2,1)S(1)}, bf16[256]{0:T(256)(128)(2,1)}, u32[]{:S(2)}) copy-start(bf16[256]{0:T(256)(128)(2,1)} %gain_ref.3) | copy-start | bytes 1540
  44.6 13.6 %copy-start.6 = (bf16[768,256]{1,0:T(8,128)(2,1)S(1)}, bf16[768,256]{1,0:T(8,128)(2,1)}, u32[]{:S(2)}) copy-start(bf16[768,256]{1,0:T(8,128)(2,1)} %get-tuple-element.82.gate_hbm) | copy-start | bytes 1179652
  44.6 1.8 %collective-permute-start.11 = (bf16[192,1024]{1,0:T(8,128)(2,1)S(1)}, bf16[192,1024]{1,0:T(8,128)(2,1)S(1)}, u32[]{:S(2)}, u32[]{:S(2)}) collective-permute-start(bf16[192,1024]{1,0:T(8,128)(2,1)S(1)} %collective-permute-done.8.refs_2_), channel_id=1, source_target_pairs={{0,1},{1,0},{2,3},{3,2},{4,5},{5,4},{6,7},{7,6},{8,9},{9,8},{10,11... | collective-permute-start | bytes 1179656 | tf_op jit(solution)/shard_map/ppermute | solution.py:394
  57.0 11.4 %collective-permute-start.14 = (bf16[256,1024]{1,0:T(8,128)(2,1)S(1)}, bf16[256,1024]{1,0:T(8,128)(2,1)S(1)}, u32[]{:S(2)}, u32[]{:S(2)}) collective-permute-start(bf16[256,1024]{1,0:T(8,128)(2,1)S(1)} %copy-done.2), channel_id=1, source_target_pairs={{0,1},{1,0},{2,3},{3,2},{4,5},{5,4},{6,7},{7,6},{8,9},{9,8},{10,11... | collective-permute-start | bytes 1572872 | tf_op jit(solution)/shard_map/ppermute | solution.py:394
  58.2 10.2 %collective-permute-start.15 = (bf16[256,1024]{1,0:T(8,128)(2,1)S(1)}, bf16[256,1024]{1,0:T(8,128)(2,1)S(1)}, u32[]{:S(2)}, u32[]{:S(2)}) collective-permute-start(bf16[256,1024]{1,0:T(8,128)(2,1)S(1)} %collective-permute-done.2.refs_4_), channel_id=1, source_target_pairs={{0,1},{1,0},{2,3},{3,2},{4,5},{5,4},{6,7},{7,6},{8,9},{9,8},{10,11... | collective-permute-start | bytes 1572872 | tf_op jit(solution)/shard_map/ppermute | solution.py:394
  58.2 10.2 %collective-permute-start.12 = (bf16[768,256]{1,0:T(8,128)(2,1)S(1)}, bf16[768,256]{1,0:T(8,128)(2,1)S(1)}, u32[]{:S(2)}, u32[]{:S(2)}) collective-permute-start(bf16[768,256]{1,0:T(8,128)(2,1)S(1)} %get-tuple-element.75), channel_id=1, source_target_pairs={{0,4},{4,0},{8,12},{12,8},{16,20},{20,16},{24,28},{28,24},{1,5},{5... | collective-permute-start | bytes 1179656 | tf_op jit(solution)/shard_map/ppermute | solution.py:394
  58.2 13.5 %copy-start.1 = (bf16[768,1024]{1,0:T(8,128)(2,1)S(1)}, bf16[768,1024]{1,0:T(8,128)(2,1)}, u32[]{:S(2)}) copy-start(bf16[768,1024]{1,0:T(8,128)(2,1)} %refs_6_.1) | copy-start | bytes 4718596
  68.9 2.8 %collective-permute-start.17 = (bf16[768,256]{1,0:T(8,128)(2,1)S(1)}, bf16[768,256]{1,0:T(8,128)(2,1)S(1)}, u32[]{:S(2)}, u32[]{:S(2)}) collective-permute-start(bf16[768,256]{1,0:T(8,128)(2,1)S(1)} %shard_map.79.refs_0_), channel_id=1, source_target_pairs={{0,1},{1,0},{2,3},{3,2},{4,5},{5,4},{6,7},{7,6},{8,9},{9,8},{10,11... | collective-permute-start | bytes 1179656 | tf_op jit(solution)/shard_map/ppermute | solution.py:394
  70.3 10.7 %collective-permute-start.16 = (bf16[768,256]{1,0:T(8,128)(2,1)S(1)}, bf16[768,256]{1,0:T(8,128)(2,1)S(1)}, u32[]{:S(2)}, u32[]{:S(2)}) collective-permute-start(bf16[768,256]{1,0:T(8,128)(2,1)S(1)} %shard_map.79.refs_0_), channel_id=1, source_target_pairs={{0,2},{1,3},{2,0},{3,1},{4,6},{5,7},{6,4},{7,5},{8,10},{9,11},{10,... | collective-permute-start | bytes 1179656 | tf_op jit(solution)/shard_map/ppermute | solution.py:394
  81.0 2.2 %collective-permute-start.18 = (bf16[768,256]{1,0:T(8,128)(2,1)S(1)}, bf16[768,256]{1,0:T(8,128)(2,1)S(1)}, u32[]{:S(2)}, u32[]{:S(2)}) collective-permute-start(bf16[768,256]{1,0:T(8,128)(2,1)S(1)} %collective-permute-done.16.refs_0_), channel_id=1, source_target_pairs={{0,1},{1,0},{2,3},{3,2},{4,5},{5,4},{6,7},{7,6},{8,9},{9,8},{10,11... | collective-permute-start | bytes 1179656 | tf_op jit(solution)/shard_map/ppermute | solution.py:394

commit v5 on v4

--- a/solution.py
+++ b/solution.py
@@ -497,7 +497,7 @@
         ]
         + [live, sems(5), sems(2)],
         compiler_params=params(16),
-        cost_estimate=cost(6),
+        cost_estimate=cost(0.05),
     )(told, told_x, *chunk_1, w_in, query, query_x, keys_t, both, own_sums)
 
     cross_2, sums_x = barrier((cross_2, sums_x))
@@ -510,10 +510,10 @@
             pltpu.VMEM(upright, bf16), pltpu.VMEM(upright, f32), pltpu.VMEM(upright, f32), live, sems(2)
         ],
         compiler_params=params(),
-        cost_estimate=cost(4),
+        cost_estimate=cost(0.05),
     )(told_x, *near_2, *spread(cross_2, n_head // 4), w_in, query_x, sums_x)
     near = crossed(send, "seq", 1)
-    far, send, w_out, w_cross = barrier((far, send, w_out, w_cross))
+    send, w_out, w_cross = barrier((send, w_out, w_cross))
     w_all = spread(w_out, n_head // 4) + spread(w_cross, n_head // 4)
     mine, scale = pl.pallas_call(
         make_own_last_kernel(PLANES),
@@ -523,7 +523,7 @@
         scratch_shapes=[pltpu.VMEM(upright, bf16)] * 2
         + [pltpu.VMEM((2 * tok_rows, cols), bf16), pltpu.VMEM(lying, bf16), live, sems(3), sems(1)],
         compiler_params=params(),
-        cost_estimate=cost(3),
+        cost_estimate=cost(9),
     )(told, query, keys_t, values, tail, far, sums, gate, out_gain)
     near, mine, w_all = barrier((near, mine, tuple(w_all)))
     gated = pl.pallas_call(

time: 84.7 us -> 81.6 us (0.963)
  waiting for transfers between devices: 26.2 us -> 21.9 us
  Pallas kernels: 35.8 us -> 38.6 us
  starting transfers between devices: 19.8 us -> 18.3 us
    ppermute x1, waiting for transfers between devices: 5.87 us -> 3.53 us  [body(): lax.ppermute(both, 'seq', [(i, i + FAR) for i in range(1, n_seq - FAR, 2)])]
    ppermute x15, waiting for transfers between devices: 18 us -> 16 us  [crossed(): lax.ppermute(array, axis, [(i, i ^ bit) for i in range(lax.axis_size(axis...]
    ppermute x15, starting transfers between devices: 14.7 us -> 13.2 us  [crossed(): lax.ppermute(array, axis, [(i, i ^ bit) for i in range(lax.axis_size(axis...]
    pallas_call x1, Pallas kernels: 9.37 us -> 10.8 us  [body(): pl.pallas_call(make_chunk_kernel(1, n_head), in_specs=[flat] * 2 + [wide]...]
    pallas_call x1, Pallas kernels: 6.79 us -> 7.81 us  [body(): pl.pallas_call(make_own_last_kernel(PLANES), in_specs=[flat, far_off, wid...]
    unnamed x20 -> x22, local copies, waits for them, and re-layouts: 2.03 us -> 2.04 us
  transfers between devices with their start and end apart: 19 -> 19, of which waited for: 8 -> 8; matrix products, arithmetic and copies ran while one was open for 0% -> 0% of each run, Pallas kernels for 38% -> 42%
where the time goes in v5:
time: 81.6 us; the launch traced here: 81.2 us
  Pallas kernels  38.6 us (47%)
  waiting for transfers between devices  21.9 us (27%)
  starting transfers between devices  18.3 us (22%)
  local copies, waits for them, and re-layouts  2.13 us (3%)
    ppermute x15, waiting for transfers between devices, crossed(): lax.ppermute(array, axis, [(i, i ^ bit) for i in range(lax.axis_size(axis...  16 us
    ppermute x15, starting transfers between devices, crossed(): lax.ppermute(array, axis, [(i, i ^ bit) for i in range(lax.axis_size(axis...  13.2 us
    pallas_call x1, Pallas kernels, body(): pl.pallas_call(make_chunk_kernel(1, n_head), in_specs=[flat] * 2 + [wide]...  10.8 us
    pallas_call x1, Pallas kernels, body(): pl.pallas_call(make_own_last_kernel(PLANES), in_specs=[flat, far_off, wid...  7.81 us
    pallas_call x1, Pallas kernels, body(): pl.pallas_call(own_kernel, in_specs=[far_off, far_off, wide], out_specs=[...  6.84 us
    pallas_call x1, Pallas kernels, body(): pl.pallas_call(make_last_kernel(PLANES, n_head), in_specs=[flat] + [wide]...  5.1 us
    ppermute x1, waiting for transfers between devices, body(): lax.ppermute(both, 'seq', [(i, i + FAR) for i in range(1, n_seq - FAR, 2)])  3.53 us
    pallas_call x1, Pallas kernels, body(): pl.pallas_call(own_attend_kernel, in_specs=[flat] + [far_off] * 3, out_sp...  3.31 us
  transfers between devices with their start and end apart: 19, of which 8 were waited for; matrix products, arithmetic and copies ran while one was open for 0% of the time, Pallas kernels for 42%

profile of v5, /device:TPU:25, one launch (start us, length us, event | category | flops | bytes accessed | tf_op | source)
XLA Modules:
  0.0 81.2 jit_solution(14389532200650365329)
XLA Ops:
  0.0 2.6 %shard_map.73 = bf16[192,1024]{1,0:T(8,128)(2,1)} custom-call(bf16[768,1024]{1,0:T(8,128)(2,1)} %refs_6_.1, bf16[1024]{0:T(1024)(128)(2,1)} %gain_hbm), custom_call_target="tpu_custom_call" | custom-call | flops 600000000 | bytes 1800000 | tf_op jit(solution)/shard_map/pallas_call | solution.py:425
  2.6 0.0 copy-start.10
  2.6 0.0 copy-start.9
  2.6 1.3 %collective-permute-start.2 = (bf16[256,1024]{1,0:T(8,128)(2,1)S(1)}, bf16[256,1024]{1,0:T(8,128)(2,1)S(1)}, u32[]{:S(2)}, u32[]{:S(2)}) collective-permute-start(bf16[256,1024]{1,0:T(8,128)(2,1)S(1)} %copy-done.2), channel_id=1, source_target_pairs={{0,2},{1,3},{2,0},{3,1},{4,6},{5,7},{6,4},{7,5},{8,10},{9,11},{10,... | collective-permute-start | bytes 1572872 | tf_op jit(solution)/shard_map/ppermute | solution.py:394
  3.9 1.3 %collective-permute-start.1 = (bf16[192,1024]{1,0:T(8,128)(2,1)}, bf16[192,1024]{1,0:T(8,128)(2,1)S(1)}, u32[]{:S(2)}, u32[]{:S(2)}) collective-permute-start(bf16[192,1024]{1,0:T(8,128)(2,1)} %shard_map.73), channel_id=1, source_target_pairs={{0,8},{4,12},{8,16},{12,20},{16,24},{20,28},{1,9},{5,13},{9,17},{1... | collective-permute-start | bytes 1179656 | tf_op jit(solution)/shard_map/ppermute | solution.py:441
  5.2 6.8 %shard_map.74 = (bf16[768,256]{1,0:T(8,128)(2,1)}, bf16[1536,256]{1,0:T(8,128)(2,1)}, bf16[768,256]{1,0:T(8,128)(2,1)}, bf16[256,768]{1,0:T(8,128)(2,1)}, bf16[2,128,256]{2,1,0:T(8,128)(2,1)}) custom-call(bf16[768,1024]{1,0:T(8,128)(2,1)} %refs_6_.1, bf16[1024]{0:T(1024)(128)(2,1)} %gain_hbm, bf16[4,1024,256]{2,1,0:T(8,128)(2,1)} %refs_4_.3), custom_call_target="tpu_custom_call" | custom-call | flops 1200000000 | bytes 3600000 | tf_op jit(solution)/shard_map/pallas_call | solution.py:443
  12.1 1.3 %collective-permute-start.5 = (bf16[768,256]{1,0:T(8,128)(2,1)}, bf16[768,256]{1,0:T(8,128)(2,1)S(1)}, u32[]{:S(2)}, u32[]{:S(2)}) collective-permute-start(bf16[768,256]{1,0:T(8,128)(2,1)} %get-tuple-element.60.query_hbm.refs_5_), channel_id=1, source_target_pairs={{0,4},{4,0},{8,12},{12,8},{16,20},{20,16},{24,28},{28,24},{1,5},{5... | collective-permute-start | bytes 1179656 | tf_op jit(solution)/shard_map/ppermute | solution.py:394
  13.3 2.3 %collective-permute-done.1.refs_0_ = bf16[192,1024]{1,0:T(8,128)(2,1)S(1)} collective-permute-done((bf16[192,1024]{1,0:T(8,128)(2,1)}, bf16[192,1024]{1,0:T(8,128)(2,1)S(1)}, u32[]{:S(2)}, u32[]{:S(2)}) %collective-permute-start.1) | collective-permute-done | bytes 393248 | tf_op jit(solution)/shard_map/ppermute | solution.py:441
  15.7 1.0 %collective-permute-start.4 = (bf16[192,1024]{1,0:T(8,128)(2,1)S(1)}, bf16[192,1024]{1,0:T(8,128)(2,1)S(1)}, u32[]{:S(2)}, u32[]{:S(2)}) collective-permute-start(bf16[192,1024]{1,0:T(8,128)(2,1)S(1)} %collective-permute-done.1.refs_0_), channel_id=1, source_target_pairs={{0,2},{1,3},{2,0},{3,1},{4,6},{5,7},{6,4},{7,5},{8,10},{9,11},{10,... | collective-permute-start | bytes 1179656 | tf_op jit(solution)/shard_map/ppermute | solution.py:394
  16.7 1.3 %collective-permute-start.3 = (bf16[192,1024]{1,0:T(8,128)(2,1)S(1)}, bf16[192,1024]{1,0:T(8,128)(2,1)S(1)}, u32[]{:S(2)}, u32[]{:S(2)}) collective-permute-start(bf16[192,1024]{1,0:T(8,128)(2,1)S(1)} %collective-permute-done.1.refs_0_), channel_id=1, source_target_pairs={{8,16},{12,20},{16,24},{20,28},{9,17},{13,21},{17,25},{21,29},{10,... | collective-permute-start | bytes 1179656 | tf_op jit(solution)/shard_map/ppermute | solution.py:463
  18.0 0.1 copy.8
  18.1 0.1 pad_add_fusion.told_ref
  18.2 1.2 %collective-permute-start = (s32[6,17]{1,0:T(8,128)S(1)}, s32[6,17]{1,0:T(8,128)S(1)}, u32[]{:S(2)}, u32[]{:S(2)}) collective-permute-start(s32[6,17]{1,0:T(8,128)S(1)} %pad_add_fusion.told_ref), channel_id=1, source_target_pairs={{0,4},{4,0},{8,12},{12,8},{16,20},{20,16},{24,28},{28,24},{1,5},{5... | collective-permute-start | bytes 1232 | tf_op jit(solution)/shard_map/ppermute | solution.py:394
  19.4 2.7 %collective-permute-done.told_x_ref = s32[6,17]{1,0:T(8,128)S(1)} collective-permute-done((s32[6,17]{1,0:T(8,128)S(1)}, s32[6,17]{1,0:T(8,128)S(1)}, u32[]{:S(2)}, u32[]{:S(2)}) %collective-permute-start) | collective-permute-done | bytes 440 | tf_op jit(solution)/shard_map/ppermute | solution.py:394
  22.1 1.3 %collective-permute-start.6 = (bf16[2,128,256]{2,1,0:T(8,128)(2,1)}, bf16[2,128,256]{2,1,0:T(8,128)(2,1)S(1)}, u32[]{:S(2)}, u32[]{:S(2)}) collective-permute-start(bf16[2,128,256]{2,1,0:T(8,128)(2,1)} %get-tuple-element.63), channel_id=1, source_target_pairs={{0,24},{4,28},{1,25},{5,29},{2,26},{6,30},{3,27},{7,31}} | collective-permute-start | bytes 393224 | tf_op jit(solution)/shard_map/ppermute | solution.py:467
  23.4 1.9 %collective-permute-start.9 = (bf16[192,1024]{1,0:T(8,128)(2,1)S(1)}, bf16[192,1024]{1,0:T(8,128)(2,1)S(1)}, u32[]{:S(2)}, u32[]{:S(2)}) collective-permute-start(bf16[192,1024]{1,0:T(8,128)(2,1)S(1)} %collective-permute-done.1.refs_0_), channel_id=1, source_target_pairs={{0,1},{1,0},{2,3},{3,2},{4,5},{5,4},{6,7},{7,6},{8,9},{9,8},{10,11... | collective-permute-start | bytes 1179656 | tf_op jit(solution)/shard_map/ppermute | solution.py:394
  25.3 1.0 %copy-done.3 = bf16[768,256]{1,0:T(8,128)(2,1)S(1)} copy-done((bf16[768,256]{1,0:T(8,128)(2,1)S(1)}, bf16[768,256]{1,0:T(8,128)(2,1)}, u32[]{:S(2)}) %copy-start.3) | copy-done | bytes 393240
  26.3 1.0 %copy-done.5 = bf16[256,768]{1,0:T(8,128)(2,1)S(1)} copy-done((bf16[256,768]{1,0:T(8,128)(2,1)S(1)}, bf16[256,768]{1,0:T(8,128)(2,1)}, u32[]{:S(2)}) %copy-start.5) | copy-done | bytes 393240
  27.3 3.3 %shard_map.75.refs_9_ = f32[768,256]{1,0:T(8,128)S(1)} custom-call(s32[6,17]{1,0:T(8,128)S(1)} %pad_add_fusion.told_ref, bf16[768,256]{1,0:T(8,128)(2,1)S(1)} %copy-done.3, bf16[256,768]{1,0:T(8,128)(2,1)S(1)} %copy-done.5, bf16[1536,256]{1,0:T(8,128)(2,1)} %get-tuple-element.69.both_hbm.refs_8_), custom_call_target="tpu_custom_call" | custom-call | flops 1200000000 | bytes 3600000 | tf_op jit(solution)/shard_map/pallas_call | solution.py:468
  30.7 0.0 collective-permute-done.4.refs_2_
  30.7 2.3 %collective-permute-start.10 = (bf16[192,1024]{1,0:T(8,128)(2,1)S(1)}, bf16[192,1024]{1,0:T(8,128)(2,1)S(1)}, u32[]{:S(2)}, u32[]{:S(2)}) collective-permute-start(bf16[192,1024]{1,0:T(8,128)(2,1)S(1)} %collective-permute-done.4.refs_2_), channel_id=1, source_target_pairs={{0,1},{1,0},{2,3},{3,2},{4,5},{5,4},{6,7},{7,6},{8,9},{9,8},{10,11... | collective-permute-start | bytes 1179656 | tf_op jit(solution)/shard_map/ppermute | solution.py:394
  33.0 0.4 collective-permute-start.8
  33.4 1.3 %collective-permute-start.13 = (bf16[1536,256]{1,0:T(8,128)(2,1)}, bf16[1536,256]{1,0:T(8,128)(2,1)S(1)}, u32[]{:S(2)}, u32[]{:S(2)}) collective-permute-start(bf16[1536,256]{1,0:T(8,128)(2,1)} %get-tuple-element.69.both_hbm.refs_8_), channel_id=1, source_target_pairs={{4,24},{5,25},{6,26},{7,27}} | collective-permute-start | bytes 2359304 | tf_op jit(solution)/shard_map/ppermute | solution.py:484
  34.7 0.4 collective-permute-start.7
  35.1 0.0 collective-permute-done.9.refs_1_
  35.1 0.0 collective-permute-done.10.refs_3_
  35.2 10.8 %shard_map.76 = (f32[768,256]{1,0:T(8,128)S(1)}, f32[768,256]{1,0:T(8,128)S(1)}) custom-call(s32[6,17]{1,0:T(8,128)S(1)} %pad_add_fusion.told_ref, s32[6,17]{1,0:T(8,128)S(1)} %collective-permute-done.told_x_ref, bf16[192,1024]{1,0:T(8,128)(2,1)S(1)} %collective-permute-done.1.refs_0_, bf16[192,1024]{1,0:T(8,128)(2,1)S(1)} %collective-permute-done.9.refs_1_, ...), custom_call_target="tpu_custom_call" | custom-call | flops 15000000 | bytes 45000 | tf_op jit(solution)/shard_map/pallas_call | solution.py:486
  46.0 0.0 collective-permute-done.8.refs_2_
  46.0 0.0 copy-start.7
  46.0 0.0 copy-start.8
  46.0 0.2 collective-permute-start.11
  46.2 1.6 %collective-permute-done.11.refs_3_ = bf16[192,1024]{1,0:T(8,128)(2,1)S(1)} collective-permute-done((bf16[192,1024]{1,0:T(8,128)(2,1)S(1)}, bf16[192,1024]{1,0:T(8,128)(2,1)S(1)}, u32[]{:S(2)}, u32[]{:S(2)}) %collective-permute-start.11) | collective-permute-done | bytes 393248 | tf_op jit(solution)/shard_map/ppermute | solution.py:394
  47.8 5.1 %shard_map.77 = (bf16[768,256]{1,0:T(8,128)(2,1)S(1)}, bf16[256,768]{1,0:T(8,128)(2,1)S(1)}, bf16[768,256]{1,0:T(8,128)(2,1)S(1)}) custom-call(s32[6,17]{1,0:T(8,128)S(1)} %collective-permute-done.told_x_ref, bf16[192,1024]{1,0:T(8,128)(2,1)S(1)} %collective-permute-done.3.refs_0_, bf16[192,1024]{1,0:T(8,128)(2,1)S(1)} %collective-permute-done.7.refs_1_, ...), custom_call_target="tpu_custom_call" | custom-call | flops 15000000 | bytes 45000 | tf_op jit(solution)/shard_map/pallas_call | solution.py:504
  52.9 0.2 collective-permute-start.14
  53.1 0.3 collective-permute-start.15
  53.5 3.5 %collective-permute-done.13.far_hbm = bf16[1536,256]{1,0:T(8,128)(2,1)S(1)} collective-permute-done((bf16[1536,256]{1,0:T(8,128)(2,1)}, bf16[1536,256]{1,0:T(8,128)(2,1)S(1)}, u32[]{:S(2)}, u32[]{:S(2)}) %collective-permute-start.13) | collective-permute-done | bytes 786464 | tf_op jit(solution)/shard_map/ppermute | solution.py:484
  57.0 7.8 %shard_map.78 = (f32[768,256]{1,0:T(8,128)S(1)}, f32[768,256]{1,0:T(8,128)S(1)}) custom-call(s32[6,17]{1,0:T(8,128)S(1)} %pad_add_fusion.told_ref, bf16[768,256]{1,0:T(8,128)(2,1)S(1)} %copy-done.4, bf16[256,768]{1,0:T(8,128)(2,1)S(1)} %get-tuple-element.75.keys_t_ref, bf16[768,256]{1,0:T(8,128)(2,1)S(1)} %get-tuple-element.76.values_ref, ...), custom_call_target="tpu_custom_call" | custom-call | flops 2700000000 | bytes 8100000 | tf_op jit(solution)/shard_map/pallas_call | solution.py:518
  64.8 0.0 copy-start.1
  64.8 1.3 %collective-permute-done.12.near_ref = bf16[768,256]{1,0:T(8,128)(2,1)S(1)} collective-permute-done((bf16[768,256]{1,0:T(8,128)(2,1)S(1)}, bf16[768,256]{1,0:T(8,128)(2,1)S(1)}, u32[]{:S(2)}, u32[]{:S(2)}) %collective-permute-start.12) | collective-permute-done | bytes 393248 | tf_op jit(solution)/shard_map/ppermute | solution.py:394
  66.2 0.5 shard_map.79.refs_0_
  66.7 0.5 collective-permute-start.17
  67.2 1.1 %collective-permute-start.16 = (bf16[768,256]{1,0:T(8,128)(2,1)S(1)}, bf16[768,256]{1,0:T(8,128)(2,1)S(1)}, u32[]{:S(2)}, u32[]{:S(2)}) collective-permute-start(bf16[768,256]{1,0:T(8,128)(2,1)S(1)} %shard_map.79.refs_0_), channel_id=1, source_target_pairs={{0,2},{1,3},{2,0},{3,1},{4,6},{5,7},{6,4},{7,5},{8,10},{9,11},{10,... | collective-permute-start | bytes 1179656 | tf_op jit(solution)/shard_map/ppermute | solution.py:394
  68.3 0.3 collective-permute-done.17.refs_1_
  68.6 0.5 shard_map.80
  69.1 8.8 %collective-permute-done.16.refs_0_ = bf16[768,256]{1,0:T(8,128)(2,1)S(1)} collective-permute-done((bf16[768,256]{1,0:T(8,128)(2,1)S(1)}, bf16[768,256]{1,0:T(8,128)(2,1)S(1)}, u32[]{:S(2)}, u32[]{:S(2)}) %collective-permute-start.16) | collective-permute-done | bytes 393248 | tf_op jit(solution)/shard_map/ppermute | solution.py:394
  77.9 0.8 %collective-permute-start.18 = (bf16[768,256]{1,0:T(8,128)(2,1)S(1)}, bf16[768,256]{1,0:T(8,128)(2,1)S(1)}, u32[]{:S(2)}, u32[]{:S(2)}) collective-permute-start(bf16[768,256]{1,0:T(8,128)(2,1)S(1)} %collective-permute-done.16.refs_0_), channel_id=1, source_target_pairs={{0,1},{1,0},{2,3},{3,2},{4,5},{5,4},{6,7},{7,6},{8,9},{9,8},{10,11... | collective-permute-start | bytes 1179656 | tf_op jit(solution)/shard_map/ppermute | solution.py:394
  78.8 1.3 %collective-permute-done.18.refs_1_ = bf16[768,256]{1,0:T(8,128)(2,1)S(1)} collective-permute-done((bf16[768,256]{1,0:T(8,128)(2,1)S(1)}, bf16[768,256]{1,0:T(8,128)(2,1)S(1)}, u32[]{:S(2)}, u32[]{:S(2)}) %collective-permute-start.18) | collective-permute-done | bytes 393248 | tf_op jit(solution)/shard_map/ppermute | solution.py:394
  80.1 1.1 %shard_map.81 = bf16[768,256]{1,0:T(8,128)(2,1)} custom-call(bf16[768,256]{1,0:T(8,128)(2,1)S(1)} %collective-permute-done.16.refs_0_, bf16[768,256]{1,0:T(8,128)(2,1)S(1)} %collective-permute-done.18.refs_1_, bf16[512,256]{1,0:T(8,128)(2,1)S(1)} %get-tuple-element.93.refs_2_, f32[768,256]{1,0:T(8,128)S(1)} %get-tuple-element.94.refs_3_), custom_call_target="tpu_custom_call" | custom-call | flops 600000000 | bytes 1800000 | tf_op jit(solution)/shard_map/pallas_call | solution.py:555
  (23 shorter events, 0.0 us)
Async XLA Ops:
  0.0 2.6 %copy-start.2 = (bf16[256,1024]{1,0:T(8,128)(2,1)S(1)}, bf16[256,1024]{1,0:T(8,128)(2,1)}, u32[]{:S(2)}) copy-start(bf16[256,1024]{1,0:T(8,128)(2,1)} %refs_2_) | copy-start | bytes 1572868
  2.6 15.4 %copy-start.10 = (s32[6]{0:T(128)S(1)}, s32[6]{0:T(128)}, u32[]{:S(2)}) copy-start(s32[6]{0:T(128)} %param.13) | copy-start | bytes 76
  2.6 15.5 %copy-start.9 = (s32[6,16]{1,0:T(8,128)S(1)}, s32[6,16]{1,0:T(8,128)}, u32[]{:S(2)}) copy-start(s32[6,16]{1,0:T(8,128)} %param.12) | copy-start | bytes 1156
  2.6 13.1 %collective-permute-start.2 = (bf16[256,1024]{1,0:T(8,128)(2,1)S(1)}, bf16[256,1024]{1,0:T(8,128)(2,1)S(1)}, u32[]{:S(2)}, u32[]{:S(2)}) collective-permute-start(bf16[256,1024]{1,0:T(8,128)(2,1)S(1)} %copy-done.2), channel_id=1, source_target_pairs={{0,2},{1,3},{2,0},{3,1},{4,6},{5,7},{6,4},{7,5},{8,10},{9,11},{10,... | collective-permute-start | bytes 1572872 | tf_op jit(solution)/shard_map/ppermute | solution.py:394
  3.9 11.8 %collective-permute-start.1 = (bf16[192,1024]{1,0:T(8,128)(2,1)}, bf16[192,1024]{1,0:T(8,128)(2,1)S(1)}, u32[]{:S(2)}, u32[]{:S(2)}) collective-permute-start(bf16[192,1024]{1,0:T(8,128)(2,1)} %shard_map.73), channel_id=1, source_target_pairs={{0,8},{4,12},{8,16},{12,20},{16,24},{20,28},{1,9},{5,13},{9,17},{1... | collective-permute-start | bytes 1179656 | tf_op jit(solution)/shard_map/ppermute | solution.py:441
  12.1 18.6 %collective-permute-start.5 = (bf16[768,256]{1,0:T(8,128)(2,1)}, bf16[768,256]{1,0:T(8,128)(2,1)S(1)}, u32[]{:S(2)}, u32[]{:S(2)}) collective-permute-start(bf16[768,256]{1,0:T(8,128)(2,1)} %get-tuple-element.60.query_hbm.refs_5_), channel_id=1, source_target_pairs={{0,4},{4,0},{8,12},{12,8},{16,20},{20,16},{24,28},{28,24},{1,5},{5... | collective-permute-start | bytes 1179656 | tf_op jit(solution)/shard_map/ppermute | solution.py:394
  15.7 15.0 %collective-permute-start.4 = (bf16[192,1024]{1,0:T(8,128)(2,1)S(1)}, bf16[192,1024]{1,0:T(8,128)(2,1)S(1)}, u32[]{:S(2)}, u32[]{:S(2)}) collective-permute-start(bf16[192,1024]{1,0:T(8,128)(2,1)S(1)} %collective-permute-done.1.refs_0_), channel_id=1, source_target_pairs={{0,2},{1,3},{2,0},{3,1},{4,6},{5,7},{6,4},{7,5},{8,10},{9,11},{10,... | collective-permute-start | bytes 1179656 | tf_op jit(solution)/shard_map/ppermute | solution.py:394
  16.7 13.9 %collective-permute-start.3 = (bf16[192,1024]{1,0:T(8,128)(2,1)S(1)}, bf16[192,1024]{1,0:T(8,128)(2,1)S(1)}, u32[]{:S(2)}, u32[]{:S(2)}) collective-permute-start(bf16[192,1024]{1,0:T(8,128)(2,1)S(1)} %collective-permute-done.1.refs_0_), channel_id=1, source_target_pairs={{8,16},{12,20},{16,24},{20,28},{9,17},{13,21},{17,25},{21,29},{10,... | collective-permute-start | bytes 1179656 | tf_op jit(solution)/shard_map/ppermute | solution.py:463
  18.2 3.9 %collective-permute-start = (s32[6,17]{1,0:T(8,128)S(1)}, s32[6,17]{1,0:T(8,128)S(1)}, u32[]{:S(2)}, u32[]{:S(2)}) collective-permute-start(s32[6,17]{1,0:T(8,128)S(1)} %pad_add_fusion.told_ref), channel_id=1, source_target_pairs={{0,4},{4,0},{8,12},{12,8},{16,20},{20,16},{24,28},{28,24},{1,5},{5... | collective-permute-start | bytes 1232 | tf_op jit(solution)/shard_map/ppermute | solution.py:394
  22.1 8.6 %collective-permute-start.6 = (bf16[2,128,256]{2,1,0:T(8,128)(2,1)}, bf16[2,128,256]{2,1,0:T(8,128)(2,1)S(1)}, u32[]{:S(2)}, u32[]{:S(2)}) collective-permute-start(bf16[2,128,256]{2,1,0:T(8,128)(2,1)} %get-tuple-element.63), channel_id=1, source_target_pairs={{0,24},{4,28},{1,25},{5,29},{2,26},{6,30},{3,27},{7,31}} | collective-permute-start | bytes 393224 | tf_op jit(solution)/shard_map/ppermute | solution.py:467
  23.4 11.8 %collective-permute-start.9 = (bf16[192,1024]{1,0:T(8,128)(2,1)S(1)}, bf16[192,1024]{1,0:T(8,128)(2,1)S(1)}, u32[]{:S(2)}, u32[]{:S(2)}) collective-permute-start(bf16[192,1024]{1,0:T(8,128)(2,1)S(1)} %collective-permute-done.1.refs_0_), channel_id=1, source_target_pairs={{0,1},{1,0},{2,3},{3,2},{4,5},{5,4},{6,7},{7,6},{8,9},{9,8},{10,11... | collective-permute-start | bytes 1179656 | tf_op jit(solution)/shard_map/ppermute | solution.py:394
  25.3 1.0 %copy-start.3 = (bf16[768,256]{1,0:T(8,128)(2,1)S(1)}, bf16[768,256]{1,0:T(8,128)(2,1)}, u32[]{:S(2)}) copy-start(bf16[768,256]{1,0:T(8,128)(2,1)} %get-tuple-element.60.query_hbm.refs_5_) | copy-start | bytes 1179652
  26.3 1.0 %copy-start.5 = (bf16[256,768]{1,0:T(8,128)(2,1)S(1)}, bf16[256,768]{1,0:T(8,128)(2,1)}, u32[]{:S(2)}) copy-start(bf16[256,768]{1,0:T(8,128)(2,1)} %get-tuple-element.61.keys_t_hbm.refs_7_) | copy-start | bytes 1179652
  27.3 7.8 %copy-start = (bf16[4,1024,256]{2,1,0:T(8,128)(2,1)S(1)}, bf16[4,1024,256]{2,1,0:T(8,128)(2,1)}, u32[]{:S(2)}) copy-start(bf16[4,1024,256]{2,1,0:T(8,128)(2,1)} %refs_4_.3) | copy-start | bytes 6291460
  27.3 7.8 %copy-start.4 = (bf16[768,256]{1,0:T(8,128)(2,1)S(1)}, bf16[768,256]{1,0:T(8,128)(2,1)}, u32[]{:S(2)}) copy-start(bf16[768,256]{1,0:T(8,128)(2,1)} %get-tuple-element.60.query_hbm.refs_5_) | copy-start | bytes 1179652
  27.3 7.9 %copy-start.6 = (bf16[256,768]{1,0:T(8,128)(2,1)S(1)}, bf16[256,768]{1,0:T(8,128)(2,1)}, u32[]{:S(2)}) copy-start(bf16[256,768]{1,0:T(8,128)(2,1)} %get-tuple-element.61.keys_t_hbm.refs_7_) | copy-start | bytes 1179652
  30.7 4.5 %collective-permute-start.10 = (bf16[192,1024]{1,0:T(8,128)(2,1)S(1)}, bf16[192,1024]{1,0:T(8,128)(2,1)S(1)}, u32[]{:S(2)}, u32[]{:S(2)}) collective-permute-start(bf16[192,1024]{1,0:T(8,128)(2,1)S(1)} %collective-permute-done.4.refs_2_), channel_id=1, source_target_pairs={{0,1},{1,0},{2,3},{3,2},{4,5},{5,4},{6,7},{7,6},{8,9},{9,8},{10,11... | collective-permute-start | bytes 1179656 | tf_op jit(solution)/shard_map/ppermute | solution.py:394
  33.0 13.0 %collective-permute-start.8 = (bf16[192,1024]{1,0:T(8,128)(2,1)S(1)}, bf16[192,1024]{1,0:T(8,128)(2,1)S(1)}, u32[]{:S(2)}, u32[]{:S(2)}) collective-permute-start(bf16[192,1024]{1,0:T(8,128)(2,1)S(1)} %collective-permute-done.3.refs_0_), channel_id=1, source_target_pairs={{0,2},{1,3},{2,0},{3,1},{4,6},{5,7},{6,4},{7,5},{8,10},{9,11},{10,... | collective-permute-start | bytes 1179656 | tf_op jit(solution)/shard_map/ppermute | solution.py:394
  33.4 23.6 %collective-permute-start.13 = (bf16[1536,256]{1,0:T(8,128)(2,1)}, bf16[1536,256]{1,0:T(8,128)(2,1)S(1)}, u32[]{:S(2)}, u32[]{:S(2)}) collective-permute-start(bf16[1536,256]{1,0:T(8,128)(2,1)} %get-tuple-element.69.both_hbm.refs_8_), channel_id=1, source_target_pairs={{4,24},{5,25},{6,26},{7,27}} | collective-permute-start | bytes 2359304 | tf_op jit(solution)/shard_map/ppermute | solution.py:484
  34.7 11.5 %collective-permute-start.7 = (bf16[192,1024]{1,0:T(8,128)(2,1)S(1)}, bf16[192,1024]{1,0:T(8,128)(2,1)S(1)}, u32[]{:S(2)}, u32[]{:S(2)}) collective-permute-start(bf16[192,1024]{1,0:T(8,128)(2,1)S(1)} %collective-permute-done.3.refs_0_), channel_id=1, source_target_pairs={{0,1},{1,0},{2,3},{3,2},{4,5},{5,4},{6,7},{7,6},{8,9},{9,8},{10,11... | collective-permute-start | bytes 1179656 | tf_op jit(solution)/shard_map/ppermute | solution.py:394
  46.0 11.0 %copy-start.7 = (bf16[256]{0:T(256)(128)(2,1)S(1)}, bf16[256]{0:T(256)(128)(2,1)}, u32[]{:S(2)}) copy-start(bf16[256]{0:T(256)(128)(2,1)} %gain_ref.3) | copy-start | bytes 1540
  46.0 11.0 %copy-start.8 = (bf16[768,256]{1,0:T(8,128)(2,1)S(1)}, bf16[768,256]{1,0:T(8,128)(2,1)}, u32[]{:S(2)}) copy-start(bf16[768,256]{1,0:T(8,128)(2,1)} %get-tuple-element.79.gate_hbm) | copy-start | bytes 1179652
  46.0 1.8 %collective-permute-start.11 = (bf16[192,1024]{1,0:T(8,128)(2,1)S(1)}, bf16[192,1024]{1,0:T(8,128)(2,1)S(1)}, u32[]{:S(2)}, u32[]{:S(2)}) collective-permute-start(bf16[192,1024]{1,0:T(8,128)(2,1)S(1)} %collective-permute-done.8.refs_2_), channel_id=1, source_target_pairs={{0,1},{1,0},{2,3},{3,2},{4,5},{5,4},{6,7},{7,6},{8,9},{9,8},{10,11... | collective-permute-start | bytes 1179656 | tf_op jit(solution)/shard_map/ppermute | solution.py:394
  52.9 13.3 %collective-permute-start.14 = (bf16[256,1024]{1,0:T(8,128)(2,1)S(1)}, bf16[256,1024]{1,0:T(8,128)(2,1)S(1)}, u32[]{:S(2)}, u32[]{:S(2)}) collective-permute-start(bf16[256,1024]{1,0:T(8,128)(2,1)S(1)} %copy-done.2), channel_id=1, source_target_pairs={{0,1},{1,0},{2,3},{3,2},{4,5},{5,4},{6,7},{7,6},{8,9},{9,8},{10,11... | collective-permute-start | bytes 1572872 | tf_op jit(solution)/shard_map/ppermute | solution.py:394
  53.1 13.0 %collective-permute-start.15 = (bf16[256,1024]{1,0:T(8,128)(2,1)S(1)}, bf16[256,1024]{1,0:T(8,128)(2,1)S(1)}, u32[]{:S(2)}, u32[]{:S(2)}) collective-permute-start(bf16[256,1024]{1,0:T(8,128)(2,1)S(1)} %collective-permute-done.2.refs_4_), channel_id=1, source_target_pairs={{0,1},{1,0},{2,3},{3,2},{4,5},{5,4},{6,7},{7,6},{8,9},{9,8},{10,11... | collective-permute-start | bytes 1572872 | tf_op jit(solution)/shard_map/ppermute | solution.py:394
  53.5 12.7 %collective-permute-start.12 = (bf16[768,256]{1,0:T(8,128)(2,1)S(1)}, bf16[768,256]{1,0:T(8,128)(2,1)S(1)}, u32[]{:S(2)}, u32[]{:S(2)}) collective-permute-start(bf16[768,256]{1,0:T(8,128)(2,1)S(1)} %get-tuple-element.74), channel_id=1, source_target_pairs={{0,4},{4,0},{8,12},{12,8},{16,20},{20,16},{24,28},{28,24},{1,5},{5... | collective-permute-start | bytes 1179656 | tf_op jit(solution)/shard_map/ppermute | solution.py:394
  64.8 3.7 %copy-start.1 = (bf16[768,1024]{1,0:T(8,128)(2,1)S(1)}, bf16[768,1024]{1,0:T(8,128)(2,1)}, u32[]{:S(2)}) copy-start(bf16[768,1024]{1,0:T(8,128)(2,1)} %refs_6_.1) | copy-start | bytes 4718596
  66.7 1.9 %collective-permute-start.17 = (bf16[768,256]{1,0:T(8,128)(2,1)S(1)}, bf16[768,256]{1,0:T(8,128)(2,1)S(1)}, u32[]{:S(2)}, u32[]{:S(2)}) collective-permute-start(bf16[768,256]{1,0:T(8,128)(2,1)S(1)} %shard_map.79.refs_0_), channel_id=1, source_target_pairs={{0,1},{1,0},{2,3},{3,2},{4,5},{5,4},{6,7},{7,6},{8,9},{9,8},{10,11... | collective-permute-start | bytes 1179656 | tf_op jit(solution)/shard_map/ppermute | solution.py:394
  67.2 10.7 %collective-permute-start.16 = (bf16[768,256]{1,0:T(8,128)(2,1)S(1)}, bf16[768,256]{1,0:T(8,128)(2,1)S(1)}, u32[]{:S(2)}, u32[]{:S(2)}) collective-permute-start(bf16[768,256]{1,0:T(8,128)(2,1)S(1)} %shard_map.79.refs_0_), channel_id=1, source_target_pairs={{0,2},{1,3},{2,0},{3,1},{4,6},{5,7},{6,4},{7,5},{8,10},{9,11},{10,... | collective-permute-start | bytes 1179656 | tf_op jit(solution)/shard_map/ppermute | solution.py:394
  77.9 2.2 %collective-permute-start.18 = (bf16[768,256]{1,0:T(8,128)(2,1)S(1)}, bf16[768,256]{1,0:T(8,128)(2,1)S(1)}, u32[]{:S(2)}, u32[]{:S(2)}) collective-permute-start(bf16[768,256]{1,0:T(8,128)(2,1)S(1)} %collective-permute-done.16.refs_0_), channel_id=1, source_target_pairs={{0,1},{1,0},{2,3},{3,2},{4,5},{5,4},{6,7},{7,6},{8,9},{9,8},{10,11... | collective-permute-start | bytes 1179656 | tf_op jit(solution)/shard_map/ppermute | solution.py:394

commit v6 on v5

--- a/solution.py
+++ b/solution.py
@@ -475,12 +475,12 @@
         compiler_params=params(),
         cost_estimate=cost(4),
     )(told, query, keys_t, both)
-    share_2, cross_1, own_sums, query_x, tail = barrier((share_2, cross_1, own_sums, query_x, tail))
+    share_2, cross_1, own_sums, query_x = barrier((share_2, cross_1, own_sums, query_x))
     chunk_1 = spread(share_1, n_head // 4) + spread(cross_1, n_head // 4)
     cross_2 = crossed(share_2, "head", n_head // 2)
     near_2 = spread(share_2, n_head // 4)
 
-    both, query_x, share_2, tail = barrier((both, query_x, share_2, tail))
+    both, query_x, share_2 = barrier((both, query_x, share_2))
     far = lax.ppermute(both, "seq", [(i, i + FAR) for i in range(1, n_seq - FAR, 2)])
 
     sums, sums_x = pl.pallas_call(

time: 81.6 us -> 81 us (level)
  waiting for transfers between devices: 21.9 us -> 23.8 us
  Pallas kernels: 38.6 us -> 36.9 us
    ppermute x1, waiting for transfers between devices: 0.01 us -> 6.81 us  [body(): lax.ppermute(tail, 'seq', [(i, i + FAR + 1) for i in range(n_seq - FAR -...]
    ppermute x1, waiting for transfers between devices: 3.53 us -> 0.01 us  [body(): lax.ppermute(both, 'seq', [(i, i + FAR) for i in range(1, n_seq - FAR, 2)])]
    ppermute x15, waiting for transfers between devices: 16 us -> 14.7 us  [crossed(): lax.ppermute(array, axis, [(i, i ^ bit) for i in range(lax.axis_size(axis...]
    unnamed x22 -> x24, local copies, waits for them, and re-layouts: 2.04 us -> 2.04 us
  transfers between devices with their start and end apart: 19 -> 19, of which waited for: 8 -> 7; matrix products, arithmetic and copies ran while one was open for 0% -> 0% of each run, Pallas kernels for 42% -> 40%
where the time goes in v6:
time: 81 us; the launch traced here: 80.9 us
  Pallas kernels  36.9 us (46%)
  waiting for transfers between devices  23.8 us (29%)
  starting transfers between devices  17.7 us (22%)
  local copies, waits for them, and re-layouts  2.13 us (3%)
    ppermute x15, waiting for transfers between devices, crossed(): lax.ppermute(array, axis, [(i, i ^ bit) for i in range(lax.axis_size(axis...  14.7 us
    ppermute x15, starting transfers between devices, crossed(): lax.ppermute(array, axis, [(i, i ^ bit) for i in range(lax.axis_size(axis...  12.6 us
    pallas_call x1, Pallas kernels, body(): pl.pallas_call(make_chunk_kernel(1, n_head), in_specs=[flat] * 2 + [wide]...  10 us
    pallas_call x1, Pallas kernels, body(): pl.pallas_call(make_own_last_kernel(PLANES), in_specs=[flat, far_off, wid...  7.14 us
    pallas_call x1, Pallas kernels, body(): pl.pallas_call(own_kernel, in_specs=[far_off, far_off, wide], out_specs=[...  6.85 us
    ppermute x1, waiting for transfers between devices, body(): lax.ppermute(tail, 'seq', [(i, i + FAR + 1) for i in range(n_seq - FAR -...  6.81 us
    pallas_call x1, Pallas kernels, body(): pl.pallas_call(make_last_kernel(PLANES, n_head), in_specs=[flat] + [wide]...  4.83 us
    pallas_call x1, Pallas kernels, body(): pl.pallas_call(own_attend_kernel, in_specs=[flat] + [far_off] * 3, out_sp...  3.31 us
  transfers between devices with their start and end apart: 19, of which 7 were waited for; matrix products, arithmetic and copies ran while one was open for 0% of the time, Pallas kernels for 40%

profile of v6, /device:TPU:25, one launch (start us, length us, event | category | flops | bytes accessed | tf_op | source)
XLA Modules:
  0.0 80.9 jit_solution(861855686716626059)
XLA Ops:
  0.0 2.6 %shard_map.73 = bf16[192,1024]{1,0:T(8,128)(2,1)} custom-call(bf16[768,1024]{1,0:T(8,128)(2,1)} %refs_6_.1, bf16[1024]{0:T(1024)(128)(2,1)} %gain_hbm), custom_call_target="tpu_custom_call" | custom-call | flops 600000000 | bytes 1800000 | tf_op jit(solution)/shard_map/pallas_call | solution.py:425
  2.6 0.0 copy-start.10
  2.6 0.0 copy-start.9
  2.6 1.3 %collective-permute-start.2 = (bf16[256,1024]{1,0:T(8,128)(2,1)S(1)}, bf16[256,1024]{1,0:T(8,128)(2,1)S(1)}, u32[]{:S(2)}, u32[]{:S(2)}) collective-permute-start(bf16[256,1024]{1,0:T(8,128)(2,1)S(1)} %copy-done.2), channel_id=1, source_target_pairs={{0,2},{1,3},{2,0},{3,1},{4,6},{5,7},{6,4},{7,5},{8,10},{9,11},{10,... | collective-permute-start | bytes 1572872 | tf_op jit(solution)/shard_map/ppermute | solution.py:394
  3.9 1.3 %collective-permute-start.1 = (bf16[192,1024]{1,0:T(8,128)(2,1)}, bf16[192,1024]{1,0:T(8,128)(2,1)S(1)}, u32[]{:S(2)}, u32[]{:S(2)}) collective-permute-start(bf16[192,1024]{1,0:T(8,128)(2,1)} %shard_map.73), channel_id=1, source_target_pairs={{0,8},{4,12},{8,16},{12,20},{16,24},{20,28},{1,9},{5,13},{9,17},{1... | collective-permute-start | bytes 1179656 | tf_op jit(solution)/shard_map/ppermute | solution.py:441
  5.2 6.8 %shard_map.74 = (bf16[768,256]{1,0:T(8,128)(2,1)}, bf16[1536,256]{1,0:T(8,128)(2,1)}, bf16[768,256]{1,0:T(8,128)(2,1)}, bf16[256,768]{1,0:T(8,128)(2,1)}, bf16[2,128,256]{2,1,0:T(8,128)(2,1)}) custom-call(bf16[768,1024]{1,0:T(8,128)(2,1)} %refs_6_.1, bf16[1024]{0:T(1024)(128)(2,1)} %gain_hbm, bf16[4,1024,256]{2,1,0:T(8,128)(2,1)} %refs_4_.3), custom_call_target="tpu_custom_call" | custom-call | flops 1200000000 | bytes 3600000 | tf_op jit(solution)/shard_map/pallas_call | solution.py:443
  12.1 1.3 %collective-permute-start.5 = (bf16[768,256]{1,0:T(8,128)(2,1)}, bf16[768,256]{1,0:T(8,128)(2,1)S(1)}, u32[]{:S(2)}, u32[]{:S(2)}) collective-permute-start(bf16[768,256]{1,0:T(8,128)(2,1)} %get-tuple-element.58.query_hbm.refs_5_), channel_id=1, source_target_pairs={{0,4},{4,0},{8,12},{12,8},{16,20},{20,16},{24,28},{28,24},{1,5},{5... | collective-permute-start | bytes 1179656 | tf_op jit(solution)/shard_map/ppermute | solution.py:394
  13.3 2.3 %collective-permute-done.1.refs_0_ = bf16[192,1024]{1,0:T(8,128)(2,1)S(1)} collective-permute-done((bf16[192,1024]{1,0:T(8,128)(2,1)}, bf16[192,1024]{1,0:T(8,128)(2,1)S(1)}, u32[]{:S(2)}, u32[]{:S(2)}) %collective-permute-start.1) | collective-permute-done | bytes 393248 | tf_op jit(solution)/shard_map/ppermute | solution.py:441
  15.7 1.0 %collective-permute-start.4 = (bf16[192,1024]{1,0:T(8,128)(2,1)S(1)}, bf16[192,1024]{1,0:T(8,128)(2,1)S(1)}, u32[]{:S(2)}, u32[]{:S(2)}) collective-permute-start(bf16[192,1024]{1,0:T(8,128)(2,1)S(1)} %collective-permute-done.1.refs_0_), channel_id=1, source_target_pairs={{0,2},{1,3},{2,0},{3,1},{4,6},{5,7},{6,4},{7,5},{8,10},{9,11},{10,... | collective-permute-start | bytes 1179656 | tf_op jit(solution)/shard_map/ppermute | solution.py:394
  16.7 1.3 %collective-permute-start.3 = (bf16[192,1024]{1,0:T(8,128)(2,1)S(1)}, bf16[192,1024]{1,0:T(8,128)(2,1)S(1)}, u32[]{:S(2)}, u32[]{:S(2)}) collective-permute-start(bf16[192,1024]{1,0:T(8,128)(2,1)S(1)} %collective-permute-done.1.refs_0_), channel_id=1, source_target_pairs={{8,16},{12,20},{16,24},{20,28},{9,17},{13,21},{17,25},{21,29},{10,... | collective-permute-start | bytes 1179656 | tf_op jit(solution)/shard_map/ppermute | solution.py:463
  18.0 0.1 copy.8
  18.1 0.1 pad_add_fusion.told_ref
  18.2 1.2 %collective-permute-start = (s32[6,17]{1,0:T(8,128)S(1)}, s32[6,17]{1,0:T(8,128)S(1)}, u32[]{:S(2)}, u32[]{:S(2)}) collective-permute-start(s32[6,17]{1,0:T(8,128)S(1)} %pad_add_fusion.told_ref), channel_id=1, source_target_pairs={{0,4},{4,0},{8,12},{12,8},{16,20},{20,16},{24,28},{28,24},{1,5},{5... | collective-permute-start | bytes 1232 | tf_op jit(solution)/shard_map/ppermute | solution.py:394
  19.4 2.7 %collective-permute-done.told_x_ref = s32[6,17]{1,0:T(8,128)S(1)} collective-permute-done((s32[6,17]{1,0:T(8,128)S(1)}, s32[6,17]{1,0:T(8,128)S(1)}, u32[]{:S(2)}, u32[]{:S(2)}) %collective-permute-start) | collective-permute-done | bytes 440 | tf_op jit(solution)/shard_map/ppermute | solution.py:394
  22.1 1.9 %collective-permute-start.8 = (bf16[192,1024]{1,0:T(8,128)(2,1)S(1)}, bf16[192,1024]{1,0:T(8,128)(2,1)S(1)}, u32[]{:S(2)}, u32[]{:S(2)}) collective-permute-start(bf16[192,1024]{1,0:T(8,128)(2,1)S(1)} %collective-permute-done.1.refs_0_), channel_id=1, source_target_pairs={{0,1},{1,0},{2,3},{3,2},{4,5},{5,4},{6,7},{7,6},{8,9},{9,8},{10,11... | collective-permute-start | bytes 1179656 | tf_op jit(solution)/shard_map/ppermute | solution.py:394
  24.0 1.0 %copy-done.3 = bf16[768,256]{1,0:T(8,128)(2,1)S(1)} copy-done((bf16[768,256]{1,0:T(8,128)(2,1)S(1)}, bf16[768,256]{1,0:T(8,128)(2,1)}, u32[]{:S(2)}) %copy-start.3) | copy-done | bytes 393240
  25.0 1.0 %copy-done.5 = bf16[256,768]{1,0:T(8,128)(2,1)S(1)} copy-done((bf16[256,768]{1,0:T(8,128)(2,1)S(1)}, bf16[256,768]{1,0:T(8,128)(2,1)}, u32[]{:S(2)}) %copy-start.5) | copy-done | bytes 393240
  26.0 3.3 %shard_map.75.refs_9_ = f32[768,256]{1,0:T(8,128)S(1)} custom-call(s32[6,17]{1,0:T(8,128)S(1)} %pad_add_fusion.told_ref, bf16[768,256]{1,0:T(8,128)(2,1)S(1)} %copy-done.3, bf16[256,768]{1,0:T(8,128)(2,1)S(1)} %copy-done.5, bf16[1536,256]{1,0:T(8,128)(2,1)} %get-tuple-element.65.both_hbm.refs_8_), custom_call_target="tpu_custom_call" | custom-call | flops 1200000000 | bytes 3600000 | tf_op jit(solution)/shard_map/pallas_call | solution.py:468
  29.3 0.0 collective-permute-done.4.refs_2_
  29.3 0.0 collective-permute-done.3.refs_0_
  29.3 0.8 %collective-permute-start.9 = (bf16[192,1024]{1,0:T(8,128)(2,1)S(1)}, bf16[192,1024]{1,0:T(8,128)(2,1)S(1)}, u32[]{:S(2)}, u32[]{:S(2)}) collective-permute-start(bf16[192,1024]{1,0:T(8,128)(2,1)S(1)} %collective-permute-done.4.refs_2_), channel_id=1, source_target_pairs={{0,1},{1,0},{2,3},{3,2},{4,5},{5,4},{6,7},{7,6},{8,9},{9,8},{10,11... | collective-permute-start | bytes 1179656 | tf_op jit(solution)/shard_map/ppermute | solution.py:394
  30.1 0.4 collective-permute-start.7
  30.6 1.3 %collective-permute-start.13 = (bf16[1536,256]{1,0:T(8,128)(2,1)}, bf16[1536,256]{1,0:T(8,128)(2,1)S(1)}, u32[]{:S(2)}, u32[]{:S(2)}) collective-permute-start(bf16[1536,256]{1,0:T(8,128)(2,1)} %get-tuple-element.65.both_hbm.refs_8_), channel_id=1, source_target_pairs={{4,24},{5,25},{6,26},{7,27}} | collective-permute-start | bytes 2359304 | tf_op jit(solution)/shard_map/ppermute | solution.py:484
  31.8 0.3 collective-permute-start.6
  32.2 0.0 collective-permute-done.8.refs_1_
  32.2 0.0 collective-permute-done.9.refs_3_
  32.2 10.0 %shard_map.76 = (f32[768,256]{1,0:T(8,128)S(1)}, f32[768,256]{1,0:T(8,128)S(1)}) custom-call(s32[6,17]{1,0:T(8,128)S(1)} %pad_add_fusion.told_ref, s32[6,17]{1,0:T(8,128)S(1)} %collective-permute-done.told_x_ref, bf16[192,1024]{1,0:T(8,128)(2,1)S(1)} %collective-permute-done.1.refs_0_, bf16[192,1024]{1,0:T(8,128)(2,1)S(1)} %collective-permute-done.8.refs_1_, ...), custom_call_target="tpu_custom_call" | custom-call | flops 15000000 | bytes 45000 | tf_op jit(solution)/shard_map/pallas_call | solution.py:486
  42.3 0.0 copy-start.7
  42.3 0.0 copy-start.8
  42.3 0.3 collective-permute-start.10
  42.6 0.0 collective-permute-done.6.refs_1_
  42.6 1.5 %collective-permute-done.10.refs_3_ = bf16[192,1024]{1,0:T(8,128)(2,1)S(1)} collective-permute-done((bf16[192,1024]{1,0:T(8,128)(2,1)S(1)}, bf16[192,1024]{1,0:T(8,128)(2,1)S(1)}, u32[]{:S(2)}, u32[]{:S(2)}) %collective-permute-start.10) | collective-permute-done | bytes 393248 | tf_op jit(solution)/shard_map/ppermute | solution.py:394
  44.1 4.8 %shard_map.77 = (bf16[768,256]{1,0:T(8,128)(2,1)S(1)}, bf16[256,768]{1,0:T(8,128)(2,1)S(1)}, bf16[768,256]{1,0:T(8,128)(2,1)S(1)}) custom-call(s32[6,17]{1,0:T(8,128)S(1)} %collective-permute-done.told_x_ref, bf16[192,1024]{1,0:T(8,128)(2,1)S(1)} %collective-permute-done.3.refs_0_, bf16[192,1024]{1,0:T(8,128)(2,1)S(1)} %collective-permute-done.6.refs_1_, ...), custom_call_target="tpu_custom_call" | custom-call | flops 15000000 | bytes 45000 | tf_op jit(solution)/shard_map/pallas_call | solution.py:504
  48.9 0.3 collective-permute-start.14
  49.2 0.3 collective-permute-start.15
  49.5 1.3 %collective-permute-start.12 = (bf16[2,128,256]{2,1,0:T(8,128)(2,1)S(1)}, bf16[2,128,256]{2,1,0:T(8,128)(2,1)S(1)}, u32[]{:S(2)}, u32[]{:S(2)}) collective-permute-start(bf16[2,128,256]{2,1,0:T(8,128)(2,1)S(1)} %copy-done.11), channel_id=1, source_target_pairs={{0,24},{4,28},{1,25},{5,29},{2,26},{6,30},{3,27},{7,31}} | collective-permute-start | bytes 393224 | tf_op jit(solution)/shard_map/ppermute | solution.py:467
  50.8 6.8 %collective-permute-done.12.tail_ref = bf16[2,128,256]{2,1,0:T(8,128)(2,1)S(1)} collective-permute-done((bf16[2,128,256]{2,1,0:T(8,128)(2,1)S(1)}, bf16[2,128,256]{2,1,0:T(8,128)(2,1)S(1)}, u32[]{:S(2)}, u32[]{:S(2)}) %collective-permute-start.12) | collective-permute-done | bytes 131104 | tf_op jit(solution)/shard_map/ppermute | solution.py:467
  57.6 7.1 %shard_map.78 = (f32[768,256]{1,0:T(8,128)S(1)}, f32[768,256]{1,0:T(8,128)S(1)}) custom-call(s32[6,17]{1,0:T(8,128)S(1)} %pad_add_fusion.told_ref, bf16[768,256]{1,0:T(8,128)(2,1)S(1)} %copy-done.4, bf16[256,768]{1,0:T(8,128)(2,1)S(1)} %get-tuple-element.71.keys_t_ref, bf16[768,256]{1,0:T(8,128)(2,1)S(1)} %get-tuple-element.72.values_ref, ...), custom_call_target="tpu_custom_call" | custom-call | flops 2700000000 | bytes 8100000 | tf_op jit(solution)/shard_map/pallas_call | solution.py:518
  64.8 0.0 copy-start.1
  64.8 0.5 shard_map.79.refs_0_
  65.4 1.6 %collective-permute-start.17 = (bf16[768,256]{1,0:T(8,128)(2,1)S(1)}, bf16[768,256]{1,0:T(8,128)(2,1)S(1)}, u32[]{:S(2)}, u32[]{:S(2)}) collective-permute-start(bf16[768,256]{1,0:T(8,128)(2,1)S(1)} %shard_map.79.refs_0_), channel_id=1, source_target_pairs={{0,1},{1,0},{2,3},{3,2},{4,5},{5,4},{6,7},{7,6},{8,9},{9,8},{10,11... | collective-permute-start | bytes 1179656 | tf_op jit(solution)/shard_map/ppermute | solution.py:394
  66.9 1.1 %collective-permute-start.16 = (bf16[768,256]{1,0:T(8,128)(2,1)S(1)}, bf16[768,256]{1,0:T(8,128)(2,1)S(1)}, u32[]{:S(2)}, u32[]{:S(2)}) collective-permute-start(bf16[768,256]{1,0:T(8,128)(2,1)S(1)} %shard_map.79.refs_0_), channel_id=1, source_target_pairs={{0,2},{1,3},{2,0},{3,1},{4,6},{5,7},{6,4},{7,5},{8,10},{9,11},{10,... | collective-permute-start | bytes 1179656 | tf_op jit(solution)/shard_map/ppermute | solution.py:394
  68.0 0.3 collective-permute-done.17.refs_1_
  68.3 0.5 shard_map.80
  68.8 8.8 %collective-permute-done.16.refs_0_ = bf16[768,256]{1,0:T(8,128)(2,1)S(1)} collective-permute-done((bf16[768,256]{1,0:T(8,128)(2,1)S(1)}, bf16[768,256]{1,0:T(8,128)(2,1)S(1)}, u32[]{:S(2)}, u32[]{:S(2)}) %collective-permute-start.16) | collective-permute-done | bytes 393248 | tf_op jit(solution)/shard_map/ppermute | solution.py:394
  77.6 0.8 %collective-permute-start.18 = (bf16[768,256]{1,0:T(8,128)(2,1)S(1)}, bf16[768,256]{1,0:T(8,128)(2,1)S(1)}, u32[]{:S(2)}, u32[]{:S(2)}) collective-permute-start(bf16[768,256]{1,0:T(8,128)(2,1)S(1)} %collective-permute-done.16.refs_0_), channel_id=1, source_target_pairs={{0,1},{1,0},{2,3},{3,2},{4,5},{5,4},{6,7},{7,6},{8,9},{9,8},{10,11... | collective-permute-start | bytes 1179656 | tf_op jit(solution)/shard_map/ppermute | solution.py:394
  78.5 1.3 %collective-permute-done.18.refs_1_ = bf16[768,256]{1,0:T(8,128)(2,1)S(1)} collective-permute-done((bf16[768,256]{1,0:T(8,128)(2,1)S(1)}, bf16[768,256]{1,0:T(8,128)(2,1)S(1)}, u32[]{:S(2)}, u32[]{:S(2)}) %collective-permute-start.18) | collective-permute-done | bytes 393248 | tf_op jit(solution)/shard_map/ppermute | solution.py:394
  79.8 1.1 %shard_map.81 = bf16[768,256]{1,0:T(8,128)(2,1)} custom-call(bf16[768,256]{1,0:T(8,128)(2,1)S(1)} %collective-permute-done.16.refs_0_, bf16[768,256]{1,0:T(8,128)(2,1)S(1)} %collective-permute-done.18.refs_1_, bf16[512,256]{1,0:T(8,128)(2,1)S(1)} %get-tuple-element.89.refs_2_, f32[768,256]{1,0:T(8,128)S(1)} %get-tuple-element.90.refs_3_), custom_call_target="tpu_custom_call" | custom-call | flops 600000000 | bytes 1800000 | tf_op jit(solution)/shard_map/pallas_call | solution.py:555
  (25 shorter events, 0.1 us)
Async XLA Ops:
  0.0 2.6 %copy-start.2 = (bf16[256,1024]{1,0:T(8,128)(2,1)S(1)}, bf16[256,1024]{1,0:T(8,128)(2,1)}, u32[]{:S(2)}) copy-start(bf16[256,1024]{1,0:T(8,128)(2,1)} %refs_2_) | copy-start | bytes 1572868
  2.6 15.4 %copy-start.10 = (s32[6]{0:T(128)S(1)}, s32[6]{0:T(128)}, u32[]{:S(2)}) copy-start(s32[6]{0:T(128)} %param.13) | copy-start | bytes 76
  2.6 15.5 %copy-start.9 = (s32[6,16]{1,0:T(8,128)S(1)}, s32[6,16]{1,0:T(8,128)}, u32[]{:S(2)}) copy-start(s32[6,16]{1,0:T(8,128)} %param.12) | copy-start | bytes 1156
  2.6 13.1 %collective-permute-start.2 = (bf16[256,1024]{1,0:T(8,128)(2,1)S(1)}, bf16[256,1024]{1,0:T(8,128)(2,1)S(1)}, u32[]{:S(2)}, u32[]{:S(2)}) collective-permute-start(bf16[256,1024]{1,0:T(8,128)(2,1)S(1)} %copy-done.2), channel_id=1, source_target_pairs={{0,2},{1,3},{2,0},{3,1},{4,6},{5,7},{6,4},{7,5},{8,10},{9,11},{10,... | collective-permute-start | bytes 1572872 | tf_op jit(solution)/shard_map/ppermute | solution.py:394
  3.9 11.8 %collective-permute-start.1 = (bf16[192,1024]{1,0:T(8,128)(2,1)}, bf16[192,1024]{1,0:T(8,128)(2,1)S(1)}, u32[]{:S(2)}, u32[]{:S(2)}) collective-permute-start(bf16[192,1024]{1,0:T(8,128)(2,1)} %shard_map.73), channel_id=1, source_target_pairs={{0,8},{4,12},{8,16},{12,20},{16,24},{20,28},{1,9},{5,13},{9,17},{1... | collective-permute-start | bytes 1179656 | tf_op jit(solution)/shard_map/ppermute | solution.py:441
  12.1 17.2 %collective-permute-start.5 = (bf16[768,256]{1,0:T(8,128)(2,1)}, bf16[768,256]{1,0:T(8,128)(2,1)S(1)}, u32[]{:S(2)}, u32[]{:S(2)}) collective-permute-start(bf16[768,256]{1,0:T(8,128)(2,1)} %get-tuple-element.58.query_hbm.refs_5_), channel_id=1, source_target_pairs={{0,4},{4,0},{8,12},{12,8},{16,20},{20,16},{24,28},{28,24},{1,5},{5... | collective-permute-start | bytes 1179656 | tf_op jit(solution)/shard_map/ppermute | solution.py:394
  15.7 13.6 %collective-permute-start.4 = (bf16[192,1024]{1,0:T(8,128)(2,1)S(1)}, bf16[192,1024]{1,0:T(8,128)(2,1)S(1)}, u32[]{:S(2)}, u32[]{:S(2)}) collective-permute-start(bf16[192,1024]{1,0:T(8,128)(2,1)S(1)} %collective-permute-done.1.refs_0_), channel_id=1, source_target_pairs={{0,2},{1,3},{2,0},{3,1},{4,6},{5,7},{6,4},{7,5},{8,10},{9,11},{10,... | collective-permute-start | bytes 1179656 | tf_op jit(solution)/shard_map/ppermute | solution.py:394
  16.7 12.6 %collective-permute-start.3 = (bf16[192,1024]{1,0:T(8,128)(2,1)S(1)}, bf16[192,1024]{1,0:T(8,128)(2,1)S(1)}, u32[]{:S(2)}, u32[]{:S(2)}) collective-permute-start(bf16[192,1024]{1,0:T(8,128)(2,1)S(1)} %collective-permute-done.1.refs_0_), channel_id=1, source_target_pairs={{8,16},{12,20},{16,24},{20,28},{9,17},{13,21},{17,25},{21,29},{10,... | collective-permute-start | bytes 1179656 | tf_op jit(solution)/shard_map/ppermute | solution.py:463
  18.2 3.9 %collective-permute-start = (s32[6,17]{1,0:T(8,128)S(1)}, s32[6,17]{1,0:T(8,128)S(1)}, u32[]{:S(2)}, u32[]{:S(2)}) collective-permute-start(s32[6,17]{1,0:T(8,128)S(1)} %pad_add_fusion.told_ref), channel_id=1, source_target_pairs={{0,4},{4,0},{8,12},{12,8},{16,20},{20,16},{24,28},{28,24},{1,5},{5... | collective-permute-start | bytes 1232 | tf_op jit(solution)/shard_map/ppermute | solution.py:394
  22.1 10.1 %collective-permute-start.8 = (bf16[192,1024]{1,0:T(8,128)(2,1)S(1)}, bf16[192,1024]{1,0:T(8,128)(2,1)S(1)}, u32[]{:S(2)}, u32[]{:S(2)}) collective-permute-start(bf16[192,1024]{1,0:T(8,128)(2,1)S(1)} %collective-permute-done.1.refs_0_), channel_id=1, source_target_pairs={{0,1},{1,0},{2,3},{3,2},{4,5},{5,4},{6,7},{7,6},{8,9},{9,8},{10,11... | collective-permute-start | bytes 1179656 | tf_op jit(solution)/shard_map/ppermute | solution.py:394
  24.0 1.0 %copy-start.3 = (bf16[768,256]{1,0:T(8,128)(2,1)S(1)}, bf16[768,256]{1,0:T(8,128)(2,1)}, u32[]{:S(2)}) copy-start(bf16[768,256]{1,0:T(8,128)(2,1)} %get-tuple-element.58.query_hbm.refs_5_) | copy-start | bytes 1179652
  25.0 1.0 %copy-start.5 = (bf16[256,768]{1,0:T(8,128)(2,1)S(1)}, bf16[256,768]{1,0:T(8,128)(2,1)}, u32[]{:S(2)}) copy-start(bf16[256,768]{1,0:T(8,128)(2,1)} %get-tuple-element.59.keys_t_hbm.refs_7_) | copy-start | bytes 1179652
  25.9 6.3 %copy-start = (bf16[4,1024,256]{2,1,0:T(8,128)(2,1)S(1)}, bf16[4,1024,256]{2,1,0:T(8,128)(2,1)}, u32[]{:S(2)}) copy-start(bf16[4,1024,256]{2,1,0:T(8,128)(2,1)} %refs_4_.3) | copy-start | bytes 6291460
  26.0 6.3 %copy-start.4 = (bf16[768,256]{1,0:T(8,128)(2,1)S(1)}, bf16[768,256]{1,0:T(8,128)(2,1)}, u32[]{:S(2)}) copy-start(bf16[768,256]{1,0:T(8,128)(2,1)} %get-tuple-element.58.query_hbm.refs_5_) | copy-start | bytes 1179652
  26.0 6.3 %copy-start.6 = (bf16[256,768]{1,0:T(8,128)(2,1)S(1)}, bf16[256,768]{1,0:T(8,128)(2,1)}, u32[]{:S(2)}) copy-start(bf16[256,768]{1,0:T(8,128)(2,1)} %get-tuple-element.59.keys_t_hbm.refs_7_) | copy-start | bytes 1179652
  29.3 2.9 %collective-permute-start.9 = (bf16[192,1024]{1,0:T(8,128)(2,1)S(1)}, bf16[192,1024]{1,0:T(8,128)(2,1)S(1)}, u32[]{:S(2)}, u32[]{:S(2)}) collective-permute-start(bf16[192,1024]{1,0:T(8,128)(2,1)S(1)} %collective-permute-done.4.refs_2_), channel_id=1, source_target_pairs={{0,1},{1,0},{2,3},{3,2},{4,5},{5,4},{6,7},{7,6},{8,9},{9,8},{10,11... | collective-permute-start | bytes 1179656 | tf_op jit(solution)/shard_map/ppermute | solution.py:394
  30.1 12.1 %collective-permute-start.7 = (bf16[192,1024]{1,0:T(8,128)(2,1)S(1)}, bf16[192,1024]{1,0:T(8,128)(2,1)S(1)}, u32[]{:S(2)}, u32[]{:S(2)}) collective-permute-start(bf16[192,1024]{1,0:T(8,128)(2,1)S(1)} %collective-permute-done.3.refs_0_), channel_id=1, source_target_pairs={{0,2},{1,3},{2,0},{3,1},{4,6},{5,7},{6,4},{7,5},{8,10},{9,11},{10,... | collective-permute-start | bytes 1179656 | tf_op jit(solution)/shard_map/ppermute | solution.py:394
  30.6 27.1 %collective-permute-start.13 = (bf16[1536,256]{1,0:T(8,128)(2,1)}, bf16[1536,256]{1,0:T(8,128)(2,1)S(1)}, u32[]{:S(2)}, u32[]{:S(2)}) collective-permute-start(bf16[1536,256]{1,0:T(8,128)(2,1)} %get-tuple-element.65.both_hbm.refs_8_), channel_id=1, source_target_pairs={{4,24},{5,25},{6,26},{7,27}} | collective-permute-start | bytes 2359304 | tf_op jit(solution)/shard_map/ppermute | solution.py:484
  31.8 10.8 %collective-permute-start.6 = (bf16[192,1024]{1,0:T(8,128)(2,1)S(1)}, bf16[192,1024]{1,0:T(8,128)(2,1)S(1)}, u32[]{:S(2)}, u32[]{:S(2)}) collective-permute-start(bf16[192,1024]{1,0:T(8,128)(2,1)S(1)} %collective-permute-done.3.refs_0_), channel_id=1, source_target_pairs={{0,1},{1,0},{2,3},{3,2},{4,5},{5,4},{6,7},{7,6},{8,9},{9,8},{10,11... | collective-permute-start | bytes 1179656 | tf_op jit(solution)/shard_map/ppermute | solution.py:394
  42.3 7.2 %copy-start.11 = (bf16[2,128,256]{2,1,0:T(8,128)(2,1)S(1)}, bf16[2,128,256]{2,1,0:T(8,128)(2,1)}, u32[]{:S(2)}) copy-start(bf16[2,128,256]{2,1,0:T(8,128)(2,1)} %get-tuple-element.73) | copy-start | bytes 393220
  42.3 15.3 %copy-start.7 = (bf16[256]{0:T(256)(128)(2,1)S(1)}, bf16[256]{0:T(256)(128)(2,1)}, u32[]{:S(2)}) copy-start(bf16[256]{0:T(256)(128)(2,1)} %gain_ref.3) | copy-start | bytes 1540
  42.3 15.3 %copy-start.8 = (bf16[768,256]{1,0:T(8,128)(2,1)S(1)}, bf16[768,256]{1,0:T(8,128)(2,1)}, u32[]{:S(2)}) copy-start(bf16[768,256]{1,0:T(8,128)(2,1)} %get-tuple-element.75.gate_hbm) | copy-start | bytes 1179652
  42.3 1.8 %collective-permute-start.10 = (bf16[192,1024]{1,0:T(8,128)(2,1)S(1)}, bf16[192,1024]{1,0:T(8,128)(2,1)S(1)}, u32[]{:S(2)}, u32[]{:S(2)}) collective-permute-start(bf16[192,1024]{1,0:T(8,128)(2,1)S(1)} %collective-permute-done.7.refs_2_), channel_id=1, source_target_pairs={{0,1},{1,0},{2,3},{3,2},{4,5},{5,4},{6,7},{7,6},{8,9},{9,8},{10,11... | collective-permute-start | bytes 1179656 | tf_op jit(solution)/shard_map/ppermute | solution.py:394
  48.9 15.9 %collective-permute-start.14 = (bf16[256,1024]{1,0:T(8,128)(2,1)S(1)}, bf16[256,1024]{1,0:T(8,128)(2,1)S(1)}, u32[]{:S(2)}, u32[]{:S(2)}) collective-permute-start(bf16[256,1024]{1,0:T(8,128)(2,1)S(1)} %copy-done.2), channel_id=1, source_target_pairs={{0,1},{1,0},{2,3},{3,2},{4,5},{5,4},{6,7},{7,6},{8,9},{9,8},{10,11... | collective-permute-start | bytes 1572872 | tf_op jit(solution)/shard_map/ppermute | solution.py:394
  49.2 15.6 %collective-permute-start.15 = (bf16[256,1024]{1,0:T(8,128)(2,1)S(1)}, bf16[256,1024]{1,0:T(8,128)(2,1)S(1)}, u32[]{:S(2)}, u32[]{:S(2)}) collective-permute-start(bf16[256,1024]{1,0:T(8,128)(2,1)S(1)} %collective-permute-done.2.refs_4_), channel_id=1, source_target_pairs={{0,1},{1,0},{2,3},{3,2},{4,5},{5,4},{6,7},{7,6},{8,9},{9,8},{10,11... | collective-permute-start | bytes 1572872 | tf_op jit(solution)/shard_map/ppermute | solution.py:394
  49.5 15.3 %collective-permute-start.11 = (bf16[768,256]{1,0:T(8,128)(2,1)S(1)}, bf16[768,256]{1,0:T(8,128)(2,1)S(1)}, u32[]{:S(2)}, u32[]{:S(2)}) collective-permute-start(bf16[768,256]{1,0:T(8,128)(2,1)S(1)} %get-tuple-element.70), channel_id=1, source_target_pairs={{0,4},{4,0},{8,12},{12,8},{16,20},{20,16},{24,28},{28,24},{1,5},{5... | collective-permute-start | bytes 1179656 | tf_op jit(solution)/shard_map/ppermute | solution.py:394
  49.5 8.1 %collective-permute-start.12 = (bf16[2,128,256]{2,1,0:T(8,128)(2,1)S(1)}, bf16[2,128,256]{2,1,0:T(8,128)(2,1)S(1)}, u32[]{:S(2)}, u32[]{:S(2)}) collective-permute-start(bf16[2,128,256]{2,1,0:T(8,128)(2,1)S(1)} %copy-done.11), channel_id=1, source_target_pairs={{0,24},{4,28},{1,25},{5,29},{2,26},{6,30},{3,27},{7,31}} | collective-permute-start | bytes 393224 | tf_op jit(solution)/shard_map/ppermute | solution.py:467
  64.8 3.5 %copy-start.1 = (bf16[768,1024]{1,0:T(8,128)(2,1)S(1)}, bf16[768,1024]{1,0:T(8,128)(2,1)}, u32[]{:S(2)}) copy-start(bf16[768,1024]{1,0:T(8,128)(2,1)} %refs_6_.1) | copy-start | bytes 4718596
  65.4 2.9 %collective-permute-start.17 = (bf16[768,256]{1,0:T(8,128)(2,1)S(1)}, bf16[768,256]{1,0:T(8,128)(2,1)S(1)}, u32[]{:S(2)}, u32[]{:S(2)}) collective-permute-start(bf16[768,256]{1,0:T(8,128)(2,1)S(1)} %shard_map.79.refs_0_), channel_id=1, source_target_pairs={{0,1},{1,0},{2,3},{3,2},{4,5},{5,4},{6,7},{7,6},{8,9},{9,8},{10,11... | collective-permute-start | bytes 1179656 | tf_op jit(solution)/shard_map/ppermute | solution.py:394
  66.9 10.7 %collective-permute-start.16 = (bf16[768,256]{1,0:T(8,128)(2,1)S(1)}, bf16[768,256]{1,0:T(8,128)(2,1)S(1)}, u32[]{:S(2)}, u32[]{:S(2)}) collective-permute-start(bf16[768,256]{1,0:T(8,128)(2,1)S(1)} %shard_map.79.refs_0_), channel_id=1, source_target_pairs={{0,2},{1,3},{2,0},{3,1},{4,6},{5,7},{6,4},{7,5},{8,10},{9,11},{10,... | collective-permute-start | bytes 1179656 | tf_op jit(solution)/shard_map/ppermute | solution.py:394
  77.6 2.2 %collective-permute-start.18 = (bf16[768,256]{1,0:T(8,128)(2,1)S(1)}, bf16[768,256]{1,0:T(8,128)(2,1)S(1)}, u32[]{:S(2)}, u32[]{:S(2)}) collective-permute-start(bf16[768,256]{1,0:T(8,128)(2,1)S(1)} %collective-permute-done.16.refs_0_), channel_id=1, source_target_pairs={{0,1},{1,0},{2,3},{3,2},{4,5},{5,4},{6,7},{7,6},{8,9},{9,8},{10,11... | collective-permute-start | bytes 1179656 | tf_op jit(solution)/shard_map/ppermute | solution.py:394

commit v7 on v6

--- a/solution.py
+++ b/solution.py
@@ -298,15 +298,12 @@
 
 def make_own_last_kernel(back):
     def kernel(
-        told_ref, query_hbm, keys_t_ref, values_ref, tail_ref, far_hbm, before_hbm, gate_hbm, gain_ref,
-        sums_ref, scale_ref, query_ref, gate_ref, far_ref, far_t_ref, live_ref, sems, far_sems,
+        told_ref, query_hbm, keys_t_ref, values_ref, before_hbm, gate_hbm, gain_ref,
+        sums_ref, scale_ref, query_ref, gate_ref, live_ref, sems,
     ):
-        rows, cols = query_ref.shape
-        blocks = rows // BLK
-        here = lax.axis_index("seq")
-        source = here - 2 * back
+        blocks = query_ref.shape[0] // BLK
+        source = lax.axis_index("seq") - 2 * back
         copies = fetch([(query_hbm, query_ref), (before_hbm, sums_ref), (gate_hbm, gate_ref)], sems)
-        far_copies = fetch([(far_hbm, far_ref)], far_sems)
         mark(live_ref, told_ref, source * blocks, blocks, 0)
         wait(copies)
 
@@ -314,38 +311,51 @@
         def _():
             attend_all(query_ref, sums_ref, keys_t_ref, values_ref, live_ref, 0, blocks)
 
-        wait(far_copies)
-        far = here - FAR
-
-        @pl.when((far >= 0) & (here % 2 == 0))
-        def _():
-            far_t_ref[...] = far_ref[0:rows, :].astype(jnp.float32).T.astype(jnp.bfloat16)
-            mark(live_ref, told_ref, far * blocks, blocks, 0)
-            attend_all(query_ref, sums_ref, far_t_ref, far_ref.at[pl.ds(rows, rows)], live_ref, 0, blocks)
-
-        farthest = here - FAR - 1
-
-        @pl.when(farthest >= 0)
-        def _():
-            mark(live_ref, told_ref, farthest * blocks + blocks - 1, 1, 0)
-            for h in range(cols // DH):
-                at = pl.ds(h * DH, DH)
-                scores = lax.dot_general(
-                    query_ref[0:BLK, at], tail_ref[0, :, at], NT, preferred_element_type=jnp.float32
-                )
-                weights = tile(scores, live_ref[0]).astype(jnp.bfloat16)
-                sums_ref[0:BLK, at] += jnp.dot(
-                    weights, tail_ref[1, :, at], preferred_element_type=jnp.float32
-                )
-
         scale_ref[...] = gain_ref[...].reshape(1, -1).astype(jnp.float32) * gate_ref[...].astype(
             jnp.float32
         )
+
+    return kernel
+
+
+def far_kernel(
+    told_ref, query_hbm, tail_ref, far_hbm, unused, sums_ref, query_ref, far_ref, far_t_ref, live_ref, sems, far_sems
+):
+    rows, cols = query_ref.shape
+    blocks = rows // BLK
+    here = lax.axis_index("seq")
+    far = here - FAR
+    farthest = here - FAR - 1
+
+    @pl.when(far >= 0)
+    def _():
+        copies = fetch([(query_hbm, query_ref)], sems)
+        far_copies = fetch([(far_hbm, far_ref)], far_sems)
+        mark(live_ref, told_ref, far * blocks, blocks, 0)
+        wait(copies)
+        wait(far_copies)
+
+        @pl.when(here % 2 == 0)
+        def _():
+            far_t_ref[...] = far_ref[0:rows, :].astype(jnp.float32).T.astype(jnp.bfloat16)
+            attend_all(query_ref, sums_ref, far_t_ref, far_ref.at[pl.ds(rows, rows)], live_ref, 0, blocks)
+
+    @pl.when(farthest >= 0)
+    def _():
+        mark(live_ref, told_ref, farthest * blocks + blocks - 1, 1, 0)
         for h in range(cols // DH):
             at = pl.ds(h * DH, DH)
-            sums_ref[:, at] = centred(sums_ref[:, at])
-
-    return kernel
+            scores = lax.dot_general(
+                query_ref[0:BLK, at], tail_ref[0, :, at], NT, preferred_element_type=jnp.float32
+            )
+            weights = tile(scores, live_ref[0]).astype(jnp.bfloat16)
+            sums_ref[0:BLK, at] += jnp.dot(
+                weights, tail_ref[1, :, at], preferred_element_type=jnp.float32
+            )
+
+    for h in range(cols // DH):
+        at = pl.ds(h * DH, DH)
+        sums_ref[:, at] = centred(sums_ref[:, at])
 
 
 def finish_kernel(sums_ref, near_ref, scale_ref, out_ref):
@@ -517,14 +527,27 @@
     w_all = spread(w_out, n_head // 4) + spread(w_cross, n_head // 4)
     mine, scale = pl.pallas_call(
         make_own_last_kernel(PLANES),
-        in_specs=[flat, far_off, wide, wide, wide, far_off, far_off, far_off, wide],
+        in_specs=[flat, far_off, wide, wide, far_off, far_off, wide],
         out_specs=[wide] * 2,
         out_shape=[shape(f32, *upright)] * 2,
-        scratch_shapes=[pltpu.VMEM(upright, bf16)] * 2
-        + [pltpu.VMEM((2 * tok_rows, cols), bf16), pltpu.VMEM(lying, bf16), live, sems(3), sems(1)],
+        scratch_shapes=[pltpu.VMEM(upright, bf16)] * 2 + [live, sems(3)],
+        compiler_params=params(),
+        cost_estimate=cost(0.05),
+    )(told, query, keys_t, values, sums, gate, out_gain)
+    far, tail, mine = barrier((far, tail, mine))
+    mine = pl.pallas_call(
+        far_kernel,
+        in_specs=[flat, far_off, wide, far_off, wide],
+        out_specs=wide,
+        out_shape=shape(f32, *upright),
+        input_output_aliases={4: 0},
+        scratch_shapes=[
+            pltpu.VMEM(upright, bf16), pltpu.VMEM((2 * tok_rows, cols), bf16), pltpu.VMEM(lying, bf16), live,
+            sems(1), sems(1),
+        ],
         compiler_params=params(),
         cost_estimate=cost(9),
-    )(told, query, keys_t, values, tail, far, sums, gate, out_gain)
+    )(told, query, tail, far, mine)
     near, mine, w_all = barrier((near, mine, tuple(w_all)))
     gated = pl.pallas_call(
         finish_kernel,

time: 81 us -> 79.2 us (0.978)
  waiting for transfers between devices: 23.8 us -> 20.9 us
  Pallas kernels: 36.9 us -> 38.3 us
    pallas_call x0 -> x1, Pallas kernels: none -> 4.89 us  [body(): pl.pallas_call(far_kernel, in_specs=[flat, far_off, wide, far_off, wide],...]
    ppermute x1, waiting for transfers between devices: 6.81 us -> 3.08 us  [body(): lax.ppermute(tail, 'seq', [(i, i + FAR + 1) for i in range(n_seq - FAR -...]
    pallas_call x1, Pallas kernels: 7.14 us -> 3.67 us  [body(): pl.pallas_call(make_own_last_kernel(PLANES), in_specs=[flat, far_off, wid...]
  transfers between devices with their start and end apart: 19 -> 19, of which waited for: 7 -> 8; matrix products, arithmetic and copies ran while one was open for 0% -> 0% of each run, Pallas kernels for 40% -> 43%
where the time goes in v7:
time: 79.2 us; the launch traced here: 78.8 us
  Pallas kernels  38.3 us (48%)
  waiting for transfers between devices  20.9 us (26%)
  starting transfers between devices  17.2 us (22%)
  local copies, waits for them, and re-layouts  2.13 us (3%)
    ppermute x15, waiting for transfers between devices, crossed(): lax.ppermute(array, axis, [(i, i ^ bit) for i in range(lax.axis_size(axis...  15.4 us
    ppermute x15, starting transfers between devices, crossed(): lax.ppermute(array, axis, [(i, i ^ bit) for i in range(lax.axis_size(axis...  12.1 us
    pallas_call x1, Pallas kernels, body(): pl.pallas_call(make_chunk_kernel(1, n_head), in_specs=[flat] * 2 + [wide]...  9.87 us
    pallas_call x1, Pallas kernels, body(): pl.pallas_call(own_kernel, in_specs=[far_off, far_off, wide], out_specs=[...  6.85 us
    pallas_call x1, Pallas kernels, body(): pl.pallas_call(make_last_kernel(PLANES, n_head), in_specs=[flat] + [wide]...  4.99 us
    pallas_call x1, Pallas kernels, body(): pl.pallas_call(far_kernel, in_specs=[flat, far_off, wide, far_off, wide],...  4.89 us
    pallas_call x1, Pallas kernels, body(): pl.pallas_call(make_own_last_kernel(PLANES), in_specs=[flat, far_off, wid...  3.67 us
    pallas_call x1, Pallas kernels, body(): pl.pallas_call(own_attend_kernel, in_specs=[flat] + [far_off] * 3, out_sp...  3.31 us
  transfers between devices with their start and end apart: 19, of which 8 were waited for; matrix products, arithmetic and copies ran while one was open for 0% of the time, Pallas kernels for 43%

profile of v7, /device:TPU:25, one launch (start us, length us, event | category | flops | bytes accessed | tf_op | source)
XLA Modules:
  0.0 78.8 jit_solution(9694998337574191480)
XLA Ops:
  0.0 2.6 %shard_map.73 = bf16[192,1024]{1,0:T(8,128)(2,1)} custom-call(bf16[768,1024]{1,0:T(8,128)(2,1)} %refs_6_.1, bf16[1024]{0:T(1024)(128)(2,1)} %gain_hbm), custom_call_target="tpu_custom_call" | custom-call | flops 600000000 | bytes 1800000 | tf_op jit(solution)/shard_map/pallas_call | solution.py:435
  2.6 0.0 copy-start.10
  2.6 0.0 copy-start.9
  2.6 1.3 %collective-permute-start.2 = (bf16[256,1024]{1,0:T(8,128)(2,1)S(1)}, bf16[256,1024]{1,0:T(8,128)(2,1)S(1)}, u32[]{:S(2)}, u32[]{:S(2)}) collective-permute-start(bf16[256,1024]{1,0:T(8,128)(2,1)S(1)} %copy-done.4), channel_id=1, source_target_pairs={{0,2},{1,3},{2,0},{3,1},{4,6},{5,7},{6,4},{7,5},{8,10},{9,11},{10,... | collective-permute-start | bytes 1572872 | tf_op jit(solution)/shard_map/ppermute | solution.py:404
  3.9 1.3 %collective-permute-start.1 = (bf16[192,1024]{1,0:T(8,128)(2,1)}, bf16[192,1024]{1,0:T(8,128)(2,1)S(1)}, u32[]{:S(2)}, u32[]{:S(2)}) collective-permute-start(bf16[192,1024]{1,0:T(8,128)(2,1)} %shard_map.73), channel_id=1, source_target_pairs={{0,8},{4,12},{8,16},{12,20},{16,24},{20,28},{1,9},{5,13},{9,17},{1... | collective-permute-start | bytes 1179656 | tf_op jit(solution)/shard_map/ppermute | solution.py:451
  5.2 6.8 %shard_map.74 = (bf16[768,256]{1,0:T(8,128)(2,1)}, bf16[1536,256]{1,0:T(8,128)(2,1)}, bf16[768,256]{1,0:T(8,128)(2,1)}, bf16[256,768]{1,0:T(8,128)(2,1)}, bf16[2,128,256]{2,1,0:T(8,128)(2,1)}) custom-call(bf16[768,1024]{1,0:T(8,128)(2,1)} %refs_6_.1, bf16[1024]{0:T(1024)(128)(2,1)} %gain_hbm, bf16[4,1024,256]{2,1,0:T(8,128)(2,1)} %refs_4_.3), custom_call_target="tpu_custom_call" | custom-call | flops 1200000000 | bytes 3600000 | tf_op jit(solution)/shard_map/pallas_call | solution.py:453
  12.1 1.3 %collective-permute-start.5 = (bf16[768,256]{1,0:T(8,128)(2,1)}, bf16[768,256]{1,0:T(8,128)(2,1)S(1)}, u32[]{:S(2)}, u32[]{:S(2)}) collective-permute-start(bf16[768,256]{1,0:T(8,128)(2,1)} %get-tuple-element.61.query_hbm.refs_5_), channel_id=1, source_target_pairs={{0,4},{4,0},{8,12},{12,8},{16,20},{20,16},{24,28},{28,24},{1,5},{5... | collective-permute-start | bytes 1179656 | tf_op jit(solution)/shard_map/ppermute | solution.py:404
  13.3 2.3 %collective-permute-done.1.refs_0_ = bf16[192,1024]{1,0:T(8,128)(2,1)S(1)} collective-permute-done((bf16[192,1024]{1,0:T(8,128)(2,1)}, bf16[192,1024]{1,0:T(8,128)(2,1)S(1)}, u32[]{:S(2)}, u32[]{:S(2)}) %collective-permute-start.1) | collective-permute-done | bytes 393248 | tf_op jit(solution)/shard_map/ppermute | solution.py:451
  15.7 1.0 %collective-permute-start.4 = (bf16[192,1024]{1,0:T(8,128)(2,1)S(1)}, bf16[192,1024]{1,0:T(8,128)(2,1)S(1)}, u32[]{:S(2)}, u32[]{:S(2)}) collective-permute-start(bf16[192,1024]{1,0:T(8,128)(2,1)S(1)} %collective-permute-done.1.refs_0_), channel_id=1, source_target_pairs={{0,2},{1,3},{2,0},{3,1},{4,6},{5,7},{6,4},{7,5},{8,10},{9,11},{10,... | collective-permute-start | bytes 1179656 | tf_op jit(solution)/shard_map/ppermute | solution.py:404
  16.7 1.3 %collective-permute-start.3 = (bf16[192,1024]{1,0:T(8,128)(2,1)S(1)}, bf16[192,1024]{1,0:T(8,128)(2,1)S(1)}, u32[]{:S(2)}, u32[]{:S(2)}) collective-permute-start(bf16[192,1024]{1,0:T(8,128)(2,1)S(1)} %collective-permute-done.1.refs_0_), channel_id=1, source_target_pairs={{8,16},{12,20},{16,24},{20,28},{9,17},{13,21},{17,25},{21,29},{10,... | collective-permute-start | bytes 1179656 | tf_op jit(solution)/shard_map/ppermute | solution.py:473
  18.0 0.1 copy.9
  18.1 0.1 pad_add_fusion.told_ref
  18.2 1.2 %collective-permute-start = (s32[6,17]{1,0:T(8,128)S(1)}, s32[6,17]{1,0:T(8,128)S(1)}, u32[]{:S(2)}, u32[]{:S(2)}) collective-permute-start(s32[6,17]{1,0:T(8,128)S(1)} %pad_add_fusion.told_ref), channel_id=1, source_target_pairs={{0,4},{4,0},{8,12},{12,8},{16,20},{20,16},{24,28},{28,24},{1,5},{5... | collective-permute-start | bytes 1232 | tf_op jit(solution)/shard_map/ppermute | solution.py:404
  19.4 2.7 %collective-permute-done.told_x_ref = s32[6,17]{1,0:T(8,128)S(1)} collective-permute-done((s32[6,17]{1,0:T(8,128)S(1)}, s32[6,17]{1,0:T(8,128)S(1)}, u32[]{:S(2)}, u32[]{:S(2)}) %collective-permute-start) | collective-permute-done | bytes 440 | tf_op jit(solution)/shard_map/ppermute | solution.py:404
  22.1 1.9 %collective-permute-start.8 = (bf16[192,1024]{1,0:T(8,128)(2,1)S(1)}, bf16[192,1024]{1,0:T(8,128)(2,1)S(1)}, u32[]{:S(2)}, u32[]{:S(2)}) collective-permute-start(bf16[192,1024]{1,0:T(8,128)(2,1)S(1)} %collective-permute-done.1.refs_0_), channel_id=1, source_target_pairs={{0,1},{1,0},{2,3},{3,2},{4,5},{5,4},{6,7},{7,6},{8,9},{9,8},{10,11... | collective-permute-start | bytes 1179656 | tf_op jit(solution)/shard_map/ppermute | solution.py:404
  24.0 1.0 %copy-done.2 = bf16[768,256]{1,0:T(8,128)(2,1)S(1)} copy-done((bf16[768,256]{1,0:T(8,128)(2,1)S(1)}, bf16[768,256]{1,0:T(8,128)(2,1)}, u32[]{:S(2)}) %copy-start.2) | copy-done | bytes 393240
  25.0 1.0 %copy-done.5 = bf16[256,768]{1,0:T(8,128)(2,1)S(1)} copy-done((bf16[256,768]{1,0:T(8,128)(2,1)S(1)}, bf16[256,768]{1,0:T(8,128)(2,1)}, u32[]{:S(2)}) %copy-start.5) | copy-done | bytes 393240
  26.0 3.3 %shard_map.75.refs_9_ = f32[768,256]{1,0:T(8,128)S(1)} custom-call(s32[6,17]{1,0:T(8,128)S(1)} %pad_add_fusion.told_ref, bf16[768,256]{1,0:T(8,128)(2,1)S(1)} %copy-done.2, bf16[256,768]{1,0:T(8,128)(2,1)S(1)} %copy-done.5, bf16[1536,256]{1,0:T(8,128)(2,1)} %get-tuple-element.68.both_hbm.refs_8_), custom_call_target="tpu_custom_call" | custom-call | flops 1200000000 | bytes 3600000 | tf_op jit(solution)/shard_map/pallas_call | solution.py:478
  29.3 0.0 collective-permute-done.4.refs_2_
  29.3 0.0 collective-permute-done.3.refs_0_
  29.3 0.8 %collective-permute-start.9 = (bf16[192,1024]{1,0:T(8,128)(2,1)S(1)}, bf16[192,1024]{1,0:T(8,128)(2,1)S(1)}, u32[]{:S(2)}, u32[]{:S(2)}) collective-permute-start(bf16[192,1024]{1,0:T(8,128)(2,1)S(1)} %collective-permute-done.4.refs_2_), channel_id=1, source_target_pairs={{0,1},{1,0},{2,3},{3,2},{4,5},{5,4},{6,7},{7,6},{8,9},{9,8},{10,11... | collective-permute-start | bytes 1179656 | tf_op jit(solution)/shard_map/ppermute | solution.py:404
  30.1 0.4 collective-permute-start.7
  30.6 1.3 %collective-permute-start.12 = (bf16[1536,256]{1,0:T(8,128)(2,1)}, bf16[1536,256]{1,0:T(8,128)(2,1)S(1)}, u32[]{:S(2)}, u32[]{:S(2)}) collective-permute-start(bf16[1536,256]{1,0:T(8,128)(2,1)} %get-tuple-element.68.both_hbm.refs_8_), channel_id=1, source_target_pairs={{4,24},{5,25},{6,26},{7,27}} | collective-permute-start | bytes 2359304 | tf_op jit(solution)/shard_map/ppermute | solution.py:494
  31.8 0.3 collective-permute-start.6
  32.2 9.9 %shard_map.76 = (f32[768,256]{1,0:T(8,128)S(1)}, f32[768,256]{1,0:T(8,128)S(1)}) custom-call(s32[6,17]{1,0:T(8,128)S(1)} %pad_add_fusion.told_ref, s32[6,17]{1,0:T(8,128)S(1)} %collective-permute-done.told_x_ref, bf16[192,1024]{1,0:T(8,128)(2,1)S(1)} %collective-permute-done.1.refs_0_, bf16[192,1024]{1,0:T(8,128)(2,1)S(1)} %collective-permute-done.8.refs_1_, ...), custom_call_target="tpu_custom_call" | custom-call | flops 15000000 | bytes 45000 | tf_op jit(solution)/shard_map/pallas_call | solution.py:496
  42.1 0.0 copy-start.7
  42.1 0.0 copy-start.8
  42.1 0.3 collective-permute-start.10
  42.5 1.5 %collective-permute-done.10.refs_3_ = bf16[192,1024]{1,0:T(8,128)(2,1)S(1)} collective-permute-done((bf16[192,1024]{1,0:T(8,128)(2,1)S(1)}, bf16[192,1024]{1,0:T(8,128)(2,1)S(1)}, u32[]{:S(2)}, u32[]{:S(2)}) %collective-permute-start.10) | collective-permute-done | bytes 393248 | tf_op jit(solution)/shard_map/ppermute | solution.py:404
  43.9 5.0 %shard_map.77 = (bf16[768,256]{1,0:T(8,128)(2,1)S(1)}, bf16[256,768]{1,0:T(8,128)(2,1)S(1)}, bf16[768,256]{1,0:T(8,128)(2,1)S(1)}) custom-call(s32[6,17]{1,0:T(8,128)S(1)} %collective-permute-done.told_x_ref, bf16[192,1024]{1,0:T(8,128)(2,1)S(1)} %collective-permute-done.3.refs_0_, bf16[192,1024]{1,0:T(8,128)(2,1)S(1)} %collective-permute-done.6.refs_1_, ...), custom_call_target="tpu_custom_call" | custom-call | flops 15000000 | bytes 45000 | tf_op jit(solution)/shard_map/pallas_call | solution.py:514
  48.9 0.3 collective-permute-start.14
  49.2 0.3 collective-permute-start.15
  49.5 0.2 collective-permute-start.11
  49.7 1.3 %collective-permute-start.13 = (bf16[2,128,256]{2,1,0:T(8,128)(2,1)S(1)}, bf16[2,128,256]{2,1,0:T(8,128)(2,1)S(1)}, u32[]{:S(2)}, u32[]{:S(2)}) collective-permute-start(bf16[2,128,256]{2,1,0:T(8,128)(2,1)S(1)} %copy-done.11), channel_id=1, source_target_pairs={{0,24},{4,28},{1,25},{5,29},{2,26},{6,30},{3,27},{7,31}} | collective-permute-start | bytes 393224 | tf_op jit(solution)/shard_map/ppermute | solution.py:477
  51.0 3.7 %shard_map.78 = (f32[768,256]{1,0:T(8,128)S(1)}, f32[768,256]{1,0:T(8,128)S(1)}) custom-call(s32[6,17]{1,0:T(8,128)S(1)} %pad_add_fusion.told_ref, bf16[768,256]{1,0:T(8,128)(2,1)S(1)} %copy-done.3, bf16[256,768]{1,0:T(8,128)(2,1)S(1)} %get-tuple-element.75.keys_t_ref, bf16[768,256]{1,0:T(8,128)(2,1)S(1)} %get-tuple-element.76.values_ref, ...), custom_call_target="tpu_custom_call" | custom-call | flops 15000000 | bytes 45000 | tf_op jit(solution)/shard_map/pallas_call | solution.py:528
  54.7 3.1 %collective-permute-done.13.tail_ref = bf16[2,128,256]{2,1,0:T(8,128)(2,1)S(1)} collective-permute-done((bf16[2,128,256]{2,1,0:T(8,128)(2,1)S(1)}, bf16[2,128,256]{2,1,0:T(8,128)(2,1)S(1)}, u32[]{:S(2)}, u32[]{:S(2)}) %collective-permute-start.13) | collective-permute-done | bytes 131104 | tf_op jit(solution)/shard_map/ppermute | solution.py:477
  57.8 4.9 %shard_map.79.sums_ref = f32[768,256]{1,0:T(8,128)S(1)} custom-call(s32[6,17]{1,0:T(8,128)S(1)} %pad_add_fusion.told_ref, bf16[768,256]{1,0:T(8,128)(2,1)S(1)} %copy-done.3, bf16[2,128,256]{2,1,0:T(8,128)(2,1)S(1)} %collective-permute-done.13.tail_ref, bf16[1536,256]{1,0:T(8,128)(2,1)S(1)} %collective-permute-done.12.far_hbm, ...), custom_call_target="tpu_custom_call", output_to_operand_aliasing={{}: (4, {})} | custom-call | flops 2700000000 | bytes 8100000 | tf_op jit(solution)/shard_map/pallas_call | solution.py:538
  62.7 0.0 copy-start.1
  62.7 0.6 collective-permute-done.11.near_ref
  63.3 0.5 shard_map.80.refs_0_
  63.8 1.0 %collective-permute-start.17 = (bf16[768,256]{1,0:T(8,128)(2,1)S(1)}, bf16[768,256]{1,0:T(8,128)(2,1)S(1)}, u32[]{:S(2)}, u32[]{:S(2)}) collective-permute-start(bf16[768,256]{1,0:T(8,128)(2,1)S(1)} %shard_map.80.refs_0_), channel_id=1, source_target_pairs={{0,1},{1,0},{2,3},{3,2},{4,5},{5,4},{6,7},{7,6},{8,9},{9,8},{10,11... | collective-permute-start | bytes 1179656 | tf_op jit(solution)/shard_map/ppermute | solution.py:404
  64.8 0.8 %collective-permute-start.16 = (bf16[768,256]{1,0:T(8,128)(2,1)S(1)}, bf16[768,256]{1,0:T(8,128)(2,1)S(1)}, u32[]{:S(2)}, u32[]{:S(2)}) collective-permute-start(bf16[768,256]{1,0:T(8,128)(2,1)S(1)} %shard_map.80.refs_0_), channel_id=1, source_target_pairs={{0,2},{1,3},{2,0},{3,1},{4,6},{5,7},{6,4},{7,5},{8,10},{9,11},{10,... | collective-permute-start | bytes 1179656 | tf_op jit(solution)/shard_map/ppermute | solution.py:404
  65.7 0.5 collective-permute-done.17.refs_1_
  66.2 0.5 shard_map.81
  66.7 8.8 %collective-permute-done.16.refs_0_ = bf16[768,256]{1,0:T(8,128)(2,1)S(1)} collective-permute-done((bf16[768,256]{1,0:T(8,128)(2,1)S(1)}, bf16[768,256]{1,0:T(8,128)(2,1)S(1)}, u32[]{:S(2)}, u32[]{:S(2)}) %collective-permute-start.16) | collective-permute-done | bytes 393248 | tf_op jit(solution)/shard_map/ppermute | solution.py:404
  75.5 0.8 %collective-permute-start.18 = (bf16[768,256]{1,0:T(8,128)(2,1)S(1)}, bf16[768,256]{1,0:T(8,128)(2,1)S(1)}, u32[]{:S(2)}, u32[]{:S(2)}) collective-permute-start(bf16[768,256]{1,0:T(8,128)(2,1)S(1)} %collective-permute-done.16.refs_0_), channel_id=1, source_target_pairs={{0,1},{1,0},{2,3},{3,2},{4,5},{5,4},{6,7},{7,6},{8,9},{9,8},{10,11... | collective-permute-start | bytes 1179656 | tf_op jit(solution)/shard_map/ppermute | solution.py:404
  76.4 1.3 %collective-permute-done.18.refs_1_ = bf16[768,256]{1,0:T(8,128)(2,1)S(1)} collective-permute-done((bf16[768,256]{1,0:T(8,128)(2,1)S(1)}, bf16[768,256]{1,0:T(8,128)(2,1)S(1)}, u32[]{:S(2)}, u32[]{:S(2)}) %collective-permute-start.18) | collective-permute-done | bytes 393248 | tf_op jit(solution)/shard_map/ppermute | solution.py:404
  77.7 1.1 %shard_map.82 = bf16[768,256]{1,0:T(8,128)(2,1)} custom-call(bf16[768,256]{1,0:T(8,128)(2,1)S(1)} %collective-permute-done.16.refs_0_, bf16[768,256]{1,0:T(8,128)(2,1)S(1)} %collective-permute-done.18.refs_1_, bf16[512,256]{1,0:T(8,128)(2,1)S(1)} %get-tuple-element.95.refs_2_, f32[768,256]{1,0:T(8,128)S(1)} %get-tuple-element.96.refs_3_), custom_call_target="tpu_custom_call" | custom-call | flops 600000000 | bytes 1800000 | tf_op jit(solution)/shard_map/pallas_call | solution.py:578
  (26 shorter events, 0.1 us)
Async XLA Ops:
  0.0 2.6 %copy-start.4 = (bf16[256,1024]{1,0:T(8,128)(2,1)S(1)}, bf16[256,1024]{1,0:T(8,128)(2,1)}, u32[]{:S(2)}) copy-start(bf16[256,1024]{1,0:T(8,128)(2,1)} %refs_2_) | copy-start | bytes 1572868
  2.6 15.4 %copy-start.10 = (s32[6]{0:T(128)S(1)}, s32[6]{0:T(128)}, u32[]{:S(2)}) copy-start(s32[6]{0:T(128)} %param.13) | copy-start | bytes 76
  2.6 15.5 %copy-start.9 = (s32[6,16]{1,0:T(8,128)S(1)}, s32[6,16]{1,0:T(8,128)}, u32[]{:S(2)}) copy-start(s32[6,16]{1,0:T(8,128)} %param.12) | copy-start | bytes 1156
  2.6 13.1 %collective-permute-start.2 = (bf16[256,1024]{1,0:T(8,128)(2,1)S(1)}, bf16[256,1024]{1,0:T(8,128)(2,1)S(1)}, u32[]{:S(2)}, u32[]{:S(2)}) collective-permute-start(bf16[256,1024]{1,0:T(8,128)(2,1)S(1)} %copy-done.4), channel_id=1, source_target_pairs={{0,2},{1,3},{2,0},{3,1},{4,6},{5,7},{6,4},{7,5},{8,10},{9,11},{10,... | collective-permute-start | bytes 1572872 | tf_op jit(solution)/shard_map/ppermute | solution.py:404
  3.9 11.8 %collective-permute-start.1 = (bf16[192,1024]{1,0:T(8,128)(2,1)}, bf16[192,1024]{1,0:T(8,128)(2,1)S(1)}, u32[]{:S(2)}, u32[]{:S(2)}) collective-permute-start(bf16[192,1024]{1,0:T(8,128)(2,1)} %shard_map.73), channel_id=1, source_target_pairs={{0,8},{4,12},{8,16},{12,20},{16,24},{20,28},{1,9},{5,13},{9,17},{1... | collective-permute-start | bytes 1179656 | tf_op jit(solution)/shard_map/ppermute | solution.py:451
  12.1 17.2 %collective-permute-start.5 = (bf16[768,256]{1,0:T(8,128)(2,1)}, bf16[768,256]{1,0:T(8,128)(2,1)S(1)}, u32[]{:S(2)}, u32[]{:S(2)}) collective-permute-start(bf16[768,256]{1,0:T(8,128)(2,1)} %get-tuple-element.61.query_hbm.refs_5_), channel_id=1, source_target_pairs={{0,4},{4,0},{8,12},{12,8},{16,20},{20,16},{24,28},{28,24},{1,5},{5... | collective-permute-start | bytes 1179656 | tf_op jit(solution)/shard_map/ppermute | solution.py:404
  15.7 13.6 %collective-permute-start.4 = (bf16[192,1024]{1,0:T(8,128)(2,1)S(1)}, bf16[192,1024]{1,0:T(8,128)(2,1)S(1)}, u32[]{:S(2)}, u32[]{:S(2)}) collective-permute-start(bf16[192,1024]{1,0:T(8,128)(2,1)S(1)} %collective-permute-done.1.refs_0_), channel_id=1, source_target_pairs={{0,2},{1,3},{2,0},{3,1},{4,6},{5,7},{6,4},{7,5},{8,10},{9,11},{10,... | collective-permute-start | bytes 1179656 | tf_op jit(solution)/shard_map/ppermute | solution.py:404
  16.7 12.6 %collective-permute-start.3 = (bf16[192,1024]{1,0:T(8,128)(2,1)S(1)}, bf16[192,1024]{1,0:T(8,128)(2,1)S(1)}, u32[]{:S(2)}, u32[]{:S(2)}) collective-permute-start(bf16[192,1024]{1,0:T(8,128)(2,1)S(1)} %collective-permute-done.1.refs_0_), channel_id=1, source_target_pairs={{8,16},{12,20},{16,24},{20,28},{9,17},{13,21},{17,25},{21,29},{10,... | collective-permute-start | bytes 1179656 | tf_op jit(solution)/shard_map/ppermute | solution.py:473
  18.2 3.9 %collective-permute-start = (s32[6,17]{1,0:T(8,128)S(1)}, s32[6,17]{1,0:T(8,128)S(1)}, u32[]{:S(2)}, u32[]{:S(2)}) collective-permute-start(s32[6,17]{1,0:T(8,128)S(1)} %pad_add_fusion.told_ref), channel_id=1, source_target_pairs={{0,4},{4,0},{8,12},{12,8},{16,20},{20,16},{24,28},{28,24},{1,5},{5... | collective-permute-start | bytes 1232 | tf_op jit(solution)/shard_map/ppermute | solution.py:404
  22.1 10.1 %collective-permute-start.8 = (bf16[192,1024]{1,0:T(8,128)(2,1)S(1)}, bf16[192,1024]{1,0:T(8,128)(2,1)S(1)}, u32[]{:S(2)}, u32[]{:S(2)}) collective-permute-start(bf16[192,1024]{1,0:T(8,128)(2,1)S(1)} %collective-permute-done.1.refs_0_), channel_id=1, source_target_pairs={{0,1},{1,0},{2,3},{3,2},{4,5},{5,4},{6,7},{7,6},{8,9},{9,8},{10,11... | collective-permute-start | bytes 1179656 | tf_op jit(solution)/shard_map/ppermute | solution.py:404
  24.0 1.0 %copy-start.2 = (bf16[768,256]{1,0:T(8,128)(2,1)S(1)}, bf16[768,256]{1,0:T(8,128)(2,1)}, u32[]{:S(2)}) copy-start(bf16[768,256]{1,0:T(8,128)(2,1)} %get-tuple-element.61.query_hbm.refs_5_) | copy-start | bytes 1179652
  25.0 1.0 %copy-start.5 = (bf16[256,768]{1,0:T(8,128)(2,1)S(1)}, bf16[256,768]{1,0:T(8,128)(2,1)}, u32[]{:S(2)}) copy-start(bf16[256,768]{1,0:T(8,128)(2,1)} %get-tuple-element.62.keys_t_hbm.refs_7_) | copy-start | bytes 1179652
  25.9 6.3 %copy-start = (bf16[4,1024,256]{2,1,0:T(8,128)(2,1)S(1)}, bf16[4,1024,256]{2,1,0:T(8,128)(2,1)}, u32[]{:S(2)}) copy-start(bf16[4,1024,256]{2,1,0:T(8,128)(2,1)} %refs_4_.3) | copy-start | bytes 6291460
  26.0 6.3 %copy-start.3 = (bf16[768,256]{1,0:T(8,128)(2,1)S(1)}, bf16[768,256]{1,0:T(8,128)(2,1)}, u32[]{:S(2)}) copy-start(bf16[768,256]{1,0:T(8,128)(2,1)} %get-tuple-element.61.query_hbm.refs_5_) | copy-start | bytes 1179652
  26.0 6.3 %copy-start.6 = (bf16[256,768]{1,0:T(8,128)(2,1)S(1)}, bf16[256,768]{1,0:T(8,128)(2,1)}, u32[]{:S(2)}) copy-start(bf16[256,768]{1,0:T(8,128)(2,1)} %get-tuple-element.62.keys_t_hbm.refs_7_) | copy-start | bytes 1179652
  29.3 2.9 %collective-permute-start.9 = (bf16[192,1024]{1,0:T(8,128)(2,1)S(1)}, bf16[192,1024]{1,0:T(8,128)(2,1)S(1)}, u32[]{:S(2)}, u32[]{:S(2)}) collective-permute-start(bf16[192,1024]{1,0:T(8,128)(2,1)S(1)} %collective-permute-done.4.refs_2_), channel_id=1, source_target_pairs={{0,1},{1,0},{2,3},{3,2},{4,5},{5,4},{6,7},{7,6},{8,9},{9,8},{10,11... | collective-permute-start | bytes 1179656 | tf_op jit(solution)/shard_map/ppermute | solution.py:404
  30.1 12.0 %collective-permute-start.7 = (bf16[192,1024]{1,0:T(8,128)(2,1)S(1)}, bf16[192,1024]{1,0:T(8,128)(2,1)S(1)}, u32[]{:S(2)}, u32[]{:S(2)}) collective-permute-start(bf16[192,1024]{1,0:T(8,128)(2,1)S(1)} %collective-permute-done.3.refs_0_), channel_id=1, source_target_pairs={{0,2},{1,3},{2,0},{3,1},{4,6},{5,7},{6,4},{7,5},{8,10},{9,11},{10,... | collective-permute-start | bytes 1179656 | tf_op jit(solution)/shard_map/ppermute | solution.py:404
  30.6 27.2 %collective-permute-start.12 = (bf16[1536,256]{1,0:T(8,128)(2,1)}, bf16[1536,256]{1,0:T(8,128)(2,1)S(1)}, u32[]{:S(2)}, u32[]{:S(2)}) collective-permute-start(bf16[1536,256]{1,0:T(8,128)(2,1)} %get-tuple-element.68.both_hbm.refs_8_), channel_id=1, source_target_pairs={{4,24},{5,25},{6,26},{7,27}} | collective-permute-start | bytes 2359304 | tf_op jit(solution)/shard_map/ppermute | solution.py:494
  31.8 10.6 %collective-permute-start.6 = (bf16[192,1024]{1,0:T(8,128)(2,1)S(1)}, bf16[192,1024]{1,0:T(8,128)(2,1)S(1)}, u32[]{:S(2)}, u32[]{:S(2)}) collective-permute-start(bf16[192,1024]{1,0:T(8,128)(2,1)S(1)} %collective-permute-done.3.refs_0_), channel_id=1, source_target_pairs={{0,1},{1,0},{2,3},{3,2},{4,5},{5,4},{6,7},{7,6},{8,9},{9,8},{10,11... | collective-permute-start | bytes 1179656 | tf_op jit(solution)/shard_map/ppermute | solution.py:404
  42.1 7.6 %copy-start.11 = (bf16[2,128,256]{2,1,0:T(8,128)(2,1)S(1)}, bf16[2,128,256]{2,1,0:T(8,128)(2,1)}, u32[]{:S(2)}) copy-start(bf16[2,128,256]{2,1,0:T(8,128)(2,1)} %get-tuple-element.74) | copy-start | bytes 393220
  42.1 8.9 %copy-start.7 = (bf16[768,256]{1,0:T(8,128)(2,1)S(1)}, bf16[768,256]{1,0:T(8,128)(2,1)}, u32[]{:S(2)}) copy-start(bf16[768,256]{1,0:T(8,128)(2,1)} %get-tuple-element.78.gate_hbm) | copy-start | bytes 1179652
  42.1 8.9 %copy-start.8 = (bf16[256]{0:T(256)(128)(2,1)S(1)}, bf16[256]{0:T(256)(128)(2,1)}, u32[]{:S(2)}) copy-start(bf16[256]{0:T(256)(128)(2,1)} %gain_ref.3) | copy-start | bytes 1540
  42.1 1.8 %collective-permute-start.10 = (bf16[192,1024]{1,0:T(8,128)(2,1)S(1)}, bf16[192,1024]{1,0:T(8,128)(2,1)S(1)}, u32[]{:S(2)}, u32[]{:S(2)}) collective-permute-start(bf16[192,1024]{1,0:T(8,128)(2,1)S(1)} %collective-permute-done.7.refs_2_), channel_id=1, source_target_pairs={{0,1},{1,0},{2,3},{3,2},{4,5},{5,4},{6,7},{7,6},{8,9},{9,8},{10,11... | collective-permute-start | bytes 1179656 | tf_op jit(solution)/shard_map/ppermute | solution.py:404
  48.9 14.3 %collective-permute-start.14 = (bf16[256,1024]{1,0:T(8,128)(2,1)S(1)}, bf16[256,1024]{1,0:T(8,128)(2,1)S(1)}, u32[]{:S(2)}, u32[]{:S(2)}) collective-permute-start(bf16[256,1024]{1,0:T(8,128)(2,1)S(1)} %copy-done.4), channel_id=1, source_target_pairs={{0,1},{1,0},{2,3},{3,2},{4,5},{5,4},{6,7},{7,6},{8,9},{9,8},{10,11... | collective-permute-start | bytes 1572872 | tf_op jit(solution)/shard_map/ppermute | solution.py:404
  49.2 14.1 %collective-permute-start.15 = (bf16[256,1024]{1,0:T(8,128)(2,1)S(1)}, bf16[256,1024]{1,0:T(8,128)(2,1)S(1)}, u32[]{:S(2)}, u32[]{:S(2)}) collective-permute-start(bf16[256,1024]{1,0:T(8,128)(2,1)S(1)} %collective-permute-done.2.refs_4_), channel_id=1, source_target_pairs={{0,1},{1,0},{2,3},{3,2},{4,5},{5,4},{6,7},{7,6},{8,9},{9,8},{10,11... | collective-permute-start | bytes 1572872 | tf_op jit(solution)/shard_map/ppermute | solution.py:404
  49.5 13.8 %collective-permute-start.11 = (bf16[768,256]{1,0:T(8,128)(2,1)S(1)}, bf16[768,256]{1,0:T(8,128)(2,1)S(1)}, u32[]{:S(2)}, u32[]{:S(2)}) collective-permute-start(bf16[768,256]{1,0:T(8,128)(2,1)S(1)} %get-tuple-element.73), channel_id=1, source_target_pairs={{0,4},{4,0},{8,12},{12,8},{16,20},{20,16},{24,28},{28,24},{1,5},{5... | collective-permute-start | bytes 1179656 | tf_op jit(solution)/shard_map/ppermute | solution.py:404
  49.7 8.1 %collective-permute-start.13 = (bf16[2,128,256]{2,1,0:T(8,128)(2,1)S(1)}, bf16[2,128,256]{2,1,0:T(8,128)(2,1)S(1)}, u32[]{:S(2)}, u32[]{:S(2)}) collective-permute-start(bf16[2,128,256]{2,1,0:T(8,128)(2,1)S(1)} %copy-done.11), channel_id=1, source_target_pairs={{0,24},{4,28},{1,25},{5,29},{2,26},{6,30},{3,27},{7,31}} | collective-permute-start | bytes 393224 | tf_op jit(solution)/shard_map/ppermute | solution.py:477
  62.7 3.5 %copy-start.1 = (bf16[768,1024]{1,0:T(8,128)(2,1)S(1)}, bf16[768,1024]{1,0:T(8,128)(2,1)}, u32[]{:S(2)}) copy-start(bf16[768,1024]{1,0:T(8,128)(2,1)} %refs_6_.1) | copy-start | bytes 4718596
  63.8 2.4 %collective-permute-start.17 = (bf16[768,256]{1,0:T(8,128)(2,1)S(1)}, bf16[768,256]{1,0:T(8,128)(2,1)S(1)}, u32[]{:S(2)}, u32[]{:S(2)}) collective-permute-start(bf16[768,256]{1,0:T(8,128)(2,1)S(1)} %shard_map.80.refs_0_), channel_id=1, source_target_pairs={{0,1},{1,0},{2,3},{3,2},{4,5},{5,4},{6,7},{7,6},{8,9},{9,8},{10,11... | collective-permute-start | bytes 1179656 | tf_op jit(solution)/shard_map/ppermute | solution.py:404
  64.8 10.7 %collective-permute-start.16 = (bf16[768,256]{1,0:T(8,128)(2,1)S(1)}, bf16[768,256]{1,0:T(8,128)(2,1)S(1)}, u32[]{:S(2)}, u32[]{:S(2)}) collective-permute-start(bf16[768,256]{1,0:T(8,128)(2,1)S(1)} %shard_map.80.refs_0_), channel_id=1, source_target_pairs={{0,2},{1,3},{2,0},{3,1},{4,6},{5,7},{6,4},{7,5},{8,10},{9,11},{10,... | collective-permute-start | bytes 1179656 | tf_op jit(solution)/shard_map/ppermute | solution.py:404
  75.5 2.2 %collective-permute-start.18 = (bf16[768,256]{1,0:T(8,128)(2,1)S(1)}, bf16[768,256]{1,0:T(8,128)(2,1)S(1)}, u32[]{:S(2)}, u32[]{:S(2)}) collective-permute-start(bf16[768,256]{1,0:T(8,128)(2,1)S(1)} %collective-permute-done.16.refs_0_), channel_id=1, source_target_pairs={{0,1},{1,0},{2,3},{3,2},{4,5},{5,4},{6,7},{7,6},{8,9},{9,8},{10,11... | collective-permute-start | bytes 1179656 | tf_op jit(solution)/shard_map/ppermute | solution.py:404

commit v8 on v7

--- a/solution.py
+++ b/solution.py
@@ -319,7 +319,7 @@
 
 
 def far_kernel(
-    told_ref, query_hbm, tail_ref, far_hbm, unused, sums_ref, query_ref, far_ref, far_t_ref, live_ref, sems, far_sems
+    told_ref, query_hbm, tail_ref, far_ref, unused, sums_ref, query_ref, far_t_ref, live_ref, sems
 ):
     rows, cols = query_ref.shape
     blocks = rows // BLK
@@ -330,14 +330,16 @@
     @pl.when(far >= 0)
     def _():
         copies = fetch([(query_hbm, query_ref)], sems)
-        far_copies = fetch([(far_hbm, far_ref)], far_sems)
         mark(live_ref, told_ref, far * blocks, blocks, 0)
+
+        @pl.when(here % 2 == 0)
+        def _():
+            far_t_ref[...] = far_ref[0:rows, :].astype(jnp.float32).T.astype(jnp.bfloat16)
+
         wait(copies)
-        wait(far_copies)
 
         @pl.when(here % 2 == 0)
         def _():
-            far_t_ref[...] = far_ref[0:rows, :].astype(jnp.float32).T.astype(jnp.bfloat16)
             attend_all(query_ref, sums_ref, far_t_ref, far_ref.at[pl.ds(rows, rows)], live_ref, 0, blocks)
 
     @pl.when(farthest >= 0)
@@ -537,13 +539,12 @@
     far, tail, mine = barrier((far, tail, mine))
     mine = pl.pallas_call(
         far_kernel,
-        in_specs=[flat, far_off, wide, far_off, wide],
+        in_specs=[flat, far_off, wide, wide, wide],
         out_specs=wide,
         out_shape=shape(f32, *upright),
         input_output_aliases={4: 0},
         scratch_shapes=[
-            pltpu.VMEM(upright, bf16), pltpu.VMEM((2 * tok_rows, cols), bf16), pltpu.VMEM(lying, bf16), live,
-            sems(1), sems(1),
+            pltpu.VMEM(upright, bf16), pltpu.VMEM(lying, bf16), live, sems(1),
         ],
         compiler_params=params(),
         cost_estimate=cost(9),

time: 79.2 us -> 79 us (level)
  no operation moved by 1% of the time
where the time goes in v8:
time: 79 us; the launch traced here: 78.9 us
  Pallas kernels  38.5 us (49%)
  waiting for transfers between devices  20.7 us (26%)
  starting transfers between devices  17.2 us (22%)
  local copies, waits for them, and re-layouts  2.13 us (3%)
    ppermute x15, waiting for transfers between devices, crossed(): lax.ppermute(array, axis, [(i, i ^ bit) for i in range(lax.axis_size(axis...  14.8 us
    ppermute x15, starting transfers between devices, crossed(): lax.ppermute(array, axis, [(i, i ^ bit) for i in range(lax.axis_size(axis...  12.1 us
    pallas_call x1, Pallas kernels, body(): pl.pallas_call(make_chunk_kernel(1, n_head), in_specs=[flat] * 2 + [wide]...  10.4 us
    pallas_call x1, Pallas kernels, body(): pl.pallas_call(own_kernel, in_specs=[far_off, far_off, wide], out_specs=[...  6.85 us
    pallas_call x1, Pallas kernels, body(): pl.pallas_call(make_last_kernel(PLANES, n_head), in_specs=[flat] + [wide]...  4.96 us
    pallas_call x1, Pallas kernels, body(): pl.pallas_call(far_kernel, in_specs=[flat, far_off, wide, wide, wide], ou...  4.66 us
    pallas_call x1, Pallas kernels, body(): pl.pallas_call(make_own_last_kernel(PLANES), in_specs=[flat, far_off, wid...  3.59 us
    ppermute x1, waiting for transfers between devices, body(): lax.ppermute(tail, 'seq', [(i, i + FAR + 1) for i in range(n_seq - FAR -...  3.57 us
  transfers between devices with their start and end apart: 19, of which 8 were waited for; matrix products, arithmetic and copies ran while one was open for 0% of the time, Pallas kernels for 43%

profile of v8, /device:TPU:25, one launch (start us, length us, event | category | flops | bytes accessed | tf_op | source)
XLA Modules:
  0.0 78.9 jit_solution(3979404409837414146)
XLA Ops:
  0.0 2.6 %shard_map.73 = bf16[192,1024]{1,0:T(8,128)(2,1)} custom-call(bf16[768,1024]{1,0:T(8,128)(2,1)} %refs_6_.1, bf16[1024]{0:T(1024)(128)(2,1)} %gain_hbm), custom_call_target="tpu_custom_call" | custom-call | flops 600000000 | bytes 1800000 | tf_op jit(solution)/shard_map/pallas_call | solution.py:437
  2.6 0.0 copy-start.10
  2.6 0.0 copy-start.9
  2.6 1.3 %collective-permute-start.2 = (bf16[256,1024]{1,0:T(8,128)(2,1)S(1)}, bf16[256,1024]{1,0:T(8,128)(2,1)S(1)}, u32[]{:S(2)}, u32[]{:S(2)}) collective-permute-start(bf16[256,1024]{1,0:T(8,128)(2,1)S(1)} %copy-done.4), channel_id=1, source_target_pairs={{0,2},{1,3},{2,0},{3,1},{4,6},{5,7},{6,4},{7,5},{8,10},{9,11},{10,... | collective-permute-start | bytes 1572872 | tf_op jit(solution)/shard_map/ppermute | solution.py:406
  3.9 1.3 %collective-permute-start.1 = (bf16[192,1024]{1,0:T(8,128)(2,1)}, bf16[192,1024]{1,0:T(8,128)(2,1)S(1)}, u32[]{:S(2)}, u32[]{:S(2)}) collective-permute-start(bf16[192,1024]{1,0:T(8,128)(2,1)} %shard_map.73), channel_id=1, source_target_pairs={{0,8},{4,12},{8,16},{12,20},{16,24},{20,28},{1,9},{5,13},{9,17},{1... | collective-permute-start | bytes 1179656 | tf_op jit(solution)/shard_map/ppermute | solution.py:453
  5.2 6.8 %shard_map.74 = (bf16[768,256]{1,0:T(8,128)(2,1)}, bf16[1536,256]{1,0:T(8,128)(2,1)}, bf16[768,256]{1,0:T(8,128)(2,1)}, bf16[256,768]{1,0:T(8,128)(2,1)}, bf16[2,128,256]{2,1,0:T(8,128)(2,1)}) custom-call(bf16[768,1024]{1,0:T(8,128)(2,1)} %refs_6_.1, bf16[1024]{0:T(1024)(128)(2,1)} %gain_hbm, bf16[4,1024,256]{2,1,0:T(8,128)(2,1)} %refs_4_.3), custom_call_target="tpu_custom_call" | custom-call | flops 1200000000 | bytes 3600000 | tf_op jit(solution)/shard_map/pallas_call | solution.py:455
  12.1 1.3 %collective-permute-start.5 = (bf16[768,256]{1,0:T(8,128)(2,1)}, bf16[768,256]{1,0:T(8,128)(2,1)S(1)}, u32[]{:S(2)}, u32[]{:S(2)}) collective-permute-start(bf16[768,256]{1,0:T(8,128)(2,1)} %get-tuple-element.61.query_hbm.refs_5_), channel_id=1, source_target_pairs={{0,4},{4,0},{8,12},{12,8},{16,20},{20,16},{24,28},{28,24},{1,5},{5... | collective-permute-start | bytes 1179656 | tf_op jit(solution)/shard_map/ppermute | solution.py:406
  13.3 2.3 %collective-permute-done.1.refs_0_ = bf16[192,1024]{1,0:T(8,128)(2,1)S(1)} collective-permute-done((bf16[192,1024]{1,0:T(8,128)(2,1)}, bf16[192,1024]{1,0:T(8,128)(2,1)S(1)}, u32[]{:S(2)}, u32[]{:S(2)}) %collective-permute-start.1) | collective-permute-done | bytes 393248 | tf_op jit(solution)/shard_map/ppermute | solution.py:453
  15.7 0.0 collective-permute-done.2.refs_4_
  15.7 1.0 %collective-permute-start.4 = (bf16[192,1024]{1,0:T(8,128)(2,1)S(1)}, bf16[192,1024]{1,0:T(8,128)(2,1)S(1)}, u32[]{:S(2)}, u32[]{:S(2)}) collective-permute-start(bf16[192,1024]{1,0:T(8,128)(2,1)S(1)} %collective-permute-done.1.refs_0_), channel_id=1, source_target_pairs={{0,2},{1,3},{2,0},{3,1},{4,6},{5,7},{6,4},{7,5},{8,10},{9,11},{10,... | collective-permute-start | bytes 1179656 | tf_op jit(solution)/shard_map/ppermute | solution.py:406
  16.7 1.3 %collective-permute-start.3 = (bf16[192,1024]{1,0:T(8,128)(2,1)S(1)}, bf16[192,1024]{1,0:T(8,128)(2,1)S(1)}, u32[]{:S(2)}, u32[]{:S(2)}) collective-permute-start(bf16[192,1024]{1,0:T(8,128)(2,1)S(1)} %collective-permute-done.1.refs_0_), channel_id=1, source_target_pairs={{8,16},{12,20},{16,24},{20,28},{9,17},{13,21},{17,25},{21,29},{10,... | collective-permute-start | bytes 1179656 | tf_op jit(solution)/shard_map/ppermute | solution.py:475
  18.0 0.1 copy.9
  18.1 0.1 pad_add_fusion.told_ref
  18.2 1.2 %collective-permute-start = (s32[6,17]{1,0:T(8,128)S(1)}, s32[6,17]{1,0:T(8,128)S(1)}, u32[]{:S(2)}, u32[]{:S(2)}) collective-permute-start(s32[6,17]{1,0:T(8,128)S(1)} %pad_add_fusion.told_ref), channel_id=1, source_target_pairs={{0,4},{4,0},{8,12},{12,8},{16,20},{20,16},{24,28},{28,24},{1,5},{5... | collective-permute-start | bytes 1232 | tf_op jit(solution)/shard_map/ppermute | solution.py:406
  19.4 2.7 %collective-permute-done.told_x_ref = s32[6,17]{1,0:T(8,128)S(1)} collective-permute-done((s32[6,17]{1,0:T(8,128)S(1)}, s32[6,17]{1,0:T(8,128)S(1)}, u32[]{:S(2)}, u32[]{:S(2)}) %collective-permute-start) | collective-permute-done | bytes 440 | tf_op jit(solution)/shard_map/ppermute | solution.py:406
  22.1 1.9 %collective-permute-start.8 = (bf16[192,1024]{1,0:T(8,128)(2,1)S(1)}, bf16[192,1024]{1,0:T(8,128)(2,1)S(1)}, u32[]{:S(2)}, u32[]{:S(2)}) collective-permute-start(bf16[192,1024]{1,0:T(8,128)(2,1)S(1)} %collective-permute-done.1.refs_0_), channel_id=1, source_target_pairs={{0,1},{1,0},{2,3},{3,2},{4,5},{5,4},{6,7},{7,6},{8,9},{9,8},{10,11... | collective-permute-start | bytes 1179656 | tf_op jit(solution)/shard_map/ppermute | solution.py:406
  24.0 1.0 %copy-done.2 = bf16[768,256]{1,0:T(8,128)(2,1)S(1)} copy-done((bf16[768,256]{1,0:T(8,128)(2,1)S(1)}, bf16[768,256]{1,0:T(8,128)(2,1)}, u32[]{:S(2)}) %copy-start.2) | copy-done | bytes 393240
  25.0 1.0 %copy-done.5 = bf16[256,768]{1,0:T(8,128)(2,1)S(1)} copy-done((bf16[256,768]{1,0:T(8,128)(2,1)S(1)}, bf16[256,768]{1,0:T(8,128)(2,1)}, u32[]{:S(2)}) %copy-start.5) | copy-done | bytes 393240
  26.0 3.3 %shard_map.75.refs_9_ = f32[768,256]{1,0:T(8,128)S(1)} custom-call(s32[6,17]{1,0:T(8,128)S(1)} %pad_add_fusion.told_ref, bf16[768,256]{1,0:T(8,128)(2,1)S(1)} %copy-done.2, bf16[256,768]{1,0:T(8,128)(2,1)S(1)} %copy-done.5, bf16[1536,256]{1,0:T(8,128)(2,1)} %get-tuple-element.68.both_hbm.refs_8_), custom_call_target="tpu_custom_call" | custom-call | flops 1200000000 | bytes 3600000 | tf_op jit(solution)/shard_map/pallas_call | solution.py:480
  29.3 0.0 collective-permute-done.5.refs_6_.refs_5_
  29.3 0.0 collective-permute-done.4.refs_2_
  29.3 0.8 %collective-permute-start.9 = (bf16[192,1024]{1,0:T(8,128)(2,1)S(1)}, bf16[192,1024]{1,0:T(8,128)(2,1)S(1)}, u32[]{:S(2)}, u32[]{:S(2)}) collective-permute-start(bf16[192,1024]{1,0:T(8,128)(2,1)S(1)} %collective-permute-done.4.refs_2_), channel_id=1, source_target_pairs={{0,1},{1,0},{2,3},{3,2},{4,5},{5,4},{6,7},{7,6},{8,9},{9,8},{10,11... | collective-permute-start | bytes 1179656 | tf_op jit(solution)/shard_map/ppermute | solution.py:406
  30.1 0.4 collective-permute-start.7
  30.6 1.3 %collective-permute-start.12 = (bf16[1536,256]{1,0:T(8,128)(2,1)}, bf16[1536,256]{1,0:T(8,128)(2,1)S(1)}, u32[]{:S(2)}, u32[]{:S(2)}) collective-permute-start(bf16[1536,256]{1,0:T(8,128)(2,1)} %get-tuple-element.68.both_hbm.refs_8_), channel_id=1, source_target_pairs={{4,24},{5,25},{6,26},{7,27}} | collective-permute-start | bytes 2359304 | tf_op jit(solution)/shard_map/ppermute | solution.py:496
  31.8 0.3 collective-permute-start.6
  32.2 10.4 %shard_map.76 = (f32[768,256]{1,0:T(8,128)S(1)}, f32[768,256]{1,0:T(8,128)S(1)}) custom-call(s32[6,17]{1,0:T(8,128)S(1)} %pad_add_fusion.told_ref, s32[6,17]{1,0:T(8,128)S(1)} %collective-permute-done.told_x_ref, bf16[192,1024]{1,0:T(8,128)(2,1)S(1)} %collective-permute-done.1.refs_0_, bf16[192,1024]{1,0:T(8,128)(2,1)S(1)} %collective-permute-done.8.refs_1_, ...), custom_call_target="tpu_custom_call" | custom-call | flops 15000000 | bytes 45000 | tf_op jit(solution)/shard_map/pallas_call | solution.py:498
  42.6 0.0 copy-start.7
  42.6 0.0 copy-start.8
  42.6 0.3 collective-permute-start.10
  42.9 1.5 %collective-permute-done.10.refs_3_ = bf16[192,1024]{1,0:T(8,128)(2,1)S(1)} collective-permute-done((bf16[192,1024]{1,0:T(8,128)(2,1)S(1)}, bf16[192,1024]{1,0:T(8,128)(2,1)S(1)}, u32[]{:S(2)}, u32[]{:S(2)}) %collective-permute-start.10) | collective-permute-done | bytes 393248 | tf_op jit(solution)/shard_map/ppermute | solution.py:406
  44.4 5.0 %shard_map.77 = (bf16[768,256]{1,0:T(8,128)(2,1)S(1)}, bf16[256,768]{1,0:T(8,128)(2,1)S(1)}, bf16[768,256]{1,0:T(8,128)(2,1)S(1)}) custom-call(s32[6,17]{1,0:T(8,128)S(1)} %collective-permute-done.told_x_ref, bf16[192,1024]{1,0:T(8,128)(2,1)S(1)} %collective-permute-done.3.refs_0_, bf16[192,1024]{1,0:T(8,128)(2,1)S(1)} %collective-permute-done.6.refs_1_, ...), custom_call_target="tpu_custom_call" | custom-call | flops 15000000 | bytes 45000 | tf_op jit(solution)/shard_map/pallas_call | solution.py:516
  49.4 0.3 collective-permute-start.14
  49.7 0.3 collective-permute-start.15
  50.0 1.3 %collective-permute-start.13 = (bf16[2,128,256]{2,1,0:T(8,128)(2,1)S(1)}, bf16[2,128,256]{2,1,0:T(8,128)(2,1)S(1)}, u32[]{:S(2)}, u32[]{:S(2)}) collective-permute-start(bf16[2,128,256]{2,1,0:T(8,128)(2,1)S(1)} %copy-done.11), channel_id=1, source_target_pairs={{0,24},{4,28},{1,25},{5,29},{2,26},{6,30},{3,27},{7,31}} | collective-permute-start | bytes 393224 | tf_op jit(solution)/shard_map/ppermute | solution.py:479
  51.3 3.6 %shard_map.78 = (f32[768,256]{1,0:T(8,128)S(1)}, f32[768,256]{1,0:T(8,128)S(1)}) custom-call(s32[6,17]{1,0:T(8,128)S(1)} %pad_add_fusion.told_ref, bf16[768,256]{1,0:T(8,128)(2,1)S(1)} %copy-done.3, bf16[256,768]{1,0:T(8,128)(2,1)S(1)} %get-tuple-element.75.keys_t_ref, bf16[768,256]{1,0:T(8,128)(2,1)S(1)} %get-tuple-element.76.values_ref, ...), custom_call_target="tpu_custom_call" | custom-call | flops 15000000 | bytes 45000 | tf_op jit(solution)/shard_map/pallas_call | solution.py:530
  54.9 3.6 %collective-permute-done.13.tail_ref = bf16[2,128,256]{2,1,0:T(8,128)(2,1)S(1)} collective-permute-done((bf16[2,128,256]{2,1,0:T(8,128)(2,1)S(1)}, bf16[2,128,256]{2,1,0:T(8,128)(2,1)S(1)}, u32[]{:S(2)}, u32[]{:S(2)}) %collective-permute-start.13) | collective-permute-done | bytes 131104 | tf_op jit(solution)/shard_map/ppermute | solution.py:479
  58.5 4.7 %shard_map.79.sums_ref = f32[768,256]{1,0:T(8,128)S(1)} custom-call(s32[6,17]{1,0:T(8,128)S(1)} %pad_add_fusion.told_ref, bf16[768,256]{1,0:T(8,128)(2,1)S(1)} %copy-done.3, bf16[2,128,256]{2,1,0:T(8,128)(2,1)S(1)} %collective-permute-done.13.tail_ref, bf16[1536,256]{1,0:T(8,128)(2,1)S(1)} %collective-permute-done.12.far_ref, ...), custom_call_target="tpu_custom_call", output_to_operand_aliasing={{}: (4, {})} | custom-call | flops 2700000000 | bytes 8100000 | tf_op jit(solution)/shard_map/pallas_call | solution.py:540
  63.1 0.0 copy-start.1
  63.2 0.1 collective-permute-done.11.near_ref
  63.3 0.5 shard_map.80.refs_0_
  63.8 1.1 %collective-permute-start.17 = (bf16[768,256]{1,0:T(8,128)(2,1)S(1)}, bf16[768,256]{1,0:T(8,128)(2,1)S(1)}, u32[]{:S(2)}, u32[]{:S(2)}) collective-permute-start(bf16[768,256]{1,0:T(8,128)(2,1)S(1)} %shard_map.80.refs_0_), channel_id=1, source_target_pairs={{0,1},{1,0},{2,3},{3,2},{4,5},{5,4},{6,7},{7,6},{8,9},{9,8},{10,11... | collective-permute-start | bytes 1179656 | tf_op jit(solution)/shard_map/ppermute | solution.py:406
  64.9 1.1 %collective-permute-start.16 = (bf16[768,256]{1,0:T(8,128)(2,1)S(1)}, bf16[768,256]{1,0:T(8,128)(2,1)S(1)}, u32[]{:S(2)}, u32[]{:S(2)}) collective-permute-start(bf16[768,256]{1,0:T(8,128)(2,1)S(1)} %shard_map.80.refs_0_), channel_id=1, source_target_pairs={{0,2},{1,3},{2,0},{3,1},{4,6},{5,7},{6,4},{7,5},{8,10},{9,11},{10,... | collective-permute-start | bytes 1179656 | tf_op jit(solution)/shard_map/ppermute | solution.py:406
  65.9 0.3 collective-permute-done.17.refs_1_
  66.2 0.5 shard_map.81
  66.8 8.8 %collective-permute-done.16.refs_0_ = bf16[768,256]{1,0:T(8,128)(2,1)S(1)} collective-permute-done((bf16[768,256]{1,0:T(8,128)(2,1)S(1)}, bf16[768,256]{1,0:T(8,128)(2,1)S(1)}, u32[]{:S(2)}, u32[]{:S(2)}) %collective-permute-start.16) | collective-permute-done | bytes 393248 | tf_op jit(solution)/shard_map/ppermute | solution.py:406
  75.6 0.8 %collective-permute-start.18 = (bf16[768,256]{1,0:T(8,128)(2,1)S(1)}, bf16[768,256]{1,0:T(8,128)(2,1)S(1)}, u32[]{:S(2)}, u32[]{:S(2)}) collective-permute-start(bf16[768,256]{1,0:T(8,128)(2,1)S(1)} %collective-permute-done.16.refs_0_), channel_id=1, source_target_pairs={{0,1},{1,0},{2,3},{3,2},{4,5},{5,4},{6,7},{7,6},{8,9},{9,8},{10,11... | collective-permute-start | bytes 1179656 | tf_op jit(solution)/shard_map/ppermute | solution.py:406
  76.4 1.3 %collective-permute-done.18.refs_1_ = bf16[768,256]{1,0:T(8,128)(2,1)S(1)} collective-permute-done((bf16[768,256]{1,0:T(8,128)(2,1)S(1)}, bf16[768,256]{1,0:T(8,128)(2,1)S(1)}, u32[]{:S(2)}, u32[]{:S(2)}) %collective-permute-start.18) | collective-permute-done | bytes 393248 | tf_op jit(solution)/shard_map/ppermute | solution.py:406
  77.8 1.1 %shard_map.82 = bf16[768,256]{1,0:T(8,128)(2,1)} custom-call(bf16[768,256]{1,0:T(8,128)(2,1)S(1)} %collective-permute-done.16.refs_0_, bf16[768,256]{1,0:T(8,128)(2,1)S(1)} %collective-permute-done.18.refs_1_, bf16[512,256]{1,0:T(8,128)(2,1)S(1)} %get-tuple-element.95.refs_2_, f32[768,256]{1,0:T(8,128)S(1)} %get-tuple-element.96.refs_3_), custom_call_target="tpu_custom_call" | custom-call | flops 600000000 | bytes 1800000 | tf_op jit(solution)/shard_map/pallas_call | solution.py:579
  (26 shorter events, 0.1 us)
Async XLA Ops:
  0.0 2.6 %copy-start.4 = (bf16[256,1024]{1,0:T(8,128)(2,1)S(1)}, bf16[256,1024]{1,0:T(8,128)(2,1)}, u32[]{:S(2)}) copy-start(bf16[256,1024]{1,0:T(8,128)(2,1)} %refs_2_) | copy-start | bytes 1572868
  2.6 15.4 %copy-start.10 = (s32[6]{0:T(128)S(1)}, s32[6]{0:T(128)}, u32[]{:S(2)}) copy-start(s32[6]{0:T(128)} %param.13) | copy-start | bytes 76
  2.6 15.5 %copy-start.9 = (s32[6,16]{1,0:T(8,128)S(1)}, s32[6,16]{1,0:T(8,128)}, u32[]{:S(2)}) copy-start(s32[6,16]{1,0:T(8,128)} %param.12) | copy-start | bytes 1156
  2.6 13.1 %collective-permute-start.2 = (bf16[256,1024]{1,0:T(8,128)(2,1)S(1)}, bf16[256,1024]{1,0:T(8,128)(2,1)S(1)}, u32[]{:S(2)}, u32[]{:S(2)}) collective-permute-start(bf16[256,1024]{1,0:T(8,128)(2,1)S(1)} %copy-done.4), channel_id=1, source_target_pairs={{0,2},{1,3},{2,0},{3,1},{4,6},{5,7},{6,4},{7,5},{8,10},{9,11},{10,... | collective-permute-start | bytes 1572872 | tf_op jit(solution)/shard_map/ppermute | solution.py:406
  3.9 11.8 %collective-permute-start.1 = (bf16[192,1024]{1,0:T(8,128)(2,1)}, bf16[192,1024]{1,0:T(8,128)(2,1)S(1)}, u32[]{:S(2)}, u32[]{:S(2)}) collective-permute-start(bf16[192,1024]{1,0:T(8,128)(2,1)} %shard_map.73), channel_id=1, source_target_pairs={{0,8},{4,12},{8,16},{12,20},{16,24},{20,28},{1,9},{5,13},{9,17},{1... | collective-permute-start | bytes 1179656 | tf_op jit(solution)/shard_map/ppermute | solution.py:453
  12.1 17.2 %collective-permute-start.5 = (bf16[768,256]{1,0:T(8,128)(2,1)}, bf16[768,256]{1,0:T(8,128)(2,1)S(1)}, u32[]{:S(2)}, u32[]{:S(2)}) collective-permute-start(bf16[768,256]{1,0:T(8,128)(2,1)} %get-tuple-element.61.query_hbm.refs_5_), channel_id=1, source_target_pairs={{0,4},{4,0},{8,12},{12,8},{16,20},{20,16},{24,28},{28,24},{1,5},{5... | collective-permute-start | bytes 1179656 | tf_op jit(solution)/shard_map/ppermute | solution.py:406
  15.7 13.6 %collective-permute-start.4 = (bf16[192,1024]{1,0:T(8,128)(2,1)S(1)}, bf16[192,1024]{1,0:T(8,128)(2,1)S(1)}, u32[]{:S(2)}, u32[]{:S(2)}) collective-permute-start(bf16[192,1024]{1,0:T(8,128)(2,1)S(1)} %collective-permute-done.1.refs_0_), channel_id=1, source_target_pairs={{0,2},{1,3},{2,0},{3,1},{4,6},{5,7},{6,4},{7,5},{8,10},{9,11},{10,... | collective-permute-start | bytes 1179656 | tf_op jit(solution)/shard_map/ppermute | solution.py:406
  16.7 12.6 %collective-permute-start.3 = (bf16[192,1024]{1,0:T(8,128)(2,1)S(1)}, bf16[192,1024]{1,0:T(8,128)(2,1)S(1)}, u32[]{:S(2)}, u32[]{:S(2)}) collective-permute-start(bf16[192,1024]{1,0:T(8,128)(2,1)S(1)} %collective-permute-done.1.refs_0_), channel_id=1, source_target_pairs={{8,16},{12,20},{16,24},{20,28},{9,17},{13,21},{17,25},{21,29},{10,... | collective-permute-start | bytes 1179656 | tf_op jit(solution)/shard_map/ppermute | solution.py:475
  18.2 3.9 %collective-permute-start = (s32[6,17]{1,0:T(8,128)S(1)}, s32[6,17]{1,0:T(8,128)S(1)}, u32[]{:S(2)}, u32[]{:S(2)}) collective-permute-start(s32[6,17]{1,0:T(8,128)S(1)} %pad_add_fusion.told_ref), channel_id=1, source_target_pairs={{0,4},{4,0},{8,12},{12,8},{16,20},{20,16},{24,28},{28,24},{1,5},{5... | collective-permute-start | bytes 1232 | tf_op jit(solution)/shard_map/ppermute | solution.py:406
  22.1 10.1 %collective-permute-start.8 = (bf16[192,1024]{1,0:T(8,128)(2,1)S(1)}, bf16[192,1024]{1,0:T(8,128)(2,1)S(1)}, u32[]{:S(2)}, u32[]{:S(2)}) collective-permute-start(bf16[192,1024]{1,0:T(8,128)(2,1)S(1)} %collective-permute-done.1.refs_0_), channel_id=1, source_target_pairs={{0,1},{1,0},{2,3},{3,2},{4,5},{5,4},{6,7},{7,6},{8,9},{9,8},{10,11... | collective-permute-start | bytes 1179656 | tf_op jit(solution)/shard_map/ppermute | solution.py:406
  24.0 1.0 %copy-start.2 = (bf16[768,256]{1,0:T(8,128)(2,1)S(1)}, bf16[768,256]{1,0:T(8,128)(2,1)}, u32[]{:S(2)}) copy-start(bf16[768,256]{1,0:T(8,128)(2,1)} %get-tuple-element.61.query_hbm.refs_5_) | copy-start | bytes 1179652
  25.0 1.0 %copy-start.5 = (bf16[256,768]{1,0:T(8,128)(2,1)S(1)}, bf16[256,768]{1,0:T(8,128)(2,1)}, u32[]{:S(2)}) copy-start(bf16[256,768]{1,0:T(8,128)(2,1)} %get-tuple-element.62.keys_t_hbm.refs_7_) | copy-start | bytes 1179652
  25.9 6.3 %copy-start = (bf16[4,1024,256]{2,1,0:T(8,128)(2,1)S(1)}, bf16[4,1024,256]{2,1,0:T(8,128)(2,1)}, u32[]{:S(2)}) copy-start(bf16[4,1024,256]{2,1,0:T(8,128)(2,1)} %refs_4_.3) | copy-start | bytes 6291460
  26.0 6.3 %copy-start.3 = (bf16[768,256]{1,0:T(8,128)(2,1)S(1)}, bf16[768,256]{1,0:T(8,128)(2,1)}, u32[]{:S(2)}) copy-start(bf16[768,256]{1,0:T(8,128)(2,1)} %get-tuple-element.61.query_hbm.refs_5_) | copy-start | bytes 1179652
  26.0 6.3 %copy-start.6 = (bf16[256,768]{1,0:T(8,128)(2,1)S(1)}, bf16[256,768]{1,0:T(8,128)(2,1)}, u32[]{:S(2)}) copy-start(bf16[256,768]{1,0:T(8,128)(2,1)} %get-tuple-element.62.keys_t_hbm.refs_7_) | copy-start | bytes 1179652
  29.3 2.9 %collective-permute-start.9 = (bf16[192,1024]{1,0:T(8,128)(2,1)S(1)}, bf16[192,1024]{1,0:T(8,128)(2,1)S(1)}, u32[]{:S(2)}, u32[]{:S(2)}) collective-permute-start(bf16[192,1024]{1,0:T(8,128)(2,1)S(1)} %collective-permute-done.4.refs_2_), channel_id=1, source_target_pairs={{0,1},{1,0},{2,3},{3,2},{4,5},{5,4},{6,7},{7,6},{8,9},{9,8},{10,11... | collective-permute-start | bytes 1179656 | tf_op jit(solution)/shard_map/ppermute | solution.py:406
  30.1 12.5 %collective-permute-start.7 = (bf16[192,1024]{1,0:T(8,128)(2,1)S(1)}, bf16[192,1024]{1,0:T(8,128)(2,1)S(1)}, u32[]{:S(2)}, u32[]{:S(2)}) collective-permute-start(bf16[192,1024]{1,0:T(8,128)(2,1)S(1)} %collective-permute-done.3.refs_0_), channel_id=1, source_target_pairs={{0,2},{1,3},{2,0},{3,1},{4,6},{5,7},{6,4},{7,5},{8,10},{9,11},{10,... | collective-permute-start | bytes 1179656 | tf_op jit(solution)/shard_map/ppermute | solution.py:406
  30.6 27.9 %collective-permute-start.12 = (bf16[1536,256]{1,0:T(8,128)(2,1)}, bf16[1536,256]{1,0:T(8,128)(2,1)S(1)}, u32[]{:S(2)}, u32[]{:S(2)}) collective-permute-start(bf16[1536,256]{1,0:T(8,128)(2,1)} %get-tuple-element.68.both_hbm.refs_8_), channel_id=1, source_target_pairs={{4,24},{5,25},{6,26},{7,27}} | collective-permute-start | bytes 2359304 | tf_op jit(solution)/shard_map/ppermute | solution.py:496
  31.8 11.1 %collective-permute-start.6 = (bf16[192,1024]{1,0:T(8,128)(2,1)S(1)}, bf16[192,1024]{1,0:T(8,128)(2,1)S(1)}, u32[]{:S(2)}, u32[]{:S(2)}) collective-permute-start(bf16[192,1024]{1,0:T(8,128)(2,1)S(1)} %collective-permute-done.3.refs_0_), channel_id=1, source_target_pairs={{0,1},{1,0},{2,3},{3,2},{4,5},{5,4},{6,7},{7,6},{8,9},{9,8},{10,11... | collective-permute-start | bytes 1179656 | tf_op jit(solution)/shard_map/ppermute | solution.py:406
  42.6 7.4 %copy-start.11 = (bf16[2,128,256]{2,1,0:T(8,128)(2,1)S(1)}, bf16[2,128,256]{2,1,0:T(8,128)(2,1)}, u32[]{:S(2)}) copy-start(bf16[2,128,256]{2,1,0:T(8,128)(2,1)} %get-tuple-element.74) | copy-start | bytes 393220
  42.6 8.7 %copy-start.7 = (bf16[768,256]{1,0:T(8,128)(2,1)S(1)}, bf16[768,256]{1,0:T(8,128)(2,1)}, u32[]{:S(2)}) copy-start(bf16[768,256]{1,0:T(8,128)(2,1)} %get-tuple-element.78.gate_hbm) | copy-start | bytes 1179652
  42.6 8.7 %copy-start.8 = (bf16[256]{0:T(256)(128)(2,1)S(1)}, bf16[256]{0:T(256)(128)(2,1)}, u32[]{:S(2)}) copy-start(bf16[256]{0:T(256)(128)(2,1)} %gain_ref.3) | copy-start | bytes 1540
  42.6 1.8 %collective-permute-start.10 = (bf16[192,1024]{1,0:T(8,128)(2,1)S(1)}, bf16[192,1024]{1,0:T(8,128)(2,1)S(1)}, u32[]{:S(2)}, u32[]{:S(2)}) collective-permute-start(bf16[192,1024]{1,0:T(8,128)(2,1)S(1)} %collective-permute-done.7.refs_2_), channel_id=1, source_target_pairs={{0,1},{1,0},{2,3},{3,2},{4,5},{5,4},{6,7},{7,6},{8,9},{9,8},{10,11... | collective-permute-start | bytes 1179656 | tf_op jit(solution)/shard_map/ppermute | solution.py:406
  49.4 13.9 %collective-permute-start.14 = (bf16[256,1024]{1,0:T(8,128)(2,1)S(1)}, bf16[256,1024]{1,0:T(8,128)(2,1)S(1)}, u32[]{:S(2)}, u32[]{:S(2)}) collective-permute-start(bf16[256,1024]{1,0:T(8,128)(2,1)S(1)} %copy-done.4), channel_id=1, source_target_pairs={{0,1},{1,0},{2,3},{3,2},{4,5},{5,4},{6,7},{7,6},{8,9},{9,8},{10,11... | collective-permute-start | bytes 1572872 | tf_op jit(solution)/shard_map/ppermute | solution.py:406
  49.7 13.6 %collective-permute-start.15 = (bf16[256,1024]{1,0:T(8,128)(2,1)S(1)}, bf16[256,1024]{1,0:T(8,128)(2,1)S(1)}, u32[]{:S(2)}, u32[]{:S(2)}) collective-permute-start(bf16[256,1024]{1,0:T(8,128)(2,1)S(1)} %collective-permute-done.2.refs_4_), channel_id=1, source_target_pairs={{0,1},{1,0},{2,3},{3,2},{4,5},{5,4},{6,7},{7,6},{8,9},{9,8},{10,11... | collective-permute-start | bytes 1572872 | tf_op jit(solution)/shard_map/ppermute | solution.py:406
  50.0 13.3 %collective-permute-start.11 = (bf16[768,256]{1,0:T(8,128)(2,1)S(1)}, bf16[768,256]{1,0:T(8,128)(2,1)S(1)}, u32[]{:S(2)}, u32[]{:S(2)}) collective-permute-start(bf16[768,256]{1,0:T(8,128)(2,1)S(1)} %get-tuple-element.73), channel_id=1, source_target_pairs={{0,4},{4,0},{8,12},{12,8},{16,20},{20,16},{24,28},{28,24},{1,5},{5... | collective-permute-start | bytes 1179656 | tf_op jit(solution)/shard_map/ppermute | solution.py:406
  50.0 8.5 %collective-permute-start.13 = (bf16[2,128,256]{2,1,0:T(8,128)(2,1)S(1)}, bf16[2,128,256]{2,1,0:T(8,128)(2,1)S(1)}, u32[]{:S(2)}, u32[]{:S(2)}) collective-permute-start(bf16[2,128,256]{2,1,0:T(8,128)(2,1)S(1)} %copy-done.11), channel_id=1, source_target_pairs={{0,24},{4,28},{1,25},{5,29},{2,26},{6,30},{3,27},{7,31}} | collective-permute-start | bytes 393224 | tf_op jit(solution)/shard_map/ppermute | solution.py:479
  63.1 3.1 %copy-start.1 = (bf16[768,1024]{1,0:T(8,128)(2,1)S(1)}, bf16[768,1024]{1,0:T(8,128)(2,1)}, u32[]{:S(2)}) copy-start(bf16[768,1024]{1,0:T(8,128)(2,1)} %refs_6_.1) | copy-start | bytes 4718596
  63.8 2.4 %collective-permute-start.17 = (bf16[768,256]{1,0:T(8,128)(2,1)S(1)}, bf16[768,256]{1,0:T(8,128)(2,1)S(1)}, u32[]{:S(2)}, u32[]{:S(2)}) collective-permute-start(bf16[768,256]{1,0:T(8,128)(2,1)S(1)} %shard_map.80.refs_0_), channel_id=1, source_target_pairs={{0,1},{1,0},{2,3},{3,2},{4,5},{5,4},{6,7},{7,6},{8,9},{9,8},{10,11... | collective-permute-start | bytes 1179656 | tf_op jit(solution)/shard_map/ppermute | solution.py:406
  64.9 10.7 %collective-permute-start.16 = (bf16[768,256]{1,0:T(8,128)(2,1)S(1)}, bf16[768,256]{1,0:T(8,128)(2,1)S(1)}, u32[]{:S(2)}, u32[]{:S(2)}) collective-permute-start(bf16[768,256]{1,0:T(8,128)(2,1)S(1)} %shard_map.80.refs_0_), channel_id=1, source_target_pairs={{0,2},{1,3},{2,0},{3,1},{4,6},{5,7},{6,4},{7,5},{8,10},{9,11},{10,... | collective-permute-start | bytes 1179656 | tf_op jit(solution)/shard_map/ppermute | solution.py:406
  75.6 2.2 %collective-permute-start.18 = (bf16[768,256]{1,0:T(8,128)(2,1)S(1)}, bf16[768,256]{1,0:T(8,128)(2,1)S(1)}, u32[]{:S(2)}, u32[]{:S(2)}) collective-permute-start(bf16[768,256]{1,0:T(8,128)(2,1)S(1)} %collective-permute-done.16.refs_0_), channel_id=1, source_target_pairs={{0,1},{1,0},{2,3},{3,2},{4,5},{5,4},{6,7},{7,6},{8,9},{9,8},{10,11... | collective-permute-start | bytes 1179656 | tf_op jit(solution)/shard_map/ppermute | solution.py:406

commit v9 on v7

--- a/solution.py
+++ b/solution.py
@@ -473,7 +473,8 @@
     share_2 = lax.ppermute(share_1, "seq", upward[2:])
     cross_1 = crossed(share_1, "head", n_head // 2)
     told_x = crossed(told, "seq", 1)
-    told, told_x, tail = barrier((told, told_x, tail))
+    told, told_x, tail, w_out, w_cross = barrier((told, told_x, tail, w_out, w_cross))
+    w_all = spread(w_out, n_head // 4) + spread(w_cross, n_head // 4)
     tail = lax.ppermute(tail, "seq", [(i, i + FAR + 1) for i in range(n_seq - FAR - 1)])
     own_sums = pl.pallas_call(
         own_attend_kernel,
@@ -510,7 +511,7 @@
         cost_estimate=cost(0.05),
     )(told, told_x, *chunk_1, w_in, query, query_x, keys_t, both, own_sums)
 
-    cross_2, sums_x = barrier((cross_2, sums_x))
+    cross_2, sums_x, w_all = barrier((cross_2, sums_x, tuple(w_all)))
     send, keys_t, values = pl.pallas_call(
         make_last_kernel(PLANES, n_head),
         in_specs=[flat] + [wide] * (n_head + 1) + [far_off] * 2,
@@ -523,8 +524,6 @@
         cost_estimate=cost(0.05),
     )(told_x, *near_2, *spread(cross_2, n_head // 4), w_in, query_x, sums_x)
     near = crossed(send, "seq", 1)
-    send, w_out, w_cross = barrier((send, w_out, w_cross))
-    w_all = spread(w_out, n_head // 4) + spread(w_cross, n_head // 4)
     mine, scale = pl.pallas_call(
         make_own_last_kernel(PLANES),
         in_specs=[flat, far_off, wide, wide, far_off, far_off, wide],
@@ -548,7 +547,7 @@
         compiler_params=params(),
         cost_estimate=cost(9),
     )(told, query, tail, far, mine)
-    near, mine, w_all = barrier((near, mine, tuple(w_all)))
+    near, mine = barrier((near, mine))
     gated = pl.pallas_call(
         finish_kernel,
         in_specs=[wide] * 3,

time: 79.2 us -> 78.8 us (level)
  waiting for transfers between devices: 20.9 us -> 19.5 us
  Pallas kernels: 38.3 us -> 39.1 us
    ppermute x15, waiting for transfers between devices: 15.4 us -> 13.7 us  [crossed(): lax.ppermute(array, axis, [(i, i ^ bit) for i in range(lax.axis_size(axis...]
    pallas_call x1, Pallas kernels: 9.87 us -> 10.8 us  [body(): pl.pallas_call(make_chunk_kernel(1, n_head), in_specs=[flat] * 2 + [wide]...]
  transfers between devices with their start and end apart: 19 -> 19, of which waited for: 8 -> 7; matrix products, arithmetic and copies ran while one was open for 0% -> 0% of each run, Pallas kernels for 43% -> 44%
where the time goes in v9:
time: 78.8 us; the launch traced here: 78.7 us
  Pallas kernels  39.1 us (50%)
  waiting for transfers between devices  19.5 us (25%)
  starting transfers between devices  17.5 us (22%)
  local copies, waits for them, and re-layouts  2.13 us (3%)
    ppermute x15, waiting for transfers between devices, crossed(): lax.ppermute(array, axis, [(i, i ^ bit) for i in range(lax.axis_size(axis...  13.7 us
    ppermute x15, starting transfers between devices, crossed(): lax.ppermute(array, axis, [(i, i ^ bit) for i in range(lax.axis_size(axis...  12.4 us
    pallas_call x1, Pallas kernels, body(): pl.pallas_call(make_chunk_kernel(1, n_head), in_specs=[flat] * 2 + [wide]...  10.8 us
    pallas_call x1, Pallas kernels, body(): pl.pallas_call(own_kernel, in_specs=[far_off, far_off, wide], out_specs=[...  6.85 us
    pallas_call x1, Pallas kernels, body(): pl.pallas_call(make_last_kernel(PLANES, n_head), in_specs=[flat] + [wide]...  5.03 us
    pallas_call x1, Pallas kernels, body(): pl.pallas_call(far_kernel, in_specs=[flat, far_off, wide, far_off, wide],...  4.6 us
    pallas_call x1, Pallas kernels, body(): pl.pallas_call(make_own_last_kernel(PLANES), in_specs=[flat, far_off, wid...  3.84 us
    ppermute x1, waiting for transfers between devices, body(): lax.ppermute(tail, 'seq', [(i, i + FAR + 1) for i in range(n_seq - FAR -...  3.47 us
  transfers between devices with their start and end apart: 19, of which 7 were waited for; matrix products, arithmetic and copies ran while one was open for 0% of the time, Pallas kernels for 44%

profile of v9, /device:TPU:25, one launch (start us, length us, event | category | flops | bytes accessed | tf_op | source)
XLA Modules:
  0.0 78.7 jit_solution(1985558390647352356)
XLA Ops:
  0.0 2.6 %shard_map.73 = bf16[192,1024]{1,0:T(8,128)(2,1)} custom-call(bf16[768,1024]{1,0:T(8,128)(2,1)} %refs_6_.1, bf16[1024]{0:T(1024)(128)(2,1)} %gain_hbm), custom_call_target="tpu_custom_call" | custom-call | flops 600000000 | bytes 1800000 | tf_op jit(solution)/shard_map/pallas_call | solution.py:435
  2.6 0.0 copy-start.10
  2.6 0.0 copy-start.9
  2.6 1.3 %collective-permute-start.2 = (bf16[256,1024]{1,0:T(8,128)(2,1)S(1)}, bf16[256,1024]{1,0:T(8,128)(2,1)S(1)}, u32[]{:S(2)}, u32[]{:S(2)}) collective-permute-start(bf16[256,1024]{1,0:T(8,128)(2,1)S(1)} %copy-done.4), channel_id=1, source_target_pairs={{0,2},{1,3},{2,0},{3,1},{4,6},{5,7},{6,4},{7,5},{8,10},{9,11},{10,... | collective-permute-start | bytes 1572872 | tf_op jit(solution)/shard_map/ppermute | solution.py:404
  3.9 1.3 %collective-permute-start.1 = (bf16[192,1024]{1,0:T(8,128)(2,1)}, bf16[192,1024]{1,0:T(8,128)(2,1)S(1)}, u32[]{:S(2)}, u32[]{:S(2)}) collective-permute-start(bf16[192,1024]{1,0:T(8,128)(2,1)} %shard_map.73), channel_id=1, source_target_pairs={{0,8},{4,12},{8,16},{12,20},{16,24},{20,28},{1,9},{5,13},{9,17},{1... | collective-permute-start | bytes 1179656 | tf_op jit(solution)/shard_map/ppermute | solution.py:451
  5.2 6.8 %shard_map.74 = (bf16[768,256]{1,0:T(8,128)(2,1)}, bf16[1536,256]{1,0:T(8,128)(2,1)}, bf16[768,256]{1,0:T(8,128)(2,1)}, bf16[256,768]{1,0:T(8,128)(2,1)}, bf16[2,128,256]{2,1,0:T(8,128)(2,1)}) custom-call(bf16[768,1024]{1,0:T(8,128)(2,1)} %refs_6_.1, bf16[1024]{0:T(1024)(128)(2,1)} %gain_hbm, bf16[4,1024,256]{2,1,0:T(8,128)(2,1)} %refs_4_.3), custom_call_target="tpu_custom_call" | custom-call | flops 1200000000 | bytes 3600000 | tf_op jit(solution)/shard_map/pallas_call | solution.py:453
  12.1 1.3 %collective-permute-start.5 = (bf16[768,256]{1,0:T(8,128)(2,1)}, bf16[768,256]{1,0:T(8,128)(2,1)S(1)}, u32[]{:S(2)}, u32[]{:S(2)}) collective-permute-start(bf16[768,256]{1,0:T(8,128)(2,1)} %get-tuple-element.62.query_hbm.refs_5_), channel_id=1, source_target_pairs={{0,4},{4,0},{8,12},{12,8},{16,20},{20,16},{24,28},{28,24},{1,5},{5... | collective-permute-start | bytes 1179656 | tf_op jit(solution)/shard_map/ppermute | solution.py:404
  13.3 2.3 %collective-permute-done.1.refs_0_ = bf16[192,1024]{1,0:T(8,128)(2,1)S(1)} collective-permute-done((bf16[192,1024]{1,0:T(8,128)(2,1)}, bf16[192,1024]{1,0:T(8,128)(2,1)S(1)}, u32[]{:S(2)}, u32[]{:S(2)}) %collective-permute-start.1) | collective-permute-done | bytes 393248 | tf_op jit(solution)/shard_map/ppermute | solution.py:451
  15.7 0.0 collective-permute-done.2.refs_4_
  15.7 1.3 %collective-permute-start.3 = (bf16[192,1024]{1,0:T(8,128)(2,1)S(1)}, bf16[192,1024]{1,0:T(8,128)(2,1)S(1)}, u32[]{:S(2)}, u32[]{:S(2)}) collective-permute-start(bf16[192,1024]{1,0:T(8,128)(2,1)S(1)} %collective-permute-done.1.refs_0_), channel_id=1, source_target_pairs={{8,16},{12,20},{16,24},{20,28},{9,17},{13,21},{17,25},{21,29},{10,... | collective-permute-start | bytes 1179656 | tf_op jit(solution)/shard_map/ppermute | solution.py:473
  17.0 1.1 %collective-permute-start.4 = (bf16[192,1024]{1,0:T(8,128)(2,1)S(1)}, bf16[192,1024]{1,0:T(8,128)(2,1)S(1)}, u32[]{:S(2)}, u32[]{:S(2)}) collective-permute-start(bf16[192,1024]{1,0:T(8,128)(2,1)S(1)} %collective-permute-done.1.refs_0_), channel_id=1, source_target_pairs={{0,2},{1,3},{2,0},{3,1},{4,6},{5,7},{6,4},{7,5},{8,10},{9,11},{10,... | collective-permute-start | bytes 1179656 | tf_op jit(solution)/shard_map/ppermute | solution.py:404
  18.1 1.8 %collective-permute-start.8 = (bf16[192,1024]{1,0:T(8,128)(2,1)S(1)}, bf16[192,1024]{1,0:T(8,128)(2,1)S(1)}, u32[]{:S(2)}, u32[]{:S(2)}) collective-permute-start(bf16[192,1024]{1,0:T(8,128)(2,1)S(1)} %collective-permute-done.1.refs_0_), channel_id=1, source_target_pairs={{0,1},{1,0},{2,3},{3,2},{4,5},{5,4},{6,7},{7,6},{8,9},{9,8},{10,11... | collective-permute-start | bytes 1179656 | tf_op jit(solution)/shard_map/ppermute | solution.py:404
  19.9 0.1 copy.9
  20.0 0.1 pad_add_fusion.told_ref
  20.1 1.2 %collective-permute-start = (s32[6,17]{1,0:T(8,128)S(1)}, s32[6,17]{1,0:T(8,128)S(1)}, u32[]{:S(2)}, u32[]{:S(2)}) collective-permute-start(s32[6,17]{1,0:T(8,128)S(1)} %pad_add_fusion.told_ref), channel_id=1, source_target_pairs={{0,4},{4,0},{8,12},{12,8},{16,20},{20,16},{24,28},{28,24},{1,5},{5... | collective-permute-start | bytes 1232 | tf_op jit(solution)/shard_map/ppermute | solution.py:404
  21.3 1.6 %collective-permute-done.told_x_ref = s32[6,17]{1,0:T(8,128)S(1)} collective-permute-done((s32[6,17]{1,0:T(8,128)S(1)}, s32[6,17]{1,0:T(8,128)S(1)}, u32[]{:S(2)}, u32[]{:S(2)}) %collective-permute-start) | collective-permute-done | bytes 440 | tf_op jit(solution)/shard_map/ppermute | solution.py:404
  22.9 1.0 %collective-permute-start.10 = (bf16[256,1024]{1,0:T(8,128)(2,1)S(1)}, bf16[256,1024]{1,0:T(8,128)(2,1)S(1)}, u32[]{:S(2)}, u32[]{:S(2)}) collective-permute-start(bf16[256,1024]{1,0:T(8,128)(2,1)S(1)} %copy-done.4), channel_id=1, source_target_pairs={{0,1},{1,0},{2,3},{3,2},{4,5},{5,4},{6,7},{7,6},{8,9},{9,8},{10,11... | collective-permute-start | bytes 1572872 | tf_op jit(solution)/shard_map/ppermute | solution.py:404
  24.0 0.0 collective-permute-done.5.refs_6_.refs_5_
  24.0 0.0 collective-permute-start.11
  24.0 1.0 %copy-done.2 = bf16[768,256]{1,0:T(8,128)(2,1)S(1)} copy-done((bf16[768,256]{1,0:T(8,128)(2,1)S(1)}, bf16[768,256]{1,0:T(8,128)(2,1)}, u32[]{:S(2)}) %copy-start.2) | copy-done | bytes 393240
  25.0 1.0 %copy-done.5 = bf16[256,768]{1,0:T(8,128)(2,1)S(1)} copy-done((bf16[256,768]{1,0:T(8,128)(2,1)S(1)}, bf16[256,768]{1,0:T(8,128)(2,1)}, u32[]{:S(2)}) %copy-start.5) | copy-done | bytes 393240
  26.0 3.3 %shard_map.75.refs_9_ = f32[768,256]{1,0:T(8,128)S(1)} custom-call(s32[6,17]{1,0:T(8,128)S(1)} %pad_add_fusion.told_ref, bf16[768,256]{1,0:T(8,128)(2,1)S(1)} %copy-done.2, bf16[256,768]{1,0:T(8,128)(2,1)S(1)} %copy-done.5, bf16[1536,256]{1,0:T(8,128)(2,1)} %get-tuple-element.69.both_hbm.refs_8_), custom_call_target="tpu_custom_call" | custom-call | flops 1200000000 | bytes 3600000 | tf_op jit(solution)/shard_map/pallas_call | solution.py:479
  29.3 0.0 collective-permute-done.3.refs_0_
  29.3 0.6 collective-permute-start.9
  29.9 0.5 collective-permute-start.7
  30.4 1.3 %collective-permute-start.14 = (bf16[1536,256]{1,0:T(8,128)(2,1)}, bf16[1536,256]{1,0:T(8,128)(2,1)S(1)}, u32[]{:S(2)}, u32[]{:S(2)}) collective-permute-start(bf16[1536,256]{1,0:T(8,128)(2,1)} %get-tuple-element.69.both_hbm.refs_8_), channel_id=1, source_target_pairs={{4,24},{5,25},{6,26},{7,27}} | collective-permute-start | bytes 2359304 | tf_op jit(solution)/shard_map/ppermute | solution.py:495
  31.7 0.4 collective-permute-start.6
  32.1 10.8 %shard_map.76 = (f32[768,256]{1,0:T(8,128)S(1)}, f32[768,256]{1,0:T(8,128)S(1)}) custom-call(s32[6,17]{1,0:T(8,128)S(1)} %pad_add_fusion.told_ref, s32[6,17]{1,0:T(8,128)S(1)} %collective-permute-done.told_x_ref, bf16[192,1024]{1,0:T(8,128)(2,1)S(1)} %collective-permute-done.1.refs_0_, bf16[192,1024]{1,0:T(8,128)(2,1)S(1)} %collective-permute-done.8.refs_1_, ...), custom_call_target="tpu_custom_call" | custom-call | flops 15000000 | bytes 45000 | tf_op jit(solution)/shard_map/pallas_call | solution.py:497
  42.9 0.0 copy-start.7
  42.9 0.0 copy-start.8
  42.9 0.2 collective-permute-start.12
  43.1 1.6 %collective-permute-done.12.refs_3_ = bf16[192,1024]{1,0:T(8,128)(2,1)S(1)} collective-permute-done((bf16[192,1024]{1,0:T(8,128)(2,1)S(1)}, bf16[192,1024]{1,0:T(8,128)(2,1)S(1)}, u32[]{:S(2)}, u32[]{:S(2)}) %collective-permute-start.12) | collective-permute-done | bytes 393248 | tf_op jit(solution)/shard_map/ppermute | solution.py:404
  44.7 5.0 %shard_map.77 = (bf16[768,256]{1,0:T(8,128)(2,1)S(1)}, bf16[256,768]{1,0:T(8,128)(2,1)S(1)}, bf16[768,256]{1,0:T(8,128)(2,1)S(1)}) custom-call(s32[6,17]{1,0:T(8,128)S(1)} %collective-permute-done.told_x_ref, bf16[192,1024]{1,0:T(8,128)(2,1)S(1)} %collective-permute-done.3.refs_0_, bf16[192,1024]{1,0:T(8,128)(2,1)S(1)} %collective-permute-done.6.refs_1_, ...), custom_call_target="tpu_custom_call" | custom-call | flops 15000000 | bytes 45000 | tf_op jit(solution)/shard_map/pallas_call | solution.py:515
  49.7 0.1 collective-permute-start.13
  49.8 1.3 %collective-permute-start.15 = (bf16[2,128,256]{2,1,0:T(8,128)(2,1)S(1)}, bf16[2,128,256]{2,1,0:T(8,128)(2,1)S(1)}, u32[]{:S(2)}, u32[]{:S(2)}) collective-permute-start(bf16[2,128,256]{2,1,0:T(8,128)(2,1)S(1)} %copy-done.11), channel_id=1, source_target_pairs={{0,24},{4,28},{1,25},{5,29},{2,26},{6,30},{3,27},{7,31}} | collective-permute-start | bytes 393224 | tf_op jit(solution)/shard_map/ppermute | solution.py:478
  51.2 3.8 %shard_map.78 = (f32[768,256]{1,0:T(8,128)S(1)}, f32[768,256]{1,0:T(8,128)S(1)}) custom-call(s32[6,17]{1,0:T(8,128)S(1)} %pad_add_fusion.told_ref, bf16[768,256]{1,0:T(8,128)(2,1)S(1)} %copy-done.3, bf16[256,768]{1,0:T(8,128)(2,1)S(1)} %get-tuple-element.78.keys_t_ref, bf16[768,256]{1,0:T(8,128)(2,1)S(1)} %get-tuple-element.79.values_ref, ...), custom_call_target="tpu_custom_call" | custom-call | flops 15000000 | bytes 45000 | tf_op jit(solution)/shard_map/pallas_call | solution.py:527
  55.0 3.5 %collective-permute-done.15.tail_ref = bf16[2,128,256]{2,1,0:T(8,128)(2,1)S(1)} collective-permute-done((bf16[2,128,256]{2,1,0:T(8,128)(2,1)S(1)}, bf16[2,128,256]{2,1,0:T(8,128)(2,1)S(1)}, u32[]{:S(2)}, u32[]{:S(2)}) %collective-permute-start.15) | collective-permute-done | bytes 131104 | tf_op jit(solution)/shard_map/ppermute | solution.py:478
  58.5 4.6 %shard_map.79.sums_ref = f32[768,256]{1,0:T(8,128)S(1)} custom-call(s32[6,17]{1,0:T(8,128)S(1)} %pad_add_fusion.told_ref, bf16[768,256]{1,0:T(8,128)(2,1)S(1)} %copy-done.3, bf16[2,128,256]{2,1,0:T(8,128)(2,1)S(1)} %collective-permute-done.15.tail_ref, bf16[1536,256]{1,0:T(8,128)(2,1)S(1)} %collective-permute-done.14.far_hbm, ...), custom_call_target="tpu_custom_call", output_to_operand_aliasing={{}: (4, {})} | custom-call | flops 2700000000 | bytes 8100000 | tf_op jit(solution)/shard_map/pallas_call | solution.py:537
  63.1 0.0 copy-start.1
  63.1 0.5 shard_map.80.refs_0_
  63.6 1.0 %collective-permute-start.17 = (bf16[768,256]{1,0:T(8,128)(2,1)S(1)}, bf16[768,256]{1,0:T(8,128)(2,1)S(1)}, u32[]{:S(2)}, u32[]{:S(2)}) collective-permute-start(bf16[768,256]{1,0:T(8,128)(2,1)S(1)} %shard_map.80.refs_0_), channel_id=1, source_target_pairs={{0,1},{1,0},{2,3},{3,2},{4,5},{5,4},{6,7},{7,6},{8,9},{9,8},{10,11... | collective-permute-start | bytes 1179656 | tf_op jit(solution)/shard_map/ppermute | solution.py:404
  64.7 1.0 %collective-permute-start.16 = (bf16[768,256]{1,0:T(8,128)(2,1)S(1)}, bf16[768,256]{1,0:T(8,128)(2,1)S(1)}, u32[]{:S(2)}, u32[]{:S(2)}) collective-permute-start(bf16[768,256]{1,0:T(8,128)(2,1)S(1)} %shard_map.80.refs_0_), channel_id=1, source_target_pairs={{0,2},{1,3},{2,0},{3,1},{4,6},{5,7},{6,4},{7,5},{8,10},{9,11},{10,... | collective-permute-start | bytes 1179656 | tf_op jit(solution)/shard_map/ppermute | solution.py:404
  65.7 0.3 collective-permute-done.17.refs_1_
  66.0 0.5 shard_map.81
  66.6 8.8 %collective-permute-done.16.refs_0_ = bf16[768,256]{1,0:T(8,128)(2,1)S(1)} collective-permute-done((bf16[768,256]{1,0:T(8,128)(2,1)S(1)}, bf16[768,256]{1,0:T(8,128)(2,1)S(1)}, u32[]{:S(2)}, u32[]{:S(2)}) %collective-permute-start.16) | collective-permute-done | bytes 393248 | tf_op jit(solution)/shard_map/ppermute | solution.py:404
  75.3 0.8 %collective-permute-start.18 = (bf16[768,256]{1,0:T(8,128)(2,1)S(1)}, bf16[768,256]{1,0:T(8,128)(2,1)S(1)}, u32[]{:S(2)}, u32[]{:S(2)}) collective-permute-start(bf16[768,256]{1,0:T(8,128)(2,1)S(1)} %collective-permute-done.16.refs_0_), channel_id=1, source_target_pairs={{0,1},{1,0},{2,3},{3,2},{4,5},{5,4},{6,7},{7,6},{8,9},{9,8},{10,11... | collective-permute-start | bytes 1179656 | tf_op jit(solution)/shard_map/ppermute | solution.py:404
  76.2 1.3 %collective-permute-done.18.refs_1_ = bf16[768,256]{1,0:T(8,128)(2,1)S(1)} collective-permute-done((bf16[768,256]{1,0:T(8,128)(2,1)S(1)}, bf16[768,256]{1,0:T(8,128)(2,1)S(1)}, u32[]{:S(2)}, u32[]{:S(2)}) %collective-permute-start.18) | collective-permute-done | bytes 393248 | tf_op jit(solution)/shard_map/ppermute | solution.py:404
  77.5 1.1 %shard_map.82 = bf16[768,256]{1,0:T(8,128)(2,1)} custom-call(bf16[768,256]{1,0:T(8,128)(2,1)S(1)} %collective-permute-done.16.refs_0_, bf16[768,256]{1,0:T(8,128)(2,1)S(1)} %collective-permute-done.18.refs_1_, bf16[512,256]{1,0:T(8,128)(2,1)S(1)} %get-tuple-element.95.refs_2_, f32[768,256]{1,0:T(8,128)S(1)} %get-tuple-element.96.refs_3_), custom_call_target="tpu_custom_call" | custom-call | flops 600000000 | bytes 1800000 | tf_op jit(solution)/shard_map/pallas_call | solution.py:577
  (26 shorter events, 0.1 us)
Async XLA Ops:
  0.0 2.6 %copy-start.4 = (bf16[256,1024]{1,0:T(8,128)(2,1)S(1)}, bf16[256,1024]{1,0:T(8,128)(2,1)}, u32[]{:S(2)}) copy-start(bf16[256,1024]{1,0:T(8,128)(2,1)} %refs_2_) | copy-start | bytes 1572868
  2.6 17.3 %copy-start.10 = (s32[6]{0:T(128)S(1)}, s32[6]{0:T(128)}, u32[]{:S(2)}) copy-start(s32[6]{0:T(128)} %param.13) | copy-start | bytes 76
  2.6 17.4 %copy-start.9 = (s32[6,16]{1,0:T(8,128)S(1)}, s32[6,16]{1,0:T(8,128)}, u32[]{:S(2)}) copy-start(s32[6,16]{1,0:T(8,128)} %param.12) | copy-start | bytes 1156
  2.6 13.1 %collective-permute-start.2 = (bf16[256,1024]{1,0:T(8,128)(2,1)S(1)}, bf16[256,1024]{1,0:T(8,128)(2,1)S(1)}, u32[]{:S(2)}, u32[]{:S(2)}) collective-permute-start(bf16[256,1024]{1,0:T(8,128)(2,1)S(1)} %copy-done.4), channel_id=1, source_target_pairs={{0,2},{1,3},{2,0},{3,1},{4,6},{5,7},{6,4},{7,5},{8,10},{9,11},{10,... | collective-permute-start | bytes 1572872 | tf_op jit(solution)/shard_map/ppermute | solution.py:404
  3.9 11.8 %collective-permute-start.1 = (bf16[192,1024]{1,0:T(8,128)(2,1)}, bf16[192,1024]{1,0:T(8,128)(2,1)S(1)}, u32[]{:S(2)}, u32[]{:S(2)}) collective-permute-start(bf16[192,1024]{1,0:T(8,128)(2,1)} %shard_map.73), channel_id=1, source_target_pairs={{0,8},{4,12},{8,16},{12,20},{16,24},{20,28},{1,9},{5,13},{9,17},{1... | collective-permute-start | bytes 1179656 | tf_op jit(solution)/shard_map/ppermute | solution.py:451
  12.1 11.9 %collective-permute-start.5 = (bf16[768,256]{1,0:T(8,128)(2,1)}, bf16[768,256]{1,0:T(8,128)(2,1)S(1)}, u32[]{:S(2)}, u32[]{:S(2)}) collective-permute-start(bf16[768,256]{1,0:T(8,128)(2,1)} %get-tuple-element.62.query_hbm.refs_5_), channel_id=1, source_target_pairs={{0,4},{4,0},{8,12},{12,8},{16,20},{20,16},{24,28},{28,24},{1,5},{5... | collective-permute-start | bytes 1179656 | tf_op jit(solution)/shard_map/ppermute | solution.py:404
  15.7 13.6 %collective-permute-start.3 = (bf16[192,1024]{1,0:T(8,128)(2,1)S(1)}, bf16[192,1024]{1,0:T(8,128)(2,1)S(1)}, u32[]{:S(2)}, u32[]{:S(2)}) collective-permute-start(bf16[192,1024]{1,0:T(8,128)(2,1)S(1)} %collective-permute-done.1.refs_0_), channel_id=1, source_target_pairs={{8,16},{12,20},{16,24},{20,28},{9,17},{13,21},{17,25},{21,29},{10,... | collective-permute-start | bytes 1179656 | tf_op jit(solution)/shard_map/ppermute | solution.py:473
  17.0 12.3 %collective-permute-start.4 = (bf16[192,1024]{1,0:T(8,128)(2,1)S(1)}, bf16[192,1024]{1,0:T(8,128)(2,1)S(1)}, u32[]{:S(2)}, u32[]{:S(2)}) collective-permute-start(bf16[192,1024]{1,0:T(8,128)(2,1)S(1)} %collective-permute-done.1.refs_0_), channel_id=1, source_target_pairs={{0,2},{1,3},{2,0},{3,1},{4,6},{5,7},{6,4},{7,5},{8,10},{9,11},{10,... | collective-permute-start | bytes 1179656 | tf_op jit(solution)/shard_map/ppermute | solution.py:404
  18.1 12.3 %collective-permute-start.8 = (bf16[192,1024]{1,0:T(8,128)(2,1)S(1)}, bf16[192,1024]{1,0:T(8,128)(2,1)S(1)}, u32[]{:S(2)}, u32[]{:S(2)}) collective-permute-start(bf16[192,1024]{1,0:T(8,128)(2,1)S(1)} %collective-permute-done.1.refs_0_), channel_id=1, source_target_pairs={{0,1},{1,0},{2,3},{3,2},{4,5},{5,4},{6,7},{7,6},{8,9},{9,8},{10,11... | collective-permute-start | bytes 1179656 | tf_op jit(solution)/shard_map/ppermute | solution.py:404
  20.1 2.9 %collective-permute-start = (s32[6,17]{1,0:T(8,128)S(1)}, s32[6,17]{1,0:T(8,128)S(1)}, u32[]{:S(2)}, u32[]{:S(2)}) collective-permute-start(s32[6,17]{1,0:T(8,128)S(1)} %pad_add_fusion.told_ref), channel_id=1, source_target_pairs={{0,4},{4,0},{8,12},{12,8},{16,20},{20,16},{24,28},{28,24},{1,5},{5... | collective-permute-start | bytes 1232 | tf_op jit(solution)/shard_map/ppermute | solution.py:404
  22.9 19.9 %collective-permute-start.10 = (bf16[256,1024]{1,0:T(8,128)(2,1)S(1)}, bf16[256,1024]{1,0:T(8,128)(2,1)S(1)}, u32[]{:S(2)}, u32[]{:S(2)}) collective-permute-start(bf16[256,1024]{1,0:T(8,128)(2,1)S(1)} %copy-done.4), channel_id=1, source_target_pairs={{0,1},{1,0},{2,3},{3,2},{4,5},{5,4},{6,7},{7,6},{8,9},{9,8},{10,11... | collective-permute-start | bytes 1572872 | tf_op jit(solution)/shard_map/ppermute | solution.py:404
  24.0 18.9 %collective-permute-start.11 = (bf16[256,1024]{1,0:T(8,128)(2,1)S(1)}, bf16[256,1024]{1,0:T(8,128)(2,1)S(1)}, u32[]{:S(2)}, u32[]{:S(2)}) collective-permute-start(bf16[256,1024]{1,0:T(8,128)(2,1)S(1)} %collective-permute-done.2.refs_4_), channel_id=1, source_target_pairs={{0,1},{1,0},{2,3},{3,2},{4,5},{5,4},{6,7},{7,6},{8,9},{9,8},{10,11... | collective-permute-start | bytes 1572872 | tf_op jit(solution)/shard_map/ppermute | solution.py:404
  24.0 1.0 %copy-start.2 = (bf16[768,256]{1,0:T(8,128)(2,1)S(1)}, bf16[768,256]{1,0:T(8,128)(2,1)}, u32[]{:S(2)}) copy-start(bf16[768,256]{1,0:T(8,128)(2,1)} %get-tuple-element.62.query_hbm.refs_5_) | copy-start | bytes 1179652
  25.0 1.0 %copy-start.5 = (bf16[256,768]{1,0:T(8,128)(2,1)S(1)}, bf16[256,768]{1,0:T(8,128)(2,1)}, u32[]{:S(2)}) copy-start(bf16[256,768]{1,0:T(8,128)(2,1)} %get-tuple-element.63.keys_t_hbm.refs_7_) | copy-start | bytes 1179652
  26.0 6.1 %copy-start = (bf16[4,1024,256]{2,1,0:T(8,128)(2,1)S(1)}, bf16[4,1024,256]{2,1,0:T(8,128)(2,1)}, u32[]{:S(2)}) copy-start(bf16[4,1024,256]{2,1,0:T(8,128)(2,1)} %refs_4_.3) | copy-start | bytes 6291460
  26.0 6.1 %copy-start.3 = (bf16[768,256]{1,0:T(8,128)(2,1)S(1)}, bf16[768,256]{1,0:T(8,128)(2,1)}, u32[]{:S(2)}) copy-start(bf16[768,256]{1,0:T(8,128)(2,1)} %get-tuple-element.62.query_hbm.refs_5_) | copy-start | bytes 1179652
  26.0 6.1 %copy-start.6 = (bf16[256,768]{1,0:T(8,128)(2,1)S(1)}, bf16[256,768]{1,0:T(8,128)(2,1)}, u32[]{:S(2)}) copy-start(bf16[256,768]{1,0:T(8,128)(2,1)} %get-tuple-element.63.keys_t_hbm.refs_7_) | copy-start | bytes 1179652
  29.3 2.4 %collective-permute-start.9 = (bf16[192,1024]{1,0:T(8,128)(2,1)S(1)}, bf16[192,1024]{1,0:T(8,128)(2,1)S(1)}, u32[]{:S(2)}, u32[]{:S(2)}) collective-permute-start(bf16[192,1024]{1,0:T(8,128)(2,1)S(1)} %collective-permute-done.4.refs_2_), channel_id=1, source_target_pairs={{0,1},{1,0},{2,3},{3,2},{4,5},{5,4},{6,7},{7,6},{8,9},{9,8},{10,11... | collective-permute-start | bytes 1179656 | tf_op jit(solution)/shard_map/ppermute | solution.py:404
  29.9 13.0 %collective-permute-start.7 = (bf16[192,1024]{1,0:T(8,128)(2,1)S(1)}, bf16[192,1024]{1,0:T(8,128)(2,1)S(1)}, u32[]{:S(2)}, u32[]{:S(2)}) collective-permute-start(bf16[192,1024]{1,0:T(8,128)(2,1)S(1)} %collective-permute-done.3.refs_0_), channel_id=1, source_target_pairs={{0,2},{1,3},{2,0},{3,1},{4,6},{5,7},{6,4},{7,5},{8,10},{9,11},{10,... | collective-permute-start | bytes 1179656 | tf_op jit(solution)/shard_map/ppermute | solution.py:404
  30.4 28.1 %collective-permute-start.14 = (bf16[1536,256]{1,0:T(8,128)(2,1)}, bf16[1536,256]{1,0:T(8,128)(2,1)S(1)}, u32[]{:S(2)}, u32[]{:S(2)}) collective-permute-start(bf16[1536,256]{1,0:T(8,128)(2,1)} %get-tuple-element.69.both_hbm.refs_8_), channel_id=1, source_target_pairs={{4,24},{5,25},{6,26},{7,27}} | collective-permute-start | bytes 2359304 | tf_op jit(solution)/shard_map/ppermute | solution.py:495
  31.7 11.5 %collective-permute-start.6 = (bf16[192,1024]{1,0:T(8,128)(2,1)S(1)}, bf16[192,1024]{1,0:T(8,128)(2,1)S(1)}, u32[]{:S(2)}, u32[]{:S(2)}) collective-permute-start(bf16[192,1024]{1,0:T(8,128)(2,1)S(1)} %collective-permute-done.3.refs_0_), channel_id=1, source_target_pairs={{0,1},{1,0},{2,3},{3,2},{4,5},{5,4},{6,7},{7,6},{8,9},{9,8},{10,11... | collective-permute-start | bytes 1179656 | tf_op jit(solution)/shard_map/ppermute | solution.py:404
  42.9 6.9 %copy-start.11 = (bf16[2,128,256]{2,1,0:T(8,128)(2,1)S(1)}, bf16[2,128,256]{2,1,0:T(8,128)(2,1)}, u32[]{:S(2)}) copy-start(bf16[2,128,256]{2,1,0:T(8,128)(2,1)} %get-tuple-element.77) | copy-start | bytes 393220
  42.9 8.2 %copy-start.7 = (bf16[768,256]{1,0:T(8,128)(2,1)S(1)}, bf16[768,256]{1,0:T(8,128)(2,1)}, u32[]{:S(2)}) copy-start(bf16[768,256]{1,0:T(8,128)(2,1)} %get-tuple-element.81.gate_hbm) | copy-start | bytes 1179652
  42.9 8.2 %copy-start.8 = (bf16[256]{0:T(256)(128)(2,1)S(1)}, bf16[256]{0:T(256)(128)(2,1)}, u32[]{:S(2)}) copy-start(bf16[256]{0:T(256)(128)(2,1)} %gain_ref.3) | copy-start | bytes 1540
  42.9 1.8 %collective-permute-start.12 = (bf16[192,1024]{1,0:T(8,128)(2,1)S(1)}, bf16[192,1024]{1,0:T(8,128)(2,1)S(1)}, u32[]{:S(2)}, u32[]{:S(2)}) collective-permute-start(bf16[192,1024]{1,0:T(8,128)(2,1)S(1)} %collective-permute-done.7.refs_2_), channel_id=1, source_target_pairs={{0,1},{1,0},{2,3},{3,2},{4,5},{5,4},{6,7},{7,6},{8,9},{9,8},{10,11... | collective-permute-start | bytes 1179656 | tf_op jit(solution)/shard_map/ppermute | solution.py:404
  49.7 13.4 %collective-permute-start.13 = (bf16[768,256]{1,0:T(8,128)(2,1)S(1)}, bf16[768,256]{1,0:T(8,128)(2,1)S(1)}, u32[]{:S(2)}, u32[]{:S(2)}) collective-permute-start(bf16[768,256]{1,0:T(8,128)(2,1)S(1)} %get-tuple-element.76), channel_id=1, source_target_pairs={{0,4},{4,0},{8,12},{12,8},{16,20},{20,16},{24,28},{28,24},{1,5},{5... | collective-permute-start | bytes 1179656 | tf_op jit(solution)/shard_map/ppermute | solution.py:404
  49.8 8.6 %collective-permute-start.15 = (bf16[2,128,256]{2,1,0:T(8,128)(2,1)S(1)}, bf16[2,128,256]{2,1,0:T(8,128)(2,1)S(1)}, u32[]{:S(2)}, u32[]{:S(2)}) collective-permute-start(bf16[2,128,256]{2,1,0:T(8,128)(2,1)S(1)} %copy-done.11), channel_id=1, source_target_pairs={{0,24},{4,28},{1,25},{5,29},{2,26},{6,30},{3,27},{7,31}} | collective-permute-start | bytes 393224 | tf_op jit(solution)/shard_map/ppermute | solution.py:478
  63.1 2.9 %copy-start.1 = (bf16[768,1024]{1,0:T(8,128)(2,1)S(1)}, bf16[768,1024]{1,0:T(8,128)(2,1)}, u32[]{:S(2)}) copy-start(bf16[768,1024]{1,0:T(8,128)(2,1)} %refs_6_.1) | copy-start | bytes 4718596
  63.6 2.4 %collective-permute-start.17 = (bf16[768,256]{1,0:T(8,128)(2,1)S(1)}, bf16[768,256]{1,0:T(8,128)(2,1)S(1)}, u32[]{:S(2)}, u32[]{:S(2)}) collective-permute-start(bf16[768,256]{1,0:T(8,128)(2,1)S(1)} %shard_map.80.refs_0_), channel_id=1, source_target_pairs={{0,1},{1,0},{2,3},{3,2},{4,5},{5,4},{6,7},{7,6},{8,9},{9,8},{10,11... | collective-permute-start | bytes 1179656 | tf_op jit(solution)/shard_map/ppermute | solution.py:404
  64.7 10.7 %collective-permute-start.16 = (bf16[768,256]{1,0:T(8,128)(2,1)S(1)}, bf16[768,256]{1,0:T(8,128)(2,1)S(1)}, u32[]{:S(2)}, u32[]{:S(2)}) collective-permute-start(bf16[768,256]{1,0:T(8,128)(2,1)S(1)} %shard_map.80.refs_0_), channel_id=1, source_target_pairs={{0,2},{1,3},{2,0},{3,1},{4,6},{5,7},{6,4},{7,5},{8,10},{9,11},{10,... | collective-permute-start | bytes 1179656 | tf_op jit(solution)/shard_map/ppermute | solution.py:404
  75.3 2.2 %collective-permute-start.18 = (bf16[768,256]{1,0:T(8,128)(2,1)S(1)}, bf16[768,256]{1,0:T(8,128)(2,1)S(1)}, u32[]{:S(2)}, u32[]{:S(2)}) collective-permute-start(bf16[768,256]{1,0:T(8,128)(2,1)S(1)} %collective-permute-done.16.refs_0_), channel_id=1, source_target_pairs={{0,1},{1,0},{2,3},{3,2},{4,5},{5,4},{6,7},{7,6},{8,9},{9,8},{10,11... | collective-permute-start | bytes 1179656 | tf_op jit(solution)/shard_map/ppermute | solution.py:404
